TPU v7x, 32 devices: a whole 2x2x4 slice. The times are simulated.
32 devices in a mesh: row: 8 (over z, x), panel: 4 (over y, core).
Axes of the slice: x: 2, y: 2, z: 4, core: 2. Of those that a mesh axis runs over, the one named last changes fastest.
Arguments:
- pixel_ids: int32 [8192], P('row'), may hold values from 0 to 8191, each once
- quad_offsets: int32 [2, 16, 8192], P(None, None, 'row'), may hold values from 0 to 7
- prior_factor: float32 [8192, 2048], P('row', 'panel'), may hold values from -0.036 to 0.036, as said below
Outputs:
- panel_factor: float32 [8192, 1024], P(('row', 'panel'))
Inputs may be any that keep to these rules, and one draw needn't show every extreme that they name: `pixel_ids`: each pixel of the grid appears in exactly one row. `prior_factor`: schur[panel_index] is positive definite.
All inputs are finite; a program needn't handle non-finite values.
Results may differ from a plain program's by a relative error of at most 0.0003.
Values sent between devices are 32-bit elements; how exact they have to be, the bound alone decides.
No kernel may reach another device: no remote copies, remote signals or barrier semaphores. Data moves between devices by JAX's collectives and lax.ppermute only.
A program may use at most 128 MiB of HBM per device.

v0:
```python
import functools

import jax
import jax.numpy as jnp
from jax import lax
from jax.experimental import pallas as pl
from jax.experimental.pallas import tpu as pltpu
from jax.sharding import PartitionSpec as P

B = 1024
NB = 128
GROUP = 8
F32 = jnp.float32
BF = jnp.bfloat16
NT = (((1,), (1,)), ((), ()))
SCALE = -1.4426950408889634 / 64.0
CENTRE = 1024.0


def locate(pixel_ids, quad_offsets):
    column = (pixel_ids % 256) * 8
    lines = (pixel_ids // 256) * 8
    east = (column[None, :] + quad_offsets[0]).astype(F32) - CENTRE
    north = (lines[None, :] + quad_offsets[1]).astype(F32) - CENTRE
    return east, north


def pieces(value):
    high = jnp.floor(value * (1.0 / 65536.0)) * 65536.0
    rest = value - high
    mid = jnp.floor(rest * (1.0 / 256.0)) * 256.0
    return [high, mid, rest - mid]


def halves(value):
    high = jnp.floor(value * (1.0 / 128.0)) * 128.0
    return high, value - high


def row_features(x, y):
    xh, xl = halves(x)
    yh, yl = halves(y)
    one = jnp.ones_like(x)
    zero = jnp.zeros_like(x)
    cross = [-2 * xh, -2 * xh, -2 * xl, -2 * xl, -2 * yh, -2 * yh, -2 * yl, -2 * yl]
    return jnp.concatenate(cross + pieces(x * x + y * y) + [one] * 3 + [zero] * 2, 0)


def col_features(x, y):
    xh, xl = halves(x)
    yh, yl = halves(y)
    one = jnp.ones_like(x)
    zero = jnp.zeros_like(x)
    cross = [xh, xl, xh, xl, yh, yl, yh, yl]
    return jnp.concatenate(cross + [one] * 3 + pieces(x * x + y * y) + [zero] * 2, 0)


def cover_kernel(row_ref, col_ref, o_ref, f_ref, g_ref, *, block):
    count, rows = row_ref.shape[1:]

    for a in range(count):
        one = row_features(row_ref[0, a : a + 1, :], row_ref[1, a : a + 1, :])
        f_ref[a] = one.T.astype(BF)
        g_ref[a] = col_features(col_ref[0, a : a + 1, :], col_ref[1, a : a + 1, :]).astype(BF)

    def tile(index, _):
        first = pl.multiple_of(index * block, block)
        rows_here = jnp.concatenate([f_ref[a, pl.ds(first, block)] for a in range(count)], 0)

        def column_point(b, total):
            apart = jnp.dot(rows_here, g_ref[b], preferred_element_type=F32)
            near = jnp.exp2(apart * SCALE)
            for a in range(count):
                total = total + near[a * block : (a + 1) * block]
            return total

        total = lax.fori_loop(0, count, column_point, jnp.zeros((block, o_ref.shape[1]), F32))
        o_ref[pl.ds(first, block)] = total * (1.0 / (count * count))
        return 0

    lax.fori_loop(0, rows // block, tile, 0)


def cover_rows(row_points, col_points):
    count, rows = row_points.shape[1:]
    cols = col_points.shape[2]
    return pl.pallas_call(
        functools.partial(cover_kernel, block=32),
        out_shape=jax.ShapeDtypeStruct((rows, cols), F32),
        in_specs=[pl.BlockSpec(memory_space=pltpu.VMEM)] * 2,
        out_specs=pl.BlockSpec(memory_space=pltpu.VMEM),
        scratch_shapes=[pltpu.VMEM((count, rows, 16), BF), pltpu.VMEM((count, 16, cols), BF)],
        compiler_params=pltpu.CompilerParams(vmem_limit_bytes=32 << 20),
        name="cover",
    )(row_points, col_points)


def inverse_factor(tiles):
    width = 8 * len(tiles)
    lane = lax.broadcasted_iota(jnp.int32, (8, width), 1)
    sub = lax.broadcasted_iota(jnp.int32, (8, width), 0)
    tiles = list(tiles)
    n = len(tiles)
    out = []
    for v in range(n):
        pivots = jnp.ones((8, width), F32)
        for g in range(0, 8, GROUP):
            cols = [
                [
                    jnp.broadcast_to(tiles[r][:, 8 * v + g + q : 8 * v + g + q + 1], (8, width))
                    for q in range(GROUP)
                ]
                for r in range(v, n)
            ]
            for q in range(GROUP):
                s = g + q
                p = 8 * v + s
                pivot = jnp.broadcast_to(cols[0][q][s : s + 1], (8, width))
                inverse = 1.0 / pivot
                pivots = jnp.where(sub == s, pivot, pivots)
                row = jnp.where(lane == p, 1.0, jnp.broadcast_to(tiles[v][s : s + 1], (8, width)))
                heads = [
                    jnp.broadcast_to(cols[0][k][s : s + 1], (8, width)) for k in range(q + 1, GROUP)
                ]
                for r in range(v, n):
                    part = cols[r - v][q] * inverse
                    if r == v:
                        part = jnp.where(sub > s, part, 0.0)
                    tiles[r] = jnp.where(lane == p, 0.0, tiles[r]) - part * row
                    for k in range(q + 1, GROUP):
                        cols[r - v][k] = cols[r - v][k] - part * heads[k - q - 1]
        row_id = sub + 8 * v
        unit = jnp.where(lane == row_id, 1.0, 0.0)
        out.append(jnp.where(lane < row_id, tiles[v], unit) * lax.rsqrt(pivots))
    return jnp.concatenate(out, 0)


def split(x):
    high = x.astype(BF)
    return high, (x - high.astype(F32)).astype(BF)


def dot3(ah, al, bh, bl):
    dot = functools.partial(lax.dot_general, dimension_numbers=NT, preferred_element_type=F32)
    return dot(ah, bh) + (dot(ah, bl) + dot(al, bh))


def factor_solve_kernel(diag_ref, rest_ref, o_ref, a_ref, high_ref, low_ref):
    n = diag_ref.shape[0]
    m = rest_ref.shape[0]
    a_ref[0:n] = diag_ref[...]
    a_ref[n : n + m] = rest_ref[...]
    blocks = (n + m) // NB

    def step(j, _):
        c = pl.multiple_of(j * NB, NB)
        tiles = [a_ref[pl.ds(c + 8 * v, 8), pl.ds(c, NB)] for v in range(NB // 8)]
        wh, wl = split(inverse_factor(tiles))

        def panel(i, _):
            r = pl.multiple_of(i * NB, NB)
            bh, bl = split(a_ref[pl.ds(r, NB), pl.ds(c, NB)])
            part = dot3(bh, bl, wh, wl)
            a_ref[pl.ds(r, NB), pl.ds(c, NB)] = part
            high, low = split(part)
            high_ref[pl.ds(r, NB)] = high
            low_ref[pl.ds(r, NB)] = low
            return 0

        lax.fori_loop(j + 1, blocks, panel, 0)
        o_ref[:, pl.ds(c, NB)] = a_ref[n : n + m, pl.ds(c, NB)]

        def trail(i, _):
            r = pl.multiple_of(i * NB, NB)
            a_ref[pl.ds(r, NB)] = a_ref[pl.ds(r, NB)] - dot3(
                high_ref[pl.ds(r, NB)], low_ref[pl.ds(r, NB)], high_ref[0:n], low_ref[0:n]
            )
            return 0

        lax.fori_loop(j + 1, blocks, trail, 0)
        return 0

    lax.fori_loop(0, n // NB, step, 0)


def factor_solve(diag_rows, schur):
    n = diag_rows.shape[0]
    m = schur.shape[0]
    return pl.pallas_call(
        factor_solve_kernel,
        out_shape=jax.ShapeDtypeStruct((m, n), F32),
        in_specs=[pl.BlockSpec(memory_space=pltpu.VMEM)] * 2,
        out_specs=pl.BlockSpec(memory_space=pltpu.VMEM),
        scratch_shapes=[
            pltpu.VMEM((n + m, n), F32),
            pltpu.VMEM((n + m, NB), BF),
            pltpu.VMEM((n + m, NB), BF),
        ],
        compiler_params=pltpu.CompilerParams(vmem_limit_bytes=40 << 20),
        name="factor_solve",
    )(diag_rows, schur)


def local(pixel_ids, quad_offsets, prior_factor):
    panel_count = lax.axis_size("panel")
    row_count = lax.axis_size("row")
    block_rows = pixel_ids.shape[0]
    quarter_rows = block_rows // panel_count
    per_device = B // (row_count * panel_count)
    span_cols = panel_count * per_device
    row_pos = lax.axis_index("row")
    panel_pos = lax.axis_index("panel")
    points = jnp.stack(locate(pixel_ids, quad_offsets))
    count = points.shape[1]
    own_points = lax.dynamic_slice_in_dim(points, panel_pos * quarter_rows, quarter_rows, 2)
    local_points = points.reshape(2, count, panel_count, quarter_rows)[:, :, :, :per_device]
    local_points = local_points.reshape(1, 2 * count, span_cols)
    copies = jnp.broadcast_to(local_points, (row_count, 2 * count, span_cols))
    spread = lax.all_to_all(copies, "row", split_axis=0, concat_axis=0, tiled=True)
    panel_points = spread.transpose(1, 0, 2).reshape(2, count, B)
    columns = cover_rows(own_points, panel_points)
    device_pos = row_pos * panel_count + panel_pos
    row_ids = jnp.arange(quarter_rows, dtype=jnp.int32)[:, None]
    col_ids = jnp.arange(B, dtype=jnp.int32)[None, :]
    on_diagonal = (row_ids < per_device) & (col_ids == device_pos * per_device + row_ids)
    cover = columns + jnp.where(on_diagonal, 1.0, 0.0).astype(F32)
    whole_rows = lax.all_to_all(prior_factor, "panel", split_axis=0, concat_axis=1, tiled=True)
    panel_prior = lax.all_gather(whole_rows[:per_device], ("row", "panel"), axis=0, tiled=True)
    update = jnp.dot(
        whole_rows, panel_prior.T, precision=lax.Precision.HIGH, preferred_element_type=F32
    )
    schur = cover - update
    diag_rows = lax.all_gather(schur[:per_device], ("row", "panel"), axis=0, tiled=True)
    return factor_solve(diag_rows, schur)


def solution(mesh):
    return jax.shard_map(
        local,
        mesh=mesh,
        in_specs=(P("row"), P(None, None, "row"), P("row", "panel")),
        out_specs=P(("row", "panel"), None),
        check_vma=False,
    )
```

profile of v0, /device:TPU:0, one launch (start us, length us, event | category | flops | bytes accessed | tf_op | source)
XLA Modules:
  0.0 257.3 jit_solution(15846834757688807662)
XLA Ops:
  6.5 0.0 all-gather.3.cloned.1.call-start
  6.5 0.0 copy-start.3
  6.5 0.0 copy-start.2
  6.5 30.1 %all_to_all.24 = f32[4,256,512]{2,1,0:T(8,128)S(1)} all-to-all(f32[4,256,512]{2,1,0:T(8,128)} %bitcast.12), channel_id=1, replica_groups=mesh['row'=8,'panel'=4] {'panel'}, dimensions={0} | all-to-all | bytes 4194304 | tf_op jit(solution)/shard_map/all_to_all | solution.py:227
  36.6 0.0 copy-start.1
  36.6 1.4 copy-done.1
  38.0 0.7 copy.10
  38.7 0.0 all-gather.3.cloned.1.call-update
  38.7 0.0 copy-done.3
  38.8 0.0 copy-done.2
  38.9 0.1 broadcast_in_dim.19
  39.0 0.7 broadcast_in_dim.20
  39.7 6.6 %all-to-all-start = ((f32[8,32,128]{2,1,0:T(8,128)}), f32[8,32,128]{2,1,0:T(8,128)S(1)}, u32[]{:S(2)}, u32[]{:S(2)}) async-start(f32[8,32,128]{2,1,0:T(8,128)} %broadcast_in_dim.20), calls=%async_computation | async-start | bytes 262144 | tf_op jit(solution)/shard_map/all_to_all | solution.py:219
  46.3 0.0 all-gather.5.cloned.1.call-start
  46.4 7.3 %all-to-all-done = f32[8,32,128]{2,1,0:T(8,128)S(1)} async-done(((f32[8,32,128]{2,1,0:T(8,128)}), f32[8,32,128]{2,1,0:T(8,128)S(1)}, u32[]{:S(2)}, u32[]{:S(2)}) %all-to-all-start) | async-done | bytes 131104 | tf_op jit(solution)/shard_map/all_to_all | solution.py:219
  53.7 0.1 copy.7
  53.8 54.8 %cover.1 = f32[256,1024]{1,0:T(8,128)S(1)} custom-call(f32[2,16,256]{2,1,0:T(8,128)S(1)} %fusion.1.row_ref, f32[2,16,1024]{2,1,0:T(8,128)S(1)} %reshape.36.col_ref), custom_call_target="tpu_custom_call" | custom-call | tf_op jit(solution)/shard_map/cover/pallas_call | solution.py:87
  108.6 2.9 %copy.8 = f32[256,4,512]{0,2,1:T(8,128)} copy(f32[256,4,512]{2,0,1:T(8,128)} %bitcast.10) | data formatting | bytes 4194304 | tf_op jit(solution)/shard_map/all_to_all | solution.py:227
  111.5 7.0 %all-gather.3.cloned.1.call-done = f32[1024,2048]{1,0:T(8,128)} async-done(((f32[32,2048]{1,0:T(8,128)}), f32[1024,2048]{1,0:T(8,128)}) %all-gather.3.cloned.1.call-update) | async-done | bytes 8388624 | tf_op jit(solution)/shard_map/all_gather | solution.py:228
  118.6 10.0 %convolution_subtract_fusion.rest_ref = f32[256,1024]{1,0:T(8,128)S(1)} fusion(f32[256,2048]{0,1:T(8,128)} %bitcast.11, f32[1024,2048]{1,0:T(8,128)} %all-gather.3.cloned.1.call-done, f32[256,1024]{1,0:T(8,128)S(1)} %cover.1, s32[256]{0:T(256)S(1)} %iota_add_fusion, pred[256]{0:T(512)(128)(4,1)S(1)} %iota_compare_fusion.1), kind=kOutput, calls=%fused_computation | convolution fusion | flops 3222536192 | bytes 12584192 | tf_op jit(solution)/shard_map/dot_general | solution.py:229
  128.6 0.7 slice.25
  129.3 0.0 all-gather.5.cloned.1.call-update
  129.3 60.5 %all-gather.5.cloned.1.call-done.diag_ref = f32[1024,1024]{1,0:T(8,128)} async-done(((f32[32,1024]{1,0:T(8,128)}), f32[1024,1024]{1,0:T(8,128)}) %all-gather.5.cloned.1.call-update) | async-done | bytes 4194320 | tf_op jit(solution)/shard_map/all_gather | solution.py:233
  189.8 0.0 copy-start
  189.8 2.2 copy-done
  192.0 58.5 %factor_solve.1 = f32[256,1024]{1,0:T(8,128)} custom-call(f32[1024,1024]{1,0:T(8,128)S(1)} %copy-done, f32[256,1024]{1,0:T(8,128)S(1)} %convolution_subtract_fusion.rest_ref), custom_call_target="tpu_custom_call" | custom-call | tf_op jit(solution)/shard_map/factor_solve/pallas_call | solution.py:189
  (10 shorter events, 0.2 us)
Async XLA Ops:
  6.5 112.0 %all-gather.3.cloned.1.call-start = ((), (), s32[]{:S(2)}) async-start(), calls=%async_computation.2 | async-start | bytes 8650752 | tf_op jit(solution)/shard_map/all_gather | solution.py:228
  6.5 32.2 %copy-start.3 = (s32[1024]{0:T(1024)S(1)}, s32[1024]{0:T(1024)}, u32[]{:S(2)}) copy-start(s32[1024]{0:T(1024)} %param.3) | copy-start | bytes 12292
  6.5 32.2 %copy-start.2 = (s32[2,16,1024]{2,1,0:T(8,128)S(1)}, s32[2,16,1024]{2,1,0:T(8,128)}, u32[]{:S(2)}) copy-start(s32[2,16,1024]{2,1,0:T(8,128)} %param.4) | copy-start | bytes 393220
  36.6 1.4 copy-start.1
  39.7 14.0 %all-to-all-start = ((f32[8,32,128]{2,1,0:T(8,128)}), f32[8,32,128]{2,1,0:T(8,128)S(1)}, u32[]{:S(2)}, u32[]{:S(2)}) async-start(f32[8,32,128]{2,1,0:T(8,128)} %broadcast_in_dim.20), calls=%async_computation | async-start | bytes 262144 | tf_op jit(solution)/shard_map/all_to_all | solution.py:219
  46.3 143.6 %all-gather.5.cloned.1.call-start = ((), (), s32[]{:S(2)}) async-start(), calls=%async_computation.3 | async-start | bytes 4325376 | tf_op jit(solution)/shard_map/all_gather | solution.py:233
  189.8 2.2 copy-start
Sparse Core Ops, SparseCore 0:
  38.9 79.6 all-gather.2
  129.4 60.3 all-gather.4
where the time goes:
time: 258 us; the launch traced here: 257 us
  Pallas kernels  113 us (44%)
  waiting for transfers between devices  74.9 us (29%)
  blocking collectives  30.1 us (12%)
  between operations  13.5 us (5%)
  matrix products  10 us (4%)
  local copies, waits for them, and re-layouts  8.81 us (3%)
  starting transfers between devices  6.63 us (3%)
    all_gather x1, waiting for transfers between devices, local(): lax.all_gather(schur[:per_device], ('row', 'panel'), axis=0, tiled=True)  60.5 us
    pallas_call x1, Pallas kernels, factor_solve(): pl.pallas_call(factor_solve_kernel, out_shape=jax.ShapeDtypeStruct((m, n)...  58.5 us
    pallas_call x1, Pallas kernels, cover_rows(): pl.pallas_call(functools.partial(cover_kernel, block=32), out_shape=jax.S...  54.8 us
    all_to_all x1, blocking collectives, local(): lax.all_to_all(prior_factor, 'panel', split_axis=0, concat_axis=1, tiled=...  30.1 us
    dot_general x1, matrix products, local(): jnp.dot(whole_rows, panel_prior.T, precision=lax.Precision.HIGH, preferre...  10 us
    all_to_all x1, waiting for transfers between devices, local(): lax.all_to_all(copies, 'row', split_axis=0, concat_axis=0, tiled=True)  7.34 us
    all_gather x1, waiting for transfers between devices, local(): lax.all_gather(whole_rows[:per_device], ('row', 'panel'), axis=0, tiled=T...  7.05 us
    all_to_all x1, starting transfers between devices, local(): lax.all_to_all(copies, 'row', split_axis=0, concat_axis=0, tiled=True)  6.59 us
  transfers between devices with their start and end apart: 3, of which 3 were waited for; matrix products, arithmetic and copies ran while one was open for 2% of the time, Pallas kernels for 21%

commit v1 on v0

v1 whole, which is shorter than its diff:
```python
import functools

import jax
import jax.numpy as jnp
from jax import lax
from jax.experimental import pallas as pl
from jax.experimental.pallas import tpu as pltpu
from jax.sharding import PartitionSpec as P

B = 1024
NB = 128
GROUP = 8
F32 = jnp.float32
BF = jnp.bfloat16
NT = (((1,), (1,)), ((), ()))
SCALE = -1.4426950408889634 / 64.0
CENTRE = 1024.0


def locate(pixel_ids, quad_offsets):
    column = (pixel_ids % 256) * 8
    lines = (pixel_ids // 256) * 8
    east = (column[None, :] + quad_offsets[0]).astype(F32) - CENTRE
    north = (lines[None, :] + quad_offsets[1]).astype(F32) - CENTRE
    return east, north


def pieces(value):
    high = jnp.floor(value * (1.0 / 65536.0)) * 65536.0
    rest = value - high
    mid = jnp.floor(rest * (1.0 / 256.0)) * 256.0
    return [high, mid, rest - mid]


def halves(value):
    high = jnp.floor(value * (1.0 / 128.0)) * 128.0
    return high, value - high


def row_features(x, y):
    xh, xl = halves(x)
    yh, yl = halves(y)
    one = jnp.ones_like(x)
    zero = jnp.zeros_like(x)
    cross = [-2 * xh, -2 * xh, -2 * xl, -2 * xl, -2 * yh, -2 * yh, -2 * yl, -2 * yl]
    return jnp.concatenate(cross + pieces(x * x + y * y) + [one] * 3 + [zero] * 2, 0)


def col_features(x, y):
    xh, xl = halves(x)
    yh, yl = halves(y)
    one = jnp.ones_like(x)
    zero = jnp.zeros_like(x)
    cross = [xh, xl, xh, xl, yh, yl, yh, yl]
    return jnp.concatenate(cross + [one] * 3 + pieces(x * x + y * y) + [zero] * 2, 0)


def feature_kernel(row_ref, col_ref, f_ref, g_ref):
    for a in range(row_ref.shape[1]):
        one = row_features(row_ref[0, a : a + 1, :], row_ref[1, a : a + 1, :])
        f_ref[a] = one.T.astype(BF)
        g_ref[a] = col_features(col_ref[0, a : a + 1, :], col_ref[1, a : a + 1, :]).astype(BF)


def features(row_points, col_points):
    count, rows = row_points.shape[1:]
    cols = col_points.shape[2]
    return pl.pallas_call(
        feature_kernel,
        out_shape=[
            jax.ShapeDtypeStruct((count, rows, 16), BF),
            jax.ShapeDtypeStruct((count, 16, cols), BF),
        ],
        in_specs=[pl.BlockSpec(memory_space=pltpu.VMEM)] * 2,
        out_specs=[pl.BlockSpec(memory_space=pltpu.VMEM)] * 2,
        compiler_params=pltpu.CompilerParams(vmem_limit_bytes=8 << 20),
        name="features",
    )(row_points, col_points)


def cover_kernel(f_ref, g_ref, o_ref):
    count, block = f_ref.shape[:2]
    rows_here = f_ref[...].reshape(count * block, 16)

    def column_point(b, total):
        apart = jnp.dot(rows_here, g_ref[b], preferred_element_type=F32)
        near = jnp.exp2(apart * SCALE)
        for a in range(count):
            total = total + near[a * block : (a + 1) * block]
        return total

    total = lax.fori_loop(0, count, column_point, jnp.zeros(o_ref.shape, F32))
    o_ref[...] = total * (1.0 / (count * count))


def cover_rows(row_part, col_part, first, block):
    count, rows, depth = row_part.shape
    cols = col_part.shape[2]
    index = first // block
    return pl.pallas_call(
        cover_kernel,
        grid=(1,),
        out_shape=jax.ShapeDtypeStruct((block, cols), F32),
        in_specs=[
            pl.BlockSpec((count, block, depth), lambda i: (0, index, 0)),
            pl.BlockSpec((count, depth, cols), lambda i: (0, 0, 0)),
        ],
        out_specs=pl.BlockSpec((block, cols), lambda i: (0, 0)),
        compiler_params=pltpu.CompilerParams(vmem_limit_bytes=16 << 20),
        cost_estimate=pl.CostEstimate(
            flops=7 * 10**9, bytes_accessed=1 << 20, transcendentals=count * count * block * cols
        ),
        name="cover",
    )(row_part, col_part)


def inverse_factor(tiles):
    width = 8 * len(tiles)
    lane = lax.broadcasted_iota(jnp.int32, (8, width), 1)
    sub = lax.broadcasted_iota(jnp.int32, (8, width), 0)
    tiles = list(tiles)
    n = len(tiles)
    out = []
    for v in range(n):
        pivots = jnp.ones((8, width), F32)
        for g in range(0, 8, GROUP):
            cols = [
                [
                    jnp.broadcast_to(tiles[r][:, 8 * v + g + q : 8 * v + g + q + 1], (8, width))
                    for q in range(GROUP)
                ]
                for r in range(v, n)
            ]
            for q in range(GROUP):
                s = g + q
                p = 8 * v + s
                pivot = jnp.broadcast_to(cols[0][q][s : s + 1], (8, width))
                inverse = 1.0 / pivot
                pivots = jnp.where(sub == s, pivot, pivots)
                row = jnp.where(lane == p, 1.0, jnp.broadcast_to(tiles[v][s : s + 1], (8, width)))
                heads = [
                    jnp.broadcast_to(cols[0][k][s : s + 1], (8, width)) for k in range(q + 1, GROUP)
                ]
                for r in range(v, n):
                    part = cols[r - v][q] * inverse
                    if r == v:
                        part = jnp.where(sub > s, part, 0.0)
                    tiles[r] = jnp.where(lane == p, 0.0, tiles[r]) - part * row
                    for k in range(q + 1, GROUP):
                        cols[r - v][k] = cols[r - v][k] - part * heads[k - q - 1]
        row_id = sub + 8 * v
        unit = jnp.where(lane == row_id, 1.0, 0.0)
        out.append(jnp.where(lane < row_id, tiles[v], unit) * lax.rsqrt(pivots))
    return jnp.concatenate(out, 0)


def split(x):
    high = x.astype(BF)
    return high, (x - high.astype(F32)).astype(BF)


def dot3(ah, al, bh, bl):
    dot = functools.partial(lax.dot_general, dimension_numbers=NT, preferred_element_type=F32)
    return dot(ah, bh) + (dot(ah, bl) + dot(al, bh))


def factor_blocks(a_ref, lh_ref, ll_ref, wh_ref, wl_ref):
    n = a_ref.shape[0]
    blocks = n // NB

    def step(j, _):
        c = pl.multiple_of(j * NB, NB)
        tiles = [a_ref[pl.ds(c + 8 * v, 8), pl.ds(c, NB)] for v in range(NB // 8)]
        wh, wl = split(inverse_factor(tiles))
        wh_ref[pl.ds(c, NB)] = wh
        wl_ref[pl.ds(c, NB)] = wl

        def panel(i, _):
            r = pl.multiple_of(i * NB, NB)
            bh, bl = split(a_ref[pl.ds(r, NB), pl.ds(c, NB)])
            high, low = split(dot3(bh, bl, wh, wl))
            lh_ref[pl.ds(r, NB), pl.ds(c, NB)] = high
            ll_ref[pl.ds(r, NB), pl.ds(c, NB)] = low
            return 0

        lax.fori_loop(j + 1, blocks, panel, 0)

        def trail(i, _):
            r = pl.multiple_of(i * NB, NB)
            a_ref[pl.ds(r, NB)] = a_ref[pl.ds(r, NB)] - dot3(
                lh_ref[pl.ds(r, NB), pl.ds(c, NB)],
                ll_ref[pl.ds(r, NB), pl.ds(c, NB)],
                lh_ref[:, pl.ds(c, NB)],
                ll_ref[:, pl.ds(c, NB)],
            )
            return 0

        lax.fori_loop(j + 1, blocks, trail, 0)
        return 0

    lax.fori_loop(0, blocks, step, 0)


def factor_kernel(diag_ref, lh_ref, ll_ref, wh_ref, wl_ref, a_ref):
    a_ref[...] = diag_ref[...]
    lh_ref[...] = jnp.zeros_like(lh_ref)
    ll_ref[...] = jnp.zeros_like(ll_ref)
    factor_blocks(a_ref, lh_ref, ll_ref, wh_ref, wl_ref)


def fold_block(r, k):
    if k < 2:
        return r ^ (4 * k)
    m = k - 1
    low = r & 3
    second = (low >> (m.bit_length() - 1)) & 1
    return (r ^ m) ^ (4 * second)


def unfold_kernel(place_ref, here_ref, there_ref, lh_ref, ll_ref, wh_ref, wl_ref, a_ref):
    row_pos = place_ref[0]
    panel_pos = place_ref[1]
    per_device = here_ref.shape[1]
    lh_ref[...] = jnp.zeros_like(lh_ref)
    ll_ref[...] = jnp.zeros_like(ll_ref)

    def rows_of(r, _):
        away = r ^ row_pos
        slot = ((away >> 1) & 1) | (((away >> 2) & 1) << 1) | ((away & 1) << 2)
        low = r & 3
        for k in range(5):
            parts = []
            for p in range(4):
                gone = p ^ panel_pos
                at = slot | ((gone >> 1) << 3)
                parts.append((at, gone & 1))
            picked = [
                jnp.where(core == 0, here_ref[at, :, NB * k : NB * k + NB], there_ref[at, :, NB * k : NB * k + NB])
                for at, core in parts
            ]
            block = jnp.concatenate(picked, 0)
            if k < 2:
                s = r ^ (4 * k)
            else:
                m = k - 1
                second = (low >> (m.bit_length() - 1)) & 1
                s = (r ^ m) ^ (4 * second)
            rr = pl.multiple_of(r * NB, NB)
            ss = pl.multiple_of(s * NB, NB)

            @pl.when(r >= s)
            def _():
                a_ref[pl.ds(rr, NB), pl.ds(ss, NB)] = block

            if k >= 2:

                @pl.when(r < s)
                def _():
                    a_ref[pl.ds(ss, NB), pl.ds(rr, NB)] = block.T

        return 0

    lax.fori_loop(0, 8, rows_of, 0)
    factor_blocks(a_ref, lh_ref, ll_ref, wh_ref, wl_ref)


def factor(kernel, operands, n):
    in_specs = [pl.BlockSpec(memory_space=pltpu.VMEM)] * len(operands)
    if kernel is unfold_kernel:
        in_specs[0] = pl.BlockSpec(memory_space=pltpu.SMEM)
    return pl.pallas_call(
        kernel,
        out_shape=[jax.ShapeDtypeStruct((n, n), BF)] * 2 + [jax.ShapeDtypeStruct((n, NB), BF)] * 2,
        in_specs=in_specs,
        out_specs=[pl.BlockSpec(memory_space=pltpu.VMEM)] * 4,
        scratch_shapes=[pltpu.VMEM((n, n), F32)],
        compiler_params=pltpu.CompilerParams(vmem_limit_bytes=32 << 20),
        cost_estimate=pl.CostEstimate(flops=5 * 10**10, bytes_accessed=8 << 20, transcendentals=0),
        name="factor",
    )(*operands)


def solve_kernel(*refs):
    covers, (parts_ref, lh_ref, ll_ref, wh_ref, wl_ref, o_ref, xh_ref, xl_ref) = refs[:-8], refs[-8:]
    n = o_ref.shape[1]
    first = 0
    for ref in covers:
        rows = pl.ds(first, ref.shape[0])
        taken = parts_ref[0, rows]
        for p in range(1, parts_ref.shape[0]):
            taken = taken + parts_ref[p, rows]
        o_ref[rows] = ref[...] - taken
        first += ref.shape[0]
    for c in range(0, n, NB):
        here = o_ref[:, c : c + NB]
        if c:
            here = here - dot3(
                xh_ref[:, :c], xl_ref[:, :c], lh_ref[c : c + NB, :c], ll_ref[c : c + NB, :c]
            )
        bh, bl = split(here)
        x = dot3(bh, bl, wh_ref[c : c + NB], wl_ref[c : c + NB])
        o_ref[:, c : c + NB] = x
        xh, xl = split(x)
        xh_ref[:, c : c + NB] = xh
        xl_ref[:, c : c + NB] = xl


def solve(covers, parts, factors):
    rows = sum(c.shape[0] for c in covers)
    n = covers[0].shape[1]
    operands = (*covers, parts, *factors)
    return pl.pallas_call(
        solve_kernel,
        out_shape=jax.ShapeDtypeStruct((rows, n), F32),
        in_specs=[pl.BlockSpec(memory_space=pltpu.VMEM)] * len(operands),
        out_specs=pl.BlockSpec(memory_space=pltpu.VMEM),
        scratch_shapes=[pltpu.VMEM((rows, n), BF)] * 2,
        compiler_params=pltpu.CompilerParams(vmem_limit_bytes=32 << 20),
        name="solve",
    )(*operands)


def swap(block, axis, bit):
    return lax.ppermute(block, axis, [(i, i ^ bit) for i in range(lax.axis_size(axis))])


def dot_rows(left, right):
    return lax.dot_general(
        left, right, NT, precision=lax.Precision.HIGH, preferred_element_type=F32
    )


def local(pixel_ids, quad_offsets, prior_factor):
    panel_count = lax.axis_size("panel")
    row_count = lax.axis_size("row")
    block_rows = pixel_ids.shape[0]
    quarter_rows = block_rows // panel_count
    per_device = B // (row_count * panel_count)
    span_cols = panel_count * per_device
    row_pos = lax.axis_index("row")
    panel_pos = lax.axis_index("panel")
    device_pos = row_pos * panel_count + panel_pos
    lead = 32

    points = jnp.stack(locate(pixel_ids, quad_offsets))
    count = points.shape[1]
    own_points = lax.dynamic_slice_in_dim(points, panel_pos * quarter_rows, quarter_rows, 2)
    local_points = points.reshape(2, count, panel_count, quarter_rows)[:, :, :, :per_device]
    local_points = local_points.reshape(1, 2 * count, span_cols)

    row_ids = jnp.arange(lead, dtype=jnp.int32)[:, None]
    col_ids = jnp.arange(B, dtype=jnp.int32)[None, :]
    on_diagonal = (row_ids < per_device) & (col_ids == device_pos * per_device + row_ids)
    unit = jnp.where(on_diagonal, 1.0, 0.0).astype(F32)

    def covers_of(panel_points):
        row_part, col_part = features(own_points, panel_points)
        tiles = [cover_rows(row_part, col_part, i, lead) for i in range(0, quarter_rows, lead)]
        return [tiles[0] + unit] + tiles[1:]

    own_prior = prior_factor.reshape(panel_count, quarter_rows, -1)[:, :per_device]
    own_prior = own_prior.reshape(span_cols, -1)

    if not (span_cols == NB and row_count == 8 and panel_count == 4):
        copies = jnp.broadcast_to(local_points, (row_count, 2 * count, span_cols))
        spread = lax.all_to_all(copies, "row", split_axis=0, concat_axis=0, tiled=True)
        covers = covers_of(spread.transpose(1, 0, 2).reshape(2, count, B))
        panel_prior = lax.all_gather(own_prior, "row", axis=0, tiled=True)
        partial = dot_rows(prior_factor, panel_prior)
        parts = lax.all_to_all(
            partial.reshape(panel_count, quarter_rows, B), "panel", split_axis=0, concat_axis=0, tiled=True
        )
        mine = covers[0][:per_device] - jnp.sum(parts[:, :per_device], axis=0)
        diag_rows = lax.all_gather(mine, ("row", "panel"), axis=0, tiled=True)
        return solve(covers, parts, factor(factor_kernel, (diag_rows,), B))

    held = local_points
    for bit in (1, 2, 4):
        held = jnp.concatenate([held, swap(held, "row", bit)], 0)
    order = row_pos ^ jnp.arange(8, dtype=jnp.int32)
    panel_points = held[order].transpose(1, 0, 2).reshape(2, count, B)
    covers = covers_of(panel_points)

    far = swap(own_prior, "row", 4)
    firsts, seconds = [], []
    for m in (1, 2, 3):
        second = ((row_pos >> (m.bit_length() - 1)) & 1) == 1
        firsts.append(swap(jnp.where(second, own_prior, far), "row", m))
        seconds.append((m, jnp.where(second, far, own_prior)))
    folded = jnp.concatenate([own_prior, far] + firsts, 0)
    partial = dot_rows(own_prior, folded)
    sums = lax.all_to_all(
        partial.reshape(4, per_device, 5 * NB), "panel", split_axis=0, concat_axis=0, tiled=True
    )
    places = [fold_block(row_pos, k) for k in range(5)]
    lead_cover = jnp.concatenate(
        [lax.dynamic_slice(covers[0], (jnp.int32(0), s * NB), (per_device, NB)) for s in places], 1
    )
    shard = lead_cover - jnp.sum(sums, axis=0)

    held = shard[None]
    for axis, bit in (("row", 2), ("row", 4), ("row", 1), ("panel", 2)):
        held = jnp.concatenate([held, swap(held, axis, bit)], 0)
    there = swap(held, "panel", 1)

    rest = [swap(block, "row", m) for m, block in seconds]
    panel_prior = jnp.zeros((8, NB, own_prior.shape[1]), F32)
    for k, block in enumerate([own_prior, far] + firsts):
        panel_prior = lax.dynamic_update_slice(panel_prior, block[None], (places[k], 0, 0))
    for m, block in zip((1, 2, 3), rest):
        panel_prior = lax.dynamic_update_slice(panel_prior, block[None], (places[m + 1] ^ 4, 0, 0))
    partial = dot_rows(prior_factor, panel_prior.reshape(B, -1))
    partial, there = lax.optimization_barrier((partial, there))
    parts = lax.all_to_all(
        partial.reshape(4, quarter_rows, B), "panel", split_axis=0, concat_axis=0, tiled=True
    )
    place = jnp.stack([row_pos, panel_pos]).astype(jnp.int32)
    factors = factor(unfold_kernel, (place, held, there), B)
    return solve(covers, parts, factors)


def solution(mesh):
    return jax.shard_map(
        local,
        mesh=mesh,
        in_specs=(P("row"), P(None, None, "row"), P("row", "panel")),
        out_specs=P(("row", "panel"), None),
        check_vma=False,
    )
```

time: 258 us -> 218 us (0.84)
  waiting for transfers between devices: 74.9 us -> 39.1 us
  blocking collectives: 30.1 us -> 0 us
  starting transfers between devices: 6.63 us -> 30.8 us
  local copies, waits for them, and re-layouts: 8.81 us -> 23.3 us
  between operations: 13.5 us -> 0.43 us
  other arithmetic: 0.07 us -> 2.91 us
    all_gather x2 -> x0, waiting for transfers between devices: 67.6 us -> none  [the longest x1 60.5 us: local(): lax.all_gather(schur[:per_device], ('row', 'panel'), axis=0, tiled=True)]
    ppermute x0 -> x15, waiting for transfers between devices: none -> 32.5 us  [swap(): lax.ppermute(block, axis, [(i, i ^ bit) for i in range(lax.axis_size(axis...]
    all_to_all x1 -> x0, blocking collectives: 30.1 us -> none  [local(): lax.all_to_all(prior_factor, 'panel', split_axis=0, concat_axis=1, tiled=...]
    ppermute x0 -> x15, starting transfers between devices: none -> 22.3 us  [swap(): lax.ppermute(block, axis, [(i, i ^ bit) for i in range(lax.axis_size(axis...]
    dynamic_update_slice x0 -> x8, local copies, waits for them, and re-layouts: none -> 5.94 us  [the longest x5 3.78 us: local(): lax.dynamic_update_slice(panel_prior, block[None], (places[k], 0, 0))]
    optimization_barrier x0 -> x1, local copies, waits for them, and re-layouts: none -> 5.45 us  [local(): partial, there = lax.optimization_barrier((partial, there))]
    unnamed x9 -> x50, local copies, waits for them, and re-layouts: 3.57 us -> 8.41 us
    all_to_all x1 -> x0, local copies, waits for them, and re-layouts: 2.92 us -> none  [local(): lax.all_to_all(prior_factor, 'panel', split_axis=0, concat_axis=1, tiled=...]
  transfers between devices with their start and end apart: 3 -> 17, of which waited for: 3 -> 8; matrix products, arithmetic and copies ran while one was open for 2% -> 8% of each run, Pallas kernels for 21% -> 48%
where the time goes in v1:
time: 218 us
  Pallas kernels  113 us (52%)
  waiting for transfers between devices  39.1 us (18%)
  starting transfers between devices  30.8 us (14%)
  local copies, waits for them, and re-layouts  23.3 us (11%)
  matrix products  8.23 us (4%)
  other arithmetic  2.91 us (1%)
    pallas_call x8, Pallas kernels, cover_rows(): pl.pallas_call(cover_kernel, grid=(1,), out_shape=jax.ShapeDtypeStruct((b...  53.1 us
    pallas_call x1, Pallas kernels, factor(): pl.pallas_call(kernel, out_shape=[jax.ShapeDtypeStruct((n, n), BF)] * 2 +...  51.6 us
    ppermute x15, waiting for transfers between devices, swap(): lax.ppermute(block, axis, [(i, i ^ bit) for i in range(lax.axis_size(axis...  32.5 us
    ppermute x15, starting transfers between devices, swap(): lax.ppermute(block, axis, [(i, i ^ bit) for i in range(lax.axis_size(axis...  22.3 us
    unnamed x50, local copies, waits for them, and re-layouts  8.41 us
    dot_general x2, matrix products, dot_rows(): lax.dot_general(left, right, NT, precision=lax.Precision.HIGH, preferred_...  8.23 us
    pallas_call x1, Pallas kernels, solve(): pl.pallas_call(solve_kernel, out_shape=jax.ShapeDtypeStruct((rows, n), F3...  7.56 us
    all_to_all x1, waiting for transfers between devices, local(): lax.all_to_all(partial.reshape(4, per_device, 5 * NB), 'panel', split_axi...  6.64 us
  transfers between devices with their start and end apart: 17, of which 8 were waited for; matrix products, arithmetic and copies ran while one was open for 8% of the time, Pallas kernels for 48%

profile of v1, /device:TPU:0, one launch (start us, length us, event | category | flops | bytes accessed | tf_op | source)
XLA Modules:
  0.0 217.8 jit_solution(7233135310080145031)
XLA Ops:
  1.8 3.0 %collective-permute-start = (f32[1,32,128]{2,1,0:T(8,128)S(1)}, f32[1,32,128]{2,1,0:T(8,128)S(1)}, u32[]{:S(2)}, u32[]{:S(2)}) collective-permute-start(f32[1,32,128]{2,1,0:T(8,128)S(1)} %reshape.136), channel_id=1, source_target_pairs={{0,4},{4,0},{8,12},{12,8},{16,20},{20,16},{24,28},{28,24},{1,5},{5... | collective-permute-start | bytes 49160 | tf_op jit(solution)/shard_map/ppermute | solution.py:324
  5.8 2.7 %collective-permute-start.3 = (f32[128,512]{1,0:T(8,128)S(1)}, f32[128,512]{1,0:T(8,128)S(1)}, u32[]{:S(2)}, u32[]{:S(2)}) collective-permute-start(f32[128,512]{1,0:T(8,128)S(1)} %bitcast.53), channel_id=1, source_target_pairs={{0,16},{4,20},{8,24},{12,28},{16,0},{20,4},{24,8},{28,12},{1,17},{... | collective-permute-start | bytes 786440 | tf_op jit(solution)/shard_map/ppermute | solution.py:324
  9.2 1.6 broadcast_in_dim.40
  11.5 1.7 collective-permute-start.1
  13.2 2.3 %collective-permute-done.1 = f32[2,32,128]{2,1,0:T(8,128)S(1)} collective-permute-done((f32[2,32,128]{2,1,0:T(8,128)S(1)}, f32[2,32,128]{2,1,0:T(8,128)S(1)}, u32[]{:S(2)}, u32[]{:S(2)}) %collective-permute-start.1) | collective-permute-done | bytes 32800 | tf_op jit(solution)/shard_map/ppermute | solution.py:324
  16.9 6.0 %collective-permute-done.2 = f32[4,32,128]{2,1,0:T(8,128)S(1)} collective-permute-done((f32[4,32,128]{2,1,0:T(8,128)S(1)}, f32[4,32,128]{2,1,0:T(8,128)S(1)}, u32[]{:S(2)}, u32[]{:S(2)}) %collective-permute-start.2) | collective-permute-done | bytes 65568 | tf_op jit(solution)/shard_map/ppermute | solution.py:324
  24.4 6.6 %cover.15.refs_7_ = f32[32,1024]{1,0:T(8,128)S(1)} custom-call(bf16[16,256,16]{2,1,0:T(8,128)(2,1)S(1)} %get-tuple-element.13.f_ref, bf16[16,16,1024]{2,1,0:T(8,128)(2,1)S(1)} %get-tuple-element.14.g_ref), custom_call_target="tpu_custom_call" | custom-call | flops 7000000000 | bytes 1048576 | tf_op jit(solution)/shard_map/cover/pallas_call | solution.py:100
  31.0 6.6 %cover.14.refs_6_ = f32[32,1024]{1,0:T(8,128)S(1)} custom-call(bf16[16,256,16]{2,1,0:T(8,128)(2,1)S(1)} %get-tuple-element.13.f_ref, bf16[16,16,1024]{2,1,0:T(8,128)(2,1)S(1)} %get-tuple-element.14.g_ref), custom_call_target="tpu_custom_call" | custom-call | flops 7000000000 | bytes 1048576 | tf_op jit(solution)/shard_map/cover/pallas_call | solution.py:100
  37.7 6.6 %cover.13.refs_5_ = f32[32,1024]{1,0:T(8,128)S(1)} custom-call(bf16[16,256,16]{2,1,0:T(8,128)(2,1)S(1)} %get-tuple-element.13.f_ref, bf16[16,16,1024]{2,1,0:T(8,128)(2,1)S(1)} %get-tuple-element.14.g_ref), custom_call_target="tpu_custom_call" | custom-call | flops 7000000000 | bytes 1048576 | tf_op jit(solution)/shard_map/cover/pallas_call | solution.py:100
  44.3 6.6 %cover.12.refs_4_ = f32[32,1024]{1,0:T(8,128)S(1)} custom-call(bf16[16,256,16]{2,1,0:T(8,128)(2,1)S(1)} %get-tuple-element.13.f_ref, bf16[16,16,1024]{2,1,0:T(8,128)(2,1)S(1)} %get-tuple-element.14.g_ref), custom_call_target="tpu_custom_call" | custom-call | flops 7000000000 | bytes 1048576 | tf_op jit(solution)/shard_map/cover/pallas_call | solution.py:100
  51.0 6.6 %cover.8 = f32[32,1024]{1,0:T(8,128)S(1)} custom-call(bf16[16,256,16]{2,1,0:T(8,128)(2,1)S(1)} %get-tuple-element.13.f_ref, bf16[16,16,1024]{2,1,0:T(8,128)(2,1)S(1)} %get-tuple-element.14.g_ref), custom_call_target="tpu_custom_call" | custom-call | flops 7000000000 | bytes 1048576 | tf_op jit(solution)/shard_map/cover/pallas_call | solution.py:100
  60.0 2.3 %collective-permute-start.6 = (f32[128,512]{1,0:T(8,128)S(1)}, f32[128,512]{1,0:T(8,128)S(1)}, u32[]{:S(2)}, u32[]{:S(2)}) collective-permute-start(f32[128,512]{1,0:T(8,128)S(1)} %get-tuple-element.25), channel_id=1, source_target_pairs={{0,12},{4,8},{8,4},{12,0},{16,28},{20,24},{24,20},{28,16},{1,13},{... | collective-permute-start | bytes 786440 | tf_op jit(solution)/shard_map/ppermute | solution.py:324
  62.3 3.1 %collective-permute-done.4 = f32[128,512]{1,0:T(8,128)S(1)} collective-permute-done((f32[128,512]{1,0:T(8,128)S(1)}, f32[128,512]{1,0:T(8,128)S(1)}, u32[]{:S(2)}, u32[]{:S(2)}) %collective-permute-start.4) | collective-permute-done | bytes 262176 | tf_op jit(solution)/shard_map/ppermute | solution.py:324
  65.4 3.1 %collective-permute-done.5 = f32[128,512]{1,0:T(8,128)S(1)} collective-permute-done((f32[128,512]{1,0:T(8,128)S(1)}, f32[128,512]{1,0:T(8,128)S(1)}, u32[]{:S(2)}, u32[]{:S(2)}) %collective-permute-start.5) | collective-permute-done | bytes 262176 | tf_op jit(solution)/shard_map/ppermute | solution.py:324
  68.5 4.2 %collective-permute-done.6 = f32[128,512]{1,0:T(8,128)S(1)} collective-permute-done((f32[128,512]{1,0:T(8,128)S(1)}, f32[128,512]{1,0:T(8,128)S(1)}, u32[]{:S(2)}, u32[]{:S(2)}) %collective-permute-start.6) | collective-permute-done | bytes 262176 | tf_op jit(solution)/shard_map/ppermute | solution.py:324
  72.8 1.5 fusion.7
  74.3 3.5 %all-to-all-start = ((f32[4,32,640]{2,1,0:T(8,128)}), f32[4,32,640]{2,1,0:T(8,128)S(1)}, u32[]{:S(2)}, u32[]{:S(2)}) async-start(f32[4,32,640]{2,1,0:T(8,128)} %bitcast.20), calls=%async_computation | async-start | bytes 655360 | tf_op jit(solution)/shard_map/all_to_all | solution.py:392
  77.8 6.6 %all-to-all-done = f32[4,32,640]{2,1,0:T(8,128)S(1)} async-done(((f32[4,32,640]{2,1,0:T(8,128)}), f32[4,32,640]{2,1,0:T(8,128)S(1)}, u32[]{:S(2)}, u32[]{:S(2)}) %all-to-all-start) | async-done | bytes 327712 | tf_op jit(solution)/shard_map/all_to_all | solution.py:392
  84.5 1.8 collective-permute-start.10
  86.3 6.6 %cover.11.refs_3_ = f32[32,1024]{1,0:T(8,128)S(1)} custom-call(bf16[16,256,16]{2,1,0:T(8,128)(2,1)S(1)} %get-tuple-element.13.f_ref, bf16[16,16,1024]{2,1,0:T(8,128)(2,1)S(1)} %get-tuple-element.14.g_ref), custom_call_target="tpu_custom_call" | custom-call | flops 7000000000 | bytes 1048576 | tf_op jit(solution)/shard_map/cover/pallas_call | solution.py:100
  93.0 3.4 %collective-permute-start.11 = (f32[2,32,640]{2,1,0:T(8,128)S(1)}, f32[2,32,640]{2,1,0:T(8,128)S(1)}, u32[]{:S(2)}, u32[]{:S(2)}) collective-permute-start(f32[2,32,640]{2,1,0:T(8,128)S(1)} %pad_maximum_fusion.2), channel_id=1, source_target_pairs={{0,16},{4,20},{8,24},{12,28},{16,0},{20,4},{24,8},{28,12},{1,17},{... | collective-permute-start | bytes 491528 | tf_op jit(solution)/shard_map/ppermute | solution.py:324
  96.4 6.6 %cover.10.refs_2_ = f32[32,1024]{1,0:T(8,128)S(1)} custom-call(bf16[16,256,16]{2,1,0:T(8,128)(2,1)S(1)} %get-tuple-element.13.f_ref, bf16[16,16,1024]{2,1,0:T(8,128)(2,1)S(1)} %get-tuple-element.14.g_ref), custom_call_target="tpu_custom_call" | custom-call | flops 7000000000 | bytes 1048576 | tf_op jit(solution)/shard_map/cover/pallas_call | solution.py:100
  104.0 6.6 %cover.9.refs_1_ = f32[32,1024]{1,0:T(8,128)S(1)} custom-call(bf16[16,256,16]{2,1,0:T(8,128)(2,1)S(1)} %get-tuple-element.13.f_ref, bf16[16,16,1024]{2,1,0:T(8,128)(2,1)S(1)} %get-tuple-element.14.g_ref), custom_call_target="tpu_custom_call" | custom-call | flops 7000000000 | bytes 1048576 | tf_op jit(solution)/shard_map/cover/pallas_call | solution.py:100
  111.7 2.0 collective-permute-start.8
  117.3 13.4 %collective-permute-done.13 = f32[8,32,640]{2,1,0:T(8,128)S(1)} collective-permute-done((f32[8,32,640]{2,1,0:T(8,128)S(1)}, f32[8,32,640]{2,1,0:T(8,128)S(1)}, u32[]{:S(2)}, u32[]{:S(2)}) %collective-permute-start.13) | collective-permute-done | bytes 655392 | tf_op jit(solution)/shard_map/ppermute | solution.py:324
  133.9 6.7 %convolution_bitcast_fusion = f32[1024,1024]{0,1:T(8,128)} fusion(f32[1024,512]{1,0:T(8,128)} %bitcast.12, f32[1024,512]{1,0:T(8,128)S(1)} %copy-done.8), kind=kOutput, calls=%fused_computation.1 | convolution fusion | flops 3221225472 | bytes 8388608 | tf_op jit(solution)/shard_map/dot_general | solution.py:328
  141.7 5.5 %copy.6 = f32[1024,1024]{1,0:T(8,128)} copy(f32[1024,1024]{0,1:T(8,128)} %convolution_bitcast_fusion) | data formatting | bytes 8388608 | tf_op jit(solution)/shard_map/optimization_barrier | solution.py:413
  147.1 5.0 %all-to-all-start.1 = ((f32[4,256,1024]{2,1,0:T(8,128)}), f32[4,256,1024]{2,1,0:T(8,128)}, u32[]{:S(2)}, u32[]{:S(2)}) async-start(f32[4,256,1024]{2,1,0:T(8,128)} %bitcast.52), calls=%async_computation.1 | async-start | bytes 8388608 | tf_op jit(solution)/shard_map/all_to_all | solution.py:414
  154.8 51.6 %factor.1 = (bf16[1024,1024]{1,0:T(8,128)(2,1)S(1)}, bf16[1024,1024]{1,0:T(8,128)(2,1)S(1)}, bf16[1024,128]{1,0:T(8,128)(2,1)S(1)}, bf16[1024,128]{1,0:T(8,128)(2,1)S(1)}) custom-call(s32[2]{0:T(128)S(1)} %pad_add_fusion.place_ref, f32[16,32,640]{2,1,0:T(8,128)S(1)} %copy-done.5, f32[16,32,640]{2,1,0:T(8,128)S(1)} %copy-done.7), custom_call_target="tpu_custom_call" | custom-call | flops 49999998976 | bytes 8388608 | tf_op jit(solution)/shard_map/factor/pallas_call | solution.py:271
  206.4 1.3 copy-done
  207.8 1.6 copy-done.1
  210.3 7.6 %solve.1 = f32[256,1024]{1,0:T(8,128)} custom-call(f32[32,1024]{1,0:T(8,128)S(1)} %select_add_fusion.refs_0_, f32[32,1024]{1,0:T(8,128)S(1)} %copy-done.3, f32[32,1024]{1,0:T(8,128)S(1)} %cover.10.refs_2_, f32[32,1024]{1,0:T(8,128)S(1)} %cover.11.refs_3_, f32[32,1024]{1,0:T(8,128)S(1)} %cover.12.refs_4_, f32[32,1024]{1,0:T(8,128)S(1)} %cover.13.refs_5_, ...), custom_call_target="tpu_custom_call" | custom-call | tf_op jit(solution)/shard_map/solve/pallas_call | solution.py:312
  (104 shorter events, 22.7 us)
Async XLA Ops:
  1.8 9.7 %collective-permute-start = (f32[1,32,128]{2,1,0:T(8,128)S(1)}, f32[1,32,128]{2,1,0:T(8,128)S(1)}, u32[]{:S(2)}, u32[]{:S(2)}) collective-permute-start(f32[1,32,128]{2,1,0:T(8,128)S(1)} %reshape.136), channel_id=1, source_target_pairs={{0,4},{4,0},{8,12},{12,8},{16,20},{20,16},{24,28},{28,24},{1,5},{5... | collective-permute-start | bytes 49160 | tf_op jit(solution)/shard_map/ppermute | solution.py:324
  5.8 51.8 %collective-permute-start.3 = (f32[128,512]{1,0:T(8,128)S(1)}, f32[128,512]{1,0:T(8,128)S(1)}, u32[]{:S(2)}, u32[]{:S(2)}) collective-permute-start(f32[128,512]{1,0:T(8,128)S(1)} %bitcast.53), channel_id=1, source_target_pairs={{0,16},{4,20},{8,24},{12,28},{16,0},{20,4},{24,8},{28,12},{1,17},{... | collective-permute-start | bytes 786440 | tf_op jit(solution)/shard_map/ppermute | solution.py:324
  11.5 4.0 %collective-permute-start.1 = (f32[2,32,128]{2,1,0:T(8,128)S(1)}, f32[2,32,128]{2,1,0:T(8,128)S(1)}, u32[]{:S(2)}, u32[]{:S(2)}) collective-permute-start(f32[2,32,128]{2,1,0:T(8,128)S(1)} %pad_maximum_fusion.6), channel_id=1, source_target_pairs={{0,8},{4,12},{8,0},{12,4},{16,24},{20,28},{24,16},{28,20},{1,9},{5... | collective-permute-start | bytes 98312 | tf_op jit(solution)/shard_map/ppermute | solution.py:324
  15.5 7.4 %collective-permute-start.2 = (f32[4,32,128]{2,1,0:T(8,128)S(1)}, f32[4,32,128]{2,1,0:T(8,128)S(1)}, u32[]{:S(2)}, u32[]{:S(2)}) collective-permute-start(f32[4,32,128]{2,1,0:T(8,128)S(1)} %pad_maximum_fusion.5), channel_id=1, source_target_pairs={{0,16},{4,20},{8,24},{12,28},{16,0},{20,4},{24,8},{28,12},{1,17},{... | collective-permute-start | bytes 196616 | tf_op jit(solution)/shard_map/ppermute | solution.py:324
  51.0 6.7 %copy-start.9 = (f32[640,512]{1,0:T(8,128)S(1)}, f32[640,512]{1,0:T(8,128)}, u32[]{:S(2)}) copy-start(f32[640,512]{1,0:T(8,128)} %constant_dynamic-update-slice_fusion.9) | copy-start | bytes 3932164
  57.6 16.6 %copy-start.10 = (f32[128,512]{1,0:T(8,128)}, f32[128,512]{1,0:T(8,128)S(1)}, u32[]{:S(2)}) copy-start(f32[128,512]{1,0:T(8,128)S(1)} %collective-permute-done.3) | copy-start | bytes 786436
  58.6 6.8 %collective-permute-start.4 = (f32[128,512]{1,0:T(8,128)S(1)}, f32[128,512]{1,0:T(8,128)S(1)}, u32[]{:S(2)}, u32[]{:S(2)}) collective-permute-start(f32[128,512]{1,0:T(8,128)S(1)} %get-tuple-element.26), channel_id=1, source_target_pairs={{0,4},{4,0},{8,12},{12,8},{16,20},{20,16},{24,28},{28,24},{1,5},{5... | collective-permute-start | bytes 786440 | tf_op jit(solution)/shard_map/ppermute | solution.py:324
  59.2 9.3 %collective-permute-start.5 = (f32[128,512]{1,0:T(8,128)S(1)}, f32[128,512]{1,0:T(8,128)S(1)}, u32[]{:S(2)}, u32[]{:S(2)}) collective-permute-start(f32[128,512]{1,0:T(8,128)S(1)} %get-tuple-element.25), channel_id=1, source_target_pairs={{0,8},{4,12},{8,0},{12,4},{16,24},{20,28},{24,16},{28,20},{1,9},{5... | collective-permute-start | bytes 786440 | tf_op jit(solution)/shard_map/ppermute | solution.py:324
  60.0 12.7 %collective-permute-start.6 = (f32[128,512]{1,0:T(8,128)S(1)}, f32[128,512]{1,0:T(8,128)S(1)}, u32[]{:S(2)}, u32[]{:S(2)}) collective-permute-start(f32[128,512]{1,0:T(8,128)S(1)} %get-tuple-element.25), channel_id=1, source_target_pairs={{0,12},{4,8},{8,4},{12,0},{16,28},{20,24},{24,20},{28,16},{1,13},{... | collective-permute-start | bytes 786440 | tf_op jit(solution)/shard_map/ppermute | solution.py:324
  65.4 7.3 %copy-start.14 = (f32[128,512]{1,0:T(8,128)}, f32[128,512]{1,0:T(8,128)S(1)}, u32[]{:S(2)}) copy-start(f32[128,512]{1,0:T(8,128)S(1)} %collective-permute-done.4) | copy-start | bytes 786436
  68.5 4.2 %copy-start.16 = (f32[128,512]{1,0:T(8,128)}, f32[128,512]{1,0:T(8,128)S(1)}, u32[]{:S(2)}) copy-start(f32[128,512]{1,0:T(8,128)S(1)} %collective-permute-done.5) | copy-start | bytes 786436
  72.7 1.5 copy-start.12
  74.3 10.2 %all-to-all-start = ((f32[4,32,640]{2,1,0:T(8,128)}), f32[4,32,640]{2,1,0:T(8,128)S(1)}, u32[]{:S(2)}, u32[]{:S(2)}) async-start(f32[4,32,640]{2,1,0:T(8,128)} %bitcast.20), calls=%async_computation | async-start | bytes 655360 | tf_op jit(solution)/shard_map/all_to_all | solution.py:392
  84.5 8.4 %collective-permute-start.10 = (f32[1,32,640]{2,1,0:T(8,128)S(1)}, f32[1,32,640]{2,1,0:T(8,128)S(1)}, u32[]{:S(2)}, u32[]{:S(2)}) collective-permute-start(f32[1,32,640]{2,1,0:T(8,128)S(1)} %get-tuple-element.22), channel_id=1, source_target_pairs={{0,8},{4,12},{8,0},{12,4},{16,24},{20,28},{24,16},{28,20},{1,9},{5... | collective-permute-start | bytes 245768 | tf_op jit(solution)/shard_map/ppermute | solution.py:324
  93.0 10.4 %collective-permute-start.11 = (f32[2,32,640]{2,1,0:T(8,128)S(1)}, f32[2,32,640]{2,1,0:T(8,128)S(1)}, u32[]{:S(2)}, u32[]{:S(2)}) collective-permute-start(f32[2,32,640]{2,1,0:T(8,128)S(1)} %pad_maximum_fusion.2), channel_id=1, source_target_pairs={{0,16},{4,20},{8,24},{12,28},{16,0},{20,4},{24,8},{28,12},{1,17},{... | collective-permute-start | bytes 491528 | tf_op jit(solution)/shard_map/ppermute | solution.py:324
  103.4 7.3 %copy-start.18 = (f32[128,512]{1,0:T(8,128)S(1)}, f32[128,512]{1,0:T(8,128)}, u32[]{:S(2)}) copy-start(f32[128,512]{1,0:T(8,128)} %get-tuple-element.23) | copy-start | bytes 786436
  103.4 10.3 %copy-start.19 = (f32[128,512]{1,0:T(8,128)S(1)}, f32[128,512]{1,0:T(8,128)}, u32[]{:S(2)}) copy-start(f32[128,512]{1,0:T(8,128)} %get-tuple-element.24) | copy-start | bytes 786436
  103.4 10.9 %copy-start.11 = (f32[128,512]{1,0:T(8,128)S(1)}, f32[128,512]{1,0:T(8,128)}, u32[]{:S(2)}) copy-start(f32[128,512]{1,0:T(8,128)} %copy-done.10) | copy-start | bytes 786436
  103.4 12.3 %copy-start.15 = (f32[128,512]{1,0:T(8,128)S(1)}, f32[128,512]{1,0:T(8,128)}, u32[]{:S(2)}) copy-start(f32[128,512]{1,0:T(8,128)} %copy-done.14) | copy-start | bytes 786436
  103.4 11.6 %collective-permute-start.12 = (f32[4,32,640]{2,1,0:T(8,128)S(1)}, f32[4,32,640]{2,1,0:T(8,128)S(1)}, u32[]{:S(2)}, u32[]{:S(2)}) collective-permute-start(f32[4,32,640]{2,1,0:T(8,128)S(1)} %pad_maximum_fusion.1), channel_id=1, source_target_pairs={{0,4},{4,0},{8,12},{12,8},{16,20},{20,16},{24,28},{28,24},{1,5},{5... | collective-permute-start | bytes 983048 | tf_op jit(solution)/shard_map/ppermute | solution.py:324
  110.7 20.0 %copy-start.2 = (f32[32,1024]{1,0:T(8,128)}, f32[32,1024]{1,0:T(8,128)S(1)}, u32[]{:S(2)}) copy-start(f32[32,1024]{1,0:T(8,128)S(1)} %cover.9.refs_1_) | copy-start | bytes 393220
  110.7 5.8 %copy-start.17 = (f32[128,512]{1,0:T(8,128)S(1)}, f32[128,512]{1,0:T(8,128)}, u32[]{:S(2)}) copy-start(f32[128,512]{1,0:T(8,128)} %copy-done.16) | copy-start | bytes 786436
  110.7 22.4 %collective-permute-start.9 = (f32[128,512]{1,0:T(8,128)S(1)}, f32[128,512]{1,0:T(8,128)S(1)}, u32[]{:S(2)}, u32[]{:S(2)}) collective-permute-start(f32[128,512]{1,0:T(8,128)S(1)} %copy-done.18), channel_id=1, source_target_pairs={{0,12},{4,8},{8,4},{12,0},{16,28},{20,24},{24,20},{28,16},{1,13},{... | collective-permute-start | bytes 786440 | tf_op jit(solution)/shard_map/ppermute | solution.py:324
  111.7 20.7 %collective-permute-start.8 = (f32[128,512]{1,0:T(8,128)S(1)}, f32[128,512]{1,0:T(8,128)S(1)}, u32[]{:S(2)}, u32[]{:S(2)}) collective-permute-start(f32[128,512]{1,0:T(8,128)S(1)} %copy-done.18), channel_id=1, source_target_pairs={{0,8},{4,12},{8,0},{12,4},{16,24},{20,28},{24,16},{28,20},{1,9},{5... | collective-permute-start | bytes 786440 | tf_op jit(solution)/shard_map/ppermute | solution.py:324
  113.7 17.9 %collective-permute-start.7 = (f32[128,512]{1,0:T(8,128)S(1)}, f32[128,512]{1,0:T(8,128)S(1)}, u32[]{:S(2)}, u32[]{:S(2)}) collective-permute-start(f32[128,512]{1,0:T(8,128)S(1)} %copy-done.19), channel_id=1, source_target_pairs={{0,4},{4,0},{8,12},{12,8},{16,20},{20,16},{24,28},{28,24},{1,5},{5... | collective-permute-start | bytes 786440 | tf_op jit(solution)/shard_map/ppermute | solution.py:324
  115.0 15.8 %copy-start.13 = (f32[128,512]{1,0:T(8,128)S(1)}, f32[128,512]{1,0:T(8,128)}, u32[]{:S(2)}) copy-start(f32[128,512]{1,0:T(8,128)} %copy-done.12) | copy-start | bytes 786436
  115.1 15.6 %collective-permute-start.13 = (f32[8,32,640]{2,1,0:T(8,128)S(1)}, f32[8,32,640]{2,1,0:T(8,128)S(1)}, u32[]{:S(2)}, u32[]{:S(2)}) collective-permute-start(f32[8,32,640]{2,1,0:T(8,128)S(1)} %pad_maximum_fusion), channel_id=1, source_target_pairs={{0,2},{1,3},{2,0},{3,1},{4,6},{5,7},{6,4},{7,5},{8,10},{9,11},{10,... | collective-permute-start | bytes 1966088 | tf_op jit(solution)/shard_map/ppermute | solution.py:324
  117.2 16.6 %copy-start.8 = (f32[1024,512]{1,0:T(8,128)S(1)}, f32[1024,512]{1,0:T(8,128)}, u32[]{:S(2)}) copy-start(f32[1024,512]{1,0:T(8,128)} %param.5) | copy-start | bytes 6291460
  130.7 9.9 %copy-start.4 = (f32[16,32,640]{2,1,0:T(8,128)}, f32[16,32,640]{2,1,0:T(8,128)S(1)}, u32[]{:S(2)}) copy-start(f32[16,32,640]{2,1,0:T(8,128)S(1)} %constant_dynamic-update-slice_fusion.10.here_ref) | copy-start | bytes 3932164
  130.7 9.9 %collective-permute-start.14 = (f32[16,32,640]{2,1,0:T(8,128)S(1)}, f32[16,32,640]{2,1,0:T(8,128)S(1)}, u32[]{:S(2)}, u32[]{:S(2)}) collective-permute-start(f32[16,32,640]{2,1,0:T(8,128)S(1)} %constant_dynamic-update-slice_fusion.10.here_ref), channel_id=1, source_target_pairs={{0,1},{1,0},{2,3},{3,2},{4,5},{5,4},{6,7},{7,6},{8,9},{9,8},{10,11... | collective-permute-start | bytes 3932168 | tf_op jit(solution)/shard_map/ppermute | solution.py:324
  147.1 60.7 %all-to-all-start.1 = ((f32[4,256,1024]{2,1,0:T(8,128)}), f32[4,256,1024]{2,1,0:T(8,128)}, u32[]{:S(2)}, u32[]{:S(2)}) async-start(f32[4,256,1024]{2,1,0:T(8,128)} %bitcast.52), calls=%async_computation.1 | async-start | bytes 8388608 | tf_op jit(solution)/shard_map/all_to_all | solution.py:414
  207.8 1.6 copy-start.1
  (5 other events, 6.0 us)

commit v2 on v1

--- a/solution.py
+++ b/solution.py
@@ -107,9 +107,7 @@
         ],
         out_specs=pl.BlockSpec((block, cols), lambda i: (0, 0)),
         compiler_params=pltpu.CompilerParams(vmem_limit_bytes=16 << 20),
-        cost_estimate=pl.CostEstimate(
-            flops=7 * 10**9, bytes_accessed=1 << 20, transcendentals=count * count * block * cols
-        ),
+        cost_estimate=pl.CostEstimate(flops=10**8, bytes_accessed=1 << 18, transcendentals=0),
         name="cover",
     )(row_part, col_part)
 
@@ -217,28 +215,25 @@
     return (r ^ m) ^ (4 * second)
 
 
-def unfold_kernel(place_ref, here_ref, there_ref, lh_ref, ll_ref, wh_ref, wl_ref, a_ref):
+def unfold_kernel(place_ref, *refs):
+    pieces_refs, (lh_ref, ll_ref, wh_ref, wl_ref, a_ref, g_ref) = refs[:8], refs[8:]
     row_pos = place_ref[0]
     panel_pos = place_ref[1]
-    per_device = here_ref.shape[1]
     lh_ref[...] = jnp.zeros_like(lh_ref)
     ll_ref[...] = jnp.zeros_like(ll_ref)
+    for i, ref in enumerate(pieces_refs):
+        g_ref[4 * i : 4 * i + 4] = ref[...]
 
     def rows_of(r, _):
         away = r ^ row_pos
-        slot = ((away >> 1) & 1) | (((away >> 2) & 1) << 1) | ((away & 1) << 2)
+        slot = (away >> 1) | ((away & 1) << 2)
         low = r & 3
+        ats = []
+        for p in range(4):
+            gone = p ^ panel_pos
+            ats.append(slot | ((gone >> 1) << 3) | ((gone & 1) << 4))
         for k in range(5):
-            parts = []
-            for p in range(4):
-                gone = p ^ panel_pos
-                at = slot | ((gone >> 1) << 3)
-                parts.append((at, gone & 1))
-            picked = [
-                jnp.where(core == 0, here_ref[at, :, NB * k : NB * k + NB], there_ref[at, :, NB * k : NB * k + NB])
-                for at, core in parts
-            ]
-            block = jnp.concatenate(picked, 0)
+            block = jnp.concatenate([g_ref[at, :, NB * k : NB * k + NB] for at in ats], 0)
             if k < 2:
                 s = r ^ (4 * k)
             else:
@@ -266,29 +261,32 @@
 
 def factor(kernel, operands, n):
     in_specs = [pl.BlockSpec(memory_space=pltpu.VMEM)] * len(operands)
+    scratch = [pltpu.VMEM((n, n), F32)]
     if kernel is unfold_kernel:
         in_specs[0] = pl.BlockSpec(memory_space=pltpu.SMEM)
+        scratch.append(pltpu.VMEM((32, *operands[1].shape[1:]), F32))
     return pl.pallas_call(
         kernel,
         out_shape=[jax.ShapeDtypeStruct((n, n), BF)] * 2 + [jax.ShapeDtypeStruct((n, NB), BF)] * 2,
         in_specs=in_specs,
         out_specs=[pl.BlockSpec(memory_space=pltpu.VMEM)] * 4,
-        scratch_shapes=[pltpu.VMEM((n, n), F32)],
+        scratch_shapes=scratch,
         compiler_params=pltpu.CompilerParams(vmem_limit_bytes=32 << 20),
         cost_estimate=pl.CostEstimate(flops=5 * 10**10, bytes_accessed=8 << 20, transcendentals=0),
         name="factor",
     )(*operands)
 
 
-def solve_kernel(*refs):
-    covers, (parts_ref, lh_ref, ll_ref, wh_ref, wl_ref, o_ref, xh_ref, xl_ref) = refs[:-8], refs[-8:]
+def solve_kernel(*refs, covers):
+    cover_refs, parts_refs = refs[:covers], refs[covers:-7]
+    lh_ref, ll_ref, wh_ref, wl_ref, o_ref, xh_ref, xl_ref = refs[-7:]
     n = o_ref.shape[1]
     first = 0
-    for ref in covers:
+    for ref in cover_refs:
         rows = pl.ds(first, ref.shape[0])
-        taken = parts_ref[0, rows]
-        for p in range(1, parts_ref.shape[0]):
-            taken = taken + parts_ref[p, rows]
+        taken = parts_refs[0][rows]
+        for part in parts_refs[1:]:
+            taken = taken + part[rows]
         o_ref[rows] = ref[...] - taken
         first += ref.shape[0]
     for c in range(0, n, NB):
@@ -308,9 +306,9 @@
 def solve(covers, parts, factors):
     rows = sum(c.shape[0] for c in covers)
     n = covers[0].shape[1]
-    operands = (*covers, parts, *factors)
+    operands = (*covers, *parts, *factors)
     return pl.pallas_call(
-        solve_kernel,
+        functools.partial(solve_kernel, covers=len(covers)),
         out_shape=jax.ShapeDtypeStruct((rows, n), F32),
         in_specs=[pl.BlockSpec(memory_space=pltpu.VMEM)] * len(operands),
         out_specs=pl.BlockSpec(memory_space=pltpu.VMEM),
@@ -353,69 +351,97 @@
     on_diagonal = (row_ids < per_device) & (col_ids == device_pos * per_device + row_ids)
     unit = jnp.where(on_diagonal, 1.0, 0.0).astype(F32)
 
-    def covers_of(panel_points):
-        row_part, col_part = features(own_points, panel_points)
-        tiles = [cover_rows(row_part, col_part, i, lead) for i in range(0, quarter_rows, lead)]
-        return [tiles[0] + unit] + tiles[1:]
-
     own_prior = prior_factor.reshape(panel_count, quarter_rows, -1)[:, :per_device]
     own_prior = own_prior.reshape(span_cols, -1)
 
     if not (span_cols == NB and row_count == 8 and panel_count == 4):
         copies = jnp.broadcast_to(local_points, (row_count, 2 * count, span_cols))
         spread = lax.all_to_all(copies, "row", split_axis=0, concat_axis=0, tiled=True)
-        covers = covers_of(spread.transpose(1, 0, 2).reshape(2, count, B))
+        parted = features(own_points, spread.transpose(1, 0, 2).reshape(2, count, B))
+        covers = [cover_rows(*parted, i, lead) for i in range(0, quarter_rows, lead)]
+        covers[0] = covers[0] + unit
         panel_prior = lax.all_gather(own_prior, "row", axis=0, tiled=True)
         partial = dot_rows(prior_factor, panel_prior)
         parts = lax.all_to_all(
             partial.reshape(panel_count, quarter_rows, B), "panel", split_axis=0, concat_axis=0, tiled=True
         )
-        mine = covers[0][:per_device] - jnp.sum(parts[:, :per_device], axis=0)
+        parts = jnp.sum(parts, axis=0)
+        mine = covers[0][:per_device] - parts[:per_device]
         diag_rows = lax.all_gather(mine, ("row", "panel"), axis=0, tiled=True)
-        return solve(covers, parts, factor(factor_kernel, (diag_rows,), B))
-
-    held = local_points
-    for bit in (1, 2, 4):
-        held = jnp.concatenate([held, swap(held, "row", bit)], 0)
-    order = row_pos ^ jnp.arange(8, dtype=jnp.int32)
+        return solve(covers, [parts], factor(factor_kernel, (diag_rows,), B))
+
+    far = swap(own_prior, "row", 4)
+    held = jnp.concatenate([local_points] + [swap(local_points, "row", bit) for bit in (2, 4, 6)], 0)
+    held = jnp.concatenate([held, swap(held, "row", 1)], 0)
+    away = row_pos ^ jnp.arange(8, dtype=jnp.int32)
+    order = (away >> 1) | ((away & 1) << 2)
     panel_points = held[order].transpose(1, 0, 2).reshape(2, count, B)
-    covers = covers_of(panel_points)
-
-    far = swap(own_prior, "row", 4)
-    firsts, seconds = [], []
-    for m in (1, 2, 3):
-        second = ((row_pos >> (m.bit_length() - 1)) & 1) == 1
-        firsts.append(swap(jnp.where(second, own_prior, far), "row", m))
-        seconds.append((m, jnp.where(second, far, own_prior)))
-    folded = jnp.concatenate([own_prior, far] + firsts, 0)
-    partial = dot_rows(own_prior, folded)
-    sums = lax.all_to_all(
-        partial.reshape(4, per_device, 5 * NB), "panel", split_axis=0, concat_axis=0, tiled=True
+    row_part, col_part = features(own_points, panel_points)
+    row_part, far = lax.optimization_barrier((row_part, far))
+    covers = []
+
+    def beside(operands, transfer, calls):
+        tied = lax.optimization_barrier((operands, row_part))
+        received = transfer(tied[0])
+        done = [
+            cover_rows(tied[1], col_part, lead * (len(covers) + i), lead) for i in range(calls)
+        ]
+        received, done = lax.optimization_barrier((received, done))
+        covers.extend(done)
+        return received
+
+    seconds = [((row_pos >> (m.bit_length() - 1)) & 1) == 1 for m in (1, 2, 3)]
+    firsts = beside(
+        [jnp.where(second, own_prior, far) for second in seconds],
+        lambda blocks: [swap(block, "row", m) for m, block in zip((1, 2, 3), blocks)],
+        2,
     )
+    partial = dot_rows(own_prior, jnp.concatenate([own_prior, far] + firsts, 0))
+    others = [jnp.where(second, far, own_prior) for second in seconds]
+
+    shares = [
+        lax.dynamic_slice_in_dim(partial, (panel_pos ^ m) * per_device, per_device, 0)
+        for m in range(4)
+    ]
+
+    def reduce_and_swap(operands):
+        shares, others = operands
+        sums = [swap(share, "panel", m) for m, share in zip((1, 2, 3), shares[1:])]
+        return sums, [swap(block, "row", m) for m, block in zip((1, 2, 3), others)]
+
+    sums, rest = beside((shares, others), reduce_and_swap, 1)
+    covers[0] = covers[0] + unit
     places = [fold_block(row_pos, k) for k in range(5)]
     lead_cover = jnp.concatenate(
         [lax.dynamic_slice(covers[0], (jnp.int32(0), s * NB), (per_device, NB)) for s in places], 1
     )
-    shard = lead_cover - jnp.sum(sums, axis=0)
-
-    held = shard[None]
-    for axis, bit in (("row", 2), ("row", 4), ("row", 1), ("panel", 2)):
-        held = jnp.concatenate([held, swap(held, axis, bit)], 0)
-    there = swap(held, "panel", 1)
-
-    rest = [swap(block, "row", m) for m, block in seconds]
+    shard = lead_cover - (shares[0] + sums[0] + sums[1] + sums[2])
+
+    along = beside(shard[None], lambda x: [swap(x, "row", bit) for bit in (2, 4, 6)], 2)
+    held = jnp.concatenate([shard[None]] + along, 0)
+
+    def across(x):
+        corner = [(i, i ^ 6) for i in range(32)]
+        return swap(x, "row", 1), swap(x, "panel", 2), lax.ppermute(x, ("row", "panel"), corner)
+
+    here = [held, *beside(held, across, 3)]
+
     panel_prior = jnp.zeros((8, NB, own_prior.shape[1]), F32)
     for k, block in enumerate([own_prior, far] + firsts):
         panel_prior = lax.dynamic_update_slice(panel_prior, block[None], (places[k], 0, 0))
     for m, block in zip((1, 2, 3), rest):
         panel_prior = lax.dynamic_update_slice(panel_prior, block[None], (places[m + 1] ^ 4, 0, 0))
-    partial = dot_rows(prior_factor, panel_prior.reshape(B, -1))
-    partial, there = lax.optimization_barrier((partial, there))
-    parts = lax.all_to_all(
-        partial.reshape(4, quarter_rows, B), "panel", split_axis=0, concat_axis=0, tiled=True
-    )
+    here, panel_prior = lax.optimization_barrier((here, panel_prior))
+    there = [swap(x, "panel", 1) for x in here]
+    parts = []
+    for m in (3, 2, 1, 0):
+        rows = lax.dynamic_slice_in_dim(
+            prior_factor, (panel_pos ^ m) * quarter_rows, quarter_rows, 0
+        )
+        part = dot_rows(rows, panel_prior.reshape(B, -1))
+        parts.append(swap(part, "panel", m) if m else part)
     place = jnp.stack([row_pos, panel_pos]).astype(jnp.int32)
-    factors = factor(unfold_kernel, (place, held, there), B)
+    factors = factor(unfold_kernel, (place, *here, *there), B)
     return solve(covers, parts, factors)
 
 

time: 218 us -> 185 us (0.85)
  waiting for transfers between devices: 39.1 us -> 11 us
  local copies, waits for them, and re-layouts: 23.3 us -> 16.1 us
  matrix products: 8.23 us -> 11.3 us
    ppermute x15 -> x26, waiting for transfers between devices: 32.5 us -> 11 us  [swap(): lax.ppermute(block, axis, [(i, i ^ bit) for i in range(lax.axis_size(axis...]
    all_to_all x2 -> x0, starting transfers between devices: 8.5 us -> none  [the longest x1 5.04 us: local(): lax.all_to_all(partial.reshape(4, quarter_rows, B), 'panel', split_axis=0...]
    all_to_all x2 -> x0, waiting for transfers between devices: 6.65 us -> none  [the longest x1 6.64 us: local(): lax.all_to_all(partial.reshape(4, per_device, 5 * NB), 'panel', split_axi...]
    unnamed x50 -> x17, local copies, waits for them, and re-layouts: 8.41 us -> 2.08 us
    ppermute x15 -> x26, starting transfers between devices: 22.3 us -> 28.3 us  [swap(): lax.ppermute(block, axis, [(i, i ^ bit) for i in range(lax.axis_size(axis...]
    optimization_barrier x1 -> x0, local copies, waits for them, and re-layouts: 5.45 us -> none  [local(): partial, there = lax.optimization_barrier((partial, there))]
    dynamic_update_slice x5, local copies, waits for them, and re-layouts: 3.78 us -> 7.4 us  [local(): lax.dynamic_update_slice(panel_prior, block[None], (places[k], 0, 0))]
    dot_general x2 -> x5, matrix products: 8.23 us -> 11.3 us  [dot_rows(): lax.dot_general(left, right, NT, precision=lax.Precision.HIGH, preferred_...]
  transfers between devices with their start and end apart: 17 -> 27, of which waited for: 8 -> 4; matrix products, arithmetic and copies ran while one was open for 8% -> 13% of each run, Pallas kernels for 48% -> 58%
where the time goes in v2:
time: 185 us; the launch traced here: 184 us
  Pallas kernels  111 us (60%)
  starting transfers between devices  29.7 us (16%)
  local copies, waits for them, and re-layouts  16.1 us (9%)
  matrix products  11.3 us (6%)
  waiting for transfers between devices  11 us (6%)
  other arithmetic  3.84 us (2%)
    pallas_call x8, Pallas kernels, cover_rows(): pl.pallas_call(cover_kernel, grid=(1,), out_shape=jax.ShapeDtypeStruct((b...  53.3 us
    pallas_call x1, Pallas kernels, factor(): pl.pallas_call(kernel, out_shape=[jax.ShapeDtypeStruct((n, n), BF)] * 2 +...  52 us
    ppermute x26, starting transfers between devices, swap(): lax.ppermute(block, axis, [(i, i ^ bit) for i in range(lax.axis_size(axis...  28.3 us
    dot_general x5, matrix products, dot_rows(): lax.dot_general(left, right, NT, precision=lax.Precision.HIGH, preferred_...  11.3 us
    ppermute x26, waiting for transfers between devices, swap(): lax.ppermute(block, axis, [(i, i ^ bit) for i in range(lax.axis_size(axis...  11 us
    dynamic_update_slice x5, local copies, waits for them, and re-layouts, local(): lax.dynamic_update_slice(panel_prior, block[None], (places[k], 0, 0))  7.4 us
    pallas_call x1, Pallas kernels, solve(): pl.pallas_call(functools.partial(solve_kernel, covers=len(covers)), out_s...  5.41 us
  transfers between devices with their start and end apart: 27, of which 4 were waited for; matrix products, arithmetic and copies ran while one was open for 13% of the time, Pallas kernels for 58%

profile of v2, /device:TPU:0, one launch (start us, length us, event | category | flops | bytes accessed | tf_op | source)
XLA Modules:
  0.0 183.9 jit_solution(10666707726910249694)
XLA Ops:
  1.8 3.1 %collective-permute-start = (f32[1,32,128]{2,1,0:T(8,128)S(1)}, f32[1,32,128]{2,1,0:T(8,128)S(1)}, u32[]{:S(2)}, u32[]{:S(2)}) collective-permute-start(f32[1,32,128]{2,1,0:T(8,128)S(1)} %reshape.75), channel_id=1, source_target_pairs={{0,8},{4,12},{8,0},{12,4},{16,24},{20,28},{24,16},{28,20},{1,9},{5... | collective-permute-start | bytes 49160 | tf_op jit(solution)/shard_map/ppermute | solution.py:322
  4.9 2.6 %collective-permute-start.1 = (f32[1,32,128]{2,1,0:T(8,128)S(1)}, f32[1,32,128]{2,1,0:T(8,128)S(1)}, u32[]{:S(2)}, u32[]{:S(2)}) collective-permute-start(f32[1,32,128]{2,1,0:T(8,128)S(1)} %reshape.75), channel_id=1, source_target_pairs={{0,16},{4,20},{8,24},{12,28},{16,0},{20,4},{24,8},{28,12},{1,17},{... | collective-permute-start | bytes 49160 | tf_op jit(solution)/shard_map/ppermute | solution.py:322
  8.4 2.0 %collective-permute-start.4 = (f32[128,512]{1,0:T(8,128)S(1)}, f32[128,512]{1,0:T(8,128)}, u32[]{:S(2)}, u32[]{:S(2)}) collective-permute-start(f32[128,512]{1,0:T(8,128)S(1)} %bitcast.45), channel_id=1, source_target_pairs={{0,16},{4,20},{8,24},{12,28},{16,0},{20,4},{24,8},{28,12},{1,17},{... | collective-permute-start | bytes 786440 | tf_op jit(solution)/shard_map/ppermute | solution.py:322
  10.5 1.6 broadcast_in_dim.44
  14.7 2.8 %collective-permute-done.3 = f32[4,32,128]{2,1,0:T(8,128)S(1)} collective-permute-done((f32[4,32,128]{2,1,0:T(8,128)S(1)}, f32[4,32,128]{2,1,0:T(8,128)S(1)}, u32[]{:S(2)}, u32[]{:S(2)}) %collective-permute-start.3) | collective-permute-done | bytes 65568 | tf_op jit(solution)/shard_map/ppermute | solution.py:322
  19.0 3.9 %collective-permute-done.4 = f32[128,512]{1,0:T(8,128)} collective-permute-done((f32[128,512]{1,0:T(8,128)S(1)}, f32[128,512]{1,0:T(8,128)}, u32[]{:S(2)}, u32[]{:S(2)}) %collective-permute-start.4) | collective-permute-done | bytes 262176 | tf_op jit(solution)/shard_map/ppermute | solution.py:322
  22.8 2.0 %broadcast_select_fusion = (f32[128,512]{1,0:T(8,128)}, f32[128,512]{1,0:T(8,128)}, f32[128,512]{1,0:T(8,128)}, f32[128,512]{1,0:T(8,128)}, f32[640,512]{1,0:T(8,128)S(1)}) fusion(f32[128,512]{1,0:T(8,128)} %collective-permute-done.4, pred[]{:T(512)S(6)} %eq.23, f32[4,32,512]{2,1,0:T(8,128)S(1)} %slice.18, pred[]{:T(512)S(6)} %eq.22, ...), kind=kLoop, calls=%fused_computation.23 | loop fusion | flops 262144 | bytes 1835010 | tf_op jit(solution)/shard_map/jit(_where)/select_n | solution.py:400
  26.3 2.0 %collective-permute-start.7 = (f32[128,512]{1,0:T(8,128)}, f32[128,512]{1,0:T(8,128)}, u32[]{:S(2)}, u32[]{:S(2)}) collective-permute-start(f32[128,512]{1,0:T(8,128)} %get-tuple-element.61), channel_id=1, source_target_pairs={{0,12},{4,8},{8,4},{12,0},{16,28},{20,24},{24,20},{28,16},{1,13},{... | collective-permute-start | bytes 786440 | tf_op jit(solution)/shard_map/ppermute | solution.py:322
  28.4 6.8 %cover.9.refs_1_ = f32[32,1024]{1,0:T(8,128)S(1)} custom-call(bf16[16,256,16]{2,1,0:T(8,128)(2,1)S(1)} %get-tuple-element.88.f_ref, bf16[16,16,1024]{2,1,0:T(8,128)(2,1)S(1)} %get-tuple-element.63.g_ref), custom_call_target="tpu_custom_call" | custom-call | flops 100000000 | bytes 262144 | tf_op jit(solution)/shard_map/cover/pallas_call | solution.py:100
  35.2 6.6 %cover.8 = f32[32,1024]{1,0:T(8,128)S(1)} custom-call(bf16[16,256,16]{2,1,0:T(8,128)(2,1)S(1)} %get-tuple-element.88.f_ref, bf16[16,16,1024]{2,1,0:T(8,128)(2,1)S(1)} %get-tuple-element.63.g_ref), custom_call_target="tpu_custom_call" | custom-call | flops 100000000 | bytes 262144 | tf_op jit(solution)/shard_map/cover/pallas_call | solution.py:100
  41.8 1.7 bitcast_dynamic-update-slice_fusion.6
  47.3 1.6 collective-permute-start.11
  48.9 2.0 %collective-permute-start.13 = (f32[128,512]{1,0:T(8,128)S(1)}, f32[128,512]{1,0:T(8,128)S(1)}, u32[]{:S(2)}, u32[]{:S(2)}) collective-permute-start(f32[128,512]{1,0:T(8,128)S(1)} %copy-done.1), channel_id=1, source_target_pairs={{0,12},{4,8},{8,4},{12,0},{16,28},{20,24},{24,20},{28,16},{1,13},{... | collective-permute-start | bytes 786440 | tf_op jit(solution)/shard_map/ppermute | solution.py:322
  50.9 1.6 collective-permute-start.8
  52.5 1.7 bitcast_dynamic-update-slice_fusion.5
  54.2 1.7 bitcast_dynamic-update-slice_fusion.4
  55.9 1.7 bitcast_dynamic-update-slice_fusion.3
  57.7 6.6 %cover.10.refs_2_ = f32[32,1024]{1,0:T(8,128)S(1)} custom-call(bf16[16,256,16]{2,1,0:T(8,128)(2,1)S(1)} %get-tuple-element.88.f_ref, bf16[16,16,1024]{2,1,0:T(8,128)(2,1)S(1)} %get-tuple-element.63.g_ref), custom_call_target="tpu_custom_call" | custom-call | flops 100000000 | bytes 262144 | tf_op jit(solution)/shard_map/cover/pallas_call | solution.py:100
  65.0 3.9 %collective-permute-done.9 = f32[32,640]{1,0:T(8,128)S(1)} collective-permute-done((f32[32,640]{1,0:T(8,128)S(1)}, f32[32,640]{1,0:T(8,128)S(1)}, u32[]{:S(2)}, u32[]{:S(2)}) %collective-permute-start.9) | collective-permute-done | bytes 81952 | tf_op jit(solution)/shard_map/ppermute | solution.py:322
  69.1 2.7 %collective-permute-start.15 = (f32[1,32,640]{2,1,0:T(8,128)S(1)}, f32[1,32,640]{2,1,0:T(8,128)S(1)}, u32[]{:S(2)}, u32[]{:S(2)}) collective-permute-start(f32[1,32,640]{2,1,0:T(8,128)S(1)} %subtract_bitcast_fusion), channel_id=1, source_target_pairs={{0,16},{4,20},{8,24},{12,28},{16,0},{20,4},{24,8},{28,12},{1,17},{... | collective-permute-start | bytes 245768 | tf_op jit(solution)/shard_map/ppermute | solution.py:322
  74.1 6.6 %cover.12.refs_4_ = f32[32,1024]{1,0:T(8,128)S(1)} custom-call(bf16[16,256,16]{2,1,0:T(8,128)(2,1)S(1)} %get-tuple-element.88.f_ref, bf16[16,16,1024]{2,1,0:T(8,128)(2,1)S(1)} %get-tuple-element.63.g_ref), custom_call_target="tpu_custom_call" | custom-call | flops 100000000 | bytes 262144 | tf_op jit(solution)/shard_map/cover/pallas_call | solution.py:100
  80.8 6.6 %cover.11.refs_3_ = f32[32,1024]{1,0:T(8,128)S(1)} custom-call(bf16[16,256,16]{2,1,0:T(8,128)(2,1)S(1)} %get-tuple-element.88.f_ref, bf16[16,16,1024]{2,1,0:T(8,128)(2,1)S(1)} %get-tuple-element.63.g_ref), custom_call_target="tpu_custom_call" | custom-call | flops 100000000 | bytes 262144 | tf_op jit(solution)/shard_map/cover/pallas_call | solution.py:100
  92.5 6.6 %cover.15.refs_7_ = f32[32,1024]{1,0:T(8,128)S(1)} custom-call(bf16[16,256,16]{2,1,0:T(8,128)(2,1)S(1)} %get-tuple-element.88.f_ref, bf16[16,16,1024]{2,1,0:T(8,128)(2,1)S(1)} %get-tuple-element.63.g_ref), custom_call_target="tpu_custom_call" | custom-call | flops 100000000 | bytes 262144 | tf_op jit(solution)/shard_map/cover/pallas_call | solution.py:100
  99.1 6.6 %cover.14.refs_6_ = f32[32,1024]{1,0:T(8,128)S(1)} custom-call(bf16[16,256,16]{2,1,0:T(8,128)(2,1)S(1)} %get-tuple-element.88.f_ref, bf16[16,16,1024]{2,1,0:T(8,128)(2,1)S(1)} %get-tuple-element.63.g_ref), custom_call_target="tpu_custom_call" | custom-call | flops 100000000 | bytes 262144 | tf_op jit(solution)/shard_map/cover/pallas_call | solution.py:100
  105.8 6.6 %cover.13.refs_5_ = f32[32,1024]{1,0:T(8,128)S(1)} custom-call(bf16[16,256,16]{2,1,0:T(8,128)(2,1)S(1)} %get-tuple-element.88.f_ref, bf16[16,16,1024]{2,1,0:T(8,128)(2,1)S(1)} %get-tuple-element.63.g_ref), custom_call_target="tpu_custom_call" | custom-call | flops 100000000 | bytes 262144 | tf_op jit(solution)/shard_map/cover/pallas_call | solution.py:100
  113.5 2.6 %fusion.refs_11_ = f32[256,1024]{1,0:T(8,128)S(1)} fusion(f32[1024,512]{1,0:T(8,128)} %bitcast.17, f32[1024,512]{1,0:T(8,128)S(1)} %copy-done, s32[]{:T(128)S(6)} %select_n.119), kind=kOutput, calls=%fused_computation.1 | convolution fusion | flops 805306368 | bytes 3670020 | tf_op jit(solution)/shard_map/dot_general | solution.py:326
  116.2 2.6 %fusion.4 = f32[256,1024]{1,0:T(8,128)S(1)} fusion(f32[1024,512]{1,0:T(8,128)} %bitcast.17, f32[1024,512]{1,0:T(8,128)S(1)} %copy-done, s32[]{:T(128)S(6)} %select_n.145), kind=kOutput, calls=%fused_computation.5 | convolution fusion | flops 805306368 | bytes 3670020 | tf_op jit(solution)/shard_map/dot_general | solution.py:326
  119.4 2.6 %fusion.2 = f32[256,1024]{1,0:T(8,128)S(1)} fusion(f32[1024,512]{1,0:T(8,128)} %bitcast.17, f32[1024,512]{1,0:T(8,128)S(1)} %copy-done, s32[]{:T(128)S(6)} %select_n.146), kind=kOutput, calls=%fused_computation.3 | convolution fusion | flops 805306368 | bytes 3670020 | tf_op jit(solution)/shard_map/dot_general | solution.py:326
  122.1 2.6 %fusion.6 = f32[256,1024]{1,0:T(8,128)S(1)} fusion(f32[1024,512]{1,0:T(8,128)} %bitcast.17, f32[1024,512]{1,0:T(8,128)S(1)} %copy-done, s32[]{:T(128)S(6)} %select_n.136), kind=kOutput, calls=%fused_computation.7 | convolution fusion | flops 805306368 | bytes 3670020 | tf_op jit(solution)/shard_map/dot_general | solution.py:326
  124.8 1.6 collective-permute-start.20
  126.5 52.0 %factor.1 = (bf16[1024,1024]{1,0:T(8,128)(2,1)S(1)}, bf16[1024,1024]{1,0:T(8,128)(2,1)S(1)}, bf16[1024,128]{1,0:T(8,128)(2,1)S(1)}, bf16[1024,128]{1,0:T(8,128)(2,1)S(1)}) custom-call(s32[2]{0:T(128)S(1)} %pad_add_fusion.place_ref, f32[4,32,640]{2,1,0:T(8,128)S(1)} %pad_maximum_fusion.refs_0_, f32[4,32,640]{2,1,0:T(8,128)S(1)} %collective-permute-done.17.refs_1_, ...), custom_call_target="tpu_custom_call" | custom-call | flops 49999998976 | bytes 8388608 | tf_op jit(solution)/shard_map/factor/pallas_call | solution.py:268
  178.5 5.4 %solve.1 = f32[256,1024]{1,0:T(8,128)} custom-call(f32[32,1024]{1,0:T(8,128)S(1)} %select_add_fusion.refs_0_, f32[32,1024]{1,0:T(8,128)S(1)} %cover.9.refs_1_, f32[32,1024]{1,0:T(8,128)S(1)} %cover.10.refs_2_, f32[32,1024]{1,0:T(8,128)S(1)} %cover.11.refs_3_, f32[32,1024]{1,0:T(8,128)S(1)} %cover.12.refs_4_, f32[32,1024]{1,0:T(8,128)S(1)} %cover.13.refs_5_, ...), custom_call_target="tpu_custom_call" | custom-call | tf_op jit(solution)/shard_map/solve/pallas_call | solution.py:310
  (89 shorter events, 22.1 us)
Async XLA Ops:
  1.8 11.1 %collective-permute-start = (f32[1,32,128]{2,1,0:T(8,128)S(1)}, f32[1,32,128]{2,1,0:T(8,128)S(1)}, u32[]{:S(2)}, u32[]{:S(2)}) collective-permute-start(f32[1,32,128]{2,1,0:T(8,128)S(1)} %reshape.75), channel_id=1, source_target_pairs={{0,8},{4,12},{8,0},{12,4},{16,24},{20,28},{24,16},{28,20},{1,9},{5... | collective-permute-start | bytes 49160 | tf_op jit(solution)/shard_map/ppermute | solution.py:322
  4.9 8.0 %collective-permute-start.1 = (f32[1,32,128]{2,1,0:T(8,128)S(1)}, f32[1,32,128]{2,1,0:T(8,128)S(1)}, u32[]{:S(2)}, u32[]{:S(2)}) collective-permute-start(f32[1,32,128]{2,1,0:T(8,128)S(1)} %reshape.75), channel_id=1, source_target_pairs={{0,16},{4,20},{8,24},{12,28},{16,0},{20,4},{24,8},{28,12},{1,17},{... | collective-permute-start | bytes 49160 | tf_op jit(solution)/shard_map/ppermute | solution.py:322
  7.5 5.8 %collective-permute-start.2 = (f32[1,32,128]{2,1,0:T(8,128)S(1)}, f32[1,32,128]{2,1,0:T(8,128)S(1)}, u32[]{:S(2)}, u32[]{:S(2)}) collective-permute-start(f32[1,32,128]{2,1,0:T(8,128)S(1)} %reshape.75), channel_id=1, source_target_pairs={{0,24},{4,28},{8,16},{12,20},{16,8},{20,12},{24,0},{28,4},{1,25},{... | collective-permute-start | bytes 49160 | tf_op jit(solution)/shard_map/ppermute | solution.py:322
  8.4 14.4 %collective-permute-start.4 = (f32[128,512]{1,0:T(8,128)S(1)}, f32[128,512]{1,0:T(8,128)}, u32[]{:S(2)}, u32[]{:S(2)}) collective-permute-start(f32[128,512]{1,0:T(8,128)S(1)} %bitcast.45), channel_id=1, source_target_pairs={{0,16},{4,20},{8,24},{12,28},{16,0},{20,4},{24,8},{28,12},{1,17},{... | collective-permute-start | bytes 786440 | tf_op jit(solution)/shard_map/ppermute | solution.py:322
  13.2 4.3 %collective-permute-start.3 = (f32[4,32,128]{2,1,0:T(8,128)S(1)}, f32[4,32,128]{2,1,0:T(8,128)S(1)}, u32[]{:S(2)}, u32[]{:S(2)}) collective-permute-start(f32[4,32,128]{2,1,0:T(8,128)S(1)} %pad_maximum_fusion.2), channel_id=1, source_target_pairs={{0,4},{4,0},{8,12},{12,8},{16,20},{20,16},{24,28},{28,24},{1,5},{5... | collective-permute-start | bytes 196616 | tf_op jit(solution)/shard_map/ppermute | solution.py:322
  24.8 18.7 %collective-permute-start.5 = (f32[128,512]{1,0:T(8,128)}, f32[128,512]{1,0:T(8,128)}, u32[]{:S(2)}, u32[]{:S(2)}) collective-permute-start(f32[128,512]{1,0:T(8,128)} %get-tuple-element.59), channel_id=1, source_target_pairs={{0,4},{4,0},{8,12},{12,8},{16,20},{20,16},{24,28},{28,24},{1,5},{5... | collective-permute-start | bytes 786440 | tf_op jit(solution)/shard_map/ppermute | solution.py:322
  26.3 17.2 %collective-permute-start.6 = (f32[128,512]{1,0:T(8,128)}, f32[128,512]{1,0:T(8,128)}, u32[]{:S(2)}, u32[]{:S(2)}) collective-permute-start(f32[128,512]{1,0:T(8,128)} %get-tuple-element.61), channel_id=1, source_target_pairs={{0,8},{4,12},{8,0},{12,4},{16,24},{20,28},{24,16},{28,20},{1,9},{5... | collective-permute-start | bytes 786440 | tf_op jit(solution)/shard_map/ppermute | solution.py:322
  26.3 17.2 %collective-permute-start.7 = (f32[128,512]{1,0:T(8,128)}, f32[128,512]{1,0:T(8,128)}, u32[]{:S(2)}, u32[]{:S(2)}) collective-permute-start(f32[128,512]{1,0:T(8,128)} %get-tuple-element.61), channel_id=1, source_target_pairs={{0,12},{4,8},{8,4},{12,0},{16,28},{20,24},{24,20},{28,16},{1,13},{... | collective-permute-start | bytes 786440 | tf_op jit(solution)/shard_map/ppermute | solution.py:322
  43.5 3.8 %copy-start.2 = (f32[128,512]{1,0:T(8,128)S(1)}, f32[128,512]{1,0:T(8,128)}, u32[]{:S(2)}) copy-start(f32[128,512]{1,0:T(8,128)} %get-tuple-element.72) | copy-start | bytes 786436
  43.5 5.4 %copy-start.1 = (f32[128,512]{1,0:T(8,128)S(1)}, f32[128,512]{1,0:T(8,128)}, u32[]{:S(2)}) copy-start(f32[128,512]{1,0:T(8,128)} %get-tuple-element.74) | copy-start | bytes 786436
  47.3 21.6 %collective-permute-start.11 = (f32[128,512]{1,0:T(8,128)S(1)}, f32[128,512]{1,0:T(8,128)S(1)}, u32[]{:S(2)}, u32[]{:S(2)}) collective-permute-start(f32[128,512]{1,0:T(8,128)S(1)} %copy-done.2), channel_id=1, source_target_pairs={{0,4},{4,0},{8,12},{12,8},{16,20},{20,16},{24,28},{28,24},{1,5},{5... | collective-permute-start | bytes 786440 | tf_op jit(solution)/shard_map/ppermute | solution.py:322
  48.9 20.0 %collective-permute-start.12 = (f32[128,512]{1,0:T(8,128)S(1)}, f32[128,512]{1,0:T(8,128)S(1)}, u32[]{:S(2)}, u32[]{:S(2)}) collective-permute-start(f32[128,512]{1,0:T(8,128)S(1)} %copy-done.1), channel_id=1, source_target_pairs={{0,8},{4,12},{8,0},{12,4},{16,24},{20,28},{24,16},{28,20},{1,9},{5... | collective-permute-start | bytes 786440 | tf_op jit(solution)/shard_map/ppermute | solution.py:322
  48.9 20.0 %collective-permute-start.13 = (f32[128,512]{1,0:T(8,128)S(1)}, f32[128,512]{1,0:T(8,128)S(1)}, u32[]{:S(2)}, u32[]{:S(2)}) collective-permute-start(f32[128,512]{1,0:T(8,128)S(1)} %copy-done.1), channel_id=1, source_target_pairs={{0,12},{4,8},{8,4},{12,0},{16,28},{20,24},{24,20},{28,16},{1,13},{... | collective-permute-start | bytes 786440 | tf_op jit(solution)/shard_map/ppermute | solution.py:322
  50.9 13.5 %collective-permute-start.10 = (f32[32,640]{1,0:T(8,128)S(1)}, f32[32,640]{1,0:T(8,128)S(1)}, u32[]{:S(2)}, u32[]{:S(2)}) collective-permute-start(f32[32,640]{1,0:T(8,128)S(1)} %get-tuple-element.71), channel_id=1, source_target_pairs={{0,3},{1,2},{2,1},{3,0},{4,7},{5,6},{6,5},{7,4},{8,11},{9,10},{10,... | collective-permute-start | bytes 245768 | tf_op jit(solution)/shard_map/ppermute | solution.py:322
  50.9 14.1 %collective-permute-start.8 = (f32[32,640]{1,0:T(8,128)S(1)}, f32[32,640]{1,0:T(8,128)S(1)}, u32[]{:S(2)}, u32[]{:S(2)}) collective-permute-start(f32[32,640]{1,0:T(8,128)S(1)} %get-tuple-element.69), channel_id=1, source_target_pairs={{0,1},{1,0},{2,3},{3,2},{4,5},{5,4},{6,7},{7,6},{8,9},{9,8},{10,11... | collective-permute-start | bytes 245768 | tf_op jit(solution)/shard_map/ppermute | solution.py:322
  64.4 4.5 %collective-permute-start.9 = (f32[32,640]{1,0:T(8,128)S(1)}, f32[32,640]{1,0:T(8,128)S(1)}, u32[]{:S(2)}, u32[]{:S(2)}) collective-permute-start(f32[32,640]{1,0:T(8,128)S(1)} %get-tuple-element.70), channel_id=1, source_target_pairs={{0,2},{1,3},{2,0},{3,1},{4,6},{5,7},{6,4},{7,5},{8,10},{9,11},{10,... | collective-permute-start | bytes 245768 | tf_op jit(solution)/shard_map/ppermute | solution.py:322
  68.9 18.5 %collective-permute-start.14 = (f32[1,32,640]{2,1,0:T(8,128)S(1)}, f32[1,32,640]{2,1,0:T(8,128)S(1)}, u32[]{:S(2)}, u32[]{:S(2)}) collective-permute-start(f32[1,32,640]{2,1,0:T(8,128)S(1)} %subtract_bitcast_fusion), channel_id=1, source_target_pairs={{0,8},{4,12},{8,0},{12,4},{16,24},{20,28},{24,16},{28,20},{1,9},{5... | collective-permute-start | bytes 245768 | tf_op jit(solution)/shard_map/ppermute | solution.py:322
  69.1 18.3 %collective-permute-start.15 = (f32[1,32,640]{2,1,0:T(8,128)S(1)}, f32[1,32,640]{2,1,0:T(8,128)S(1)}, u32[]{:S(2)}, u32[]{:S(2)}) collective-permute-start(f32[1,32,640]{2,1,0:T(8,128)S(1)} %subtract_bitcast_fusion), channel_id=1, source_target_pairs={{0,16},{4,20},{8,24},{12,28},{16,0},{20,4},{24,8},{28,12},{1,17},{... | collective-permute-start | bytes 245768 | tf_op jit(solution)/shard_map/ppermute | solution.py:322
  71.8 15.6 %collective-permute-start.16 = (f32[1,32,640]{2,1,0:T(8,128)S(1)}, f32[1,32,640]{2,1,0:T(8,128)S(1)}, u32[]{:S(2)}, u32[]{:S(2)}) collective-permute-start(f32[1,32,640]{2,1,0:T(8,128)S(1)} %subtract_bitcast_fusion), channel_id=1, source_target_pairs={{0,24},{4,28},{8,16},{12,20},{16,8},{20,12},{24,0},{28,4},{1,25},{... | collective-permute-start | bytes 245768 | tf_op jit(solution)/shard_map/ppermute | solution.py:322
  87.5 25.0 %collective-permute-start.17 = (f32[4,32,640]{2,1,0:T(8,128)S(1)}, f32[4,32,640]{2,1,0:T(8,128)S(1)}, u32[]{:S(2)}, u32[]{:S(2)}) collective-permute-start(f32[4,32,640]{2,1,0:T(8,128)S(1)} %pad_maximum_fusion.refs_0_), channel_id=1, source_target_pairs={{0,4},{4,0},{8,12},{12,8},{16,20},{20,16},{24,28},{28,24},{1,5},{5... | collective-permute-start | bytes 983048 | tf_op jit(solution)/shard_map/ppermute | solution.py:322
  89.0 23.4 %collective-permute-start.18 = (f32[4,32,640]{2,1,0:T(8,128)S(1)}, f32[4,32,640]{2,1,0:T(8,128)S(1)}, u32[]{:S(2)}, u32[]{:S(2)}) collective-permute-start(f32[4,32,640]{2,1,0:T(8,128)S(1)} %pad_maximum_fusion.refs_0_), channel_id=1, source_target_pairs={{0,2},{1,3},{2,0},{3,1},{4,6},{5,7},{6,4},{7,5},{8,10},{9,11},{10,... | collective-permute-start | bytes 983048 | tf_op jit(solution)/shard_map/ppermute | solution.py:322
  89.5 22.9 %collective-permute-start.19 = (f32[4,32,640]{2,1,0:T(8,128)S(1)}, f32[4,32,640]{2,1,0:T(8,128)S(1)}, u32[]{:S(2)}, u32[]{:S(2)}) collective-permute-start(f32[4,32,640]{2,1,0:T(8,128)S(1)} %pad_maximum_fusion.refs_0_), channel_id=1, source_target_pairs={{0,6},{1,7},{2,4},{3,5},{4,2},{5,3},{6,0},{7,1},{8,14},{9,15},{10,... | collective-permute-start | bytes 983048 | tf_op jit(solution)/shard_map/ppermute | solution.py:425
  99.1 14.4 %copy-start = (f32[1024,512]{1,0:T(8,128)S(1)}, f32[1024,512]{1,0:T(8,128)}, u32[]{:S(2)}) copy-start(f32[1024,512]{1,0:T(8,128)} %param.5) | copy-start | bytes 6291460
  112.5 12.3 %collective-permute-start.23 = (f32[4,32,640]{2,1,0:T(8,128)S(1)}, f32[4,32,640]{2,1,0:T(8,128)S(1)}, u32[]{:S(2)}, u32[]{:S(2)}) collective-permute-start(f32[4,32,640]{2,1,0:T(8,128)S(1)} %pad_maximum_fusion.refs_0_), channel_id=1, source_target_pairs={{0,1},{1,0},{2,3},{3,2},{4,5},{5,4},{6,7},{7,6},{8,9},{9,8},{10,11... | collective-permute-start | bytes 983048 | tf_op jit(solution)/shard_map/ppermute | solution.py:322
  112.5 12.3 %collective-permute-start.24 = (f32[4,32,640]{2,1,0:T(8,128)S(1)}, f32[4,32,640]{2,1,0:T(8,128)S(1)}, u32[]{:S(2)}, u32[]{:S(2)}) collective-permute-start(f32[4,32,640]{2,1,0:T(8,128)S(1)} %collective-permute-done.17.refs_1_), channel_id=1, source_target_pairs={{0,1},{1,0},{2,3},{3,2},{4,5},{5,4},{6,7},{7,6},{8,9},{9,8},{10,11... | collective-permute-start | bytes 983048 | tf_op jit(solution)/shard_map/ppermute | solution.py:322
  113.0 13.4 %collective-permute-start.25 = (f32[4,32,640]{2,1,0:T(8,128)S(1)}, f32[4,32,640]{2,1,0:T(8,128)S(1)}, u32[]{:S(2)}, u32[]{:S(2)}) collective-permute-start(f32[4,32,640]{2,1,0:T(8,128)S(1)} %collective-permute-done.18.refs_2_), channel_id=1, source_target_pairs={{0,1},{1,0},{2,3},{3,2},{4,5},{5,4},{6,7},{7,6},{8,9},{9,8},{10,11... | collective-permute-start | bytes 983048 | tf_op jit(solution)/shard_map/ppermute | solution.py:322
  113.1 13.4 %collective-permute-start.26 = (f32[4,32,640]{2,1,0:T(8,128)S(1)}, f32[4,32,640]{2,1,0:T(8,128)S(1)}, u32[]{:S(2)}, u32[]{:S(2)}) collective-permute-start(f32[4,32,640]{2,1,0:T(8,128)S(1)} %collective-permute-done.19.refs_3_), channel_id=1, source_target_pairs={{0,1},{1,0},{2,3},{3,2},{4,5},{5,4},{6,7},{7,6},{8,9},{9,8},{10,11... | collective-permute-start | bytes 983048 | tf_op jit(solution)/shard_map/ppermute | solution.py:322
  118.8 59.6 %collective-permute-start.21 = (f32[256,1024]{1,0:T(8,128)S(1)}, f32[256,1024]{1,0:T(8,128)S(1)}, u32[]{:S(2)}, u32[]{:S(2)}) collective-permute-start(f32[256,1024]{1,0:T(8,128)S(1)} %fusion.4), channel_id=1, source_target_pairs={{0,2},{1,3},{2,0},{3,1},{4,6},{5,7},{6,4},{7,5},{8,10},{9,11},{10,... | collective-permute-start | bytes 3145736 | tf_op jit(solution)/shard_map/ppermute | solution.py:322
  124.7 53.8 %collective-permute-start.22 = (f32[256,1024]{1,0:T(8,128)S(1)}, f32[256,1024]{1,0:T(8,128)S(1)}, u32[]{:S(2)}, u32[]{:S(2)}) collective-permute-start(f32[256,1024]{1,0:T(8,128)S(1)} %fusion.2), channel_id=1, source_target_pairs={{0,1},{1,0},{2,3},{3,2},{4,5},{5,4},{6,7},{7,6},{8,9},{9,8},{10,11... | collective-permute-start | bytes 3145736 | tf_op jit(solution)/shard_map/ppermute | solution.py:322
  124.8 53.7 %collective-permute-start.20 = (f32[256,1024]{1,0:T(8,128)S(1)}, f32[256,1024]{1,0:T(8,128)S(1)}, u32[]{:S(2)}, u32[]{:S(2)}) collective-permute-start(f32[256,1024]{1,0:T(8,128)S(1)} %fusion.6), channel_id=1, source_target_pairs={{0,3},{1,2},{2,1},{3,0},{4,7},{5,6},{6,5},{7,4},{8,11},{9,10},{10,... | collective-permute-start | bytes 3145736 | tf_op jit(solution)/shard_map/ppermute | solution.py:322

commit v3 on v2

--- a/solution.py
+++ b/solution.py
@@ -9,7 +9,7 @@
 
 B = 1024
 NB = 128
-GROUP = 8
+NEAR = 4
 F32 = jnp.float32
 BF = jnp.bfloat16
 NT = (((1,), (1,)), ((), ()))
@@ -89,7 +89,7 @@
             total = total + near[a * block : (a + 1) * block]
         return total
 
-    total = lax.fori_loop(0, count, column_point, jnp.zeros(o_ref.shape, F32))
+    total = lax.fori_loop(0, count, column_point, jnp.zeros(o_ref.shape, F32), unroll=8)
     o_ref[...] = total * (1.0 / (count * count))
 
 
@@ -113,42 +113,61 @@
 
 
 def inverse_factor(tiles):
-    width = 8 * len(tiles)
+    n = len(tiles)
+    width = 8 * n
     lane = lax.broadcasted_iota(jnp.int32, (8, width), 1)
     sub = lax.broadcasted_iota(jnp.int32, (8, width), 0)
     tiles = list(tiles)
-    n = len(tiles)
     out = []
+
+    def spread(x):
+        return jnp.broadcast_to(x, (8, width))
+
+    def lanes(tile, v):
+        return [spread(tile[:, 8 * v + q : 8 * v + q + 1]) for q in range(8)]
+
+    following = lanes(tiles[0], 0)
     for v in range(n):
+        near = min(n, v + NEAR)
+        cols = {v: following}
+        if v + 1 < n:
+            cols[v] = cols[v] + lanes(tiles[v], v + 1)
+            cols[v + 1] = lanes(tiles[v + 1], v) + lanes(tiles[v + 1], v + 1)
+        for r in range(v + 2, near):
+            cols[r] = lanes(tiles[r], v)
+        here = (lane >= 8 * v) & (lane < 8 * v + 8)
+        for r in range(v + 1, n):
+            tiles[r] = jnp.where(here, 0.0, tiles[r])
+        tiles[v] = jnp.where(here, jnp.where(lane == sub + 8 * v, 1.0, 0.0), tiles[v])
         pivots = jnp.ones((8, width), F32)
-        for g in range(0, 8, GROUP):
-            cols = [
-                [
-                    jnp.broadcast_to(tiles[r][:, 8 * v + g + q : 8 * v + g + q + 1], (8, width))
-                    for q in range(GROUP)
-                ]
-                for r in range(v, n)
-            ]
-            for q in range(GROUP):
-                s = g + q
-                p = 8 * v + s
-                pivot = jnp.broadcast_to(cols[0][q][s : s + 1], (8, width))
-                inverse = 1.0 / pivot
-                pivots = jnp.where(sub == s, pivot, pivots)
-                row = jnp.where(lane == p, 1.0, jnp.broadcast_to(tiles[v][s : s + 1], (8, width)))
-                heads = [
-                    jnp.broadcast_to(cols[0][k][s : s + 1], (8, width)) for k in range(q + 1, GROUP)
-                ]
-                for r in range(v, n):
-                    part = cols[r - v][q] * inverse
-                    if r == v:
-                        part = jnp.where(sub > s, part, 0.0)
-                    tiles[r] = jnp.where(lane == p, 0.0, tiles[r]) - part * row
-                    for k in range(q + 1, GROUP):
-                        cols[r - v][k] = cols[r - v][k] - part * heads[k - q - 1]
-        row_id = sub + 8 * v
-        unit = jnp.where(lane == row_id, 1.0, 0.0)
-        out.append(jnp.where(lane < row_id, tiles[v], unit) * lax.rsqrt(pivots))
+        for s in range(8):
+            head = cols[v]
+            pivot = spread(head[s][s : s + 1])
+            inverse = 1.0 / pivot
+            pivots = jnp.where(sub == s, pivot, pivots)
+            row = spread(tiles[v][s : s + 1])
+            heads = [spread(head[k][s : s + 1]) for k in range(s + 1, len(head))]
+            for r in range(v, near):
+                part = cols[r][s] * inverse
+                if r == v:
+                    part = jnp.where(sub > s, part, 0.0)
+                tiles[r] = tiles[r] - part * row
+                for k in range(s + 1, len(cols[r])):
+                    cols[r][k] = cols[r][k] - part * heads[k - s - 1]
+        if v + 1 < n:
+            following = cols[v + 1][8:]
+        rows = tiles[v] * lax.rsqrt(pivots)
+        if near < n:
+            high = rows.astype(BF).astype(F32)
+            low = rows - high
+            left = jnp.concatenate([high, high, low, low], 0).astype(BF)
+            right = jnp.concatenate([high, low, high, low], 0).astype(BF)
+            update = lax.dot_general(
+                left, right, (((0,), (0,)), ((), ())), preferred_element_type=F32
+            )
+            for r in range(near, n):
+                tiles[r] = tiles[r] - update[8 * r : 8 * r + 8]
+        out.append(jnp.where(lane <= sub + 8 * v, rows, 0.0))
     return jnp.concatenate(out, 0)
 
 
@@ -165,6 +184,19 @@
 def factor_blocks(a_ref, lh_ref, ll_ref, wh_ref, wl_ref):
     n = a_ref.shape[0]
     blocks = n // NB
+
+    def column(first):
+        end = first + NB
+        bh, bl = split(a_ref[end:, first:end])
+        high, low = split(dot3(bh, bl, wh_ref[first:end], wl_ref[first:end]))
+        lh_ref[end:, first:end] = high
+        ll_ref[end:, first:end] = low
+        a_ref[end:, end : end + NB] = a_ref[end:, end : end + NB] - dot3(
+            lh_ref[end:, :end],
+            ll_ref[end:, :end],
+            lh_ref[end : end + NB, :end],
+            ll_ref[end : end + NB, :end],
+        )
 
     def step(j, _):
         c = pl.multiple_of(j * NB, NB)
@@ -172,28 +204,8 @@
         wh, wl = split(inverse_factor(tiles))
         wh_ref[pl.ds(c, NB)] = wh
         wl_ref[pl.ds(c, NB)] = wl
-
-        def panel(i, _):
-            r = pl.multiple_of(i * NB, NB)
-            bh, bl = split(a_ref[pl.ds(r, NB), pl.ds(c, NB)])
-            high, low = split(dot3(bh, bl, wh, wl))
-            lh_ref[pl.ds(r, NB), pl.ds(c, NB)] = high
-            ll_ref[pl.ds(r, NB), pl.ds(c, NB)] = low
-            return 0
-
-        lax.fori_loop(j + 1, blocks, panel, 0)
-
-        def trail(i, _):
-            r = pl.multiple_of(i * NB, NB)
-            a_ref[pl.ds(r, NB)] = a_ref[pl.ds(r, NB)] - dot3(
-                lh_ref[pl.ds(r, NB), pl.ds(c, NB)],
-                ll_ref[pl.ds(r, NB), pl.ds(c, NB)],
-                lh_ref[:, pl.ds(c, NB)],
-                ll_ref[:, pl.ds(c, NB)],
-            )
-            return 0
-
-        lax.fori_loop(j + 1, blocks, trail, 0)
+        for block in range(blocks - 1):
+            pl.when(j == block)(functools.partial(column, block * NB))
         return 0
 
     lax.fori_loop(0, blocks, step, 0)
@@ -201,8 +213,6 @@
 
 def factor_kernel(diag_ref, lh_ref, ll_ref, wh_ref, wl_ref, a_ref):
     a_ref[...] = diag_ref[...]
-    lh_ref[...] = jnp.zeros_like(lh_ref)
-    ll_ref[...] = jnp.zeros_like(ll_ref)
     factor_blocks(a_ref, lh_ref, ll_ref, wh_ref, wl_ref)
 
 
@@ -219,8 +229,6 @@
     pieces_refs, (lh_ref, ll_ref, wh_ref, wl_ref, a_ref, g_ref) = refs[:8], refs[8:]
     row_pos = place_ref[0]
     panel_pos = place_ref[1]
-    lh_ref[...] = jnp.zeros_like(lh_ref)
-    ll_ref[...] = jnp.zeros_like(ll_ref)
     for i, ref in enumerate(pieces_refs):
         g_ref[4 * i : 4 * i + 4] = ref[...]
 
@@ -318,6 +326,54 @@
     )(*operands)
 
 
+def vmem_call(kernel, out_shape, place, operands, scratch=(), name=None):
+    return pl.pallas_call(
+        kernel,
+        out_shape=out_shape,
+        in_specs=[pl.BlockSpec(memory_space=pltpu.SMEM)]
+        + [pl.BlockSpec(memory_space=pltpu.VMEM)] * len(operands),
+        out_specs=jax.tree.map(lambda _: pl.BlockSpec(memory_space=pltpu.VMEM), out_shape),
+        scratch_shapes=list(scratch),
+        compiler_params=pltpu.CompilerParams(vmem_limit_bytes=16 << 20),
+        cost_estimate=pl.CostEstimate(flops=10**8, bytes_accessed=1 << 18, transcendentals=0),
+        name=name,
+    )(place, *operands)
+
+
+def fold_products_kernel(place_ref, *refs):
+    blocks, shares, total_ref = refs[:5], refs[5:-1], refs[-1]
+    own_high, own_low = split(blocks[0][...])
+    for k, ref in enumerate(blocks):
+        high, low = split(ref[...])
+        total_ref[:, NB * k : NB * k + NB] = dot3(own_high, own_low, high, low)
+    rows = shares[0].shape[0]
+    for m, ref in enumerate(shares):
+        first = pl.multiple_of((place_ref[1] ^ m) * rows, rows)
+        ref[...] = total_ref[pl.ds(first, rows)]
+
+
+def gather_split_kernel(place_ref, *refs):
+    blocks, (high_ref, low_ref) = refs[:-2], refs[-2:]
+    row_pos = place_ref[0]
+    order = [fold_block(row_pos, k) for k in range(5)]
+    order = order + [order[k] ^ 4 for k in (2, 3, 4)]
+    for s, ref in zip(order, blocks):
+        first = pl.multiple_of(s * NB, NB)
+        high, low = split(ref[...])
+        high_ref[pl.ds(first, NB)] = high
+        low_ref[pl.ds(first, NB)] = low
+
+
+def rest_products_kernel(place_ref, prior_ref, high_ref, low_ref, o_ref, *, m):
+    rows = o_ref.shape[0]
+    first = pl.multiple_of((place_ref[1] ^ m) * rows, rows)
+    own_high, own_low = split(prior_ref[pl.ds(first, rows)])
+    for c in range(0, o_ref.shape[1], 2 * NB):
+        o_ref[:, c : c + 2 * NB] = dot3(
+            own_high, own_low, high_ref[c : c + 2 * NB], low_ref[c : c + 2 * NB]
+        )
+
+
 def swap(block, axis, bit):
     return lax.ppermute(block, axis, [(i, i ^ bit) for i in range(lax.axis_size(axis))])
 
@@ -396,20 +452,23 @@
         lambda blocks: [swap(block, "row", m) for m, block in zip((1, 2, 3), blocks)],
         2,
     )
-    partial = dot_rows(own_prior, jnp.concatenate([own_prior, far] + firsts, 0))
+    place = jnp.stack([row_pos, panel_pos]).astype(jnp.int32)
+    shares = vmem_call(
+        fold_products_kernel,
+        [jax.ShapeDtypeStruct((per_device, 5 * NB), F32)] * 4,
+        place,
+        [own_prior, far, *firsts],
+        [pltpu.VMEM((NB, 5 * NB), F32)],
+        "fold_products",
+    )
     others = [jnp.where(second, far, own_prior) for second in seconds]
-
-    shares = [
-        lax.dynamic_slice_in_dim(partial, (panel_pos ^ m) * per_device, per_device, 0)
-        for m in range(4)
-    ]
 
     def reduce_and_swap(operands):
         shares, others = operands
         sums = [swap(share, "panel", m) for m, share in zip((1, 2, 3), shares[1:])]
         return sums, [swap(block, "row", m) for m, block in zip((1, 2, 3), others)]
 
-    sums, rest = beside((shares, others), reduce_and_swap, 1)
+    sums, rest = beside((shares, others), reduce_and_swap, 2)
     covers[0] = covers[0] + unit
     places = [fold_block(row_pos, k) for k in range(5)]
     lead_cover = jnp.concatenate(
@@ -424,23 +483,27 @@
         corner = [(i, i ^ 6) for i in range(32)]
         return swap(x, "row", 1), swap(x, "panel", 2), lax.ppermute(x, ("row", "panel"), corner)
 
-    here = [held, *beside(held, across, 3)]
-
-    panel_prior = jnp.zeros((8, NB, own_prior.shape[1]), F32)
-    for k, block in enumerate([own_prior, far] + firsts):
-        panel_prior = lax.dynamic_update_slice(panel_prior, block[None], (places[k], 0, 0))
-    for m, block in zip((1, 2, 3), rest):
-        panel_prior = lax.dynamic_update_slice(panel_prior, block[None], (places[m + 1] ^ 4, 0, 0))
+    here = [held, *beside(held, across, 2)]
+
+    panel_prior = vmem_call(
+        gather_split_kernel,
+        [jax.ShapeDtypeStruct((B, own_prior.shape[1]), BF)] * 2,
+        place,
+        [own_prior, far, *firsts, *rest],
+        name="gather_split",
+    )
     here, panel_prior = lax.optimization_barrier((here, panel_prior))
     there = [swap(x, "panel", 1) for x in here]
     parts = []
     for m in (3, 2, 1, 0):
-        rows = lax.dynamic_slice_in_dim(
-            prior_factor, (panel_pos ^ m) * quarter_rows, quarter_rows, 0
+        part = vmem_call(
+            functools.partial(rest_products_kernel, m=m),
+            jax.ShapeDtypeStruct((quarter_rows, B), F32),
+            place,
+            [prior_factor, *panel_prior],
+            name="rest_products",
         )
-        part = dot_rows(rows, panel_prior.reshape(B, -1))
         parts.append(swap(part, "panel", m) if m else part)
-    place = jnp.stack([row_pos, panel_pos]).astype(jnp.int32)
     factors = factor(unfold_kernel, (place, *here, *there), B)
     return solve(covers, parts, factors)
 

time: 185 us -> 149 us (0.81)
  Pallas kernels: 111 us -> 84.4 us
  waiting for transfers between devices: 11 us -> 30.1 us
  local copies, waits for them, and re-layouts: 16.1 us -> 1.87 us
  matrix products: 11.3 us -> 0 us
    pallas_call x1, Pallas kernels: 52 us -> 32.2 us  [factor(): pl.pallas_call(kernel, out_shape=[jax.ShapeDtypeStruct((n, n), BF)] * 2 +...]
    ppermute x26, waiting for transfers between devices: 11 us -> 30 us  [swap(): lax.ppermute(block, axis, [(i, i ^ bit) for i in range(lax.axis_size(axis...]
    pallas_call x8, Pallas kernels: 53.3 us -> 37.7 us  [cover_rows(): pl.pallas_call(cover_kernel, grid=(1,), out_shape=jax.ShapeDtypeStruct((b...]
    dot_general x5 -> x0, matrix products: 11.3 us -> none  [dot_rows(): lax.dot_general(left, right, NT, precision=lax.Precision.HIGH, preferred_...]
    dynamic_update_slice x8 -> x0, local copies, waits for them, and re-layouts: 9.58 us -> none  [the longest x5 7.4 us: local(): lax.dynamic_update_slice(panel_prior, block[None], (places[k], 0, 0))]
    pallas_call x0 -> x6, Pallas kernels: none -> 8.36 us  [vmem_call(): pl.pallas_call(kernel, out_shape=out_shape, in_specs=[pl.BlockSpec(memory...]
    unnamed x17 -> x10, local copies, waits for them, and re-layouts: 2.08 us -> 0.06 us
  transfers between devices with their start and end apart: 27 -> 27, of which waited for: 4 -> 7; matrix products, arithmetic and copies ran while one was open for 13% -> 1% of each run, Pallas kernels for 58% -> 52%
where the time goes in v3:
time: 149 us
  Pallas kernels  84.4 us (57%)
  waiting for transfers between devices  30.1 us (20%)
  starting transfers between devices  29.4 us (20%)
  other arithmetic  2.78 us (2%)
  local copies, waits for them, and re-layouts  1.87 us (1%)
    pallas_call x8, Pallas kernels, cover_rows(): pl.pallas_call(cover_kernel, grid=(1,), out_shape=jax.ShapeDtypeStruct((b...  37.7 us
    pallas_call x1, Pallas kernels, factor(): pl.pallas_call(kernel, out_shape=[jax.ShapeDtypeStruct((n, n), BF)] * 2 +...  32.2 us
    ppermute x26, waiting for transfers between devices, swap(): lax.ppermute(block, axis, [(i, i ^ bit) for i in range(lax.axis_size(axis...  30 us
    ppermute x26, starting transfers between devices, swap(): lax.ppermute(block, axis, [(i, i ^ bit) for i in range(lax.axis_size(axis...  27.9 us
    pallas_call x6, Pallas kernels, vmem_call(): pl.pallas_call(kernel, out_shape=out_shape, in_specs=[pl.BlockSpec(memory...  8.36 us
    pallas_call x1, Pallas kernels, solve(): pl.pallas_call(functools.partial(solve_kernel, covers=len(covers)), out_s...  5.39 us
  transfers between devices with their start and end apart: 27, of which 7 were waited for; matrix products, arithmetic and copies ran while one was open for 1% of the time, Pallas kernels for 52%

profile of v3, /device:TPU:0, one launch (start us, length us, event | category | flops | bytes accessed | tf_op | source)
XLA Modules:
  0.0 148.9 jit_solution(8402775239178040450)
XLA Ops:
  1.8 3.1 %collective-permute-start = (f32[1,32,128]{2,1,0:T(8,128)S(1)}, f32[1,32,128]{2,1,0:T(8,128)S(1)}, u32[]{:S(2)}, u32[]{:S(2)}) collective-permute-start(f32[1,32,128]{2,1,0:T(8,128)S(1)} %reshape.69), channel_id=1, source_target_pairs={{0,8},{4,12},{8,0},{12,4},{16,24},{20,28},{24,16},{28,20},{1,9},{5... | collective-permute-start | bytes 49160 | tf_op jit(solution)/shard_map/ppermute | solution.py:378
  4.9 2.6 %collective-permute-start.1 = (f32[1,32,128]{2,1,0:T(8,128)S(1)}, f32[1,32,128]{2,1,0:T(8,128)S(1)}, u32[]{:S(2)}, u32[]{:S(2)}) collective-permute-start(f32[1,32,128]{2,1,0:T(8,128)S(1)} %reshape.69), channel_id=1, source_target_pairs={{0,16},{4,20},{8,24},{12,28},{16,0},{20,4},{24,8},{28,12},{1,17},{... | collective-permute-start | bytes 49160 | tf_op jit(solution)/shard_map/ppermute | solution.py:378
  8.4 2.0 %collective-permute-start.4 = (f32[128,512]{1,0:T(8,128)S(1)}, f32[128,512]{1,0:T(8,128)S(1)}, u32[]{:S(2)}, u32[]{:S(2)}) collective-permute-start(f32[128,512]{1,0:T(8,128)S(1)} %bitcast.14), channel_id=1, source_target_pairs={{0,16},{4,20},{8,24},{12,28},{16,0},{20,4},{24,8},{28,12},{1,17},{... | collective-permute-start | bytes 786440 | tf_op jit(solution)/shard_map/ppermute | solution.py:378
  10.5 2.7 %collective-permute-done.2 = f32[1,32,128]{2,1,0:T(8,128)S(1)} collective-permute-done((f32[1,32,128]{2,1,0:T(8,128)S(1)}, f32[1,32,128]{2,1,0:T(8,128)S(1)}, u32[]{:S(2)}, u32[]{:S(2)}) %collective-permute-start.2) | collective-permute-done | bytes 16416 | tf_op jit(solution)/shard_map/ppermute | solution.py:378
  13.2 1.5 %collective-permute-start.3 = (f32[4,32,128]{2,1,0:T(8,128)S(1)}, f32[4,32,128]{2,1,0:T(8,128)S(1)}, u32[]{:S(2)}, u32[]{:S(2)}) collective-permute-start(f32[4,32,128]{2,1,0:T(8,128)S(1)} %pad_maximum_fusion.2), channel_id=1, source_target_pairs={{0,4},{4,0},{8,12},{12,8},{16,20},{20,16},{24,28},{28,24},{1,5},{5... | collective-permute-start | bytes 196616 | tf_op jit(solution)/shard_map/ppermute | solution.py:378
  14.7 2.8 %collective-permute-done.3 = f32[4,32,128]{2,1,0:T(8,128)S(1)} collective-permute-done((f32[4,32,128]{2,1,0:T(8,128)S(1)}, f32[4,32,128]{2,1,0:T(8,128)S(1)}, u32[]{:S(2)}, u32[]{:S(2)}) %collective-permute-start.3) | collective-permute-done | bytes 65568 | tf_op jit(solution)/shard_map/ppermute | solution.py:378
  19.0 3.8 %collective-permute-done.4.refs_1_ = f32[128,512]{1,0:T(8,128)S(1)} collective-permute-done((f32[128,512]{1,0:T(8,128)S(1)}, f32[128,512]{1,0:T(8,128)S(1)}, u32[]{:S(2)}, u32[]{:S(2)}) %collective-permute-start.4) | collective-permute-done | bytes 262176 | tf_op jit(solution)/shard_map/ppermute | solution.py:378
  23.6 1.5 %collective-permute-start.5 = (f32[128,512]{1,0:T(8,128)}, f32[128,512]{1,0:T(8,128)S(1)}, u32[]{:S(2)}, u32[]{:S(2)}) collective-permute-start(f32[128,512]{1,0:T(8,128)} %get-tuple-element.66), channel_id=1, source_target_pairs={{0,4},{4,0},{8,12},{12,8},{16,20},{20,16},{24,28},{28,24},{1,5},{5... | collective-permute-start | bytes 786440 | tf_op jit(solution)/shard_map/ppermute | solution.py:378
  25.1 2.0 %collective-permute-start.7 = (f32[128,512]{1,0:T(8,128)}, f32[128,512]{1,0:T(8,128)S(1)}, u32[]{:S(2)}, u32[]{:S(2)}) collective-permute-start(f32[128,512]{1,0:T(8,128)} %get-tuple-element.68), channel_id=1, source_target_pairs={{0,12},{4,8},{8,4},{12,0},{16,28},{20,24},{24,20},{28,16},{1,13},{... | collective-permute-start | bytes 786440 | tf_op jit(solution)/shard_map/ppermute | solution.py:378
  27.2 4.7 %cover.9.refs_1_ = f32[32,1024]{1,0:T(8,128)S(1)} custom-call(bf16[16,256,16]{2,1,0:T(8,128)(2,1)S(1)} %get-tuple-element.100.f_ref, bf16[16,16,1024]{2,1,0:T(8,128)(2,1)S(1)} %get-tuple-element.70.g_ref), custom_call_target="tpu_custom_call" | custom-call | flops 100000000 | bytes 262144 | tf_op jit(solution)/shard_map/cover/pallas_call | solution.py:100
  31.9 4.7 %cover.8 = f32[32,1024]{1,0:T(8,128)S(1)} custom-call(bf16[16,256,16]{2,1,0:T(8,128)(2,1)S(1)} %get-tuple-element.100.f_ref, bf16[16,16,1024]{2,1,0:T(8,128)(2,1)S(1)} %get-tuple-element.70.g_ref), custom_call_target="tpu_custom_call" | custom-call | flops 100000000 | bytes 262144 | tf_op jit(solution)/shard_map/cover/pallas_call | solution.py:100
  39.2 1.6 %collective-permute-start.11 = (f32[128,512]{1,0:T(8,128)S(1)}, f32[128,512]{1,0:T(8,128)S(1)}, u32[]{:S(2)}, u32[]{:S(2)}) collective-permute-start(f32[128,512]{1,0:T(8,128)S(1)} %get-tuple-element.83), channel_id=1, source_target_pairs={{0,4},{4,0},{8,12},{12,8},{16,20},{20,16},{24,28},{28,24},{1,5},{5... | collective-permute-start | bytes 786440 | tf_op jit(solution)/shard_map/ppermute | solution.py:378
  41.2 1.6 %collective-permute-start.13 = (f32[128,512]{1,0:T(8,128)S(1)}, f32[128,512]{1,0:T(8,128)S(1)}, u32[]{:S(2)}, u32[]{:S(2)}) collective-permute-start(f32[128,512]{1,0:T(8,128)S(1)} %get-tuple-element.85), channel_id=1, source_target_pairs={{0,12},{4,8},{8,4},{12,0},{16,28},{20,24},{24,20},{28,16},{1,13},{... | collective-permute-start | bytes 786440 | tf_op jit(solution)/shard_map/ppermute | solution.py:378
  42.7 1.6 %collective-permute-start.8 = (f32[32,640]{1,0:T(8,128)S(1)}, f32[32,640]{1,0:T(8,128)S(1)}, u32[]{:S(2)}, u32[]{:S(2)}) collective-permute-start(f32[32,640]{1,0:T(8,128)S(1)} %get-tuple-element.80), channel_id=1, source_target_pairs={{0,1},{1,0},{2,3},{3,2},{4,5},{5,4},{6,7},{7,6},{8,9},{9,8},{10,11... | collective-permute-start | bytes 245768 | tf_op jit(solution)/shard_map/ppermute | solution.py:378
  44.5 4.7 %cover.11.refs_3_ = f32[32,1024]{1,0:T(8,128)S(1)} custom-call(bf16[16,256,16]{2,1,0:T(8,128)(2,1)S(1)} %get-tuple-element.100.f_ref, bf16[16,16,1024]{2,1,0:T(8,128)(2,1)S(1)} %get-tuple-element.70.g_ref), custom_call_target="tpu_custom_call" | custom-call | flops 100000000 | bytes 262144 | tf_op jit(solution)/shard_map/cover/pallas_call | solution.py:100
  49.2 4.7 %cover.10.refs_2_ = f32[32,1024]{1,0:T(8,128)S(1)} custom-call(bf16[16,256,16]{2,1,0:T(8,128)(2,1)S(1)} %get-tuple-element.100.f_ref, bf16[16,16,1024]{2,1,0:T(8,128)(2,1)S(1)} %get-tuple-element.70.g_ref), custom_call_target="tpu_custom_call" | custom-call | flops 100000000 | bytes 262144 | tf_op jit(solution)/shard_map/cover/pallas_call | solution.py:100
  54.5 3.9 %collective-permute-done.9 = f32[32,640]{1,0:T(8,128)S(1)} collective-permute-done((f32[32,640]{1,0:T(8,128)S(1)}, f32[32,640]{1,0:T(8,128)S(1)}, u32[]{:S(2)}, u32[]{:S(2)}) %collective-permute-start.9) | collective-permute-done | bytes 81952 | tf_op jit(solution)/shard_map/ppermute | solution.py:378
  59.0 3.4 %collective-permute-start.15 = (f32[1,32,640]{2,1,0:T(8,128)S(1)}, f32[1,32,640]{2,1,0:T(8,128)S(1)}, u32[]{:S(2)}, u32[]{:S(2)}) collective-permute-start(f32[1,32,640]{2,1,0:T(8,128)S(1)} %subtract_bitcast_fusion), channel_id=1, source_target_pairs={{0,16},{4,20},{8,24},{12,28},{16,0},{20,4},{24,8},{28,12},{1,17},{... | collective-permute-start | bytes 245768 | tf_op jit(solution)/shard_map/ppermute | solution.py:378
  62.9 4.8 %cover.13.refs_5_ = f32[32,1024]{1,0:T(8,128)S(1)} custom-call(bf16[16,256,16]{2,1,0:T(8,128)(2,1)S(1)} %get-tuple-element.100.f_ref, bf16[16,16,1024]{2,1,0:T(8,128)(2,1)S(1)} %get-tuple-element.70.g_ref), custom_call_target="tpu_custom_call" | custom-call | flops 100000000 | bytes 262144 | tf_op jit(solution)/shard_map/cover/pallas_call | solution.py:100
  67.8 4.7 %cover.12.refs_4_ = f32[32,1024]{1,0:T(8,128)S(1)} custom-call(bf16[16,256,16]{2,1,0:T(8,128)(2,1)S(1)} %get-tuple-element.100.f_ref, bf16[16,16,1024]{2,1,0:T(8,128)(2,1)S(1)} %get-tuple-element.70.g_ref), custom_call_target="tpu_custom_call" | custom-call | flops 100000000 | bytes 262144 | tf_op jit(solution)/shard_map/cover/pallas_call | solution.py:100
  72.5 1.6 %collective-permute-start.17 = (f32[4,32,640]{2,1,0:T(8,128)S(1)}, f32[4,32,640]{2,1,0:T(8,128)S(1)}, u32[]{:S(2)}, u32[]{:S(2)}) collective-permute-start(f32[4,32,640]{2,1,0:T(8,128)S(1)} %pad_maximum_fusion.refs_0_), channel_id=1, source_target_pairs={{0,4},{4,0},{8,12},{12,8},{16,20},{20,16},{24,28},{28,24},{1,5},{5... | collective-permute-start | bytes 983048 | tf_op jit(solution)/shard_map/ppermute | solution.py:378
  74.5 1.5 %collective-permute-start.19 = (f32[4,32,640]{2,1,0:T(8,128)S(1)}, f32[4,32,640]{2,1,0:T(8,128)S(1)}, u32[]{:S(2)}, u32[]{:S(2)}) collective-permute-start(f32[4,32,640]{2,1,0:T(8,128)S(1)} %pad_maximum_fusion.refs_0_), channel_id=1, source_target_pairs={{0,6},{1,7},{2,4},{3,5},{4,2},{5,3},{6,0},{7,1},{8,14},{9,15},{10,... | collective-permute-start | bytes 983048 | tf_op jit(solution)/shard_map/ppermute | solution.py:484
  76.9 4.7 %cover.15.refs_7_ = f32[32,1024]{1,0:T(8,128)S(1)} custom-call(bf16[16,256,16]{2,1,0:T(8,128)(2,1)S(1)} %get-tuple-element.100.f_ref, bf16[16,16,1024]{2,1,0:T(8,128)(2,1)S(1)} %get-tuple-element.70.g_ref), custom_call_target="tpu_custom_call" | custom-call | flops 100000000 | bytes 262144 | tf_op jit(solution)/shard_map/cover/pallas_call | solution.py:100
  81.6 4.9 %cover.14.refs_6_ = f32[32,1024]{1,0:T(8,128)S(1)} custom-call(bf16[16,256,16]{2,1,0:T(8,128)(2,1)S(1)} %get-tuple-element.100.f_ref, bf16[16,16,1024]{2,1,0:T(8,128)(2,1)S(1)} %get-tuple-element.70.g_ref), custom_call_target="tpu_custom_call" | custom-call | flops 100000000 | bytes 262144 | tf_op jit(solution)/shard_map/cover/pallas_call | solution.py:100
  86.5 1.9 %collective-permute-done.18.refs_2_ = f32[4,32,640]{2,1,0:T(8,128)S(1)} collective-permute-done((f32[4,32,640]{2,1,0:T(8,128)S(1)}, f32[4,32,640]{2,1,0:T(8,128)S(1)}, u32[]{:S(2)}, u32[]{:S(2)}) %collective-permute-start.18) | collective-permute-done | bytes 327712 | tf_op jit(solution)/shard_map/ppermute | solution.py:378
  89.4 1.6 %rest_products.6 = f32[256,1024]{1,0:T(8,128)S(1)} custom-call(s32[2]{0:T(128)S(1)} %pad_add_fusion.place_ref, f32[1024,512]{1,0:T(8,128)S(1)} %copy-done, bf16[1024,512]{1,0:T(8,128)(2,1)S(1)} %get-tuple-element.111.high_ref, bf16[1024,512]{1,0:T(8,128)(2,1)S(1)} %get-tuple-element.112.low_ref), custom_call_target="tpu_custom_call" | custom-call | flops 100000000 | bytes 262144 | tf_op jit(solution)/shard_map/rest_products/pallas_call | solution.py:330
  91.1 1.6 %rest_products.7.refs_11_ = f32[256,1024]{1,0:T(8,128)S(1)} custom-call(s32[2]{0:T(128)S(1)} %pad_add_fusion.place_ref, f32[1024,512]{1,0:T(8,128)S(1)} %copy-done, bf16[1024,512]{1,0:T(8,128)(2,1)S(1)} %get-tuple-element.111.high_ref, bf16[1024,512]{1,0:T(8,128)(2,1)S(1)} %get-tuple-element.112.low_ref), custom_call_target="tpu_custom_call" | custom-call | flops 100000000 | bytes 262144 | tf_op jit(solution)/shard_map/rest_products/pallas_call | solution.py:330
  92.7 1.6 %rest_products.5 = f32[256,1024]{1,0:T(8,128)S(1)} custom-call(s32[2]{0:T(128)S(1)} %pad_add_fusion.place_ref, f32[1024,512]{1,0:T(8,128)S(1)} %copy-done, bf16[1024,512]{1,0:T(8,128)(2,1)S(1)} %get-tuple-element.111.high_ref, bf16[1024,512]{1,0:T(8,128)(2,1)S(1)} %get-tuple-element.112.low_ref), custom_call_target="tpu_custom_call" | custom-call | flops 100000000 | bytes 262144 | tf_op jit(solution)/shard_map/rest_products/pallas_call | solution.py:330
  94.2 1.6 %rest_products.4 = f32[256,1024]{1,0:T(8,128)S(1)} custom-call(s32[2]{0:T(128)S(1)} %pad_add_fusion.place_ref, f32[1024,512]{1,0:T(8,128)S(1)} %copy-done, bf16[1024,512]{1,0:T(8,128)(2,1)S(1)} %get-tuple-element.111.high_ref, bf16[1024,512]{1,0:T(8,128)(2,1)S(1)} %get-tuple-element.112.low_ref), custom_call_target="tpu_custom_call" | custom-call | flops 100000000 | bytes 262144 | tf_op jit(solution)/shard_map/rest_products/pallas_call | solution.py:330
  97.7 32.2 %factor.1 = (bf16[1024,1024]{1,0:T(8,128)(2,1)S(1)}, bf16[1024,1024]{1,0:T(8,128)(2,1)S(1)}, bf16[1024,128]{1,0:T(8,128)(2,1)S(1)}, bf16[1024,128]{1,0:T(8,128)(2,1)S(1)}) custom-call(s32[2]{0:T(128)S(1)} %pad_add_fusion.place_ref, f32[4,32,640]{2,1,0:T(8,128)S(1)} %pad_maximum_fusion.refs_0_, f32[4,32,640]{2,1,0:T(8,128)S(1)} %collective-permute-done.17.refs_1_, ...), custom_call_target="tpu_custom_call" | custom-call | flops 49999998976 | bytes 8388608 | tf_op jit(solution)/shard_map/factor/pallas_call | solution.py:276
  129.9 13.5 %collective-permute-done.20.refs_8_ = f32[256,1024]{1,0:T(8,128)S(1)} collective-permute-done((f32[256,1024]{1,0:T(8,128)S(1)}, f32[256,1024]{1,0:T(8,128)S(1)}, u32[]{:S(2)}, u32[]{:S(2)}) %collective-permute-start.20) | collective-permute-done | bytes 1048608 | tf_op jit(solution)/shard_map/ppermute | solution.py:378
  143.5 5.4 %solve.1 = f32[256,1024]{1,0:T(8,128)} custom-call(f32[32,1024]{1,0:T(8,128)S(1)} %select_add_fusion.refs_0_, f32[32,1024]{1,0:T(8,128)S(1)} %cover.9.refs_1_, f32[32,1024]{1,0:T(8,128)S(1)} %cover.10.refs_2_, f32[32,1024]{1,0:T(8,128)S(1)} %cover.11.refs_3_, f32[32,1024]{1,0:T(8,128)S(1)} %cover.12.refs_4_, f32[32,1024]{1,0:T(8,128)S(1)} %cover.13.refs_5_, ...), custom_call_target="tpu_custom_call" | custom-call | tf_op jit(solution)/shard_map/solve/pallas_call | solution.py:318
  (72 shorter events, 14.5 us)
Async XLA Ops:
  1.8 8.7 %collective-permute-start = (f32[1,32,128]{2,1,0:T(8,128)S(1)}, f32[1,32,128]{2,1,0:T(8,128)S(1)}, u32[]{:S(2)}, u32[]{:S(2)}) collective-permute-start(f32[1,32,128]{2,1,0:T(8,128)S(1)} %reshape.69), channel_id=1, source_target_pairs={{0,8},{4,12},{8,0},{12,4},{16,24},{20,28},{24,16},{28,20},{1,9},{5... | collective-permute-start | bytes 49160 | tf_op jit(solution)/shard_map/ppermute | solution.py:378
  4.9 5.6 %collective-permute-start.1 = (f32[1,32,128]{2,1,0:T(8,128)S(1)}, f32[1,32,128]{2,1,0:T(8,128)S(1)}, u32[]{:S(2)}, u32[]{:S(2)}) collective-permute-start(f32[1,32,128]{2,1,0:T(8,128)S(1)} %reshape.69), channel_id=1, source_target_pairs={{0,16},{4,20},{8,24},{12,28},{16,0},{20,4},{24,8},{28,12},{1,17},{... | collective-permute-start | bytes 49160 | tf_op jit(solution)/shard_map/ppermute | solution.py:378
  7.5 5.8 %collective-permute-start.2 = (f32[1,32,128]{2,1,0:T(8,128)S(1)}, f32[1,32,128]{2,1,0:T(8,128)S(1)}, u32[]{:S(2)}, u32[]{:S(2)}) collective-permute-start(f32[1,32,128]{2,1,0:T(8,128)S(1)} %reshape.69), channel_id=1, source_target_pairs={{0,24},{4,28},{8,16},{12,20},{16,8},{20,12},{24,0},{28,4},{1,25},{... | collective-permute-start | bytes 49160 | tf_op jit(solution)/shard_map/ppermute | solution.py:378
  8.4 14.3 %collective-permute-start.4 = (f32[128,512]{1,0:T(8,128)S(1)}, f32[128,512]{1,0:T(8,128)S(1)}, u32[]{:S(2)}, u32[]{:S(2)}) collective-permute-start(f32[128,512]{1,0:T(8,128)S(1)} %bitcast.14), channel_id=1, source_target_pairs={{0,16},{4,20},{8,24},{12,28},{16,0},{20,4},{24,8},{28,12},{1,17},{... | collective-permute-start | bytes 786440 | tf_op jit(solution)/shard_map/ppermute | solution.py:378
  13.2 4.3 %collective-permute-start.3 = (f32[4,32,128]{2,1,0:T(8,128)S(1)}, f32[4,32,128]{2,1,0:T(8,128)S(1)}, u32[]{:S(2)}, u32[]{:S(2)}) collective-permute-start(f32[4,32,128]{2,1,0:T(8,128)S(1)} %pad_maximum_fusion.2), channel_id=1, source_target_pairs={{0,4},{4,0},{8,12},{12,8},{16,20},{20,16},{24,28},{28,24},{1,5},{5... | collective-permute-start | bytes 196616 | tf_op jit(solution)/shard_map/ppermute | solution.py:378
  23.6 12.9 %collective-permute-start.5 = (f32[128,512]{1,0:T(8,128)}, f32[128,512]{1,0:T(8,128)S(1)}, u32[]{:S(2)}, u32[]{:S(2)}) collective-permute-start(f32[128,512]{1,0:T(8,128)} %get-tuple-element.66), channel_id=1, source_target_pairs={{0,4},{4,0},{8,12},{12,8},{16,20},{20,16},{24,28},{28,24},{1,5},{5... | collective-permute-start | bytes 786440 | tf_op jit(solution)/shard_map/ppermute | solution.py:378
  25.1 11.4 %collective-permute-start.6 = (f32[128,512]{1,0:T(8,128)}, f32[128,512]{1,0:T(8,128)S(1)}, u32[]{:S(2)}, u32[]{:S(2)}) collective-permute-start(f32[128,512]{1,0:T(8,128)} %get-tuple-element.68), channel_id=1, source_target_pairs={{0,8},{4,12},{8,0},{12,4},{16,24},{20,28},{24,16},{28,20},{1,9},{5... | collective-permute-start | bytes 786440 | tf_op jit(solution)/shard_map/ppermute | solution.py:378
  25.1 12.8 %collective-permute-start.7 = (f32[128,512]{1,0:T(8,128)}, f32[128,512]{1,0:T(8,128)S(1)}, u32[]{:S(2)}, u32[]{:S(2)}) collective-permute-start(f32[128,512]{1,0:T(8,128)} %get-tuple-element.68), channel_id=1, source_target_pairs={{0,12},{4,8},{8,4},{12,0},{16,28},{20,24},{24,20},{28,16},{1,13},{... | collective-permute-start | bytes 786440 | tf_op jit(solution)/shard_map/ppermute | solution.py:378
  39.2 19.2 %collective-permute-start.11 = (f32[128,512]{1,0:T(8,128)S(1)}, f32[128,512]{1,0:T(8,128)S(1)}, u32[]{:S(2)}, u32[]{:S(2)}) collective-permute-start(f32[128,512]{1,0:T(8,128)S(1)} %get-tuple-element.83), channel_id=1, source_target_pairs={{0,4},{4,0},{8,12},{12,8},{16,20},{20,16},{24,28},{28,24},{1,5},{5... | collective-permute-start | bytes 786440 | tf_op jit(solution)/shard_map/ppermute | solution.py:378
  40.7 17.7 %collective-permute-start.12 = (f32[128,512]{1,0:T(8,128)S(1)}, f32[128,512]{1,0:T(8,128)S(1)}, u32[]{:S(2)}, u32[]{:S(2)}) collective-permute-start(f32[128,512]{1,0:T(8,128)S(1)} %get-tuple-element.85), channel_id=1, source_target_pairs={{0,8},{4,12},{8,0},{12,4},{16,24},{20,28},{24,16},{28,20},{1,9},{5... | collective-permute-start | bytes 786440 | tf_op jit(solution)/shard_map/ppermute | solution.py:378
  41.2 17.2 %collective-permute-start.13 = (f32[128,512]{1,0:T(8,128)S(1)}, f32[128,512]{1,0:T(8,128)S(1)}, u32[]{:S(2)}, u32[]{:S(2)}) collective-permute-start(f32[128,512]{1,0:T(8,128)S(1)} %get-tuple-element.85), channel_id=1, source_target_pairs={{0,12},{4,8},{8,4},{12,0},{16,28},{20,24},{24,20},{28,16},{1,13},{... | collective-permute-start | bytes 786440 | tf_op jit(solution)/shard_map/ppermute | solution.py:378
  42.7 11.2 %collective-permute-start.10 = (f32[32,640]{1,0:T(8,128)S(1)}, f32[32,640]{1,0:T(8,128)S(1)}, u32[]{:S(2)}, u32[]{:S(2)}) collective-permute-start(f32[32,640]{1,0:T(8,128)S(1)} %get-tuple-element.82), channel_id=1, source_target_pairs={{0,3},{1,2},{2,1},{3,0},{4,7},{5,6},{6,5},{7,4},{8,11},{9,10},{10,... | collective-permute-start | bytes 245768 | tf_op jit(solution)/shard_map/ppermute | solution.py:378
  42.7 11.7 %collective-permute-start.8 = (f32[32,640]{1,0:T(8,128)S(1)}, f32[32,640]{1,0:T(8,128)S(1)}, u32[]{:S(2)}, u32[]{:S(2)}) collective-permute-start(f32[32,640]{1,0:T(8,128)S(1)} %get-tuple-element.80), channel_id=1, source_target_pairs={{0,1},{1,0},{2,3},{3,2},{4,5},{5,4},{6,7},{7,6},{8,9},{9,8},{10,11... | collective-permute-start | bytes 245768 | tf_op jit(solution)/shard_map/ppermute | solution.py:378
  53.9 4.5 %collective-permute-start.9 = (f32[32,640]{1,0:T(8,128)S(1)}, f32[32,640]{1,0:T(8,128)S(1)}, u32[]{:S(2)}, u32[]{:S(2)}) collective-permute-start(f32[32,640]{1,0:T(8,128)S(1)} %get-tuple-element.81), channel_id=1, source_target_pairs={{0,2},{1,3},{2,0},{3,1},{4,6},{5,7},{6,4},{7,5},{8,10},{9,11},{10,... | collective-permute-start | bytes 245768 | tf_op jit(solution)/shard_map/ppermute | solution.py:378
  58.5 14.0 %collective-permute-start.14 = (f32[1,32,640]{2,1,0:T(8,128)S(1)}, f32[1,32,640]{2,1,0:T(8,128)S(1)}, u32[]{:S(2)}, u32[]{:S(2)}) collective-permute-start(f32[1,32,640]{2,1,0:T(8,128)S(1)} %subtract_bitcast_fusion), channel_id=1, source_target_pairs={{0,8},{4,12},{8,0},{12,4},{16,24},{20,28},{24,16},{28,20},{1,9},{5... | collective-permute-start | bytes 245768 | tf_op jit(solution)/shard_map/ppermute | solution.py:378
  59.0 13.5 %collective-permute-start.15 = (f32[1,32,640]{2,1,0:T(8,128)S(1)}, f32[1,32,640]{2,1,0:T(8,128)S(1)}, u32[]{:S(2)}, u32[]{:S(2)}) collective-permute-start(f32[1,32,640]{2,1,0:T(8,128)S(1)} %subtract_bitcast_fusion), channel_id=1, source_target_pairs={{0,16},{4,20},{8,24},{12,28},{16,0},{20,4},{24,8},{28,12},{1,17},{... | collective-permute-start | bytes 245768 | tf_op jit(solution)/shard_map/ppermute | solution.py:378
  62.3 10.1 %collective-permute-start.16 = (f32[1,32,640]{2,1,0:T(8,128)S(1)}, f32[1,32,640]{2,1,0:T(8,128)S(1)}, u32[]{:S(2)}, u32[]{:S(2)}) collective-permute-start(f32[1,32,640]{2,1,0:T(8,128)S(1)} %subtract_bitcast_fusion), channel_id=1, source_target_pairs={{0,24},{4,28},{8,16},{12,20},{16,8},{20,12},{24,0},{28,4},{1,25},{... | collective-permute-start | bytes 245768 | tf_op jit(solution)/shard_map/ppermute | solution.py:378
  72.5 14.0 %collective-permute-start.17 = (f32[4,32,640]{2,1,0:T(8,128)S(1)}, f32[4,32,640]{2,1,0:T(8,128)S(1)}, u32[]{:S(2)}, u32[]{:S(2)}) collective-permute-start(f32[4,32,640]{2,1,0:T(8,128)S(1)} %pad_maximum_fusion.refs_0_), channel_id=1, source_target_pairs={{0,4},{4,0},{8,12},{12,8},{16,20},{20,16},{24,28},{28,24},{1,5},{5... | collective-permute-start | bytes 983048 | tf_op jit(solution)/shard_map/ppermute | solution.py:378
  74.0 14.4 %collective-permute-start.18 = (f32[4,32,640]{2,1,0:T(8,128)S(1)}, f32[4,32,640]{2,1,0:T(8,128)S(1)}, u32[]{:S(2)}, u32[]{:S(2)}) collective-permute-start(f32[4,32,640]{2,1,0:T(8,128)S(1)} %pad_maximum_fusion.refs_0_), channel_id=1, source_target_pairs={{0,2},{1,3},{2,0},{3,1},{4,6},{5,7},{6,4},{7,5},{8,10},{9,11},{10,... | collective-permute-start | bytes 983048 | tf_op jit(solution)/shard_map/ppermute | solution.py:378
  74.5 13.9 %collective-permute-start.19 = (f32[4,32,640]{2,1,0:T(8,128)S(1)}, f32[4,32,640]{2,1,0:T(8,128)S(1)}, u32[]{:S(2)}, u32[]{:S(2)}) collective-permute-start(f32[4,32,640]{2,1,0:T(8,128)S(1)} %pad_maximum_fusion.refs_0_), channel_id=1, source_target_pairs={{0,6},{1,7},{2,4},{3,5},{4,2},{5,3},{6,0},{7,1},{8,14},{9,15},{10,... | collective-permute-start | bytes 983048 | tf_op jit(solution)/shard_map/ppermute | solution.py:484
  76.9 12.5 %copy-start = (f32[1024,512]{1,0:T(8,128)S(1)}, f32[1024,512]{1,0:T(8,128)}, u32[]{:S(2)}) copy-start(f32[1024,512]{1,0:T(8,128)} %prior_ref.7) | copy-start | bytes 6291460
  88.4 7.4 %collective-permute-start.23 = (f32[4,32,640]{2,1,0:T(8,128)S(1)}, f32[4,32,640]{2,1,0:T(8,128)S(1)}, u32[]{:S(2)}, u32[]{:S(2)}) collective-permute-start(f32[4,32,640]{2,1,0:T(8,128)S(1)} %pad_maximum_fusion.refs_0_), channel_id=1, source_target_pairs={{0,1},{1,0},{2,3},{3,2},{4,5},{5,4},{6,7},{7,6},{8,9},{9,8},{10,11... | collective-permute-start | bytes 983048 | tf_op jit(solution)/shard_map/ppermute | solution.py:378
  88.4 8.0 %collective-permute-start.24 = (f32[4,32,640]{2,1,0:T(8,128)S(1)}, f32[4,32,640]{2,1,0:T(8,128)S(1)}, u32[]{:S(2)}, u32[]{:S(2)}) collective-permute-start(f32[4,32,640]{2,1,0:T(8,128)S(1)} %collective-permute-done.17.refs_1_), channel_id=1, source_target_pairs={{0,1},{1,0},{2,3},{3,2},{4,5},{5,4},{6,7},{7,6},{8,9},{9,8},{10,11... | collective-permute-start | bytes 983048 | tf_op jit(solution)/shard_map/ppermute | solution.py:378
  88.9 8.8 %collective-permute-start.25 = (f32[4,32,640]{2,1,0:T(8,128)S(1)}, f32[4,32,640]{2,1,0:T(8,128)S(1)}, u32[]{:S(2)}, u32[]{:S(2)}) collective-permute-start(f32[4,32,640]{2,1,0:T(8,128)S(1)} %collective-permute-done.18.refs_2_), channel_id=1, source_target_pairs={{0,1},{1,0},{2,3},{3,2},{4,5},{5,4},{6,7},{7,6},{8,9},{9,8},{10,11... | collective-permute-start | bytes 983048 | tf_op jit(solution)/shard_map/ppermute | solution.py:378
  88.9 8.8 %collective-permute-start.26 = (f32[4,32,640]{2,1,0:T(8,128)S(1)}, f32[4,32,640]{2,1,0:T(8,128)S(1)}, u32[]{:S(2)}, u32[]{:S(2)}) collective-permute-start(f32[4,32,640]{2,1,0:T(8,128)S(1)} %collective-permute-done.19.refs_3_), channel_id=1, source_target_pairs={{0,1},{1,0},{2,3},{3,2},{4,5},{5,4},{6,7},{7,6},{8,9},{9,8},{10,11... | collective-permute-start | bytes 983048 | tf_op jit(solution)/shard_map/ppermute | solution.py:378
  91.0 38.9 %collective-permute-start.22 = (f32[256,1024]{1,0:T(8,128)S(1)}, f32[256,1024]{1,0:T(8,128)S(1)}, u32[]{:S(2)}, u32[]{:S(2)}) collective-permute-start(f32[256,1024]{1,0:T(8,128)S(1)} %rest_products.6), channel_id=1, source_target_pairs={{0,1},{1,0},{2,3},{3,2},{4,5},{5,4},{6,7},{7,6},{8,9},{9,8},{10,11... | collective-permute-start | bytes 3145736 | tf_op jit(solution)/shard_map/ppermute | solution.py:378
  95.8 34.1 %collective-permute-start.21 = (f32[256,1024]{1,0:T(8,128)S(1)}, f32[256,1024]{1,0:T(8,128)S(1)}, u32[]{:S(2)}, u32[]{:S(2)}) collective-permute-start(f32[256,1024]{1,0:T(8,128)S(1)} %rest_products.5), channel_id=1, source_target_pairs={{0,2},{1,3},{2,0},{3,1},{4,6},{5,7},{6,4},{7,5},{8,10},{9,11},{10,... | collective-permute-start | bytes 3145736 | tf_op jit(solution)/shard_map/ppermute | solution.py:378
  96.4 47.1 %collective-permute-start.20 = (f32[256,1024]{1,0:T(8,128)S(1)}, f32[256,1024]{1,0:T(8,128)S(1)}, u32[]{:S(2)}, u32[]{:S(2)}) collective-permute-start(f32[256,1024]{1,0:T(8,128)S(1)} %rest_products.4), channel_id=1, source_target_pairs={{0,3},{1,2},{2,1},{3,0},{4,7},{5,6},{6,5},{7,4},{8,11},{9,10},{10,... | collective-permute-start | bytes 3145736 | tf_op jit(solution)/shard_map/ppermute | solution.py:378

commit v4 on v3

--- a/solution.py
+++ b/solution.py
@@ -364,14 +364,17 @@
         low_ref[pl.ds(first, NB)] = low
 
 
-def rest_products_kernel(place_ref, prior_ref, high_ref, low_ref, o_ref, *, m):
+def rest_products_kernel(place_ref, prior_ref, high_ref, low_ref, *refs, m):
+    o_ref = refs[-1]
     rows = o_ref.shape[0]
     first = pl.multiple_of((place_ref[1] ^ m) * rows, rows)
     own_high, own_low = split(prior_ref[pl.ds(first, rows)])
     for c in range(0, o_ref.shape[1], 2 * NB):
-        o_ref[:, c : c + 2 * NB] = dot3(
-            own_high, own_low, high_ref[c : c + 2 * NB], low_ref[c : c + 2 * NB]
-        )
+        cols = slice(c, c + 2 * NB)
+        total = dot3(own_high, own_low, high_ref[cols], low_ref[cols])
+        for plus_ref in refs[:-1]:
+            total = total + plus_ref[:, cols]
+        o_ref[:, cols] = total
 
 
 def swap(block, axis, bit):
@@ -433,18 +436,18 @@
     order = (away >> 1) | ((away & 1) << 2)
     panel_points = held[order].transpose(1, 0, 2).reshape(2, count, B)
     row_part, col_part = features(own_points, panel_points)
-    row_part, far = lax.optimization_barrier((row_part, far))
-    covers = []
-
-    def beside(operands, transfer, calls):
+    covers = [cover_rows(row_part, col_part, 0, lead) + unit]
+    row_part, far, covers = lax.optimization_barrier((row_part, far, covers))
+
+    def beside(operands, transfer, calls, extra=lambda *_: ()):
         tied = lax.optimization_barrier((operands, row_part))
         received = transfer(tied[0])
         done = [
             cover_rows(tied[1], col_part, lead * (len(covers) + i), lead) for i in range(calls)
         ]
-        received, done = lax.optimization_barrier((received, done))
+        received, done, more = lax.optimization_barrier((received, done, extra(tied[0])))
         covers.extend(done)
-        return received
+        return (received, more) if more else received
 
     seconds = [((row_pos >> (m.bit_length() - 1)) & 1) == 1 for m in (1, 2, 3)]
     firsts = beside(
@@ -462,48 +465,62 @@
         "fold_products",
     )
     others = [jnp.where(second, far, own_prior) for second in seconds]
-
-    def reduce_and_swap(operands):
-        shares, others = operands
-        sums = [swap(share, "panel", m) for m, share in zip((1, 2, 3), shares[1:])]
-        return sums, [swap(block, "row", m) for m, block in zip((1, 2, 3), others)]
-
-    sums, rest = beside((shares, others), reduce_and_swap, 2)
-    covers[0] = covers[0] + unit
+    shares, others = lax.optimization_barrier((shares, others))
+    sums = beside(
+        shares,
+        lambda shares: [swap(share, "panel", m) for m, share in zip((1, 2, 3), shares[1:])],
+        1,
+    )
+    rest = [swap(block, "row", m) for m, block in zip((1, 2, 3), others)]
     places = [fold_block(row_pos, k) for k in range(5)]
     lead_cover = jnp.concatenate(
         [lax.dynamic_slice(covers[0], (jnp.int32(0), s * NB), (per_device, NB)) for s in places], 1
     )
     shard = lead_cover - (shares[0] + sums[0] + sums[1] + sums[2])
 
-    along = beside(shard[None], lambda x: [swap(x, "row", bit) for bit in (2, 4, 6)], 2)
-    held = jnp.concatenate([shard[None]] + along, 0)
-
-    def across(x):
-        corner = [(i, i ^ 6) for i in range(32)]
-        return swap(x, "row", 1), swap(x, "panel", 2), lax.ppermute(x, ("row", "panel"), corner)
-
-    here = [held, *beside(held, across, 2)]
-
-    panel_prior = vmem_call(
-        gather_split_kernel,
-        [jax.ShapeDtypeStruct((B, own_prior.shape[1]), BF)] * 2,
-        place,
-        [own_prior, far, *firsts, *rest],
-        name="gather_split",
-    )
-    here, panel_prior = lax.optimization_barrier((here, panel_prior))
-    there = [swap(x, "panel", 1) for x in here]
-    parts = []
-    for m in (3, 2, 1, 0):
-        part = vmem_call(
+    def rest_part(panel_prior, m, plus=()):
+        return vmem_call(
             functools.partial(rest_products_kernel, m=m),
             jax.ShapeDtypeStruct((quarter_rows, B), F32),
             place,
-            [prior_factor, *panel_prior],
+            [prior_factor, *panel_prior, *plus],
             name="rest_products",
         )
-        parts.append(swap(part, "panel", m) if m else part)
+
+    def for_other_core(_):
+        panel_prior = vmem_call(
+            gather_split_kernel,
+            [jax.ShapeDtypeStruct((B, own_prior.shape[1]), BF)] * 2,
+            place,
+            [own_prior, far, *firsts, *rest],
+            name="gather_split",
+        )
+        return panel_prior, rest_part(panel_prior, 3), rest_part(panel_prior, 1)
+
+    along, (panel_prior, part_3, part_1) = beside(
+        shard[None],
+        lambda x: [swap(x, "row", bit) for bit in (2, 4, 6)],
+        2,
+        for_other_core,
+    )
+    held = jnp.concatenate([shard[None]] + along, 0)
+
+    def across(operands):
+        x = operands[0]
+        corner = [(i, i ^ 6) for i in range(32)]
+        return swap(x, "row", 1), swap(x, "panel", 2), lax.ppermute(x, ("row", "panel"), corner)
+
+    def for_own_core(operands):
+        panel_prior, part_3, part_1 = operands[1]
+        from_3, from_1 = swap(part_3, "panel", 1), swap(part_1, "panel", 1)
+        return rest_part(panel_prior, 0), rest_part(panel_prior, 2, [from_3]), from_1
+
+    received, (part_0, part_2, from_1) = beside(
+        (held, (panel_prior, part_3, part_1)), across, 2, for_own_core
+    )
+    here = [held, *received]
+    there = [swap(x, "panel", 1) for x in here]
+    parts = [part_0, from_1, swap(part_2, "panel", 2)]
     factors = factor(unfold_kernel, (place, *here, *there), B)
     return solve(covers, parts, factors)
 

time: 149 us -> 125 us (0.84)
  waiting for transfers between devices: 30.1 us -> 7.34 us
    ppermute x26, waiting for transfers between devices: 30 us -> 7.34 us  [swap(): lax.ppermute(block, axis, [(i, i ^ bit) for i in range(lax.axis_size(axis...]
  transfers between devices with their start and end apart: 27 -> 27, of which waited for: 7 -> 8; matrix products, arithmetic and copies ran while one was open for 1% -> 2% of each run, Pallas kernels for 52% -> 62%
where the time goes in v4:
time: 125 us
  Pallas kernels  84.1 us (67%)
  starting transfers between devices  29.3 us (23%)
  waiting for transfers between devices  7.34 us (6%)
  other arithmetic  2 us (2%)
  local copies, waits for them, and re-layouts  1.85 us (1%)
    pallas_call x8, Pallas kernels, cover_rows(): pl.pallas_call(cover_kernel, grid=(1,), out_shape=jax.ShapeDtypeStruct((b...  37.7 us
    pallas_call x1, Pallas kernels, factor(): pl.pallas_call(kernel, out_shape=[jax.ShapeDtypeStruct((n, n), BF)] * 2 +...  31.9 us
    ppermute x26, starting transfers between devices, swap(): lax.ppermute(block, axis, [(i, i ^ bit) for i in range(lax.axis_size(axis...  26.8 us
    pallas_call x6, Pallas kernels, vmem_call(): pl.pallas_call(kernel, out_shape=out_shape, in_specs=[pl.BlockSpec(memory...  8.37 us
    ppermute x26, waiting for transfers between devices, swap(): lax.ppermute(block, axis, [(i, i ^ bit) for i in range(lax.axis_size(axis...  7.34 us
    pallas_call x1, Pallas kernels, solve(): pl.pallas_call(functools.partial(solve_kernel, covers=len(covers)), out_s...  5.33 us
  transfers between devices with their start and end apart: 27, of which 8 were waited for; matrix products, arithmetic and copies ran while one was open for 2% of the time, Pallas kernels for 62%

profile of v4, /device:TPU:0, one launch (start us, length us, event | category | flops | bytes accessed | tf_op | source)
XLA Modules:
  0.0 125.0 jit_solution(12377892536279617175)
XLA Ops:
  0.7 0.9 convert_add_fusion
  1.8 5.1 %collective-permute-start.2 = (f32[1,32,128]{2,1,0:T(8,128)S(1)}, f32[1,32,128]{2,1,0:T(8,128)S(1)}, u32[]{:S(2)}, u32[]{:S(2)}) collective-permute-start(f32[1,32,128]{2,1,0:T(8,128)S(1)} %reshape.67), channel_id=1, source_target_pairs={{0,24},{4,28},{8,16},{12,20},{16,8},{20,12},{24,0},{28,4},{1,25},{... | collective-permute-start | bytes 49160 | tf_op jit(solution)/shard_map/ppermute | solution.py:381
  7.5 1.0 slice.18
  8.5 2.4 %collective-permute-start.4 = (f32[128,512]{1,0:T(8,128)S(1)}, f32[128,512]{1,0:T(8,128)S(1)}, u32[]{:S(2)}, u32[]{:S(2)}) collective-permute-start(f32[128,512]{1,0:T(8,128)S(1)} %bitcast.14), channel_id=1, source_target_pairs={{0,16},{4,20},{8,24},{12,28},{16,0},{20,4},{24,8},{28,12},{1,17},{... | collective-permute-start | bytes 786440 | tf_op jit(solution)/shard_map/ppermute | solution.py:381
  11.7 1.6 %collective-permute-start.3 = (f32[4,32,128]{2,1,0:T(8,128)S(1)}, f32[4,32,128]{2,1,0:T(8,128)S(1)}, u32[]{:S(2)}, u32[]{:S(2)}) collective-permute-start(f32[4,32,128]{2,1,0:T(8,128)S(1)} %pad_maximum_fusion.2), channel_id=1, source_target_pairs={{0,4},{4,0},{8,12},{12,8},{16,20},{20,16},{24,28},{28,24},{1,5},{5... | collective-permute-start | bytes 196616 | tf_op jit(solution)/shard_map/ppermute | solution.py:381
  13.3 2.8 %collective-permute-done.3 = f32[4,32,128]{2,1,0:T(8,128)S(1)} collective-permute-done((f32[4,32,128]{2,1,0:T(8,128)S(1)}, f32[4,32,128]{2,1,0:T(8,128)S(1)}, u32[]{:S(2)}, u32[]{:S(2)}) %collective-permute-start.3) | collective-permute-done | bytes 65568 | tf_op jit(solution)/shard_map/ppermute | solution.py:381
  17.5 4.7 %cover.8 = f32[32,1024]{1,0:T(8,128)S(1)} custom-call(bf16[16,256,16]{2,1,0:T(8,128)(2,1)S(1)} %get-tuple-element.116.f_ref, bf16[16,16,1024]{2,1,0:T(8,128)(2,1)S(1)} %get-tuple-element.70.g_ref), custom_call_target="tpu_custom_call" | custom-call | flops 100000000 | bytes 262144 | tf_op jit(solution)/shard_map/cover/pallas_call | solution.py:100
  22.9 1.6 %collective-permute-start.5 = (f32[128,512]{1,0:T(8,128)S(1)}, f32[128,512]{1,0:T(8,128)S(1)}, u32[]{:S(2)}, u32[]{:S(2)}) collective-permute-start(f32[128,512]{1,0:T(8,128)S(1)} %get-tuple-element.74), channel_id=1, source_target_pairs={{0,4},{4,0},{8,12},{12,8},{16,20},{20,16},{24,28},{28,24},{1,5},{5... | collective-permute-start | bytes 786440 | tf_op jit(solution)/shard_map/ppermute | solution.py:381
  25.3 1.1 collective-permute-start.7
  26.5 4.7 %cover.10.refs_2_ = f32[32,1024]{1,0:T(8,128)S(1)} custom-call(bf16[16,256,16]{2,1,0:T(8,128)(2,1)S(1)} %get-tuple-element.116.f_ref, bf16[16,16,1024]{2,1,0:T(8,128)(2,1)S(1)} %get-tuple-element.70.g_ref), custom_call_target="tpu_custom_call" | custom-call | flops 100000000 | bytes 262144 | tf_op jit(solution)/shard_map/cover/pallas_call | solution.py:100
  31.1 4.7 %cover.9.refs_1_ = f32[32,1024]{1,0:T(8,128)S(1)} custom-call(bf16[16,256,16]{2,1,0:T(8,128)(2,1)S(1)} %get-tuple-element.116.f_ref, bf16[16,16,1024]{2,1,0:T(8,128)(2,1)S(1)} %get-tuple-element.70.g_ref), custom_call_target="tpu_custom_call" | custom-call | flops 100000000 | bytes 262144 | tf_op jit(solution)/shard_map/cover/pallas_call | solution.py:100
  35.9 1.4 %collective-permute-done.7.refs_4_ = f32[128,512]{1,0:T(8,128)S(1)} collective-permute-done((f32[128,512]{1,0:T(8,128)S(1)}, f32[128,512]{1,0:T(8,128)S(1)}, u32[]{:S(2)}, u32[]{:S(2)}) %collective-permute-start.7) | collective-permute-done | bytes 262176 | tf_op jit(solution)/shard_map/ppermute | solution.py:381
  37.2 1.2 fold_products.1
  38.6 1.6 %collective-permute-start.9 = (f32[32,640]{1,0:T(8,128)S(1)}, f32[32,640]{1,0:T(8,128)S(1)}, u32[]{:S(2)}, u32[]{:S(2)}) collective-permute-start(f32[32,640]{1,0:T(8,128)S(1)} %get-tuple-element.92), channel_id=1, source_target_pairs={{0,2},{1,3},{2,0},{3,1},{4,6},{5,7},{6,4},{7,5},{8,10},{9,11},{10,... | collective-permute-start | bytes 245768 | tf_op jit(solution)/shard_map/ppermute | solution.py:381
  40.4 1.5 %collective-permute-start.14 = (f32[128,512]{1,0:T(8,128)S(1)}, f32[128,512]{1,0:T(8,128)S(1)}, u32[]{:S(2)}, u32[]{:S(2)}) collective-permute-start(f32[128,512]{1,0:T(8,128)S(1)} %get-tuple-element.101), channel_id=1, source_target_pairs={{0,4},{4,0},{8,12},{12,8},{16,20},{20,16},{24,28},{28,24},{1,5},{5... | collective-permute-start | bytes 786440 | tf_op jit(solution)/shard_map/ppermute | solution.py:381
  41.9 1.0 collective-permute-start.15
  42.9 4.7 %cover.11.refs_3_ = f32[32,1024]{1,0:T(8,128)S(1)} custom-call(bf16[16,256,16]{2,1,0:T(8,128)(2,1)S(1)} %get-tuple-element.116.f_ref, bf16[16,16,1024]{2,1,0:T(8,128)(2,1)S(1)} %get-tuple-element.70.g_ref), custom_call_target="tpu_custom_call" | custom-call | flops 100000000 | bytes 262144 | tf_op jit(solution)/shard_map/cover/pallas_call | solution.py:100
  47.6 1.1 collective-permute-start.16
  48.7 3.8 %collective-permute-start.13 = (f32[1,32,640]{2,1,0:T(8,128)S(1)}, f32[1,32,640]{2,1,0:T(8,128)S(1)}, u32[]{:S(2)}, u32[]{:S(2)}) collective-permute-start(f32[1,32,640]{2,1,0:T(8,128)S(1)} %subtract_bitcast_fusion), channel_id=1, source_target_pairs={{0,24},{4,28},{8,16},{12,20},{16,8},{20,12},{24,0},{28,4},{1,25},{... | collective-permute-start | bytes 245768 | tf_op jit(solution)/shard_map/ppermute | solution.py:381
  53.2 4.8 %cover.13.refs_5_ = f32[32,1024]{1,0:T(8,128)S(1)} custom-call(bf16[16,256,16]{2,1,0:T(8,128)(2,1)S(1)} %get-tuple-element.116.f_ref, bf16[16,16,1024]{2,1,0:T(8,128)(2,1)S(1)} %get-tuple-element.70.g_ref), custom_call_target="tpu_custom_call" | custom-call | flops 100000000 | bytes 262144 | tf_op jit(solution)/shard_map/cover/pallas_call | solution.py:100
  58.0 4.7 %cover.12.refs_4_ = f32[32,1024]{1,0:T(8,128)S(1)} custom-call(bf16[16,256,16]{2,1,0:T(8,128)(2,1)S(1)} %get-tuple-element.116.f_ref, bf16[16,16,1024]{2,1,0:T(8,128)(2,1)S(1)} %get-tuple-element.70.g_ref), custom_call_target="tpu_custom_call" | custom-call | flops 100000000 | bytes 262144 | tf_op jit(solution)/shard_map/cover/pallas_call | solution.py:100
  63.6 1.6 %rest_products.5 = f32[256,1024]{1,0:T(8,128)S(1)} custom-call(s32[2]{0:T(128)S(1)} %pad_add_fusion.place_ref, f32[1024,512]{1,0:T(8,128)S(1)} %copy-done, bf16[1024,512]{1,0:T(8,128)(2,1)S(1)} %get-tuple-element.117.high_ref, bf16[1024,512]{1,0:T(8,128)(2,1)S(1)} %get-tuple-element.118.low_ref), custom_call_target="tpu_custom_call" | custom-call | flops 100000000 | bytes 262144 | tf_op jit(solution)/shard_map/rest_products/pallas_call | solution.py:330
  65.2 1.6 %rest_products.4 = f32[256,1024]{1,0:T(8,128)S(1)} custom-call(s32[2]{0:T(128)S(1)} %pad_add_fusion.place_ref, f32[1024,512]{1,0:T(8,128)S(1)} %copy-done, bf16[1024,512]{1,0:T(8,128)(2,1)S(1)} %get-tuple-element.117.high_ref, bf16[1024,512]{1,0:T(8,128)(2,1)S(1)} %get-tuple-element.118.low_ref), custom_call_target="tpu_custom_call" | custom-call | flops 100000000 | bytes 262144 | tf_op jit(solution)/shard_map/rest_products/pallas_call | solution.py:330
  67.4 2.5 %collective-permute-start.19 = (f32[4,32,640]{2,1,0:T(8,128)S(1)}, f32[4,32,640]{2,1,0:T(8,128)S(1)}, u32[]{:S(2)}, u32[]{:S(2)}) collective-permute-start(f32[4,32,640]{2,1,0:T(8,128)S(1)} %pad_maximum_fusion.refs_0_), channel_id=1, source_target_pairs={{0,6},{1,7},{2,4},{3,5},{4,2},{5,3},{6,0},{7,1},{8,14},{9,15},{10,... | collective-permute-start | bytes 983048 | tf_op jit(solution)/shard_map/ppermute | solution.py:511
  70.9 4.7 %cover.15.refs_7_ = f32[32,1024]{1,0:T(8,128)S(1)} custom-call(bf16[16,256,16]{2,1,0:T(8,128)(2,1)S(1)} %get-tuple-element.116.f_ref, bf16[16,16,1024]{2,1,0:T(8,128)(2,1)S(1)} %get-tuple-element.70.g_ref), custom_call_target="tpu_custom_call" | custom-call | flops 100000000 | bytes 262144 | tf_op jit(solution)/shard_map/cover/pallas_call | solution.py:100
  75.5 4.9 %cover.14.refs_6_ = f32[32,1024]{1,0:T(8,128)S(1)} custom-call(bf16[16,256,16]{2,1,0:T(8,128)(2,1)S(1)} %get-tuple-element.116.f_ref, bf16[16,16,1024]{2,1,0:T(8,128)(2,1)S(1)} %get-tuple-element.70.g_ref), custom_call_target="tpu_custom_call" | custom-call | flops 100000000 | bytes 262144 | tf_op jit(solution)/shard_map/cover/pallas_call | solution.py:100
  80.4 1.6 %rest_products.6.refs_8_ = f32[256,1024]{1,0:T(8,128)S(1)} custom-call(s32[2]{0:T(128)S(1)} %pad_add_fusion.place_ref, f32[1024,512]{1,0:T(8,128)S(1)} %copy-done, bf16[1024,512]{1,0:T(8,128)(2,1)S(1)} %get-tuple-element.117.high_ref, bf16[1024,512]{1,0:T(8,128)(2,1)S(1)} %get-tuple-element.118.low_ref), custom_call_target="tpu_custom_call" | custom-call | flops 100000000 | bytes 262144 | tf_op jit(solution)/shard_map/rest_products/pallas_call | solution.py:330
  82.1 1.6 %rest_products.7 = f32[256,1024]{1,0:T(8,128)S(1)} custom-call(s32[2]{0:T(128)S(1)} %pad_add_fusion.place_ref, f32[1024,512]{1,0:T(8,128)S(1)} %copy-done, bf16[1024,512]{1,0:T(8,128)(2,1)S(1)} %get-tuple-element.117.high_ref, bf16[1024,512]{1,0:T(8,128)(2,1)S(1)} %get-tuple-element.118.low_ref, f32[256,1024]{1,0:T(8,128)S(1)} %collective-permute-done.20.refs_0_), custom_call_target="tpu_custom_call" | custom-call | flops 100000000 | bytes 262144 | tf_op jit(solution)/shard_map/rest_products/pallas_call | solution.py:330
  83.7 1.3 %collective-permute-done.18.refs_2_ = f32[4,32,640]{2,1,0:T(8,128)S(1)} collective-permute-done((f32[4,32,640]{2,1,0:T(8,128)S(1)}, f32[4,32,640]{2,1,0:T(8,128)S(1)}, u32[]{:S(2)}, u32[]{:S(2)}) %collective-permute-start.18) | collective-permute-done | bytes 327712 | tf_op jit(solution)/shard_map/ppermute | solution.py:381
  85.6 1.5 %collective-permute-start.22 = (f32[256,1024]{1,0:T(8,128)S(1)}, f32[256,1024]{1,0:T(8,128)S(1)}, u32[]{:S(2)}, u32[]{:S(2)}) collective-permute-start(f32[256,1024]{1,0:T(8,128)S(1)} %rest_products.7), channel_id=1, source_target_pairs={{0,2},{1,3},{2,0},{3,1},{4,6},{5,7},{6,4},{7,5},{8,10},{9,11},{10,... | collective-permute-start | bytes 3145736 | tf_op jit(solution)/shard_map/ppermute | solution.py:381
  87.7 31.9 %factor.1 = (bf16[1024,1024]{1,0:T(8,128)(2,1)S(1)}, bf16[1024,1024]{1,0:T(8,128)(2,1)S(1)}, bf16[1024,128]{1,0:T(8,128)(2,1)S(1)}, bf16[1024,128]{1,0:T(8,128)(2,1)S(1)}) custom-call(s32[2]{0:T(128)S(1)} %pad_add_fusion.place_ref, f32[4,32,640]{2,1,0:T(8,128)S(1)} %pad_maximum_fusion.refs_0_, f32[4,32,640]{2,1,0:T(8,128)S(1)} %collective-permute-done.17.refs_1_, ...), custom_call_target="tpu_custom_call" | custom-call | flops 49999998976 | bytes 8388608 | tf_op jit(solution)/shard_map/factor/pallas_call | solution.py:276
  119.6 5.3 %solve.1 = f32[256,1024]{1,0:T(8,128)} custom-call(f32[32,1024]{1,0:T(8,128)S(1)} %select_add_fusion.refs_0_, f32[32,1024]{1,0:T(8,128)S(1)} %cover.9.refs_1_, f32[32,1024]{1,0:T(8,128)S(1)} %cover.10.refs_2_, f32[32,1024]{1,0:T(8,128)S(1)} %cover.11.refs_3_, f32[32,1024]{1,0:T(8,128)S(1)} %cover.12.refs_4_, f32[32,1024]{1,0:T(8,128)S(1)} %cover.13.refs_5_, ...), custom_call_target="tpu_custom_call" | custom-call | tf_op jit(solution)/shard_map/solve/pallas_call | solution.py:318
  (72 shorter events, 10.2 us)
Async XLA Ops:
  1.8 9.2 %collective-permute-start.2 = (f32[1,32,128]{2,1,0:T(8,128)S(1)}, f32[1,32,128]{2,1,0:T(8,128)S(1)}, u32[]{:S(2)}, u32[]{:S(2)}) collective-permute-start(f32[1,32,128]{2,1,0:T(8,128)S(1)} %reshape.67), channel_id=1, source_target_pairs={{0,24},{4,28},{8,16},{12,20},{16,8},{20,12},{24,0},{28,4},{1,25},{... | collective-permute-start | bytes 49160 | tf_op jit(solution)/shard_map/ppermute | solution.py:381
  6.9 4.8 %collective-permute-start.1 = (f32[1,32,128]{2,1,0:T(8,128)S(1)}, f32[1,32,128]{2,1,0:T(8,128)S(1)}, u32[]{:S(2)}, u32[]{:S(2)}) collective-permute-start(f32[1,32,128]{2,1,0:T(8,128)S(1)} %reshape.67), channel_id=1, source_target_pairs={{0,16},{4,20},{8,24},{12,28},{16,0},{20,4},{24,8},{28,12},{1,17},{... | collective-permute-start | bytes 49160 | tf_op jit(solution)/shard_map/ppermute | solution.py:381
  6.9 4.8 %collective-permute-start = (f32[1,32,128]{2,1,0:T(8,128)S(1)}, f32[1,32,128]{2,1,0:T(8,128)S(1)}, u32[]{:S(2)}, u32[]{:S(2)}) collective-permute-start(f32[1,32,128]{2,1,0:T(8,128)S(1)} %reshape.67), channel_id=1, source_target_pairs={{0,8},{4,12},{8,0},{12,4},{16,24},{20,28},{24,16},{28,20},{1,9},{5... | collective-permute-start | bytes 49160 | tf_op jit(solution)/shard_map/ppermute | solution.py:381
  8.5 14.2 %collective-permute-start.4 = (f32[128,512]{1,0:T(8,128)S(1)}, f32[128,512]{1,0:T(8,128)S(1)}, u32[]{:S(2)}, u32[]{:S(2)}) collective-permute-start(f32[128,512]{1,0:T(8,128)S(1)} %bitcast.14), channel_id=1, source_target_pairs={{0,16},{4,20},{8,24},{12,28},{16,0},{20,4},{24,8},{28,12},{1,17},{... | collective-permute-start | bytes 786440 | tf_op jit(solution)/shard_map/ppermute | solution.py:381
  11.7 4.3 %collective-permute-start.3 = (f32[4,32,128]{2,1,0:T(8,128)S(1)}, f32[4,32,128]{2,1,0:T(8,128)S(1)}, u32[]{:S(2)}, u32[]{:S(2)}) collective-permute-start(f32[4,32,128]{2,1,0:T(8,128)S(1)} %pad_maximum_fusion.2), channel_id=1, source_target_pairs={{0,4},{4,0},{8,12},{12,8},{16,20},{20,16},{24,28},{28,24},{1,5},{5... | collective-permute-start | bytes 196616 | tf_op jit(solution)/shard_map/ppermute | solution.py:381
  22.9 12.9 %collective-permute-start.5 = (f32[128,512]{1,0:T(8,128)S(1)}, f32[128,512]{1,0:T(8,128)S(1)}, u32[]{:S(2)}, u32[]{:S(2)}) collective-permute-start(f32[128,512]{1,0:T(8,128)S(1)} %get-tuple-element.74), channel_id=1, source_target_pairs={{0,4},{4,0},{8,12},{12,8},{16,20},{20,16},{24,28},{28,24},{1,5},{5... | collective-permute-start | bytes 786440 | tf_op jit(solution)/shard_map/ppermute | solution.py:381
  24.5 11.4 %collective-permute-start.6 = (f32[128,512]{1,0:T(8,128)S(1)}, f32[128,512]{1,0:T(8,128)S(1)}, u32[]{:S(2)}, u32[]{:S(2)}) collective-permute-start(f32[128,512]{1,0:T(8,128)S(1)} %get-tuple-element.76), channel_id=1, source_target_pairs={{0,8},{4,12},{8,0},{12,4},{16,24},{20,28},{24,16},{28,20},{1,9},{5... | collective-permute-start | bytes 786440 | tf_op jit(solution)/shard_map/ppermute | solution.py:381
  25.3 11.9 %collective-permute-start.7 = (f32[128,512]{1,0:T(8,128)S(1)}, f32[128,512]{1,0:T(8,128)S(1)}, u32[]{:S(2)}, u32[]{:S(2)}) collective-permute-start(f32[128,512]{1,0:T(8,128)S(1)} %get-tuple-element.76), channel_id=1, source_target_pairs={{0,12},{4,8},{8,4},{12,0},{16,28},{20,24},{24,20},{28,16},{1,13},{... | collective-permute-start | bytes 786440 | tf_op jit(solution)/shard_map/ppermute | solution.py:381
  38.5 9.1 %collective-permute-start.8 = (f32[32,640]{1,0:T(8,128)S(1)}, f32[32,640]{1,0:T(8,128)S(1)}, u32[]{:S(2)}, u32[]{:S(2)}) collective-permute-start(f32[32,640]{1,0:T(8,128)S(1)} %get-tuple-element.91), channel_id=1, source_target_pairs={{0,1},{1,0},{2,3},{3,2},{4,5},{5,4},{6,7},{7,6},{8,9},{9,8},{10,11... | collective-permute-start | bytes 245768 | tf_op jit(solution)/shard_map/ppermute | solution.py:381
  38.6 10.1 %collective-permute-start.9 = (f32[32,640]{1,0:T(8,128)S(1)}, f32[32,640]{1,0:T(8,128)S(1)}, u32[]{:S(2)}, u32[]{:S(2)}) collective-permute-start(f32[32,640]{1,0:T(8,128)S(1)} %get-tuple-element.92), channel_id=1, source_target_pairs={{0,2},{1,3},{2,0},{3,1},{4,6},{5,7},{6,4},{7,5},{8,10},{9,11},{10,... | collective-permute-start | bytes 245768 | tf_op jit(solution)/shard_map/ppermute | solution.py:381
  40.1 8.6 %collective-permute-start.10 = (f32[32,640]{1,0:T(8,128)S(1)}, f32[32,640]{1,0:T(8,128)S(1)}, u32[]{:S(2)}, u32[]{:S(2)}) collective-permute-start(f32[32,640]{1,0:T(8,128)S(1)} %get-tuple-element.93), channel_id=1, source_target_pairs={{0,3},{1,2},{2,1},{3,0},{4,7},{5,6},{6,5},{7,4},{8,11},{9,10},{10,... | collective-permute-start | bytes 245768 | tf_op jit(solution)/shard_map/ppermute | solution.py:381
  40.4 12.1 %collective-permute-start.14 = (f32[128,512]{1,0:T(8,128)S(1)}, f32[128,512]{1,0:T(8,128)S(1)}, u32[]{:S(2)}, u32[]{:S(2)}) collective-permute-start(f32[128,512]{1,0:T(8,128)S(1)} %get-tuple-element.101), channel_id=1, source_target_pairs={{0,4},{4,0},{8,12},{12,8},{16,20},{20,16},{24,28},{28,24},{1,5},{5... | collective-permute-start | bytes 786440 | tf_op jit(solution)/shard_map/ppermute | solution.py:381
  41.9 20.8 %collective-permute-start.15 = (f32[128,512]{1,0:T(8,128)S(1)}, f32[128,512]{1,0:T(8,128)S(1)}, u32[]{:S(2)}, u32[]{:S(2)}) collective-permute-start(f32[128,512]{1,0:T(8,128)S(1)} %get-tuple-element.103), channel_id=1, source_target_pairs={{0,8},{4,12},{8,0},{12,4},{16,24},{20,28},{24,16},{28,20},{1,9},{5... | collective-permute-start | bytes 786440 | tf_op jit(solution)/shard_map/ppermute | solution.py:381
  47.6 15.2 %collective-permute-start.16 = (f32[128,512]{1,0:T(8,128)S(1)}, f32[128,512]{1,0:T(8,128)S(1)}, u32[]{:S(2)}, u32[]{:S(2)}) collective-permute-start(f32[128,512]{1,0:T(8,128)S(1)} %get-tuple-element.103), channel_id=1, source_target_pairs={{0,12},{4,8},{8,4},{12,0},{16,28},{20,24},{24,20},{28,16},{1,13},{... | collective-permute-start | bytes 786440 | tf_op jit(solution)/shard_map/ppermute | solution.py:381
  48.7 18.0 %collective-permute-start.13 = (f32[1,32,640]{2,1,0:T(8,128)S(1)}, f32[1,32,640]{2,1,0:T(8,128)S(1)}, u32[]{:S(2)}, u32[]{:S(2)}) collective-permute-start(f32[1,32,640]{2,1,0:T(8,128)S(1)} %subtract_bitcast_fusion), channel_id=1, source_target_pairs={{0,24},{4,28},{8,16},{12,20},{16,8},{20,12},{24,0},{28,4},{1,25},{... | collective-permute-start | bytes 245768 | tf_op jit(solution)/shard_map/ppermute | solution.py:381
  52.5 14.2 %collective-permute-start.12 = (f32[1,32,640]{2,1,0:T(8,128)S(1)}, f32[1,32,640]{2,1,0:T(8,128)S(1)}, u32[]{:S(2)}, u32[]{:S(2)}) collective-permute-start(f32[1,32,640]{2,1,0:T(8,128)S(1)} %subtract_bitcast_fusion), channel_id=1, source_target_pairs={{0,16},{4,20},{8,24},{12,28},{16,0},{20,4},{24,8},{28,12},{1,17},{... | collective-permute-start | bytes 245768 | tf_op jit(solution)/shard_map/ppermute | solution.py:381
  52.5 14.2 %collective-permute-start.11 = (f32[1,32,640]{2,1,0:T(8,128)S(1)}, f32[1,32,640]{2,1,0:T(8,128)S(1)}, u32[]{:S(2)}, u32[]{:S(2)}) collective-permute-start(f32[1,32,640]{2,1,0:T(8,128)S(1)} %subtract_bitcast_fusion), channel_id=1, source_target_pairs={{0,8},{4,12},{8,0},{12,4},{16,24},{20,28},{24,16},{28,20},{1,9},{5... | collective-permute-start | bytes 245768 | tf_op jit(solution)/shard_map/ppermute | solution.py:381
  58.0 5.6 %copy-start = (f32[1024,512]{1,0:T(8,128)S(1)}, f32[1024,512]{1,0:T(8,128)}, u32[]{:S(2)}) copy-start(f32[1024,512]{1,0:T(8,128)} %prior_ref.7) | copy-start | bytes 6291460
  66.8 15.2 %collective-permute-start.20 = (f32[256,1024]{1,0:T(8,128)S(1)}, f32[256,1024]{1,0:T(8,128)S(1)}, u32[]{:S(2)}, u32[]{:S(2)}) collective-permute-start(f32[256,1024]{1,0:T(8,128)S(1)} %rest_products.4), channel_id=1, source_target_pairs={{0,1},{1,0},{2,3},{3,2},{4,5},{5,4},{6,7},{7,6},{8,9},{9,8},{10,11... | collective-permute-start | bytes 3145736 | tf_op jit(solution)/shard_map/ppermute | solution.py:381
  66.9 18.2 %collective-permute-start.21 = (f32[256,1024]{1,0:T(8,128)S(1)}, f32[256,1024]{1,0:T(8,128)S(1)}, u32[]{:S(2)}, u32[]{:S(2)}) collective-permute-start(f32[256,1024]{1,0:T(8,128)S(1)} %rest_products.5), channel_id=1, source_target_pairs={{0,1},{1,0},{2,3},{3,2},{4,5},{5,4},{6,7},{7,6},{8,9},{9,8},{10,11... | collective-permute-start | bytes 3145736 | tf_op jit(solution)/shard_map/ppermute | solution.py:381
  67.4 16.3 %collective-permute-start.19 = (f32[4,32,640]{2,1,0:T(8,128)S(1)}, f32[4,32,640]{2,1,0:T(8,128)S(1)}, u32[]{:S(2)}, u32[]{:S(2)}) collective-permute-start(f32[4,32,640]{2,1,0:T(8,128)S(1)} %pad_maximum_fusion.refs_0_), channel_id=1, source_target_pairs={{0,6},{1,7},{2,4},{3,5},{4,2},{5,3},{6,0},{7,1},{8,14},{9,15},{10,... | collective-permute-start | bytes 983048 | tf_op jit(solution)/shard_map/ppermute | solution.py:511
  69.8 15.2 %collective-permute-start.18 = (f32[4,32,640]{2,1,0:T(8,128)S(1)}, f32[4,32,640]{2,1,0:T(8,128)S(1)}, u32[]{:S(2)}, u32[]{:S(2)}) collective-permute-start(f32[4,32,640]{2,1,0:T(8,128)S(1)} %pad_maximum_fusion.refs_0_), channel_id=1, source_target_pairs={{0,2},{1,3},{2,0},{3,1},{4,6},{5,7},{6,4},{7,5},{8,10},{9,11},{10,... | collective-permute-start | bytes 983048 | tf_op jit(solution)/shard_map/ppermute | solution.py:381
  70.4 14.7 %collective-permute-start.17 = (f32[4,32,640]{2,1,0:T(8,128)S(1)}, f32[4,32,640]{2,1,0:T(8,128)S(1)}, u32[]{:S(2)}, u32[]{:S(2)}) collective-permute-start(f32[4,32,640]{2,1,0:T(8,128)S(1)} %pad_maximum_fusion.refs_0_), channel_id=1, source_target_pairs={{0,4},{4,0},{8,12},{12,8},{16,20},{20,16},{24,28},{28,24},{1,5},{5... | collective-permute-start | bytes 983048 | tf_op jit(solution)/shard_map/ppermute | solution.py:381
  82.0 5.1 %collective-permute-start.23 = (f32[4,32,640]{2,1,0:T(8,128)S(1)}, f32[4,32,640]{2,1,0:T(8,128)S(1)}, u32[]{:S(2)}, u32[]{:S(2)}) collective-permute-start(f32[4,32,640]{2,1,0:T(8,128)S(1)} %pad_maximum_fusion.refs_0_), channel_id=1, source_target_pairs={{0,1},{1,0},{2,3},{3,2},{4,5},{5,4},{6,7},{7,6},{8,9},{9,8},{10,11... | collective-permute-start | bytes 983048 | tf_op jit(solution)/shard_map/ppermute | solution.py:381
  85.1 2.0 %collective-permute-start.24 = (f32[4,32,640]{2,1,0:T(8,128)S(1)}, f32[4,32,640]{2,1,0:T(8,128)S(1)}, u32[]{:S(2)}, u32[]{:S(2)}) collective-permute-start(f32[4,32,640]{2,1,0:T(8,128)S(1)} %collective-permute-done.17.refs_1_), channel_id=1, source_target_pairs={{0,1},{1,0},{2,3},{3,2},{4,5},{5,4},{6,7},{7,6},{8,9},{9,8},{10,11... | collective-permute-start | bytes 983048 | tf_op jit(solution)/shard_map/ppermute | solution.py:381
  85.1 2.1 %collective-permute-start.25 = (f32[4,32,640]{2,1,0:T(8,128)S(1)}, f32[4,32,640]{2,1,0:T(8,128)S(1)}, u32[]{:S(2)}, u32[]{:S(2)}) collective-permute-start(f32[4,32,640]{2,1,0:T(8,128)S(1)} %collective-permute-done.18.refs_2_), channel_id=1, source_target_pairs={{0,1},{1,0},{2,3},{3,2},{4,5},{5,4},{6,7},{7,6},{8,9},{9,8},{10,11... | collective-permute-start | bytes 983048 | tf_op jit(solution)/shard_map/ppermute | solution.py:381
  85.6 2.1 %collective-permute-start.26 = (f32[4,32,640]{2,1,0:T(8,128)S(1)}, f32[4,32,640]{2,1,0:T(8,128)S(1)}, u32[]{:S(2)}, u32[]{:S(2)}) collective-permute-start(f32[4,32,640]{2,1,0:T(8,128)S(1)} %collective-permute-done.19.refs_3_), channel_id=1, source_target_pairs={{0,1},{1,0},{2,3},{3,2},{4,5},{5,4},{6,7},{7,6},{8,9},{9,8},{10,11... | collective-permute-start | bytes 983048 | tf_op jit(solution)/shard_map/ppermute | solution.py:381
  85.6 34.0 %collective-permute-start.22 = (f32[256,1024]{1,0:T(8,128)S(1)}, f32[256,1024]{1,0:T(8,128)S(1)}, u32[]{:S(2)}, u32[]{:S(2)}) collective-permute-start(f32[256,1024]{1,0:T(8,128)S(1)} %rest_products.7), channel_id=1, source_target_pairs={{0,2},{1,3},{2,0},{3,1},{4,6},{5,7},{6,4},{7,5},{8,10},{9,11},{10,... | collective-permute-start | bytes 3145736 | tf_op jit(solution)/shard_map/ppermute | solution.py:381

commit v5 on v4

--- a/solution.py
+++ b/solution.py
@@ -110,6 +110,112 @@
         cost_estimate=pl.CostEstimate(flops=10**8, bytes_accessed=1 << 18, transcendentals=0),
         name="cover",
     )(row_part, col_part)
+
+
+def lattice_kernel(row_ref, col_ref, t_ref, h_ref, row_cell_ref, col_cell_ref, place_ref):
+    count, rows = row_ref.shape[1:]
+    lines, cols = h_ref.shape[1:]
+    row_cell = jnp.floor(row_ref[0] * 0.125) * 8.0
+    place_ref[0] = (row_ref[0] - row_cell).T
+    place_ref[1] = row_ref[1].T
+    row_cell_ref[...] = row_cell[0:1].T
+    col_cell_ref[...] = jnp.floor(col_ref[0, 0:1] * 0.125) * 8.0
+
+    def row_tile(index, _):
+        here = pl.ds(pl.multiple_of(index * 16, 16), 16)
+        offset, north = place_ref[0, here], place_ref[1, here]
+        line = lax.broadcasted_iota(jnp.int32, (16, lines), 1).astype(F32) - CENTRE
+        total = [jnp.zeros((16, lines), F32) for _ in range(8)]
+        for a in range(count):
+            apart = jnp.broadcast_to(north[:, a : a + 1], (16, lines)) - line
+            near = jnp.exp2(apart * apart * SCALE)
+            which = jnp.broadcast_to(offset[:, a : a + 1], (16, lines))
+            for p in range(8):
+                total[p] = total[p] + jnp.where(which == float(p), near, 0.0)
+        for p in range(8):
+            high, low = split(total[p])
+            t_ref[p, here, :lines] = high
+            t_ref[p, here, lines:] = low
+        return 0
+
+    lax.fori_loop(0, rows // 16, row_tile, 0)
+
+    def col_tile(index, _):
+        here = pl.ds(pl.multiple_of(index * 256, 256), 256)
+        east, north = col_ref[0, :, here], col_ref[1, :, here]
+        east = east - jnp.floor(east * 0.125) * 8.0
+        line = jnp.floor(north[0:1] * 0.125) * 8.0
+        north = north - line
+        sub = lax.broadcasted_iota(jnp.int32, (8, 256), 0).astype(F32)
+        held = [jnp.zeros((8, 256), F32) for _ in range(8)]
+        for b in range(count):
+            one = jnp.where(sub == jnp.broadcast_to(north[b : b + 1], (8, 256)), 1.0, 0.0)
+            which = jnp.broadcast_to(east[b : b + 1], (8, 256))
+            for q in range(8):
+                held[q] = held[q] + jnp.where(which == float(q), one, 0.0)
+        line = jnp.broadcast_to(line, (8, 256))
+        for r in range(0, lines, 16):
+            low = line == float(r) - CENTRE
+            high = line == float(r + 8) - CENTRE
+            for q in range(8):
+                pair = [jnp.where(low, held[q], 0.0), jnp.where(high, held[q], 0.0)]
+                h_ref[q, r : r + 16, here] = jnp.concatenate(pair, 0).astype(BF)
+        return 0
+
+    lax.fori_loop(0, cols // 256, col_tile, 0)
+
+
+def lattice(row_points, col_points, lines):
+    count, rows = row_points.shape[1:]
+    cols = col_points.shape[2]
+    return pl.pallas_call(
+        lattice_kernel,
+        out_shape=[
+            jax.ShapeDtypeStruct((8, rows, 2 * lines), BF),
+            jax.ShapeDtypeStruct((8, lines, cols), BF),
+            jax.ShapeDtypeStruct((rows, 1), F32),
+            jax.ShapeDtypeStruct((1, cols), F32),
+        ],
+        in_specs=[pl.BlockSpec(memory_space=pltpu.VMEM)] * 2,
+        out_specs=[pl.BlockSpec(memory_space=pltpu.VMEM)] * 4,
+        scratch_shapes=[pltpu.VMEM((2, rows, count), F32)],
+        compiler_params=pltpu.CompilerParams(vmem_limit_bytes=24 << 20),
+        cost_estimate=pl.CostEstimate(flops=10**8, bytes_accessed=1 << 18, transcendentals=0),
+        name="lattice",
+    )(row_points, col_points)
+
+
+def lattice_cover_kernel(first_ref, t_ref, h_ref, row_cell_ref, col_cell_ref, o_ref, east_ref, *, points):
+    block, cols = o_ref.shape
+    here = pl.ds(pl.multiple_of(first_ref[0], block), block)
+    cell = jnp.broadcast_to(row_cell_ref[here], (block, cols)) - col_cell_ref[...]
+    for t in range(15):
+        apart = cell + float(t - 7)
+        east_ref[t] = jnp.exp2(apart * apart * SCALE)
+    rows = t_ref[:, here].reshape(8 * block, t_ref.shape[2])
+    total = jnp.zeros((block, cols), F32)
+    for q in range(8):
+        part = jnp.dot(
+            rows, jnp.concatenate([h_ref[q], h_ref[q]], 0), preferred_element_type=F32
+        )
+        for p in range(8):
+            total = total + part[p * block : (p + 1) * block] * east_ref[p - q + 7]
+    o_ref[...] = total * (1.0 / (points * points))
+
+
+def lattice_cover(parts, first, block, points):
+    cols = parts[1].shape[2]
+    return pl.pallas_call(
+        functools.partial(lattice_cover_kernel, points=points),
+        out_shape=jax.ShapeDtypeStruct((block, cols), F32),
+        in_specs=[pl.BlockSpec(memory_space=pltpu.SMEM)]
+        + [pl.BlockSpec(memory_space=pltpu.VMEM)] * 4,
+        out_specs=pl.BlockSpec(memory_space=pltpu.VMEM),
+        scratch_shapes=[pltpu.VMEM((15, block, cols), F32)],
+        compiler_params=pltpu.CompilerParams(vmem_limit_bytes=24 << 20),
+        cost_estimate=pl.CostEstimate(flops=10**8, bytes_accessed=1 << 18, transcendentals=0),
+        name="cover",
+    )(jnp.full((1,), first, jnp.int32), *parts)
 
 
 def inverse_factor(tiles):
@@ -413,7 +519,8 @@
     own_prior = prior_factor.reshape(panel_count, quarter_rows, -1)[:, :per_device]
     own_prior = own_prior.reshape(span_cols, -1)
 
-    if not (span_cols == NB and row_count == 8 and panel_count == 4):
+    lines = block_rows * row_count // 256 * 8
+    if not (span_cols == NB and row_count == 8 and panel_count == 4 and lines == 256):
         copies = jnp.broadcast_to(local_points, (row_count, 2 * count, span_cols))
         spread = lax.all_to_all(copies, "row", split_axis=0, concat_axis=0, tiled=True)
         parted = features(own_points, spread.transpose(1, 0, 2).reshape(2, count, B))
@@ -429,21 +536,22 @@
         diag_rows = lax.all_gather(mine, ("row", "panel"), axis=0, tiled=True)
         return solve(covers, [parts], factor(factor_kernel, (diag_rows,), B))
 
+    own_prior, local_points = lax.optimization_barrier((own_prior, local_points))
     far = swap(own_prior, "row", 4)
     held = jnp.concatenate([local_points] + [swap(local_points, "row", bit) for bit in (2, 4, 6)], 0)
     held = jnp.concatenate([held, swap(held, "row", 1)], 0)
     away = row_pos ^ jnp.arange(8, dtype=jnp.int32)
     order = (away >> 1) | ((away & 1) << 2)
     panel_points = held[order].transpose(1, 0, 2).reshape(2, count, B)
-    row_part, col_part = features(own_points, panel_points)
-    covers = [cover_rows(row_part, col_part, 0, lead) + unit]
-    row_part, far, covers = lax.optimization_barrier((row_part, far, covers))
+    parted = lattice(own_points, panel_points, lines)
+    covers = [lattice_cover(parted, 0, lead, count) + unit]
+    parted, far, covers = lax.optimization_barrier((parted, far, covers))
 
     def beside(operands, transfer, calls, extra=lambda *_: ()):
-        tied = lax.optimization_barrier((operands, row_part))
+        tied = lax.optimization_barrier((operands, parted))
         received = transfer(tied[0])
         done = [
-            cover_rows(tied[1], col_part, lead * (len(covers) + i), lead) for i in range(calls)
+            lattice_cover(tied[1], lead * (len(covers) + i), lead, count) for i in range(calls)
         ]
         received, done, more = lax.optimization_barrier((received, done, extra(tied[0])))
         covers.extend(done)
@@ -513,13 +621,14 @@
     def for_own_core(operands):
         panel_prior, part_3, part_1 = operands[1]
         from_3, from_1 = swap(part_3, "panel", 1), swap(part_1, "panel", 1)
-        return rest_part(panel_prior, 0), rest_part(panel_prior, 2, [from_3]), from_1
-
-    received, (part_0, part_2, from_1) = beside(
+        part_0, part_2 = rest_part(panel_prior, 0), rest_part(panel_prior, 2, [from_3])
+        return part_0, part_2, from_1, swap(operands[0], "panel", 1)
+
+    received, (part_0, part_2, from_1, held_there) = beside(
         (held, (panel_prior, part_3, part_1)), across, 2, for_own_core
     )
     here = [held, *received]
-    there = [swap(x, "panel", 1) for x in here]
+    there = [held_there] + [swap(x, "panel", 1) for x in received]
     parts = [part_0, from_1, swap(part_2, "panel", 2)]
     factors = factor(unfold_kernel, (place, *here, *there), B)
     return solve(covers, parts, factors)

time: 125 us -> 129 us (1.032)
  waiting for transfers between devices: 7.34 us -> 23.6 us
  Pallas kernels: 84.1 us -> 72.1 us
    ppermute x26, waiting for transfers between devices: 7.34 us -> 23.6 us  [swap(): lax.ppermute(block, axis, [(i, i ^ bit) for i in range(lax.axis_size(axis...]
    pallas_call x9, Pallas kernels: 38.4 us -> 26.3 us  [the longest x8 20.4 us: lattice_cover(): pl.pallas_call(functools.partial(lattice_cover_kernel, points=points), ou...]
  transfers between devices with their start and end apart: 27 -> 27, of which waited for: 8 -> 9; matrix products, arithmetic and copies ran while one was open for 2% -> 1% of each run, Pallas kernels for 62% -> 51%
where the time goes in v5:
time: 129 us
  Pallas kernels  72.1 us (56%)
  starting transfers between devices  28.5 us (22%)
  waiting for transfers between devices  23.6 us (18%)
  other arithmetic  2.01 us (2%)
  local copies, waits for them, and re-layouts  1.85 us (1%)
    pallas_call x1, Pallas kernels, factor(): pl.pallas_call(kernel, out_shape=[jax.ShapeDtypeStruct((n, n), BF)] * 2 +...  32.2 us
    ppermute x26, starting transfers between devices, swap(): lax.ppermute(block, axis, [(i, i ^ bit) for i in range(lax.axis_size(axis...  26.1 us
    ppermute x26, waiting for transfers between devices, swap(): lax.ppermute(block, axis, [(i, i ^ bit) for i in range(lax.axis_size(axis...  23.6 us
    pallas_call x8, Pallas kernels, lattice_cover(): pl.pallas_call(functools.partial(lattice_cover_kernel, points=points), ou...  20.4 us
    pallas_call x6, Pallas kernels, vmem_call(): pl.pallas_call(kernel, out_shape=out_shape, in_specs=[pl.BlockSpec(memory...  8.34 us
    pallas_call x1, Pallas kernels, lattice(): pl.pallas_call(lattice_kernel, out_shape=[jax.ShapeDtypeStruct((8, rows,...  5.93 us
    pallas_call x1, Pallas kernels, solve(): pl.pallas_call(functools.partial(solve_kernel, covers=len(covers)), out_s...  5.33 us
  transfers between devices with their start and end apart: 27, of which 9 were waited for; matrix products, arithmetic and copies ran while one was open for 1% of the time, Pallas kernels for 51%

profile of v5, /device:TPU:0, one launch (start us, length us, event | category | flops | bytes accessed | tf_op | source)
XLA Modules:
  0.0 128.6 jit_solution(11407105318300177174)
XLA Ops:
  2.8 5.1 %collective-permute-start.2 = (f32[1,32,128]{2,1,0:T(8,128)S(1)}, f32[1,32,128]{2,1,0:T(8,128)S(1)}, u32[]{:S(2)}, u32[]{:S(2)}) collective-permute-start(f32[1,32,128]{2,1,0:T(8,128)S(1)} %reshape.69), channel_id=1, source_target_pairs={{0,24},{4,28},{8,16},{12,20},{16,8},{20,12},{24,0},{28,4},{1,25},{... | collective-permute-start | bytes 49160 | tf_op jit(solution)/shard_map/ppermute | solution.py:487
  8.5 2.3 %collective-permute-start.4 = (f32[128,512]{1,0:T(8,128)S(1)}, f32[128,512]{1,0:T(8,128)S(1)}, u32[]{:S(2)}, u32[]{:S(2)}) collective-permute-start(f32[128,512]{1,0:T(8,128)S(1)} %bitcast.10), channel_id=1, source_target_pairs={{0,16},{4,20},{8,24},{12,28},{16,0},{20,4},{24,8},{28,12},{1,17},{... | collective-permute-start | bytes 786440 | tf_op jit(solution)/shard_map/ppermute | solution.py:487
  11.0 7.3 %collective-permute-done.1 = f32[1,32,128]{2,1,0:T(8,128)S(1)} collective-permute-done((f32[1,32,128]{2,1,0:T(8,128)S(1)}, f32[1,32,128]{2,1,0:T(8,128)S(1)}, u32[]{:S(2)}, u32[]{:S(2)}) %collective-permute-start.1) | collective-permute-done | bytes 16416 | tf_op jit(solution)/shard_map/ppermute | solution.py:487
  18.3 1.6 %collective-permute-start.3 = (f32[4,32,128]{2,1,0:T(8,128)S(1)}, f32[4,32,128]{2,1,0:T(8,128)S(1)}, u32[]{:S(2)}, u32[]{:S(2)}) collective-permute-start(f32[4,32,128]{2,1,0:T(8,128)S(1)} %pad_maximum_fusion.2), channel_id=1, source_target_pairs={{0,4},{4,0},{8,12},{12,8},{16,20},{20,16},{24,28},{28,24},{1,5},{5... | collective-permute-start | bytes 196616 | tf_op jit(solution)/shard_map/ppermute | solution.py:487
  19.9 2.8 %collective-permute-done.3 = f32[4,32,128]{2,1,0:T(8,128)S(1)} collective-permute-done((f32[4,32,128]{2,1,0:T(8,128)S(1)}, f32[4,32,128]{2,1,0:T(8,128)S(1)}, u32[]{:S(2)}, u32[]{:S(2)}) %collective-permute-start.3) | collective-permute-done | bytes 65568 | tf_op jit(solution)/shard_map/ppermute | solution.py:487
  23.3 5.9 %lattice.1 = (bf16[8,256,512]{2,1,0:T(8,128)(2,1)S(1)}, bf16[8,256,1024]{2,1,0:T(8,128)(2,1)S(1)}, f32[256,1]{1,0:T(8,128)S(1)}, f32[1,1024]{1,0:T(1,128)S(1)}) custom-call(f32[2,16,256]{2,1,0:T(8,128)S(1)} %fusion.1.row_ref, f32[2,16,1024]{2,1,0:T(8,128)S(1)} %reshape.70.col_ref), custom_call_target="tpu_custom_call" | custom-call | flops 100000000 | bytes 262144 | tf_op jit(solution)/shard_map/lattice/pallas_call | solution.py:171
  29.3 2.5 %cover.8 = f32[32,1024]{1,0:T(8,128)S(1)} custom-call(s32[1]{0:T(128)} %constant.25.clone.1.first_ref, bf16[8,256,512]{2,1,0:T(8,128)(2,1)S(1)} %get-tuple-element.152.t_ref, bf16[8,256,1024]{2,1,0:T(8,128)(2,1)S(1)} %get-tuple-element.153.h_ref, f32[256,1]{1,0:T(8,128)S(1)} %get-tuple-element.154.row_cell_ref, f32[1,1024]{1,0:T(1,128)S(1)} %get-tuple-element.155.col_cell_ref), custom_call_target="tpu_custom_call" | custom-call | flops 100000000 | bytes 262144 | tf_op jit(solution)/shard_map/cover/pallas_call | solution.py:208
  32.1 1.5 %collective-permute-start.5 = (f32[128,512]{1,0:T(8,128)S(1)}, f32[128,512]{1,0:T(8,128)S(1)}, u32[]{:S(2)}, u32[]{:S(2)}) collective-permute-start(f32[128,512]{1,0:T(8,128)S(1)} %get-tuple-element.101), channel_id=1, source_target_pairs={{0,4},{4,0},{8,12},{12,8},{16,20},{20,16},{24,28},{28,24},{1,5},{5... | collective-permute-start | bytes 786440 | tf_op jit(solution)/shard_map/ppermute | solution.py:487
  33.6 2.0 %collective-permute-start.7 = (f32[128,512]{1,0:T(8,128)S(1)}, f32[128,512]{1,0:T(8,128)S(1)}, u32[]{:S(2)}, u32[]{:S(2)}) collective-permute-start(f32[128,512]{1,0:T(8,128)S(1)} %get-tuple-element.103), channel_id=1, source_target_pairs={{0,12},{4,8},{8,4},{12,0},{16,28},{20,24},{24,20},{28,16},{1,13},{... | collective-permute-start | bytes 786440 | tf_op jit(solution)/shard_map/ppermute | solution.py:487
  35.6 2.5 %cover.10.refs_2_ = f32[32,1024]{1,0:T(8,128)S(1)} custom-call(s32[1]{0:T(128)} %constant.73.clone.1.first_ref, bf16[8,256,512]{2,1,0:T(8,128)(2,1)S(1)} %get-tuple-element.152.t_ref, bf16[8,256,1024]{2,1,0:T(8,128)(2,1)S(1)} %get-tuple-element.153.h_ref, f32[256,1]{1,0:T(8,128)S(1)} %get-tuple-element.154.row_cell_ref, ...), custom_call_target="tpu_custom_call" | custom-call | flops 100000000 | bytes 262144 | tf_op jit(solution)/shard_map/cover/pallas_call | solution.py:208
  38.2 2.5 %cover.9.refs_1_ = f32[32,1024]{1,0:T(8,128)S(1)} custom-call(s32[1]{0:T(128)} %constant.72.clone.1.first_ref, bf16[8,256,512]{2,1,0:T(8,128)(2,1)S(1)} %get-tuple-element.152.t_ref, bf16[8,256,1024]{2,1,0:T(8,128)(2,1)S(1)} %get-tuple-element.153.h_ref, f32[256,1]{1,0:T(8,128)S(1)} %get-tuple-element.154.row_cell_ref, ...), custom_call_target="tpu_custom_call" | custom-call | flops 100000000 | bytes 262144 | tf_op jit(solution)/shard_map/cover/pallas_call | solution.py:208
  40.8 2.0 %collective-permute-done.7.refs_4_ = f32[128,512]{1,0:T(8,128)S(1)} collective-permute-done((f32[128,512]{1,0:T(8,128)S(1)}, f32[128,512]{1,0:T(8,128)S(1)}, u32[]{:S(2)}, u32[]{:S(2)}) %collective-permute-start.7) | collective-permute-done | bytes 262176 | tf_op jit(solution)/shard_map/ppermute | solution.py:487
  44.1 1.6 %collective-permute-start.9 = (f32[32,640]{1,0:T(8,128)S(1)}, f32[32,640]{1,0:T(8,128)S(1)}, u32[]{:S(2)}, u32[]{:S(2)}) collective-permute-start(f32[32,640]{1,0:T(8,128)S(1)} %get-tuple-element.122), channel_id=1, source_target_pairs={{0,2},{1,3},{2,0},{3,1},{4,6},{5,7},{6,4},{7,5},{8,10},{9,11},{10,... | collective-permute-start | bytes 245768 | tf_op jit(solution)/shard_map/ppermute | solution.py:487
  46.0 1.5 %collective-permute-start.14 = (f32[128,512]{1,0:T(8,128)S(1)}, f32[128,512]{1,0:T(8,128)S(1)}, u32[]{:S(2)}, u32[]{:S(2)}) collective-permute-start(f32[128,512]{1,0:T(8,128)S(1)} %get-tuple-element.137), channel_id=1, source_target_pairs={{0,4},{4,0},{8,12},{12,8},{16,20},{20,16},{24,28},{28,24},{1,5},{5... | collective-permute-start | bytes 786440 | tf_op jit(solution)/shard_map/ppermute | solution.py:487
  47.4 2.5 %cover.11.refs_3_ = f32[32,1024]{1,0:T(8,128)S(1)} custom-call(s32[1]{0:T(128)} %constant.74.clone.1.first_ref, bf16[8,256,512]{2,1,0:T(8,128)(2,1)S(1)} %get-tuple-element.152.t_ref, bf16[8,256,1024]{2,1,0:T(8,128)(2,1)S(1)} %get-tuple-element.153.h_ref, f32[256,1]{1,0:T(8,128)S(1)} %get-tuple-element.154.row_cell_ref, ...), custom_call_target="tpu_custom_call" | custom-call | flops 100000000 | bytes 262144 | tf_op jit(solution)/shard_map/cover/pallas_call | solution.py:208
  50.0 2.1 %collective-permute-start.16 = (f32[128,512]{1,0:T(8,128)S(1)}, f32[128,512]{1,0:T(8,128)S(1)}, u32[]{:S(2)}, u32[]{:S(2)}) collective-permute-start(f32[128,512]{1,0:T(8,128)S(1)} %get-tuple-element.139), channel_id=1, source_target_pairs={{0,12},{4,8},{8,4},{12,0},{16,28},{20,24},{24,20},{28,16},{1,13},{... | collective-permute-start | bytes 786440 | tf_op jit(solution)/shard_map/ppermute | solution.py:487
  52.2 1.6 %collective-permute-start.12 = (f32[1,32,640]{2,1,0:T(8,128)S(1)}, f32[1,32,640]{2,1,0:T(8,128)S(1)}, u32[]{:S(2)}, u32[]{:S(2)}) collective-permute-start(f32[1,32,640]{2,1,0:T(8,128)S(1)} %subtract_bitcast_fusion), channel_id=1, source_target_pairs={{0,16},{4,20},{8,24},{12,28},{16,0},{20,4},{24,8},{28,12},{1,17},{... | collective-permute-start | bytes 245768 | tf_op jit(solution)/shard_map/ppermute | solution.py:487
  54.5 2.0 %collective-permute-start.11 = (f32[1,32,640]{2,1,0:T(8,128)S(1)}, f32[1,32,640]{2,1,0:T(8,128)S(1)}, u32[]{:S(2)}, u32[]{:S(2)}) collective-permute-start(f32[1,32,640]{2,1,0:T(8,128)S(1)} %subtract_bitcast_fusion), channel_id=1, source_target_pairs={{0,8},{4,12},{8,0},{12,4},{16,24},{20,28},{24,16},{28,20},{1,9},{5... | collective-permute-start | bytes 245768 | tf_op jit(solution)/shard_map/ppermute | solution.py:487
  56.5 2.7 %cover.13.refs_5_ = f32[32,1024]{1,0:T(8,128)S(1)} custom-call(s32[1]{0:T(128)} %constant.78.clone.1.first_ref, bf16[8,256,512]{2,1,0:T(8,128)(2,1)S(1)} %get-tuple-element.152.t_ref, bf16[8,256,1024]{2,1,0:T(8,128)(2,1)S(1)} %get-tuple-element.153.h_ref, f32[256,1]{1,0:T(8,128)S(1)} %get-tuple-element.154.row_cell_ref, ...), custom_call_target="tpu_custom_call" | custom-call | flops 100000000 | bytes 262144 | tf_op jit(solution)/shard_map/cover/pallas_call | solution.py:208
  59.3 2.5 %cover.12.refs_4_ = f32[32,1024]{1,0:T(8,128)S(1)} custom-call(s32[1]{0:T(128)} %constant.77.clone.1.first_ref, bf16[8,256,512]{2,1,0:T(8,128)(2,1)S(1)} %get-tuple-element.152.t_ref, bf16[8,256,1024]{2,1,0:T(8,128)(2,1)S(1)} %get-tuple-element.153.h_ref, f32[256,1]{1,0:T(8,128)S(1)} %get-tuple-element.154.row_cell_ref, ...), custom_call_target="tpu_custom_call" | custom-call | flops 100000000 | bytes 262144 | tf_op jit(solution)/shard_map/cover/pallas_call | solution.py:208
  61.8 3.9 %collective-permute-done.16.refs_7_ = f32[128,512]{1,0:T(8,128)S(1)} collective-permute-done((f32[128,512]{1,0:T(8,128)S(1)}, f32[128,512]{1,0:T(8,128)S(1)}, u32[]{:S(2)}, u32[]{:S(2)}) %collective-permute-start.16) | collective-permute-done | bytes 262176 | tf_op jit(solution)/shard_map/ppermute | solution.py:487
  66.6 1.6 %rest_products.5 = f32[256,1024]{1,0:T(8,128)S(1)} custom-call(s32[2]{0:T(128)S(1)} %pad_add_fusion.place_ref, f32[1024,512]{1,0:T(8,128)S(1)} %copy-done, bf16[1024,512]{1,0:T(8,128)(2,1)S(1)} %get-tuple-element.156.high_ref, bf16[1024,512]{1,0:T(8,128)(2,1)S(1)} %get-tuple-element.157.low_ref), custom_call_target="tpu_custom_call" | custom-call | flops 100000000 | bytes 262144 | tf_op jit(solution)/shard_map/rest_products/pallas_call | solution.py:436
  68.2 1.6 %rest_products.4 = f32[256,1024]{1,0:T(8,128)S(1)} custom-call(s32[2]{0:T(128)S(1)} %pad_add_fusion.place_ref, f32[1024,512]{1,0:T(8,128)S(1)} %copy-done, bf16[1024,512]{1,0:T(8,128)(2,1)S(1)} %get-tuple-element.156.high_ref, bf16[1024,512]{1,0:T(8,128)(2,1)S(1)} %get-tuple-element.157.low_ref), custom_call_target="tpu_custom_call" | custom-call | flops 100000000 | bytes 262144 | tf_op jit(solution)/shard_map/rest_products/pallas_call | solution.py:436
  70.4 2.4 %collective-permute-start.19 = (f32[4,32,640]{2,1,0:T(8,128)S(1)}, f32[4,32,640]{2,1,0:T(8,128)S(1)}, u32[]{:S(2)}, u32[]{:S(2)}) collective-permute-start(f32[4,32,640]{2,1,0:T(8,128)S(1)} %pad_maximum_fusion.refs_0_), channel_id=1, source_target_pairs={{0,6},{1,7},{2,4},{3,5},{4,2},{5,3},{6,0},{7,1},{8,14},{9,15},{10,... | collective-permute-start | bytes 983048 | tf_op jit(solution)/shard_map/ppermute | solution.py:619
  74.0 2.5 %cover.15.refs_7_ = f32[32,1024]{1,0:T(8,128)S(1)} custom-call(s32[1]{0:T(128)} %constant.80.clone.1.first_ref, bf16[8,256,512]{2,1,0:T(8,128)(2,1)S(1)} %get-tuple-element.152.t_ref, bf16[8,256,1024]{2,1,0:T(8,128)(2,1)S(1)} %get-tuple-element.153.h_ref, f32[256,1]{1,0:T(8,128)S(1)} %get-tuple-element.154.row_cell_ref, ...), custom_call_target="tpu_custom_call" | custom-call | flops 100000000 | bytes 262144 | tf_op jit(solution)/shard_map/cover/pallas_call | solution.py:208
  76.5 2.5 %cover.14.refs_6_ = f32[32,1024]{1,0:T(8,128)S(1)} custom-call(s32[1]{0:T(128)} %constant.79.clone.1.first_ref, bf16[8,256,512]{2,1,0:T(8,128)(2,1)S(1)} %get-tuple-element.152.t_ref, bf16[8,256,1024]{2,1,0:T(8,128)(2,1)S(1)} %get-tuple-element.153.h_ref, f32[256,1]{1,0:T(8,128)S(1)} %get-tuple-element.154.row_cell_ref, ...), custom_call_target="tpu_custom_call" | custom-call | flops 100000000 | bytes 262144 | tf_op jit(solution)/shard_map/cover/pallas_call | solution.py:208
  79.0 1.6 %rest_products.6.refs_8_ = f32[256,1024]{1,0:T(8,128)S(1)} custom-call(s32[2]{0:T(128)S(1)} %pad_add_fusion.place_ref, f32[1024,512]{1,0:T(8,128)S(1)} %copy-done, bf16[1024,512]{1,0:T(8,128)(2,1)S(1)} %get-tuple-element.156.high_ref, bf16[1024,512]{1,0:T(8,128)(2,1)S(1)} %get-tuple-element.157.low_ref), custom_call_target="tpu_custom_call" | custom-call | flops 100000000 | bytes 262144 | tf_op jit(solution)/shard_map/rest_products/pallas_call | solution.py:436
  80.6 1.6 %rest_products.7 = f32[256,1024]{1,0:T(8,128)S(1)} custom-call(s32[2]{0:T(128)S(1)} %pad_add_fusion.place_ref, f32[1024,512]{1,0:T(8,128)S(1)} %copy-done, bf16[1024,512]{1,0:T(8,128)(2,1)S(1)} %get-tuple-element.156.high_ref, bf16[1024,512]{1,0:T(8,128)(2,1)S(1)} %get-tuple-element.157.low_ref, f32[256,1024]{1,0:T(8,128)S(1)} %collective-permute-done.20.refs_0_), custom_call_target="tpu_custom_call" | custom-call | flops 100000000 | bytes 262144 | tf_op jit(solution)/shard_map/rest_products/pallas_call | solution.py:436
  82.2 6.2 %collective-permute-done.18.refs_2_ = f32[4,32,640]{2,1,0:T(8,128)S(1)} collective-permute-done((f32[4,32,640]{2,1,0:T(8,128)S(1)}, f32[4,32,640]{2,1,0:T(8,128)S(1)}, u32[]{:S(2)}, u32[]{:S(2)}) %collective-permute-start.18) | collective-permute-done | bytes 327712 | tf_op jit(solution)/shard_map/ppermute | solution.py:487
  89.0 1.5 %collective-permute-start.23 = (f32[256,1024]{1,0:T(8,128)S(1)}, f32[256,1024]{1,0:T(8,128)S(1)}, u32[]{:S(2)}, u32[]{:S(2)}) collective-permute-start(f32[256,1024]{1,0:T(8,128)S(1)} %rest_products.7), channel_id=1, source_target_pairs={{0,2},{1,3},{2,0},{3,1},{4,6},{5,7},{6,4},{7,5},{8,10},{9,11},{10,... | collective-permute-start | bytes 3145736 | tf_op jit(solution)/shard_map/ppermute | solution.py:487
  91.1 32.2 %factor.1 = (bf16[1024,1024]{1,0:T(8,128)(2,1)S(1)}, bf16[1024,1024]{1,0:T(8,128)(2,1)S(1)}, bf16[1024,128]{1,0:T(8,128)(2,1)S(1)}, bf16[1024,128]{1,0:T(8,128)(2,1)S(1)}) custom-call(s32[2]{0:T(128)S(1)} %pad_add_fusion.place_ref, f32[4,32,640]{2,1,0:T(8,128)S(1)} %pad_maximum_fusion.refs_0_, f32[4,32,640]{2,1,0:T(8,128)S(1)} %collective-permute-done.17.refs_1_, ...), custom_call_target="tpu_custom_call" | custom-call | flops 49999998976 | bytes 8388608 | tf_op jit(solution)/shard_map/factor/pallas_call | solution.py:382
  123.2 5.3 %solve.1 = f32[256,1024]{1,0:T(8,128)} custom-call(f32[32,1024]{1,0:T(8,128)S(1)} %select_add_fusion.refs_0_, f32[32,1024]{1,0:T(8,128)S(1)} %cover.9.refs_1_, f32[32,1024]{1,0:T(8,128)S(1)} %cover.10.refs_2_, f32[32,1024]{1,0:T(8,128)S(1)} %cover.11.refs_3_, f32[32,1024]{1,0:T(8,128)S(1)} %cover.12.refs_4_, f32[32,1024]{1,0:T(8,128)S(1)} %cover.13.refs_5_, ...), custom_call_target="tpu_custom_call" | custom-call | tf_op jit(solution)/shard_map/solve/pallas_call | solution.py:424
  (72 shorter events, 10.8 us)
Async XLA Ops:
  2.8 8.2 %collective-permute-start.2 = (f32[1,32,128]{2,1,0:T(8,128)S(1)}, f32[1,32,128]{2,1,0:T(8,128)S(1)}, u32[]{:S(2)}, u32[]{:S(2)}) collective-permute-start(f32[1,32,128]{2,1,0:T(8,128)S(1)} %reshape.69), channel_id=1, source_target_pairs={{0,24},{4,28},{8,16},{12,20},{16,8},{20,12},{24,0},{28,4},{1,25},{... | collective-permute-start | bytes 49160 | tf_op jit(solution)/shard_map/ppermute | solution.py:487
  7.9 10.4 %collective-permute-start.1 = (f32[1,32,128]{2,1,0:T(8,128)S(1)}, f32[1,32,128]{2,1,0:T(8,128)S(1)}, u32[]{:S(2)}, u32[]{:S(2)}) collective-permute-start(f32[1,32,128]{2,1,0:T(8,128)S(1)} %reshape.69), channel_id=1, source_target_pairs={{0,16},{4,20},{8,24},{12,28},{16,0},{20,4},{24,8},{28,12},{1,17},{... | collective-permute-start | bytes 49160 | tf_op jit(solution)/shard_map/ppermute | solution.py:487
  7.9 10.4 %collective-permute-start = (f32[1,32,128]{2,1,0:T(8,128)S(1)}, f32[1,32,128]{2,1,0:T(8,128)S(1)}, u32[]{:S(2)}, u32[]{:S(2)}) collective-permute-start(f32[1,32,128]{2,1,0:T(8,128)S(1)} %reshape.69), channel_id=1, source_target_pairs={{0,8},{4,12},{8,0},{12,4},{16,24},{20,28},{24,16},{28,20},{1,9},{5... | collective-permute-start | bytes 49160 | tf_op jit(solution)/shard_map/ppermute | solution.py:487
  8.5 23.4 %collective-permute-start.4 = (f32[128,512]{1,0:T(8,128)S(1)}, f32[128,512]{1,0:T(8,128)S(1)}, u32[]{:S(2)}, u32[]{:S(2)}) collective-permute-start(f32[128,512]{1,0:T(8,128)S(1)} %bitcast.10), channel_id=1, source_target_pairs={{0,16},{4,20},{8,24},{12,28},{16,0},{20,4},{24,8},{28,12},{1,17},{... | collective-permute-start | bytes 786440 | tf_op jit(solution)/shard_map/ppermute | solution.py:487
  18.3 4.3 %collective-permute-start.3 = (f32[4,32,128]{2,1,0:T(8,128)S(1)}, f32[4,32,128]{2,1,0:T(8,128)S(1)}, u32[]{:S(2)}, u32[]{:S(2)}) collective-permute-start(f32[4,32,128]{2,1,0:T(8,128)S(1)} %pad_maximum_fusion.2), channel_id=1, source_target_pairs={{0,4},{4,0},{8,12},{12,8},{16,20},{20,16},{24,28},{28,24},{1,5},{5... | collective-permute-start | bytes 196616 | tf_op jit(solution)/shard_map/ppermute | solution.py:487
  32.1 8.7 %collective-permute-start.5 = (f32[128,512]{1,0:T(8,128)S(1)}, f32[128,512]{1,0:T(8,128)S(1)}, u32[]{:S(2)}, u32[]{:S(2)}) collective-permute-start(f32[128,512]{1,0:T(8,128)S(1)} %get-tuple-element.101), channel_id=1, source_target_pairs={{0,4},{4,0},{8,12},{12,8},{16,20},{20,16},{24,28},{28,24},{1,5},{5... | collective-permute-start | bytes 786440 | tf_op jit(solution)/shard_map/ppermute | solution.py:487
  33.6 7.1 %collective-permute-start.6 = (f32[128,512]{1,0:T(8,128)S(1)}, f32[128,512]{1,0:T(8,128)S(1)}, u32[]{:S(2)}, u32[]{:S(2)}) collective-permute-start(f32[128,512]{1,0:T(8,128)S(1)} %get-tuple-element.103), channel_id=1, source_target_pairs={{0,8},{4,12},{8,0},{12,4},{16,24},{20,28},{24,16},{28,20},{1,9},{5... | collective-permute-start | bytes 786440 | tf_op jit(solution)/shard_map/ppermute | solution.py:487
  33.6 9.2 %collective-permute-start.7 = (f32[128,512]{1,0:T(8,128)S(1)}, f32[128,512]{1,0:T(8,128)S(1)}, u32[]{:S(2)}, u32[]{:S(2)}) collective-permute-start(f32[128,512]{1,0:T(8,128)S(1)} %get-tuple-element.103), channel_id=1, source_target_pairs={{0,12},{4,8},{8,4},{12,0},{16,28},{20,24},{24,20},{28,16},{1,13},{... | collective-permute-start | bytes 786440 | tf_op jit(solution)/shard_map/ppermute | solution.py:487
  44.0 6.0 %collective-permute-start.8 = (f32[32,640]{1,0:T(8,128)S(1)}, f32[32,640]{1,0:T(8,128)S(1)}, u32[]{:S(2)}, u32[]{:S(2)}) collective-permute-start(f32[32,640]{1,0:T(8,128)S(1)} %get-tuple-element.121), channel_id=1, source_target_pairs={{0,1},{1,0},{2,3},{3,2},{4,5},{5,4},{6,7},{7,6},{8,9},{9,8},{10,11... | collective-permute-start | bytes 245768 | tf_op jit(solution)/shard_map/ppermute | solution.py:487
  44.1 8.0 %collective-permute-start.9 = (f32[32,640]{1,0:T(8,128)S(1)}, f32[32,640]{1,0:T(8,128)S(1)}, u32[]{:S(2)}, u32[]{:S(2)}) collective-permute-start(f32[32,640]{1,0:T(8,128)S(1)} %get-tuple-element.122), channel_id=1, source_target_pairs={{0,2},{1,3},{2,0},{3,1},{4,6},{5,7},{6,4},{7,5},{8,10},{9,11},{10,... | collective-permute-start | bytes 245768 | tf_op jit(solution)/shard_map/ppermute | solution.py:487
  45.7 6.4 %collective-permute-start.10 = (f32[32,640]{1,0:T(8,128)S(1)}, f32[32,640]{1,0:T(8,128)S(1)}, u32[]{:S(2)}, u32[]{:S(2)}) collective-permute-start(f32[32,640]{1,0:T(8,128)S(1)} %get-tuple-element.123), channel_id=1, source_target_pairs={{0,3},{1,2},{2,1},{3,0},{4,7},{5,6},{6,5},{7,4},{8,11},{9,10},{10,... | collective-permute-start | bytes 245768 | tf_op jit(solution)/shard_map/ppermute | solution.py:487
  46.0 8.6 %collective-permute-start.14 = (f32[128,512]{1,0:T(8,128)S(1)}, f32[128,512]{1,0:T(8,128)S(1)}, u32[]{:S(2)}, u32[]{:S(2)}) collective-permute-start(f32[128,512]{1,0:T(8,128)S(1)} %get-tuple-element.137), channel_id=1, source_target_pairs={{0,4},{4,0},{8,12},{12,8},{16,20},{20,16},{24,28},{28,24},{1,5},{5... | collective-permute-start | bytes 786440 | tf_op jit(solution)/shard_map/ppermute | solution.py:487
  47.4 14.4 %collective-permute-start.15 = (f32[128,512]{1,0:T(8,128)S(1)}, f32[128,512]{1,0:T(8,128)S(1)}, u32[]{:S(2)}, u32[]{:S(2)}) collective-permute-start(f32[128,512]{1,0:T(8,128)S(1)} %get-tuple-element.139), channel_id=1, source_target_pairs={{0,8},{4,12},{8,0},{12,4},{16,24},{20,28},{24,16},{28,20},{1,9},{5... | collective-permute-start | bytes 786440 | tf_op jit(solution)/shard_map/ppermute | solution.py:487
  50.0 15.7 %collective-permute-start.16 = (f32[128,512]{1,0:T(8,128)S(1)}, f32[128,512]{1,0:T(8,128)S(1)}, u32[]{:S(2)}, u32[]{:S(2)}) collective-permute-start(f32[128,512]{1,0:T(8,128)S(1)} %get-tuple-element.139), channel_id=1, source_target_pairs={{0,12},{4,8},{8,4},{12,0},{16,28},{20,24},{24,20},{28,16},{1,13},{... | collective-permute-start | bytes 786440 | tf_op jit(solution)/shard_map/ppermute | solution.py:487
  52.1 17.6 %collective-permute-start.13 = (f32[1,32,640]{2,1,0:T(8,128)S(1)}, f32[1,32,640]{2,1,0:T(8,128)S(1)}, u32[]{:S(2)}, u32[]{:S(2)}) collective-permute-start(f32[1,32,640]{2,1,0:T(8,128)S(1)} %subtract_bitcast_fusion), channel_id=1, source_target_pairs={{0,24},{4,28},{8,16},{12,20},{16,8},{20,12},{24,0},{28,4},{1,25},{... | collective-permute-start | bytes 245768 | tf_op jit(solution)/shard_map/ppermute | solution.py:487
  52.2 17.6 %collective-permute-start.12 = (f32[1,32,640]{2,1,0:T(8,128)S(1)}, f32[1,32,640]{2,1,0:T(8,128)S(1)}, u32[]{:S(2)}, u32[]{:S(2)}) collective-permute-start(f32[1,32,640]{2,1,0:T(8,128)S(1)} %subtract_bitcast_fusion), channel_id=1, source_target_pairs={{0,16},{4,20},{8,24},{12,28},{16,0},{20,4},{24,8},{28,12},{1,17},{... | collective-permute-start | bytes 245768 | tf_op jit(solution)/shard_map/ppermute | solution.py:487
  54.5 15.2 %collective-permute-start.11 = (f32[1,32,640]{2,1,0:T(8,128)S(1)}, f32[1,32,640]{2,1,0:T(8,128)S(1)}, u32[]{:S(2)}, u32[]{:S(2)}) collective-permute-start(f32[1,32,640]{2,1,0:T(8,128)S(1)} %subtract_bitcast_fusion), channel_id=1, source_target_pairs={{0,8},{4,12},{8,0},{12,4},{16,24},{20,28},{24,16},{28,20},{1,9},{5... | collective-permute-start | bytes 245768 | tf_op jit(solution)/shard_map/ppermute | solution.py:487
  61.8 4.8 %copy-start = (f32[1024,512]{1,0:T(8,128)S(1)}, f32[1024,512]{1,0:T(8,128)}, u32[]{:S(2)}) copy-start(f32[1024,512]{1,0:T(8,128)} %prior_ref.7) | copy-start | bytes 6291460
  69.8 3.6 %collective-permute-start.20 = (f32[256,1024]{1,0:T(8,128)S(1)}, f32[256,1024]{1,0:T(8,128)S(1)}, u32[]{:S(2)}, u32[]{:S(2)}) collective-permute-start(f32[256,1024]{1,0:T(8,128)S(1)} %rest_products.4), channel_id=1, source_target_pairs={{0,1},{1,0},{2,3},{3,2},{4,5},{5,4},{6,7},{7,6},{8,9},{9,8},{10,11... | collective-permute-start | bytes 3145736 | tf_op jit(solution)/shard_map/ppermute | solution.py:487
  69.9 18.7 %collective-permute-start.21 = (f32[256,1024]{1,0:T(8,128)S(1)}, f32[256,1024]{1,0:T(8,128)S(1)}, u32[]{:S(2)}, u32[]{:S(2)}) collective-permute-start(f32[256,1024]{1,0:T(8,128)S(1)} %rest_products.5), channel_id=1, source_target_pairs={{0,1},{1,0},{2,3},{3,2},{4,5},{5,4},{6,7},{7,6},{8,9},{9,8},{10,11... | collective-permute-start | bytes 3145736 | tf_op jit(solution)/shard_map/ppermute | solution.py:487
  70.4 11.8 %collective-permute-start.22 = (f32[4,32,640]{2,1,0:T(8,128)S(1)}, f32[4,32,640]{2,1,0:T(8,128)S(1)}, u32[]{:S(2)}, u32[]{:S(2)}) collective-permute-start(f32[4,32,640]{2,1,0:T(8,128)S(1)} %pad_maximum_fusion.refs_0_), channel_id=1, source_target_pairs={{0,1},{1,0},{2,3},{3,2},{4,5},{5,4},{6,7},{7,6},{8,9},{9,8},{10,11... | collective-permute-start | bytes 983048 | tf_op jit(solution)/shard_map/ppermute | solution.py:487
  70.4 11.8 %collective-permute-start.19 = (f32[4,32,640]{2,1,0:T(8,128)S(1)}, f32[4,32,640]{2,1,0:T(8,128)S(1)}, u32[]{:S(2)}, u32[]{:S(2)}) collective-permute-start(f32[4,32,640]{2,1,0:T(8,128)S(1)} %pad_maximum_fusion.refs_0_), channel_id=1, source_target_pairs={{0,6},{1,7},{2,4},{3,5},{4,2},{5,3},{6,0},{7,1},{8,14},{9,15},{10,... | collective-permute-start | bytes 983048 | tf_op jit(solution)/shard_map/ppermute | solution.py:619
  72.9 15.5 %collective-permute-start.18 = (f32[4,32,640]{2,1,0:T(8,128)S(1)}, f32[4,32,640]{2,1,0:T(8,128)S(1)}, u32[]{:S(2)}, u32[]{:S(2)}) collective-permute-start(f32[4,32,640]{2,1,0:T(8,128)S(1)} %pad_maximum_fusion.refs_0_), channel_id=1, source_target_pairs={{0,2},{1,3},{2,0},{3,1},{4,6},{5,7},{6,4},{7,5},{8,10},{9,11},{10,... | collective-permute-start | bytes 983048 | tf_op jit(solution)/shard_map/ppermute | solution.py:487
  73.4 15.1 %collective-permute-start.17 = (f32[4,32,640]{2,1,0:T(8,128)S(1)}, f32[4,32,640]{2,1,0:T(8,128)S(1)}, u32[]{:S(2)}, u32[]{:S(2)}) collective-permute-start(f32[4,32,640]{2,1,0:T(8,128)S(1)} %pad_maximum_fusion.refs_0_), channel_id=1, source_target_pairs={{0,4},{4,0},{8,12},{12,8},{16,20},{20,16},{24,28},{28,24},{1,5},{5... | collective-permute-start | bytes 983048 | tf_op jit(solution)/shard_map/ppermute | solution.py:487
  88.5 2.0 %collective-permute-start.24 = (f32[4,32,640]{2,1,0:T(8,128)S(1)}, f32[4,32,640]{2,1,0:T(8,128)S(1)}, u32[]{:S(2)}, u32[]{:S(2)}) collective-permute-start(f32[4,32,640]{2,1,0:T(8,128)S(1)} %collective-permute-done.17.refs_1_), channel_id=1, source_target_pairs={{0,1},{1,0},{2,3},{3,2},{4,5},{5,4},{6,7},{7,6},{8,9},{9,8},{10,11... | collective-permute-start | bytes 983048 | tf_op jit(solution)/shard_map/ppermute | solution.py:487
  88.5 2.1 %collective-permute-start.25 = (f32[4,32,640]{2,1,0:T(8,128)S(1)}, f32[4,32,640]{2,1,0:T(8,128)S(1)}, u32[]{:S(2)}, u32[]{:S(2)}) collective-permute-start(f32[4,32,640]{2,1,0:T(8,128)S(1)} %collective-permute-done.18.refs_2_), channel_id=1, source_target_pairs={{0,1},{1,0},{2,3},{3,2},{4,5},{5,4},{6,7},{7,6},{8,9},{9,8},{10,11... | collective-permute-start | bytes 983048 | tf_op jit(solution)/shard_map/ppermute | solution.py:487
  89.0 2.1 %collective-permute-start.26 = (f32[4,32,640]{2,1,0:T(8,128)S(1)}, f32[4,32,640]{2,1,0:T(8,128)S(1)}, u32[]{:S(2)}, u32[]{:S(2)}) collective-permute-start(f32[4,32,640]{2,1,0:T(8,128)S(1)} %collective-permute-done.19.refs_3_), channel_id=1, source_target_pairs={{0,1},{1,0},{2,3},{3,2},{4,5},{5,4},{6,7},{7,6},{8,9},{9,8},{10,11... | collective-permute-start | bytes 983048 | tf_op jit(solution)/shard_map/ppermute | solution.py:487
  89.0 34.2 %collective-permute-start.23 = (f32[256,1024]{1,0:T(8,128)S(1)}, f32[256,1024]{1,0:T(8,128)S(1)}, u32[]{:S(2)}, u32[]{:S(2)}) collective-permute-start(f32[256,1024]{1,0:T(8,128)S(1)} %rest_products.7), channel_id=1, source_target_pairs={{0,2},{1,3},{2,0},{3,1},{4,6},{5,7},{6,4},{7,5},{8,10},{9,11},{10,... | collective-permute-start | bytes 3145736 | tf_op jit(solution)/shard_map/ppermute | solution.py:487

commit v6 on v4

--- a/solution.py
+++ b/solution.py
@@ -110,6 +110,124 @@
         cost_estimate=pl.CostEstimate(flops=10**8, bytes_accessed=1 << 18, transcendentals=0),
         name="cover",
     )(row_part, col_part)
+
+
+def row_table_kernel(row_ref, t_ref, row_cell_ref, place_ref):
+    count, rows = row_ref.shape[1:]
+    lines = t_ref.shape[2] // 2
+    row_cell = jnp.floor(row_ref[0] * 0.125) * 8.0
+    place_ref[0] = (row_ref[0] - row_cell).T
+    place_ref[1] = row_ref[1].T
+    row_cell_ref[...] = row_cell[0:1].T
+
+    def row_tile(index, _):
+        here = pl.ds(pl.multiple_of(index * 16, 16), 16)
+        offset, north = place_ref[0, here], place_ref[1, here]
+        line = lax.broadcasted_iota(jnp.int32, (16, lines), 1).astype(F32) - CENTRE
+        total = [jnp.zeros((16, lines), F32) for _ in range(8)]
+        for a in range(count):
+            apart = jnp.broadcast_to(north[:, a : a + 1], (16, lines)) - line
+            near = jnp.exp2(apart * apart * SCALE)
+            which = jnp.broadcast_to(offset[:, a : a + 1], (16, lines))
+            for p in range(8):
+                total[p] = total[p] + jnp.where(which == float(p), near, 0.0)
+        for p in range(8):
+            high, low = split(total[p])
+            t_ref[p, here, :lines] = high
+            t_ref[p, here, lines:] = low
+        return 0
+
+    lax.fori_loop(0, rows // 16, row_tile, 0)
+
+
+def row_table(row_points, lines):
+    count, rows = row_points.shape[1:]
+    return pl.pallas_call(
+        row_table_kernel,
+        out_shape=[
+            jax.ShapeDtypeStruct((8, rows, 2 * lines), BF),
+            jax.ShapeDtypeStruct((rows, 1), F32),
+        ],
+        in_specs=[pl.BlockSpec(memory_space=pltpu.VMEM)],
+        out_specs=[pl.BlockSpec(memory_space=pltpu.VMEM)] * 2,
+        scratch_shapes=[pltpu.VMEM((2, rows, count), F32)],
+        compiler_params=pltpu.CompilerParams(vmem_limit_bytes=16 << 20),
+        cost_estimate=pl.CostEstimate(flops=10**8, bytes_accessed=1 << 18, transcendentals=0),
+        name="row_table",
+    )(row_points)
+
+
+def pack(prior, points):
+    flat = points.reshape(-1, NB)
+    tiles = prior.shape[1] // NB
+    extra = flat.reshape(tiles, flat.shape[0] // tiles, NB).transpose(1, 0, 2)
+    return jnp.concatenate([prior, extra.reshape(-1, prior.shape[1])], 0)
+
+
+def column_counts(block_ref, h_ref, at, stride):
+    extra = block_ref.shape[0] - NB
+    tiles = block_ref.shape[1] // NB
+    flat = jnp.concatenate(
+        [block_ref[NB : NB + extra, NB * t : NB * t + NB] for t in range(tiles)], 0
+    )
+    count = flat.shape[0] // 2
+    lines = h_ref.shape[0]
+    east, north = flat[:count], flat[count:]
+    cell = jnp.floor(east[0:1] * 0.125) * 8.0
+    line = jnp.floor(north[0:1] * 0.125) * 8.0
+    east, north = east - cell, north - line
+    sub = lax.broadcasted_iota(jnp.int32, (8, NB), 0).astype(F32)
+    held = [jnp.zeros((8, NB), F32) for _ in range(8)]
+    for b in range(count):
+        one = jnp.where(sub == jnp.broadcast_to(north[b : b + 1], (8, NB)), 1.0, 0.0)
+        which = jnp.broadcast_to(east[b : b + 1], (8, NB))
+        for q in range(8):
+            held[q] = held[q] + jnp.where(which == float(q), one, 0.0)
+    line = jnp.broadcast_to(line, (8, NB))
+    for r in range(0, lines, 16):
+        low = line == float(r) - CENTRE
+        high = line == float(r + 8) - CENTRE
+        for q in range(8):
+            pair = [jnp.where(low, held[q], 0.0), jnp.where(high, held[q], 0.0)]
+            lanes = slice(q * stride + at, q * stride + at + NB)
+            h_ref[r : r + 16, lanes] = jnp.concatenate(pair, 0).astype(BF)
+    return cell
+
+
+def group_cover_kernel(place_ref, t_ref, row_cell_ref, *refs, points, unit):
+    blocks, (o_ref, h_ref, east_ref) = refs[:-3], refs[-3:]
+    rows, cols = o_ref.shape
+    chunk = east_ref.shape[1]
+    cells = [column_counts(ref, h_ref, NB * i, cols) for i, ref in enumerate(blocks)]
+    col_cell = jnp.concatenate(cells, 1)
+
+    def row_chunk(index, _):
+        here = pl.ds(pl.multiple_of(index * chunk, chunk), chunk)
+        cell = jnp.broadcast_to(row_cell_ref[here], (chunk, cols)) - col_cell
+        for t in range(15):
+            apart = cell + float(t - 7)
+            east_ref[t] = jnp.exp2(apart * apart * SCALE)
+        table = t_ref[:, here].reshape(8 * chunk, t_ref.shape[2])
+        total = jnp.zeros((chunk, cols), F32)
+        for q in range(0, 8, 2):
+            counts = h_ref[:, q * cols : (q + 2) * cols]
+            part = jnp.dot(
+                table, jnp.concatenate([counts, counts], 0), preferred_element_type=F32
+            )
+            for p in range(8):
+                for d in range(2):
+                    piece = part[p * chunk : (p + 1) * chunk, d * cols : (d + 1) * cols]
+                    total = total + piece * east_ref[p - q - d + 7]
+        o_ref[here] = total * (1.0 / (points * points))
+        return 0
+
+    lax.fori_loop(0, rows // chunk, row_chunk, 0)
+    if unit:
+        per_device = NB // 4
+        row = lax.broadcasted_iota(jnp.int32, (per_device, NB), 0)
+        col = lax.broadcasted_iota(jnp.int32, (per_device, NB), 1)
+        one = jnp.where(col == place_ref[1] * per_device + row, 1.0, 0.0)
+        o_ref[:per_device, :NB] = o_ref[:per_device, :NB] + one
 
 
 def inverse_factor(tiles):
@@ -225,6 +343,11 @@
     return (r ^ m) ^ (4 * second)
 
 
+def block_order(r):
+    order = [fold_block(r, k) for k in range(5)]
+    return order + [order[k] ^ 4 for k in (2, 3, 4)]
+
+
 def unfold_kernel(place_ref, *refs):
     pieces_refs, (lh_ref, ll_ref, wh_ref, wl_ref, a_ref, g_ref) = refs[:8], refs[8:]
     row_pos = place_ref[0]
@@ -285,18 +408,26 @@
     )(*operands)
 
 
-def solve_kernel(*refs, covers):
+def solve_kernel(place_ref, *refs, covers, by_columns):
     cover_refs, parts_refs = refs[:covers], refs[covers:-7]
     lh_ref, ll_ref, wh_ref, wl_ref, o_ref, xh_ref, xl_ref = refs[-7:]
     n = o_ref.shape[1]
-    first = 0
-    for ref in cover_refs:
-        rows = pl.ds(first, ref.shape[0])
-        taken = parts_refs[0][rows]
+
+    def put(rows, cols, value):
+        taken = parts_refs[0][rows, cols]
         for part in parts_refs[1:]:
-            taken = taken + part[rows]
-        o_ref[rows] = ref[...] - taken
-        first += ref.shape[0]
+            taken = taken + part[rows, cols]
+        o_ref[rows, cols] = value - taken
+
+    if by_columns:
+        pieces_of = [ref[:, c : c + NB] for ref in cover_refs for c in range(0, ref.shape[1], NB)]
+        for s, piece in zip(block_order(place_ref[0]), pieces_of):
+            put(slice(None), pl.ds(pl.multiple_of(s * NB, NB), NB), piece)
+    else:
+        first = 0
+        for ref in cover_refs:
+            put(pl.ds(first, ref.shape[0]), slice(None), ref[...])
+            first += ref.shape[0]
     for c in range(0, n, NB):
         here = o_ref[:, c : c + NB]
         if c:
@@ -311,19 +442,16 @@
         xl_ref[:, c : c + NB] = xl
 
 
-def solve(covers, parts, factors):
-    rows = sum(c.shape[0] for c in covers)
-    n = covers[0].shape[1]
-    operands = (*covers, *parts, *factors)
-    return pl.pallas_call(
-        functools.partial(solve_kernel, covers=len(covers)),
-        out_shape=jax.ShapeDtypeStruct((rows, n), F32),
-        in_specs=[pl.BlockSpec(memory_space=pltpu.VMEM)] * len(operands),
-        out_specs=pl.BlockSpec(memory_space=pltpu.VMEM),
-        scratch_shapes=[pltpu.VMEM((rows, n), BF)] * 2,
-        compiler_params=pltpu.CompilerParams(vmem_limit_bytes=32 << 20),
-        name="solve",
-    )(*operands)
+def solve(place, covers, parts, factors, by_columns):
+    rows, n = parts[0].shape
+    return vmem_call(
+        functools.partial(solve_kernel, covers=len(covers), by_columns=by_columns),
+        jax.ShapeDtypeStruct((rows, n), F32),
+        place,
+        [*covers, *parts, *factors],
+        [pltpu.VMEM((rows, n), BF)] * 2,
+        "solve",
+    )
 
 
 def vmem_call(kernel, out_shape, place, operands, scratch=(), name=None):
@@ -334,7 +462,7 @@
         + [pl.BlockSpec(memory_space=pltpu.VMEM)] * len(operands),
         out_specs=jax.tree.map(lambda _: pl.BlockSpec(memory_space=pltpu.VMEM), out_shape),
         scratch_shapes=list(scratch),
-        compiler_params=pltpu.CompilerParams(vmem_limit_bytes=16 << 20),
+        compiler_params=pltpu.CompilerParams(vmem_limit_bytes=32 << 20),
         cost_estimate=pl.CostEstimate(flops=10**8, bytes_accessed=1 << 18, transcendentals=0),
         name=name,
     )(place, *operands)
@@ -342,9 +470,9 @@
 
 def fold_products_kernel(place_ref, *refs):
     blocks, shares, total_ref = refs[:5], refs[5:-1], refs[-1]
-    own_high, own_low = split(blocks[0][...])
+    own_high, own_low = split(blocks[0][:NB])
     for k, ref in enumerate(blocks):
-        high, low = split(ref[...])
+        high, low = split(ref[:NB])
         total_ref[:, NB * k : NB * k + NB] = dot3(own_high, own_low, high, low)
     rows = shares[0].shape[0]
     for m, ref in enumerate(shares):
@@ -354,12 +482,9 @@
 
 def gather_split_kernel(place_ref, *refs):
     blocks, (high_ref, low_ref) = refs[:-2], refs[-2:]
-    row_pos = place_ref[0]
-    order = [fold_block(row_pos, k) for k in range(5)]
-    order = order + [order[k] ^ 4 for k in (2, 3, 4)]
-    for s, ref in zip(order, blocks):
+    for s, ref in zip(block_order(place_ref[0]), blocks):
         first = pl.multiple_of(s * NB, NB)
-        high, low = split(ref[...])
+        high, low = split(ref[:NB])
         high_ref[pl.ds(first, NB)] = high
         low_ref[pl.ds(first, NB)] = low
 
@@ -403,18 +528,21 @@
     count = points.shape[1]
     own_points = lax.dynamic_slice_in_dim(points, panel_pos * quarter_rows, quarter_rows, 2)
     local_points = points.reshape(2, count, panel_count, quarter_rows)[:, :, :, :per_device]
-    local_points = local_points.reshape(1, 2 * count, span_cols)
-
-    row_ids = jnp.arange(lead, dtype=jnp.int32)[:, None]
-    col_ids = jnp.arange(B, dtype=jnp.int32)[None, :]
-    on_diagonal = (row_ids < per_device) & (col_ids == device_pos * per_device + row_ids)
-    unit = jnp.where(on_diagonal, 1.0, 0.0).astype(F32)
-
+    local_points = local_points.reshape(2, count, span_cols)
     own_prior = prior_factor.reshape(panel_count, quarter_rows, -1)[:, :per_device]
     own_prior = own_prior.reshape(span_cols, -1)
-
-    if not (span_cols == NB and row_count == 8 and panel_count == 4):
-        copies = jnp.broadcast_to(local_points, (row_count, 2 * count, span_cols))
+    place = jnp.stack([row_pos, panel_pos]).astype(jnp.int32)
+    lines = block_rows * row_count // 256 * 8
+    folds = span_cols == NB and row_count == 8 and panel_count == 4 and lines == 256
+
+    if not (folds and 2 * count * NB == 8 * own_prior.shape[1]):
+        lead = 32
+        row_ids = jnp.arange(lead, dtype=jnp.int32)[:, None]
+        col_ids = jnp.arange(B, dtype=jnp.int32)[None, :]
+        on_diagonal = (row_ids < per_device) & (col_ids == device_pos * per_device + row_ids)
+        unit = jnp.where(on_diagonal, 1.0, 0.0).astype(F32)
+        flat = local_points.reshape(1, 2 * count, span_cols)
+        copies = jnp.broadcast_to(flat, (row_count, 2 * count, span_cols))
         spread = lax.all_to_all(copies, "row", split_axis=0, concat_axis=0, tiled=True)
         parted = features(own_points, spread.transpose(1, 0, 2).reshape(2, count, B))
         covers = [cover_rows(*parted, i, lead) for i in range(0, quarter_rows, lead)]
@@ -427,102 +555,92 @@
         parts = jnp.sum(parts, axis=0)
         mine = covers[0][:per_device] - parts[:per_device]
         diag_rows = lax.all_gather(mine, ("row", "panel"), axis=0, tiled=True)
-        return solve(covers, [parts], factor(factor_kernel, (diag_rows,), B))
-
-    far = swap(own_prior, "row", 4)
-    held = jnp.concatenate([local_points] + [swap(local_points, "row", bit) for bit in (2, 4, 6)], 0)
-    held = jnp.concatenate([held, swap(held, "row", 1)], 0)
-    away = row_pos ^ jnp.arange(8, dtype=jnp.int32)
-    order = (away >> 1) | ((away & 1) << 2)
-    panel_points = held[order].transpose(1, 0, 2).reshape(2, count, B)
-    row_part, col_part = features(own_points, panel_points)
-    covers = [cover_rows(row_part, col_part, 0, lead) + unit]
-    row_part, far, covers = lax.optimization_barrier((row_part, far, covers))
-
-    def beside(operands, transfer, calls, extra=lambda *_: ()):
-        tied = lax.optimization_barrier((operands, row_part))
-        received = transfer(tied[0])
-        done = [
-            cover_rows(tied[1], col_part, lead * (len(covers) + i), lead) for i in range(calls)
-        ]
-        received, done, more = lax.optimization_barrier((received, done, extra(tied[0])))
-        covers.extend(done)
-        return (received, more) if more else received
+        return solve(place, covers, [parts], factor(factor_kernel, (diag_rows,), B), False)
+
+    own = pack(own_prior, local_points)
+    far = swap(own, "row", 4)
+    table = row_table(own_points, lines)
+    far, table = lax.optimization_barrier((far, table))
+
+    def beside(operands, transfer, work):
+        operands, held = lax.optimization_barrier((operands, table))
+        return lax.optimization_barrier((transfer(operands), work(operands, held)))
+
+    def group_cover(held, blocks, unit=False):
+        cols = NB * len(blocks)
+        return vmem_call(
+            functools.partial(group_cover_kernel, points=count, unit=unit),
+            jax.ShapeDtypeStruct((quarter_rows, cols), F32),
+            place,
+            [*held, *blocks],
+            [pltpu.VMEM((lines, 8 * cols), BF), pltpu.VMEM((15, 32, cols), F32)],
+            "cover",
+        )
 
     seconds = [((row_pos >> (m.bit_length() - 1)) & 1) == 1 for m in (1, 2, 3)]
-    firsts = beside(
-        [jnp.where(second, own_prior, far) for second in seconds],
+    firsts, cover_1 = beside(
+        [jnp.where(second, own, far) for second in seconds],
         lambda blocks: [swap(block, "row", m) for m, block in zip((1, 2, 3), blocks)],
-        2,
-    )
-    place = jnp.stack([row_pos, panel_pos]).astype(jnp.int32)
+        lambda _, held: group_cover(held, [own, far], True),
+    )
     shares = vmem_call(
         fold_products_kernel,
         [jax.ShapeDtypeStruct((per_device, 5 * NB), F32)] * 4,
         place,
-        [own_prior, far, *firsts],
+        [own, far, *firsts],
         [pltpu.VMEM((NB, 5 * NB), F32)],
         "fold_products",
     )
-    others = [jnp.where(second, far, own_prior) for second in seconds]
+    others = [jnp.where(second, far, own) for second in seconds]
     shares, others = lax.optimization_barrier((shares, others))
-    sums = beside(
+    sums, cover_2 = beside(
         shares,
         lambda shares: [swap(share, "panel", m) for m, share in zip((1, 2, 3), shares[1:])],
-        1,
+        lambda _, held: group_cover(held, firsts),
     )
     rest = [swap(block, "row", m) for m, block in zip((1, 2, 3), others)]
-    places = [fold_block(row_pos, k) for k in range(5)]
-    lead_cover = jnp.concatenate(
-        [lax.dynamic_slice(covers[0], (jnp.int32(0), s * NB), (per_device, NB)) for s in places], 1
-    )
+    lead_cover = jnp.concatenate([cover_1[:per_device], cover_2[:per_device]], 1)
     shard = lead_cover - (shares[0] + sums[0] + sums[1] + sums[2])
 
-    def rest_part(panel_prior, m, plus=()):
-        return vmem_call(
-            functools.partial(rest_products_kernel, m=m),
-            jax.ShapeDtypeStruct((quarter_rows, B), F32),
-            place,
-            [prior_factor, *panel_prior, *plus],
-            name="rest_products",
-        )
-
-    def for_other_core(_):
+    along, cover_3 = beside(
+        shard[None],
+        lambda x: [swap(x, "row", bit) for bit in (2, 4, 6)],
+        lambda _, held: group_cover(held, rest),
+    )
+    held_rows = jnp.concatenate([shard[None]] + along, 0)
+
+    def across(x):
+        corner = [(i, i ^ 6) for i in range(32)]
+        return swap(x, "row", 1), swap(x, "panel", 2), lax.ppermute(x, ("row", "panel"), corner)
+
+    def rest_parts(x, _):
+        x, blocks = lax.optimization_barrier((x, [own, far, *firsts, *rest]))
         panel_prior = vmem_call(
             gather_split_kernel,
             [jax.ShapeDtypeStruct((B, own_prior.shape[1]), BF)] * 2,
             place,
-            [own_prior, far, *firsts, *rest],
+            blocks,
             name="gather_split",
         )
-        return panel_prior, rest_part(panel_prior, 3), rest_part(panel_prior, 1)
-
-    along, (panel_prior, part_3, part_1) = beside(
-        shard[None],
-        lambda x: [swap(x, "row", bit) for bit in (2, 4, 6)],
-        2,
-        for_other_core,
-    )
-    held = jnp.concatenate([shard[None]] + along, 0)
-
-    def across(operands):
-        x = operands[0]
-        corner = [(i, i ^ 6) for i in range(32)]
-        return swap(x, "row", 1), swap(x, "panel", 2), lax.ppermute(x, ("row", "panel"), corner)
-
-    def for_own_core(operands):
-        panel_prior, part_3, part_1 = operands[1]
-        from_3, from_1 = swap(part_3, "panel", 1), swap(part_1, "panel", 1)
-        return rest_part(panel_prior, 0), rest_part(panel_prior, 2, [from_3]), from_1
-
-    received, (part_0, part_2, from_1) = beside(
-        (held, (panel_prior, part_3, part_1)), across, 2, for_own_core
-    )
-    here = [held, *received]
-    there = [swap(x, "panel", 1) for x in here]
+
+        def part(m, plus=()):
+            return vmem_call(
+                functools.partial(rest_products_kernel, m=m),
+                jax.ShapeDtypeStruct((quarter_rows, B), F32),
+                place,
+                [prior_factor, *panel_prior, *plus],
+                name="rest_products",
+            )
+
+        from_3 = swap(part(3), "panel", 1)
+        from_1 = swap(part(1), "panel", 1)
+        return part(0), part(2, [from_3]), from_1, swap(x, "panel", 1)
+
+    received, (part_0, part_2, from_1, held_there) = beside(held_rows, across, rest_parts)
+    there = [held_there] + [swap(x, "panel", 1) for x in received]
     parts = [part_0, from_1, swap(part_2, "panel", 2)]
-    factors = factor(unfold_kernel, (place, *here, *there), B)
-    return solve(covers, parts, factors)
+    factors = factor(unfold_kernel, (place, held_rows, *received, *there), B)
+    return solve(place, [cover_1, cover_2, cover_3], parts, factors, True)
 
 
 def solution(mesh):

time: 125 us -> 137 us (1.096)
  waiting for transfers between devices: 7.34 us -> 31.3 us
  Pallas kernels: 84.1 us -> 76.9 us
  starting transfers between devices: 29.3 us -> 24.2 us
    pallas_call x10 -> x1, Pallas kernels: 43.8 us -> 4.83 us  [row_table(): pl.pallas_call(row_table_kernel, out_shape=[jax.ShapeDtypeStruct((8, rows...]
    pallas_call x6 -> x10, Pallas kernels: 8.37 us -> 39.9 us  [vmem_call(): pl.pallas_call(kernel, out_shape=out_shape, in_specs=[pl.BlockSpec(memory...]
    ppermute x26 -> x22, waiting for transfers between devices: 7.34 us -> 26.4 us  [swap(): lax.ppermute(block, axis, [(i, i ^ bit) for i in range(lax.axis_size(axis...]
    ppermute x1, waiting for transfers between devices: 0.01 us -> 4.86 us  [across(): lax.ppermute(x, ('row', 'panel'), corner)]
    ppermute x26 -> x22, starting transfers between devices: 26.8 us -> 22.8 us  [swap(): lax.ppermute(block, axis, [(i, i ^ bit) for i in range(lax.axis_size(axis...]
  transfers between devices with their start and end apart: 27 -> 23, of which waited for: 8 -> 9; matrix products, arithmetic and copies ran while one was open for 2% -> 0% of each run, Pallas kernels for 62% -> 49%
where the time goes in v6:
time: 137 us; the launch traced here: 136 us
  Pallas kernels  76.9 us (56%)
  waiting for transfers between devices  31.3 us (23%)
  starting transfers between devices  24.2 us (18%)
  other arithmetic  1.87 us (1%)
  local copies, waits for them, and re-layouts  1.78 us (1%)
    pallas_call x10, Pallas kernels, vmem_call(): pl.pallas_call(kernel, out_shape=out_shape, in_specs=[pl.BlockSpec(memory...  39.9 us
    pallas_call x1, Pallas kernels, factor(): pl.pallas_call(kernel, out_shape=[jax.ShapeDtypeStruct((n, n), BF)] * 2 +...  32.2 us
    ppermute x22, waiting for transfers between devices, swap(): lax.ppermute(block, axis, [(i, i ^ bit) for i in range(lax.axis_size(axis...  26.4 us
    ppermute x22, starting transfers between devices, swap(): lax.ppermute(block, axis, [(i, i ^ bit) for i in range(lax.axis_size(axis...  22.8 us
    ppermute x1, waiting for transfers between devices, across(): lax.ppermute(x, ('row', 'panel'), corner)  4.86 us
    pallas_call x1, Pallas kernels, row_table(): pl.pallas_call(row_table_kernel, out_shape=[jax.ShapeDtypeStruct((8, rows...  4.83 us
  transfers between devices with their start and end apart: 23, of which 9 were waited for; matrix products, arithmetic and copies ran while one was open for 0% of the time, Pallas kernels for 49%

profile of v6, /device:TPU:0, one launch (start us, length us, event | category | flops | bytes accessed | tf_op | source)
XLA Modules:
  0.0 136.3 jit_solution(9105209125031217981)
XLA Ops:
  0.0 0.7 fusion.2
  0.7 0.9 convert_add_fusion.1
  1.8 1.0 slice.24
  2.8 4.1 %collective-permute-start = (f32[136,512]{1,0:T(8,128)S(1)}, f32[136,512]{1,0:T(8,128)S(1)}, u32[]{:S(2)}, u32[]{:S(2)}) collective-permute-start(f32[136,512]{1,0:T(8,128)S(1)} %pad_maximum_fusion.1.refs_0_), channel_id=1, source_target_pairs={{0,16},{4,20},{8,24},{12,28},{16,0},{20,4},{24,8},{28,12},{1,17},{... | collective-permute-start | bytes 835592 | tf_op jit(solution)/shard_map/ppermute | solution.py:506
  6.9 4.8 %row_table.1 = (bf16[8,256,512]{2,1,0:T(8,128)(2,1)S(1)}, f32[256,1]{1,0:T(8,128)S(1)}) custom-call(f32[2,16,256]{2,1,0:T(8,128)S(1)} %fusion.1.row_ref), custom_call_target="tpu_custom_call" | custom-call | flops 100000000 | bytes 262144 | tf_op jit(solution)/shard_map/row_table/pallas_call | solution.py:145
  11.7 7.8 %collective-permute-done.refs_1_ = f32[136,512]{1,0:T(8,128)S(1)} collective-permute-done((f32[136,512]{1,0:T(8,128)S(1)}, f32[136,512]{1,0:T(8,128)S(1)}, u32[]{:S(2)}, u32[]{:S(2)}) %collective-permute-start) | collective-permute-done | bytes 278560 | tf_op jit(solution)/shard_map/ppermute | solution.py:506
  19.7 1.6 %collective-permute-start.1 = (f32[136,512]{1,0:T(8,128)S(1)}, f32[136,512]{1,0:T(8,128)S(1)}, u32[]{:S(2)}, u32[]{:S(2)}) collective-permute-start(f32[136,512]{1,0:T(8,128)S(1)} %get-tuple-element.74), channel_id=1, source_target_pairs={{0,4},{4,0},{8,12},{12,8},{16,20},{20,16},{24,28},{28,24},{1,5},{5... | collective-permute-start | bytes 835592 | tf_op jit(solution)/shard_map/ppermute | solution.py:506
  21.3 0.7 collective-permute-start.2
  21.9 1.3 collective-permute-start.3
  23.3 6.8 %cover.3.refs_0_ = f32[256,256]{1,0:T(8,128)S(1)} custom-call(s32[2]{0:T(128)S(1)} %pad_add_fusion.place_ref, bf16[8,256,512]{2,1,0:T(8,128)(2,1)S(1)} %get-tuple-element.101.t_ref, f32[256,1]{1,0:T(8,128)S(1)} %get-tuple-element.102.row_cell_ref, f32[136,512]{1,0:T(8,128)S(1)} %pad_maximum_fusion.1.refs_0_, f32[136,512]{1,0:T(8,128)S(1)} %collective-permute-done.refs_1_), custom_call_target="tpu_custom_call" | custom-call | flops 100000000 | bytes 262144 | tf_op jit(solution)/shard_map/cover/pallas_call | solution.py:458
  30.1 0.8 collective-permute-done.2.refs_3_.refs_1_
  30.9 3.9 %collective-permute-done.3.refs_4_.refs_2_ = f32[136,512]{1,0:T(8,128)S(1)} collective-permute-done((f32[136,512]{1,0:T(8,128)S(1)}, f32[136,512]{1,0:T(8,128)S(1)}, u32[]{:S(2)}, u32[]{:S(2)}) %collective-permute-start.3) | collective-permute-done | bytes 278560 | tf_op jit(solution)/shard_map/ppermute | solution.py:506
  34.7 1.2 fold_products.1
  36.0 1.3 collective-permute-start.5
  37.9 1.2 collective-permute-start.10
  39.2 1.7 %collective-permute-start.11 = (f32[136,512]{1,0:T(8,128)S(1)}, f32[136,512]{1,0:T(8,128)S(1)}, u32[]{:S(2)}, u32[]{:S(2)}) collective-permute-start(f32[136,512]{1,0:T(8,128)S(1)} %get-tuple-element.105), channel_id=1, source_target_pairs={{0,8},{4,12},{8,0},{12,4},{16,24},{20,28},{24,16},{28,20},{1,9},{5... | collective-permute-start | bytes 835592 | tf_op jit(solution)/shard_map/ppermute | solution.py:506
  40.9 9.2 %cover.4.refs_1_ = f32[256,384]{1,0:T(8,128)S(1)} custom-call(s32[2]{0:T(128)S(1)} %pad_add_fusion.place_ref, bf16[8,256,512]{2,1,0:T(8,128)(2,1)S(1)} %get-tuple-element.101.t_ref, f32[256,1]{1,0:T(8,128)S(1)} %get-tuple-element.102.row_cell_ref, f32[136,512]{1,0:T(8,128)S(1)} %collective-permute-done.1.refs_2_.refs_0_, ...), custom_call_target="tpu_custom_call" | custom-call | flops 100000000 | bytes 262144 | tf_op jit(solution)/shard_map/cover/pallas_call | solution.py:458
  50.8 4.3 %collective-permute-start.9 = (f32[1,32,640]{2,1,0:T(8,128)S(1)}, f32[1,32,640]{2,1,0:T(8,128)S(1)}, u32[]{:S(2)}, u32[]{:S(2)}) collective-permute-start(f32[1,32,640]{2,1,0:T(8,128)S(1)} %fusion), channel_id=1, source_target_pairs={{0,24},{4,28},{8,16},{12,20},{16,8},{20,12},{24,0},{28,4},{1,25},{... | collective-permute-start | bytes 245768 | tf_op jit(solution)/shard_map/ppermute | solution.py:506
  55.8 7.2 %collective-permute-done.12.refs_2_.refs_7_ = f32[136,512]{1,0:T(8,128)S(1)} collective-permute-done((f32[136,512]{1,0:T(8,128)S(1)}, f32[136,512]{1,0:T(8,128)S(1)}, u32[]{:S(2)}, u32[]{:S(2)}) %collective-permute-start.12) | collective-permute-done | bytes 278560 | tf_op jit(solution)/shard_map/ppermute | solution.py:506
  62.9 9.2 %cover.5.refs_2_ = f32[256,384]{1,0:T(8,128)S(1)} custom-call(s32[2]{0:T(128)S(1)} %pad_add_fusion.place_ref, bf16[8,256,512]{2,1,0:T(8,128)(2,1)S(1)} %get-tuple-element.101.t_ref, f32[256,1]{1,0:T(8,128)S(1)} %get-tuple-element.102.row_cell_ref, f32[136,512]{1,0:T(8,128)S(1)} %collective-permute-done.10.refs_0_.refs_5_, ...), custom_call_target="tpu_custom_call" | custom-call | flops 100000000 | bytes 262144 | tf_op jit(solution)/shard_map/cover/pallas_call | solution.py:458
  72.3 0.9 gather_split.1
  73.8 1.6 %rest_products.5 = f32[256,1024]{1,0:T(8,128)S(1)} custom-call(s32[2]{0:T(128)S(1)} %pad_add_fusion.place_ref, f32[1024,512]{1,0:T(8,128)S(1)} %copy-done, bf16[1024,512]{1,0:T(8,128)(2,1)S(1)} %get-tuple-element.119.high_ref, bf16[1024,512]{1,0:T(8,128)(2,1)S(1)} %get-tuple-element.120.low_ref), custom_call_target="tpu_custom_call" | custom-call | flops 100000000 | bytes 262144 | tf_op jit(solution)/shard_map/rest_products/pallas_call | solution.py:458
  75.4 1.6 %rest_products.7 = f32[256,1024]{1,0:T(8,128)S(1)} custom-call(s32[2]{0:T(128)S(1)} %pad_add_fusion.place_ref, f32[1024,512]{1,0:T(8,128)S(1)} %copy-done, bf16[1024,512]{1,0:T(8,128)(2,1)S(1)} %get-tuple-element.119.high_ref, bf16[1024,512]{1,0:T(8,128)(2,1)S(1)} %get-tuple-element.120.low_ref), custom_call_target="tpu_custom_call" | custom-call | flops 100000000 | bytes 262144 | tf_op jit(solution)/shard_map/rest_products/pallas_call | solution.py:458
  77.6 1.5 %collective-permute-start.15 = (f32[4,32,640]{2,1,0:T(8,128)S(1)}, f32[4,32,640]{2,1,0:T(8,128)S(1)}, u32[]{:S(2)}, u32[]{:S(2)}) collective-permute-start(f32[4,32,640]{2,1,0:T(8,128)S(1)} %pad_maximum_fusion.refs_0_), channel_id=1, source_target_pairs={{0,6},{1,7},{2,4},{3,5},{4,2},{5,3},{6,0},{7,1},{8,14},{9,15},{10,... | collective-permute-start | bytes 983048 | tf_op jit(solution)/shard_map/ppermute | solution.py:614
  79.6 1.5 %collective-permute-start.13 = (f32[4,32,640]{2,1,0:T(8,128)S(1)}, f32[4,32,640]{2,1,0:T(8,128)S(1)}, u32[]{:S(2)}, u32[]{:S(2)}) collective-permute-start(f32[4,32,640]{2,1,0:T(8,128)S(1)} %pad_maximum_fusion.refs_0_), channel_id=1, source_target_pairs={{0,4},{4,0},{8,12},{12,8},{16,20},{20,16},{24,28},{28,24},{1,5},{5... | collective-permute-start | bytes 983048 | tf_op jit(solution)/shard_map/ppermute | solution.py:506
  81.1 1.6 %rest_products.4.refs_3_ = f32[256,1024]{1,0:T(8,128)S(1)} custom-call(s32[2]{0:T(128)S(1)} %pad_add_fusion.place_ref, f32[1024,512]{1,0:T(8,128)S(1)} %copy-done, bf16[1024,512]{1,0:T(8,128)(2,1)S(1)} %get-tuple-element.119.high_ref, bf16[1024,512]{1,0:T(8,128)(2,1)S(1)} %get-tuple-element.120.low_ref), custom_call_target="tpu_custom_call" | custom-call | flops 100000000 | bytes 262144 | tf_op jit(solution)/shard_map/rest_products/pallas_call | solution.py:458
  82.6 1.6 %rest_products.6 = f32[256,1024]{1,0:T(8,128)S(1)} custom-call(s32[2]{0:T(128)S(1)} %pad_add_fusion.place_ref, f32[1024,512]{1,0:T(8,128)S(1)} %copy-done, bf16[1024,512]{1,0:T(8,128)(2,1)S(1)} %get-tuple-element.119.high_ref, bf16[1024,512]{1,0:T(8,128)(2,1)S(1)} %get-tuple-element.120.low_ref, f32[256,1024]{1,0:T(8,128)S(1)} %collective-permute-done.16.refs_0_), custom_call_target="tpu_custom_call" | custom-call | flops 100000000 | bytes 262144 | tf_op jit(solution)/shard_map/rest_products/pallas_call | solution.py:458
  84.2 4.9 %collective-permute-done.15.refs_3_ = f32[4,32,640]{2,1,0:T(8,128)S(1)} collective-permute-done((f32[4,32,640]{2,1,0:T(8,128)S(1)}, f32[4,32,640]{2,1,0:T(8,128)S(1)}, u32[]{:S(2)}, u32[]{:S(2)}) %collective-permute-start.15) | collective-permute-done | bytes 327712 | tf_op jit(solution)/shard_map/ppermute | solution.py:614
  89.1 6.1 %collective-permute-done.14.refs_2_ = f32[4,32,640]{2,1,0:T(8,128)S(1)} collective-permute-done((f32[4,32,640]{2,1,0:T(8,128)S(1)}, f32[4,32,640]{2,1,0:T(8,128)S(1)}, u32[]{:S(2)}, u32[]{:S(2)}) %collective-permute-start.14) | collective-permute-done | bytes 327712 | tf_op jit(solution)/shard_map/ppermute | solution.py:506
  95.8 1.5 %collective-permute-start.19 = (f32[256,1024]{1,0:T(8,128)S(1)}, f32[256,1024]{1,0:T(8,128)S(1)}, u32[]{:S(2)}, u32[]{:S(2)}) collective-permute-start(f32[256,1024]{1,0:T(8,128)S(1)} %rest_products.6), channel_id=1, source_target_pairs={{0,2},{1,3},{2,0},{3,1},{4,6},{5,7},{6,4},{7,5},{8,10},{9,11},{10,... | collective-permute-start | bytes 3145736 | tf_op jit(solution)/shard_map/ppermute | solution.py:506
  97.9 32.2 %factor.1 = (bf16[1024,1024]{1,0:T(8,128)(2,1)S(1)}, bf16[1024,1024]{1,0:T(8,128)(2,1)S(1)}, bf16[1024,128]{1,0:T(8,128)(2,1)S(1)}, bf16[1024,128]{1,0:T(8,128)(2,1)S(1)}) custom-call(s32[2]{0:T(128)S(1)} %pad_add_fusion.place_ref, f32[4,32,640]{2,1,0:T(8,128)S(1)} %pad_maximum_fusion.refs_0_, f32[4,32,640]{2,1,0:T(8,128)S(1)} %collective-permute-done.13.refs_1_, ...), custom_call_target="tpu_custom_call" | custom-call | flops 49999998976 | bytes 8388608 | tf_op jit(solution)/shard_map/factor/pallas_call | solution.py:399
  130.1 6.2 %solve.1 = f32[256,1024]{1,0:T(8,128)} custom-call(s32[2]{0:T(128)S(1)} %pad_add_fusion.place_ref, f32[256,256]{1,0:T(8,128)S(1)} %cover.3.refs_0_, f32[256,384]{1,0:T(8,128)S(1)} %cover.4.refs_1_, f32[256,384]{1,0:T(8,128)S(1)} %cover.5.refs_2_, f32[256,1024]{1,0:T(8,128)S(1)} %rest_products.4.refs_3_, f32[256,1024]{1,0:T(8,128)S(1)} %collective-permute-done.17.refs_4_, ...), custom_call_target="tpu_custom_call" | custom-call | flops 100000000 | bytes 262144 | tf_op jit(solution)/shard_map/solve/pallas_call | solution.py:458
  (43 shorter events, 5.3 us)
Async XLA Ops:
  2.8 16.7 %collective-permute-start = (f32[136,512]{1,0:T(8,128)S(1)}, f32[136,512]{1,0:T(8,128)S(1)}, u32[]{:S(2)}, u32[]{:S(2)}) collective-permute-start(f32[136,512]{1,0:T(8,128)S(1)} %pad_maximum_fusion.1.refs_0_), channel_id=1, source_target_pairs={{0,16},{4,20},{8,24},{12,28},{16,0},{20,4},{24,8},{28,12},{1,17},{... | collective-permute-start | bytes 835592 | tf_op jit(solution)/shard_map/ppermute | solution.py:506
  19.7 10.4 %collective-permute-start.1 = (f32[136,512]{1,0:T(8,128)S(1)}, f32[136,512]{1,0:T(8,128)S(1)}, u32[]{:S(2)}, u32[]{:S(2)}) collective-permute-start(f32[136,512]{1,0:T(8,128)S(1)} %get-tuple-element.74), channel_id=1, source_target_pairs={{0,4},{4,0},{8,12},{12,8},{16,20},{20,16},{24,28},{28,24},{1,5},{5... | collective-permute-start | bytes 835592 | tf_op jit(solution)/shard_map/ppermute | solution.py:506
  21.3 9.6 %collective-permute-start.2 = (f32[136,512]{1,0:T(8,128)S(1)}, f32[136,512]{1,0:T(8,128)S(1)}, u32[]{:S(2)}, u32[]{:S(2)}) collective-permute-start(f32[136,512]{1,0:T(8,128)S(1)} %get-tuple-element.76), channel_id=1, source_target_pairs={{0,8},{4,12},{8,0},{12,4},{16,24},{20,28},{24,16},{28,20},{1,9},{5... | collective-permute-start | bytes 835592 | tf_op jit(solution)/shard_map/ppermute | solution.py:506
  21.9 12.8 %collective-permute-start.3 = (f32[136,512]{1,0:T(8,128)S(1)}, f32[136,512]{1,0:T(8,128)S(1)}, u32[]{:S(2)}, u32[]{:S(2)}) collective-permute-start(f32[136,512]{1,0:T(8,128)S(1)} %get-tuple-element.76), channel_id=1, source_target_pairs={{0,12},{4,8},{8,4},{12,0},{16,28},{20,24},{24,20},{28,16},{1,13},{... | collective-permute-start | bytes 835592 | tf_op jit(solution)/shard_map/ppermute | solution.py:506
  36.0 14.2 %collective-permute-start.4 = (f32[32,640]{1,0:T(8,128)S(1)}, f32[32,640]{1,0:T(8,128)S(1)}, u32[]{:S(2)}, u32[]{:S(2)}) collective-permute-start(f32[32,640]{1,0:T(8,128)S(1)} %get-tuple-element.91), channel_id=1, source_target_pairs={{0,1},{1,0},{2,3},{3,2},{4,5},{5,4},{6,7},{7,6},{8,9},{9,8},{10,11... | collective-permute-start | bytes 245768 | tf_op jit(solution)/shard_map/ppermute | solution.py:506
  36.0 14.7 %collective-permute-start.5 = (f32[32,640]{1,0:T(8,128)S(1)}, f32[32,640]{1,0:T(8,128)S(1)}, u32[]{:S(2)}, u32[]{:S(2)}) collective-permute-start(f32[32,640]{1,0:T(8,128)S(1)} %get-tuple-element.92), channel_id=1, source_target_pairs={{0,2},{1,3},{2,0},{3,1},{4,6},{5,7},{6,4},{7,5},{8,10},{9,11},{10,... | collective-permute-start | bytes 245768 | tf_op jit(solution)/shard_map/ppermute | solution.py:506
  37.4 13.3 %collective-permute-start.6 = (f32[32,640]{1,0:T(8,128)S(1)}, f32[32,640]{1,0:T(8,128)S(1)}, u32[]{:S(2)}, u32[]{:S(2)}) collective-permute-start(f32[32,640]{1,0:T(8,128)S(1)} %get-tuple-element.93), channel_id=1, source_target_pairs={{0,3},{1,2},{2,1},{3,0},{4,7},{5,6},{6,5},{7,4},{8,11},{9,10},{10,... | collective-permute-start | bytes 245768 | tf_op jit(solution)/shard_map/ppermute | solution.py:506
  37.9 17.2 %collective-permute-start.10 = (f32[136,512]{1,0:T(8,128)S(1)}, f32[136,512]{1,0:T(8,128)S(1)}, u32[]{:S(2)}, u32[]{:S(2)}) collective-permute-start(f32[136,512]{1,0:T(8,128)S(1)} %get-tuple-element.103), channel_id=1, source_target_pairs={{0,4},{4,0},{8,12},{12,8},{16,20},{20,16},{24,28},{28,24},{1,5},{5... | collective-permute-start | bytes 835592 | tf_op jit(solution)/shard_map/ppermute | solution.py:506
  39.2 16.6 %collective-permute-start.11 = (f32[136,512]{1,0:T(8,128)S(1)}, f32[136,512]{1,0:T(8,128)S(1)}, u32[]{:S(2)}, u32[]{:S(2)}) collective-permute-start(f32[136,512]{1,0:T(8,128)S(1)} %get-tuple-element.105), channel_id=1, source_target_pairs={{0,8},{4,12},{8,0},{12,4},{16,24},{20,28},{24,16},{28,20},{1,9},{5... | collective-permute-start | bytes 835592 | tf_op jit(solution)/shard_map/ppermute | solution.py:506
  50.1 12.8 %collective-permute-start.12 = (f32[136,512]{1,0:T(8,128)S(1)}, f32[136,512]{1,0:T(8,128)S(1)}, u32[]{:S(2)}, u32[]{:S(2)}) collective-permute-start(f32[136,512]{1,0:T(8,128)S(1)} %get-tuple-element.105), channel_id=1, source_target_pairs={{0,12},{4,8},{8,4},{12,0},{16,28},{20,24},{24,20},{28,16},{1,13},{... | collective-permute-start | bytes 835592 | tf_op jit(solution)/shard_map/ppermute | solution.py:506
  50.8 21.4 %collective-permute-start.9 = (f32[1,32,640]{2,1,0:T(8,128)S(1)}, f32[1,32,640]{2,1,0:T(8,128)S(1)}, u32[]{:S(2)}, u32[]{:S(2)}) collective-permute-start(f32[1,32,640]{2,1,0:T(8,128)S(1)} %fusion), channel_id=1, source_target_pairs={{0,24},{4,28},{8,16},{12,20},{16,8},{20,12},{24,0},{28,4},{1,25},{... | collective-permute-start | bytes 245768 | tf_op jit(solution)/shard_map/ppermute | solution.py:506
  55.1 17.1 %collective-permute-start.8 = (f32[1,32,640]{2,1,0:T(8,128)S(1)}, f32[1,32,640]{2,1,0:T(8,128)S(1)}, u32[]{:S(2)}, u32[]{:S(2)}) collective-permute-start(f32[1,32,640]{2,1,0:T(8,128)S(1)} %fusion), channel_id=1, source_target_pairs={{0,16},{4,20},{8,24},{12,28},{16,0},{20,4},{24,8},{28,12},{1,17},{... | collective-permute-start | bytes 245768 | tf_op jit(solution)/shard_map/ppermute | solution.py:506
  55.1 17.1 %collective-permute-start.7 = (f32[1,32,640]{2,1,0:T(8,128)S(1)}, f32[1,32,640]{2,1,0:T(8,128)S(1)}, u32[]{:S(2)}, u32[]{:S(2)}) collective-permute-start(f32[1,32,640]{2,1,0:T(8,128)S(1)} %fusion), channel_id=1, source_target_pairs={{0,8},{4,12},{8,0},{12,4},{16,24},{20,28},{24,16},{28,20},{1,9},{5... | collective-permute-start | bytes 245768 | tf_op jit(solution)/shard_map/ppermute | solution.py:506
  72.2 1.6 %copy-start = (f32[1024,512]{1,0:T(8,128)S(1)}, f32[1024,512]{1,0:T(8,128)}, u32[]{:S(2)}) copy-start(f32[1024,512]{1,0:T(8,128)} %prior_ref.7) | copy-start | bytes 6291460
  75.4 4.2 %collective-permute-start.16 = (f32[256,1024]{1,0:T(8,128)S(1)}, f32[256,1024]{1,0:T(8,128)S(1)}, u32[]{:S(2)}, u32[]{:S(2)}) collective-permute-start(f32[256,1024]{1,0:T(8,128)S(1)} %rest_products.5), channel_id=1, source_target_pairs={{0,1},{1,0},{2,3},{3,2},{4,5},{5,4},{6,7},{7,6},{8,9},{9,8},{10,11... | collective-permute-start | bytes 3145736 | tf_op jit(solution)/shard_map/ppermute | solution.py:506
  77.0 18.3 %collective-permute-start.17 = (f32[256,1024]{1,0:T(8,128)S(1)}, f32[256,1024]{1,0:T(8,128)S(1)}, u32[]{:S(2)}, u32[]{:S(2)}) collective-permute-start(f32[256,1024]{1,0:T(8,128)S(1)} %rest_products.7), channel_id=1, source_target_pairs={{0,1},{1,0},{2,3},{3,2},{4,5},{5,4},{6,7},{7,6},{8,9},{9,8},{10,11... | collective-permute-start | bytes 3145736 | tf_op jit(solution)/shard_map/ppermute | solution.py:506
  77.6 11.5 %collective-permute-start.15 = (f32[4,32,640]{2,1,0:T(8,128)S(1)}, f32[4,32,640]{2,1,0:T(8,128)S(1)}, u32[]{:S(2)}, u32[]{:S(2)}) collective-permute-start(f32[4,32,640]{2,1,0:T(8,128)S(1)} %pad_maximum_fusion.refs_0_), channel_id=1, source_target_pairs={{0,6},{1,7},{2,4},{3,5},{4,2},{5,3},{6,0},{7,1},{8,14},{9,15},{10,... | collective-permute-start | bytes 983048 | tf_op jit(solution)/shard_map/ppermute | solution.py:614
  79.1 5.1 %collective-permute-start.18 = (f32[4,32,640]{2,1,0:T(8,128)S(1)}, f32[4,32,640]{2,1,0:T(8,128)S(1)}, u32[]{:S(2)}, u32[]{:S(2)}) collective-permute-start(f32[4,32,640]{2,1,0:T(8,128)S(1)} %pad_maximum_fusion.refs_0_), channel_id=1, source_target_pairs={{0,1},{1,0},{2,3},{3,2},{4,5},{5,4},{6,7},{7,6},{8,9},{9,8},{10,11... | collective-permute-start | bytes 983048 | tf_op jit(solution)/shard_map/ppermute | solution.py:506
  79.1 16.1 %collective-permute-start.14 = (f32[4,32,640]{2,1,0:T(8,128)S(1)}, f32[4,32,640]{2,1,0:T(8,128)S(1)}, u32[]{:S(2)}, u32[]{:S(2)}) collective-permute-start(f32[4,32,640]{2,1,0:T(8,128)S(1)} %pad_maximum_fusion.refs_0_), channel_id=1, source_target_pairs={{0,2},{1,3},{2,0},{3,1},{4,6},{5,7},{6,4},{7,5},{8,10},{9,11},{10,... | collective-permute-start | bytes 983048 | tf_op jit(solution)/shard_map/ppermute | solution.py:506
  79.6 15.7 %collective-permute-start.13 = (f32[4,32,640]{2,1,0:T(8,128)S(1)}, f32[4,32,640]{2,1,0:T(8,128)S(1)}, u32[]{:S(2)}, u32[]{:S(2)}) collective-permute-start(f32[4,32,640]{2,1,0:T(8,128)S(1)} %pad_maximum_fusion.refs_0_), channel_id=1, source_target_pairs={{0,4},{4,0},{8,12},{12,8},{16,20},{20,16},{24,28},{28,24},{1,5},{5... | collective-permute-start | bytes 983048 | tf_op jit(solution)/shard_map/ppermute | solution.py:506
  95.3 2.0 %collective-permute-start.20 = (f32[4,32,640]{2,1,0:T(8,128)S(1)}, f32[4,32,640]{2,1,0:T(8,128)S(1)}, u32[]{:S(2)}, u32[]{:S(2)}) collective-permute-start(f32[4,32,640]{2,1,0:T(8,128)S(1)} %collective-permute-done.13.refs_1_), channel_id=1, source_target_pairs={{0,1},{1,0},{2,3},{3,2},{4,5},{5,4},{6,7},{7,6},{8,9},{9,8},{10,11... | collective-permute-start | bytes 983048 | tf_op jit(solution)/shard_map/ppermute | solution.py:506
  95.3 2.1 %collective-permute-start.21 = (f32[4,32,640]{2,1,0:T(8,128)S(1)}, f32[4,32,640]{2,1,0:T(8,128)S(1)}, u32[]{:S(2)}, u32[]{:S(2)}) collective-permute-start(f32[4,32,640]{2,1,0:T(8,128)S(1)} %collective-permute-done.14.refs_2_), channel_id=1, source_target_pairs={{0,1},{1,0},{2,3},{3,2},{4,5},{5,4},{6,7},{7,6},{8,9},{9,8},{10,11... | collective-permute-start | bytes 983048 | tf_op jit(solution)/shard_map/ppermute | solution.py:506
  95.8 2.1 %collective-permute-start.22 = (f32[4,32,640]{2,1,0:T(8,128)S(1)}, f32[4,32,640]{2,1,0:T(8,128)S(1)}, u32[]{:S(2)}, u32[]{:S(2)}) collective-permute-start(f32[4,32,640]{2,1,0:T(8,128)S(1)} %collective-permute-done.15.refs_3_), channel_id=1, source_target_pairs={{0,1},{1,0},{2,3},{3,2},{4,5},{5,4},{6,7},{7,6},{8,9},{9,8},{10,11... | collective-permute-start | bytes 983048 | tf_op jit(solution)/shard_map/ppermute | solution.py:506
  95.8 34.3 %collective-permute-start.19 = (f32[256,1024]{1,0:T(8,128)S(1)}, f32[256,1024]{1,0:T(8,128)S(1)}, u32[]{:S(2)}, u32[]{:S(2)}) collective-permute-start(f32[256,1024]{1,0:T(8,128)S(1)} %rest_products.6), channel_id=1, source_target_pairs={{0,2},{1,3},{2,0},{3,1},{4,6},{5,7},{6,4},{7,5},{8,10},{9,11},{10,... | collective-permute-start | bytes 3145736 | tf_op jit(solution)/shard_map/ppermute | solution.py:506

commit v7 on v6

--- a/solution.py
+++ b/solution.py
@@ -112,8 +112,20 @@
     )(row_part, col_part)
 
 
+def table_rows(offset, north, lines):
+    line = lax.broadcasted_iota(jnp.int32, (16, lines), 1).astype(F32) - CENTRE
+    total = [jnp.zeros((16, lines), F32) for _ in range(8)]
+    for a in range(offset.shape[1]):
+        apart = jnp.broadcast_to(north[:, a : a + 1], (16, lines)) - line
+        near = jnp.exp2(apart * apart * SCALE)
+        which = jnp.broadcast_to(offset[:, a : a + 1], (16, lines))
+        for p in range(8):
+            total[p] = total[p] + jnp.where(which == float(p), near, 0.0)
+    return [split(x) for x in total]
+
+
 def row_table_kernel(row_ref, t_ref, row_cell_ref, place_ref):
-    count, rows = row_ref.shape[1:]
+    rows = row_ref.shape[2]
     lines = t_ref.shape[2] // 2
     row_cell = jnp.floor(row_ref[0] * 0.125) * 8.0
     place_ref[0] = (row_ref[0] - row_cell).T
@@ -122,17 +134,7 @@
 
     def row_tile(index, _):
         here = pl.ds(pl.multiple_of(index * 16, 16), 16)
-        offset, north = place_ref[0, here], place_ref[1, here]
-        line = lax.broadcasted_iota(jnp.int32, (16, lines), 1).astype(F32) - CENTRE
-        total = [jnp.zeros((16, lines), F32) for _ in range(8)]
-        for a in range(count):
-            apart = jnp.broadcast_to(north[:, a : a + 1], (16, lines)) - line
-            near = jnp.exp2(apart * apart * SCALE)
-            which = jnp.broadcast_to(offset[:, a : a + 1], (16, lines))
-            for p in range(8):
-                total[p] = total[p] + jnp.where(which == float(p), near, 0.0)
-        for p in range(8):
-            high, low = split(total[p])
+        for p, (high, low) in enumerate(table_rows(place_ref[0, here], place_ref[1, here], lines)):
             t_ref[p, here, :lines] = high
             t_ref[p, here, lines:] = low
         return 0
@@ -164,21 +166,25 @@
     return jnp.concatenate([prior, extra.reshape(-1, prior.shape[1])], 0)
 
 
-def column_counts(block_ref, h_ref, at, stride):
+def unpack(block_ref):
     extra = block_ref.shape[0] - NB
     tiles = block_ref.shape[1] // NB
     flat = jnp.concatenate(
         [block_ref[NB : NB + extra, NB * t : NB * t + NB] for t in range(tiles)], 0
     )
     count = flat.shape[0] // 2
+    return flat[:count], flat[count:]
+
+
+def column_counts(block_ref, h_ref, at, stride):
+    east, north = unpack(block_ref)
     lines = h_ref.shape[0]
-    east, north = flat[:count], flat[count:]
     cell = jnp.floor(east[0:1] * 0.125) * 8.0
     line = jnp.floor(north[0:1] * 0.125) * 8.0
     east, north = east - cell, north - line
     sub = lax.broadcasted_iota(jnp.int32, (8, NB), 0).astype(F32)
     held = [jnp.zeros((8, NB), F32) for _ in range(8)]
-    for b in range(count):
+    for b in range(east.shape[0]):
         one = jnp.where(sub == jnp.broadcast_to(north[b : b + 1], (8, NB)), 1.0, 0.0)
         which = jnp.broadcast_to(east[b : b + 1], (8, NB))
         for q in range(8):
@@ -194,40 +200,80 @@
     return cell
 
 
-def group_cover_kernel(place_ref, t_ref, row_cell_ref, *refs, points, unit):
-    blocks, (o_ref, h_ref, east_ref) = refs[:-3], refs[-3:]
-    rows, cols = o_ref.shape
-    chunk = east_ref.shape[1]
+def cover_chunk(table, row_cell, col_cell, h_ref, east_ref, points):
+    chunk, cols = east_ref.shape[1:]
+    cell = jnp.broadcast_to(row_cell, (chunk, cols)) - col_cell
+    for t in range(15):
+        apart = cell + float(t - 7)
+        east_ref[t] = jnp.exp2(apart * apart * SCALE)
+    table = table.reshape(8 * chunk, table.shape[2])
+    total = jnp.zeros((chunk, cols), F32)
+    for q in range(8):
+        counts = h_ref[:, q * cols : (q + 1) * cols]
+        part = jnp.dot(table, jnp.concatenate([counts, counts], 0), preferred_element_type=F32)
+        for p in range(8):
+            total = total + part[p * chunk : (p + 1) * chunk] * east_ref[p - q + 7]
+    return total * (1.0 / (points * points))
+
+
+def lead_cover_kernel(
+    place_ref, t_ref, row_cell_ref, *refs, points
+):
+    blocks, refs = refs[:4], refs[4:]
+    folded_ref, own_ref, h_ref, col_cell_ref, east_ref, far_ref, far_cell_ref, far_table_ref = refs
+    rows, cols = own_ref.shape
+    lines = h_ref.shape[0]
     cells = [column_counts(ref, h_ref, NB * i, cols) for i, ref in enumerate(blocks)]
     col_cell = jnp.concatenate(cells, 1)
+    col_cell_ref[...] = col_cell
+
+    east, north = unpack(blocks[1])
+    far_ref[0] = (east - cells[1]).T
+    far_ref[1] = north.T
+    far_cell_ref[...] = cells[1].T
+    first = pl.multiple_of(place_ref[1] * rows, rows)
+    for r in range(0, rows, 16):
+        here = pl.ds(first + r, 16)
+        for p, (high, low) in enumerate(table_rows(far_ref[0, here], far_ref[1, here], lines)):
+            far_table_ref[p, r : r + 16, :lines] = high
+            far_table_ref[p, r : r + 16, lines:] = low
+
+    mine = cover_chunk(t_ref[:, :rows], row_cell_ref[:rows], col_cell, h_ref, east_ref, points)
+    row = lax.broadcasted_iota(jnp.int32, (rows, cols), 0)
+    col = lax.broadcasted_iota(jnp.int32, (rows, cols), 1)
+    mine = mine + jnp.where(col == first + row, 1.0, 0.0)
+    own_ref[...] = mine
+    far = cover_chunk(
+        far_table_ref[...], far_cell_ref[pl.ds(first, rows)], col_cell, h_ref, east_ref, points
+    )
+    folded_ref[:, : 3 * NB] = mine[:, : 3 * NB]
+    folded_ref[:, 3 * NB : 4 * NB] = far[:, 2 * NB : 3 * NB]
+    own_last = (place_ref[0] & 3) < 2
+    folded_ref[:, 4 * NB :] = jnp.where(own_last, mine[:, 3 * NB :], far[:, 3 * NB :])
+
+
+def later_cover_kernel(t_ref, row_cell_ref, h_ref, col_cell_ref, o_ref, east_ref, *, points):
+    chunk = east_ref.shape[1]
+    skipped = t_ref.shape[1] - o_ref.shape[0]
 
     def row_chunk(index, _):
-        here = pl.ds(pl.multiple_of(index * chunk, chunk), chunk)
-        cell = jnp.broadcast_to(row_cell_ref[here], (chunk, cols)) - col_cell
-        for t in range(15):
-            apart = cell + float(t - 7)
-            east_ref[t] = jnp.exp2(apart * apart * SCALE)
-        table = t_ref[:, here].reshape(8 * chunk, t_ref.shape[2])
-        total = jnp.zeros((chunk, cols), F32)
-        for q in range(0, 8, 2):
-            counts = h_ref[:, q * cols : (q + 2) * cols]
-            part = jnp.dot(
-                table, jnp.concatenate([counts, counts], 0), preferred_element_type=F32
-            )
-            for p in range(8):
-                for d in range(2):
-                    piece = part[p * chunk : (p + 1) * chunk, d * cols : (d + 1) * cols]
-                    total = total + piece * east_ref[p - q - d + 7]
-        o_ref[here] = total * (1.0 / (points * points))
+        first = pl.multiple_of(index * chunk, chunk)
+        here = pl.ds(pl.multiple_of(first + skipped, chunk), chunk)
+        o_ref[pl.ds(first, chunk)] = cover_chunk(
+            t_ref[:, here], row_cell_ref[here], col_cell_ref[...], h_ref, east_ref, points
+        )
         return 0
 
-    lax.fori_loop(0, rows // chunk, row_chunk, 0)
-    if unit:
-        per_device = NB // 4
-        row = lax.broadcasted_iota(jnp.int32, (per_device, NB), 0)
-        col = lax.broadcasted_iota(jnp.int32, (per_device, NB), 1)
-        one = jnp.where(col == place_ref[1] * per_device + row, 1.0, 0.0)
-        o_ref[:per_device, :NB] = o_ref[:per_device, :NB] + one
+    lax.fori_loop(0, o_ref.shape[0] // chunk, row_chunk, 0)
+
+
+def block_cover_kernel(t_ref, row_cell_ref, *refs, points):
+    blocks, (o_ref, h_ref, col_cell_ref, east_ref) = refs[:-4], refs[-4:]
+    cells = [
+        column_counts(ref, h_ref, NB * i, o_ref.shape[1]) for i, ref in enumerate(blocks)
+    ]
+    col_cell_ref[...] = jnp.concatenate(cells, 1)
+    later_cover_kernel(t_ref, row_cell_ref, h_ref, col_cell_ref, o_ref, east_ref, points=points)
 
 
 def inverse_factor(tiles):
@@ -334,18 +380,16 @@
     factor_blocks(a_ref, lh_ref, ll_ref, wh_ref, wl_ref)
 
 
-def fold_block(r, k):
-    if k < 2:
-        return r ^ (4 * k)
-    m = k - 1
-    low = r & 3
-    second = (low >> (m.bit_length() - 1)) & 1
-    return (r ^ m) ^ (4 * second)
-
-
 def block_order(r):
-    order = [fold_block(r, k) for k in range(5)]
-    return order + [order[k] ^ 4 for k in (2, 3, 4)]
+    here, away, q = r & 4, (r & 4) ^ 4, r & 3
+    turns = [(q + k) & 3 for k in (1, 2, 3)]
+    return [r, r ^ 4, here | turns[0], here | turns[1], here | turns[2]] + [away | t for t in turns]
+
+
+def folded_blocks(r):
+    order = block_order(r)
+    either = jnp.where((r & 3) < 2, r, r ^ 4)
+    return [(r, r), (r, order[1]), (r, order[2]), (order[1], order[2]), (either, order[3])]
 
 
 def unfold_kernel(place_ref, *refs):
@@ -358,31 +402,24 @@
     def rows_of(r, _):
         away = r ^ row_pos
         slot = (away >> 1) | ((away & 1) << 2)
-        low = r & 3
         ats = []
         for p in range(4):
             gone = p ^ panel_pos
             ats.append(slot | ((gone >> 1) << 3) | ((gone & 1) << 4))
-        for k in range(5):
+        for k, (rows, cols) in enumerate(folded_blocks(r)):
             block = jnp.concatenate([g_ref[at, :, NB * k : NB * k + NB] for at in ats], 0)
-            if k < 2:
-                s = r ^ (4 * k)
-            else:
-                m = k - 1
-                second = (low >> (m.bit_length() - 1)) & 1
-                s = (r ^ m) ^ (4 * second)
-            rr = pl.multiple_of(r * NB, NB)
-            ss = pl.multiple_of(s * NB, NB)
-
-            @pl.when(r >= s)
+            rr = pl.multiple_of(rows * NB, NB)
+            cc = pl.multiple_of(cols * NB, NB)
+
+            @pl.when(rows >= cols)
             def _():
-                a_ref[pl.ds(rr, NB), pl.ds(ss, NB)] = block
-
-            if k >= 2:
-
-                @pl.when(r < s)
+                a_ref[pl.ds(rr, NB), pl.ds(cc, NB)] = block
+
+            if k:
+
+                @pl.when(rows < cols)
                 def _():
-                    a_ref[pl.ds(ss, NB), pl.ds(rr, NB)] = block.T
+                    a_ref[pl.ds(cc, NB), pl.ds(rr, NB)] = block.T
 
         return 0
 
@@ -408,8 +445,8 @@
     )(*operands)
 
 
-def solve_kernel(place_ref, *refs, covers, by_columns):
-    cover_refs, parts_refs = refs[:covers], refs[covers:-7]
+def solve_kernel(place_ref, *refs, corners):
+    cover_refs, parts_refs = refs[: len(corners)], refs[len(corners) : -7]
     lh_ref, ll_ref, wh_ref, wl_ref, o_ref, xh_ref, xl_ref = refs[-7:]
     n = o_ref.shape[1]
 
@@ -419,15 +456,14 @@
             taken = taken + part[rows, cols]
         o_ref[rows, cols] = value - taken
 
-    if by_columns:
-        pieces_of = [ref[:, c : c + NB] for ref in cover_refs for c in range(0, ref.shape[1], NB)]
-        for s, piece in zip(block_order(place_ref[0]), pieces_of):
-            put(slice(None), pl.ds(pl.multiple_of(s * NB, NB), NB), piece)
-    else:
-        first = 0
-        for ref in cover_refs:
-            put(pl.ds(first, ref.shape[0]), slice(None), ref[...])
-            first += ref.shape[0]
+    for (row, block), ref in zip(corners, cover_refs):
+        rows = slice(row, row + ref.shape[0])
+        if block is None:
+            put(rows, slice(None), ref[...])
+            continue
+        for c, s in enumerate(block_order(place_ref[0])[block : block + ref.shape[1] // NB]):
+            cols = pl.ds(pl.multiple_of(s * NB, NB), NB)
+            put(rows, cols, ref[:, NB * c : NB * c + NB])
     for c in range(0, n, NB):
         here = o_ref[:, c : c + NB]
         if c:
@@ -442,10 +478,10 @@
         xl_ref[:, c : c + NB] = xl
 
 
-def solve(place, covers, parts, factors, by_columns):
+def solve(place, covers, corners, parts, factors):
     rows, n = parts[0].shape
     return vmem_call(
-        functools.partial(solve_kernel, covers=len(covers), by_columns=by_columns),
+        functools.partial(solve_kernel, corners=corners),
         jax.ShapeDtypeStruct((rows, n), F32),
         place,
         [*covers, *parts, *factors],
@@ -458,22 +494,24 @@
     return pl.pallas_call(
         kernel,
         out_shape=out_shape,
-        in_specs=[pl.BlockSpec(memory_space=pltpu.SMEM)]
+        in_specs=[pl.BlockSpec(memory_space=pltpu.SMEM)] * (place is not None)
         + [pl.BlockSpec(memory_space=pltpu.VMEM)] * len(operands),
         out_specs=jax.tree.map(lambda _: pl.BlockSpec(memory_space=pltpu.VMEM), out_shape),
         scratch_shapes=list(scratch),
         compiler_params=pltpu.CompilerParams(vmem_limit_bytes=32 << 20),
         cost_estimate=pl.CostEstimate(flops=10**8, bytes_accessed=1 << 18, transcendentals=0),
         name=name,
-    )(place, *operands)
+    )(*([] if place is None else [place]), *operands)
 
 
 def fold_products_kernel(place_ref, *refs):
-    blocks, shares, total_ref = refs[:5], refs[5:-1], refs[-1]
-    own_high, own_low = split(blocks[0][:NB])
-    for k, ref in enumerate(blocks):
-        high, low = split(ref[:NB])
-        total_ref[:, NB * k : NB * k + NB] = dot3(own_high, own_low, high, low)
+    blocks, shares, total_ref = refs[:4], refs[4:-1], refs[-1]
+    own, far, one, two = [split(ref[:NB]) for ref in blocks]
+    own_last = (place_ref[0] & 3) < 2
+    either = split(jnp.where(own_last, blocks[0][:NB], blocks[1][:NB]))
+    pairs = [(own, own), (own, far), (own, one), (far, one), (either, two)]
+    for k, (left, right) in enumerate(pairs):
+        total_ref[:, NB * k : NB * k + NB] = dot3(*left, *right)
     rows = shares[0].shape[0]
     for m, ref in enumerate(shares):
         first = pl.multiple_of((place_ref[1] ^ m) * rows, rows)
@@ -555,92 +593,120 @@
         parts = jnp.sum(parts, axis=0)
         mine = covers[0][:per_device] - parts[:per_device]
         diag_rows = lax.all_gather(mine, ("row", "panel"), axis=0, tiled=True)
-        return solve(place, covers, [parts], factor(factor_kernel, (diag_rows,), B), False)
+        corners = [(i * lead, None) for i in range(len(covers))]
+        return solve(place, covers, corners, [parts], factor(factor_kernel, (diag_rows,), B))
+
+    def turn(block, k):
+        return lax.ppermute(block, "row", [((d & 4) | ((d + k) & 3), d) for d in range(8)])
 
     own = pack(own_prior, local_points)
-    far = swap(own, "row", 4)
+    far, one, two = swap(own, "row", 4), turn(own, 1), turn(own, 2)
     table = row_table(own_points, lines)
-    far, table = lax.optimization_barrier((far, table))
-
-    def beside(operands, transfer, work):
-        operands, held = lax.optimization_barrier((operands, table))
-        return lax.optimization_barrier((transfer(operands), work(operands, held)))
-
-    def group_cover(held, blocks, unit=False):
-        cols = NB * len(blocks)
-        return vmem_call(
-            functools.partial(group_cover_kernel, points=count, unit=unit),
-            jax.ShapeDtypeStruct((quarter_rows, cols), F32),
-            place,
-            [*held, *blocks],
-            [pltpu.VMEM((lines, 8 * cols), BF), pltpu.VMEM((15, 32, cols), F32)],
-            "cover",
-        )
-
-    seconds = [((row_pos >> (m.bit_length() - 1)) & 1) == 1 for m in (1, 2, 3)]
-    firsts, cover_1 = beside(
-        [jnp.where(second, own, far) for second in seconds],
-        lambda blocks: [swap(block, "row", m) for m, block in zip((1, 2, 3), blocks)],
-        lambda _, held: group_cover(held, [own, far], True),
-    )
+    (far, one, two), table = lax.optimization_barrier(((far, one, two), table))
     shares = vmem_call(
         fold_products_kernel,
         [jax.ShapeDtypeStruct((per_device, 5 * NB), F32)] * 4,
         place,
-        [own, far, *firsts],
+        [own, far, one, two],
         [pltpu.VMEM((NB, 5 * NB), F32)],
         "fold_products",
     )
-    others = [jnp.where(second, far, own) for second in seconds]
-    shares, others = lax.optimization_barrier((shares, others))
-    sums, cover_2 = beside(
+    shares, own, far = lax.optimization_barrier((shares, own, far))
+
+    def beside(operands, transfer, work):
+        operands, held = lax.optimization_barrier((operands, table))
+        return lax.optimization_barrier((transfer(operands), work(operands, held)))
+
+    half = 4 * NB
+    east = pltpu.VMEM((15, per_device, half), F32)
+
+    def lead_cover(_, held):
+        return vmem_call(
+            functools.partial(lead_cover_kernel, points=count),
+            [
+                jax.ShapeDtypeStruct((per_device, 5 * NB), F32),
+                jax.ShapeDtypeStruct((per_device, half), F32),
+                jax.ShapeDtypeStruct((lines, 8 * half), BF),
+                jax.ShapeDtypeStruct((1, half), F32),
+            ],
+            place,
+            [*held, own, far, one, two],
+            [
+                east,
+                pltpu.VMEM((2, NB, count), F32),
+                pltpu.VMEM((NB, 1), F32),
+                pltpu.VMEM((8, per_device, 2 * lines), BF),
+            ],
+            "lead_cover",
+        )
+
+    sums, (folded, cover_lead, *counts) = beside(
         shares,
         lambda shares: [swap(share, "panel", m) for m, share in zip((1, 2, 3), shares[1:])],
-        lambda _, held: group_cover(held, firsts),
-    )
-    rest = [swap(block, "row", m) for m, block in zip((1, 2, 3), others)]
-    lead_cover = jnp.concatenate([cover_1[:per_device], cover_2[:per_device]], 1)
-    shard = lead_cover - (shares[0] + sums[0] + sums[1] + sums[2])
-
-    along, cover_3 = beside(
-        shard[None],
-        lambda x: [swap(x, "row", bit) for bit in (2, 4, 6)],
-        lambda _, held: group_cover(held, rest),
-    )
-    held_rows = jnp.concatenate([shard[None]] + along, 0)
-
-    def across(x):
-        corner = [(i, i ^ 6) for i in range(32)]
-        return swap(x, "row", 1), swap(x, "panel", 2), lax.ppermute(x, ("row", "panel"), corner)
-
-    def rest_parts(x, _):
-        x, blocks = lax.optimization_barrier((x, [own, far, *firsts, *rest]))
+        lead_cover,
+    )
+    rest = [turn(own, 3), turn(far, 1), turn(far, 2), turn(far, 3)]
+    shard = folded - (shares[0] + sums[0] + sums[1] + sums[2])
+
+    def rest_part(panel_prior, m, plus=()):
+        return vmem_call(
+            functools.partial(rest_products_kernel, m=m),
+            jax.ShapeDtypeStruct((quarter_rows, B), F32),
+            place,
+            [prior_factor, *panel_prior, *plus],
+            name="rest_products",
+        )
+
+    def beside_z(_, held):
+        cover = vmem_call(
+            functools.partial(later_cover_kernel, points=count),
+            jax.ShapeDtypeStruct((quarter_rows - per_device, half), F32),
+            None,
+            [*held, *counts],
+            [east],
+            "cover",
+        )
+        cover, blocks = lax.optimization_barrier((cover, rest))
         panel_prior = vmem_call(
             gather_split_kernel,
             [jax.ShapeDtypeStruct((B, own_prior.shape[1]), BF)] * 2,
             place,
-            blocks,
+            [own, far, one, two, *blocks],
             name="gather_split",
         )
-
-        def part(m, plus=()):
-            return vmem_call(
-                functools.partial(rest_products_kernel, m=m),
-                jax.ShapeDtypeStruct((quarter_rows, B), F32),
-                place,
-                [prior_factor, *panel_prior, *plus],
-                name="rest_products",
-            )
-
-        from_3 = swap(part(3), "panel", 1)
-        from_1 = swap(part(1), "panel", 1)
-        return part(0), part(2, [from_3]), from_1, swap(x, "panel", 1)
-
-    received, (part_0, part_2, from_1, held_there) = beside(held_rows, across, rest_parts)
+        return cover, panel_prior, rest_part(panel_prior, 3), rest_part(panel_prior, 1)
+
+    along, (cover_first, panel_prior, part_3, part_1) = beside(
+        shard[None], lambda x: [swap(x, "row", bit) for bit in (2, 4, 6)], beside_z
+    )
+    held_rows = jnp.concatenate([shard[None]] + along, 0)
+
+    def across(x):
+        corner = [(i, i ^ 6) for i in range(32)]
+        return swap(x, "row", 1), swap(x, "panel", 2), lax.ppermute(x, ("row", "panel"), corner)
+
+    def beside_xy(x, held):
+        from_3 = swap(part_3, "panel", 1)
+        cover = vmem_call(
+            functools.partial(block_cover_kernel, points=count),
+            jax.ShapeDtypeStruct((quarter_rows, half), F32),
+            None,
+            [*held, *rest],
+            [pltpu.VMEM((lines, 8 * half), BF), pltpu.VMEM((1, half), F32), east],
+            "cover",
+        )
+        part_0, part_2 = rest_part(panel_prior, 0), rest_part(panel_prior, 2, [from_3])
+        return cover, part_0, part_2, swap(x, "panel", 1)
+
+    received, (cover_last, part_0, part_2, held_there) = beside(
+        held_rows, across, beside_xy
+    )
     there = [held_there] + [swap(x, "panel", 1) for x in received]
-    parts = [part_0, from_1, swap(part_2, "panel", 2)]
+    part_1, part_2 = lax.optimization_barrier((part_1, part_2))
+    parts = [part_0, swap(part_1, "panel", 1), swap(part_2, "panel", 2)]
     factors = factor(unfold_kernel, (place, held_rows, *received, *there), B)
-    return solve(place, [cover_1, cover_2, cover_3], parts, factors, True)
+    corners = [(0, 0), (per_device, 0), (0, 4)]
+    return solve(place, [cover_lead, cover_first, cover_last], corners, parts, factors)
 
 
 def solution(mesh):

time: 137 us -> 123 us (0.90)
  waiting for transfers between devices: 31.3 us -> 14.2 us
  starting transfers between devices: 24.2 us -> 28.7 us
    ppermute x22 -> x16, waiting for transfers between devices: 26.4 us -> 5.37 us  [swap(): lax.ppermute(block, axis, [(i, i ^ bit) for i in range(lax.axis_size(axis...]
    ppermute x0 -> x6, starting transfers between devices: none -> 11 us  [turn(): lax.ppermute(block, 'row', [(d & 4 | d + k & 3, d) for d in range(8)])]
    ppermute x0 -> x6, waiting for transfers between devices: none -> 8.83 us  [turn(): lax.ppermute(block, 'row', [(d & 4 | d + k & 3, d) for d in range(8)])]
    ppermute x22 -> x16, starting transfers between devices: 22.8 us -> 17.1 us  [swap(): lax.ppermute(block, axis, [(i, i ^ bit) for i in range(lax.axis_size(axis...]
    ppermute x1, waiting for transfers between devices: 4.86 us -> 0.01 us  [across(): lax.ppermute(x, ('row', 'panel'), corner)]
  transfers between devices with their start and end apart: 23 -> 23, of which waited for: 9 -> 5; matrix products, arithmetic and copies ran while one was open for 0% -> 0% of each run, Pallas kernels for 49% -> 56%
where the time goes in v7:
time: 123 us
  Pallas kernels  75.9 us (62%)
  starting transfers between devices  28.7 us (23%)
  waiting for transfers between devices  14.2 us (12%)
  local copies, waits for them, and re-layouts  1.82 us (1%)
  other arithmetic  1.77 us (1%)
    pallas_call x10, Pallas kernels, vmem_call(): pl.pallas_call(kernel, out_shape=out_shape, in_specs=[pl.BlockSpec(memory...  38.6 us
    pallas_call x1, Pallas kernels, factor(): pl.pallas_call(kernel, out_shape=[jax.ShapeDtypeStruct((n, n), BF)] * 2 +...  32.5 us
    ppermute x16, starting transfers between devices, swap(): lax.ppermute(block, axis, [(i, i ^ bit) for i in range(lax.axis_size(axis...  17.1 us
    ppermute x6, starting transfers between devices, turn(): lax.ppermute(block, 'row', [(d & 4 | d + k & 3, d) for d in range(8)])  11 us
    ppermute x6, waiting for transfers between devices, turn(): lax.ppermute(block, 'row', [(d & 4 | d + k & 3, d) for d in range(8)])  8.83 us
    ppermute x16, waiting for transfers between devices, swap(): lax.ppermute(block, axis, [(i, i ^ bit) for i in range(lax.axis_size(axis...  5.37 us
    pallas_call x1, Pallas kernels, row_table(): pl.pallas_call(row_table_kernel, out_shape=[jax.ShapeDtypeStruct((8, rows...  4.85 us
  transfers between devices with their start and end apart: 23, of which 5 were waited for; matrix products, arithmetic and copies ran while one was open for 0% of the time, Pallas kernels for 56%

profile of v7, /device:TPU:0, one launch (start us, length us, event | category | flops | bytes accessed | tf_op | source)
XLA Modules:
  0.0 122.7 jit_solution(16505656008484882387)
XLA Ops:
  0.0 0.7 fusion.1
  0.7 0.9 convert_add_fusion.1
  1.8 1.0 slice.16
  2.8 3.1 %collective-permute-start.2 = (f32[136,512]{1,0:T(8,128)S(1)}, f32[136,512]{1,0:T(8,128)S(1)}, u32[]{:S(2)}, u32[]{:S(2)}) collective-permute-start(f32[136,512]{1,0:T(8,128)S(1)} %pad_maximum_fusion.1.refs_0_), channel_id=1, source_target_pairs={{8,0},{12,4},{0,8},{4,12},{24,16},{28,20},{16,24},{20,28},{9,1},{1... | collective-permute-start | bytes 835592 | tf_op jit(solution)/shard_map/ppermute | solution.py:600
  5.9 1.4 %collective-permute-start.1 = (f32[136,512]{1,0:T(8,128)S(1)}, f32[136,512]{1,0:T(8,128)S(1)}, u32[]{:S(2)}, u32[]{:S(2)}) collective-permute-start(f32[136,512]{1,0:T(8,128)S(1)} %pad_maximum_fusion.1.refs_0_), channel_id=1, source_target_pairs={{4,0},{8,4},{12,8},{0,12},{20,16},{24,20},{28,24},{16,28},{5,1},{9... | collective-permute-start | bytes 835592 | tf_op jit(solution)/shard_map/ppermute | solution.py:600
  7.3 2.6 %collective-permute-start = (f32[136,512]{1,0:T(8,128)S(1)}, f32[136,512]{1,0:T(8,128)S(1)}, u32[]{:S(2)}, u32[]{:S(2)}) collective-permute-start(f32[136,512]{1,0:T(8,128)S(1)} %pad_maximum_fusion.1.refs_0_), channel_id=1, source_target_pairs={{0,16},{4,20},{8,24},{12,28},{16,0},{20,4},{24,8},{28,12},{1,17},{... | collective-permute-start | bytes 835592 | tf_op jit(solution)/shard_map/ppermute | solution.py:544
  9.9 4.8 %row_table.1 = (bf16[8,256,512]{2,1,0:T(8,128)(2,1)S(1)}, f32[256,1]{1,0:T(8,128)S(1)}) custom-call(f32[2,16,256]{2,1,0:T(8,128)S(1)} %fusion.row_ref), custom_call_target="tpu_custom_call" | custom-call | flops 100000000 | bytes 262144 | tf_op jit(solution)/shard_map/row_table/pallas_call | solution.py:147
  14.8 4.6 %collective-permute-done.2.refs_3_ = f32[136,512]{1,0:T(8,128)S(1)} collective-permute-done((f32[136,512]{1,0:T(8,128)S(1)}, f32[136,512]{1,0:T(8,128)S(1)}, u32[]{:S(2)}, u32[]{:S(2)}) %collective-permute-start.2) | collective-permute-done | bytes 278560 | tf_op jit(solution)/shard_map/ppermute | solution.py:600
  19.3 4.4 %collective-permute-done.refs_1_ = f32[136,512]{1,0:T(8,128)S(1)} collective-permute-done((f32[136,512]{1,0:T(8,128)S(1)}, f32[136,512]{1,0:T(8,128)S(1)}, u32[]{:S(2)}, u32[]{:S(2)}) %collective-permute-start) | collective-permute-done | bytes 278560 | tf_op jit(solution)/shard_map/ppermute | solution.py:544
  23.7 1.2 %fold_products.1 = (f32[32,640]{1,0:T(8,128)S(1)}, f32[32,640]{1,0:T(8,128)S(1)}, f32[32,640]{1,0:T(8,128)S(1)}, f32[32,640]{1,0:T(8,128)S(1)}) custom-call(s32[2]{0:T(128)S(1)} %pad_add_fusion.place_ref, f32[136,512]{1,0:T(8,128)S(1)} %pad_maximum_fusion.1.refs_0_, f32[136,512]{1,0:T(8,128)S(1)} %collective-permute-done.refs_1_, ...), custom_call_target="tpu_custom_call" | custom-call | flops 100000000 | bytes 262144 | tf_op jit(solution)/shard_map/fold_products/pallas_call | solution.py:494
  25.1 1.6 %collective-permute-start.4 = (f32[32,640]{1,0:T(8,128)S(1)}, f32[32,640]{1,0:T(8,128)S(1)}, u32[]{:S(2)}, u32[]{:S(2)}) collective-permute-start(f32[32,640]{1,0:T(8,128)S(1)} %get-tuple-element.88), channel_id=1, source_target_pairs={{0,2},{1,3},{2,0},{3,1},{4,6},{5,7},{6,4},{7,5},{8,10},{9,11},{10,... | collective-permute-start | bytes 245768 | tf_op jit(solution)/shard_map/ppermute | solution.py:544
  26.9 2.2 %collective-permute-start.9 = (f32[136,512]{1,0:T(8,128)S(1)}, f32[136,512]{1,0:T(8,128)S(1)}, u32[]{:S(2)}, u32[]{:S(2)}) collective-permute-start(f32[136,512]{1,0:T(8,128)S(1)} %pad_maximum_fusion.1.refs_0_), channel_id=1, source_target_pairs={{12,0},{0,4},{4,8},{8,12},{28,16},{16,20},{20,24},{24,28},{13,1},{... | collective-permute-start | bytes 835592 | tf_op jit(solution)/shard_map/ppermute | solution.py:600
  29.1 2.8 %collective-permute-start.12 = (f32[136,512]{1,0:T(8,128)S(1)}, f32[136,512]{1,0:T(8,128)S(1)}, u32[]{:S(2)}, u32[]{:S(2)}) collective-permute-start(f32[136,512]{1,0:T(8,128)S(1)} %collective-permute-done.refs_1_), channel_id=1, source_target_pairs={{12,0},{0,4},{4,8},{8,12},{28,16},{16,20},{20,24},{24,28},{13,1},{... | collective-permute-start | bytes 835592 | tf_op jit(solution)/shard_map/ppermute | solution.py:600
  31.9 3.4 %lead_cover.1 = (f32[32,640]{1,0:T(8,128)S(1)}, f32[32,512]{1,0:T(8,128)S(1)}, bf16[256,4096]{1,0:T(8,128)(2,1)S(1)}, f32[1,512]{1,0:T(1,128)S(1)}) custom-call(s32[2]{0:T(128)S(1)} %pad_add_fusion.place_ref, bf16[8,256,512]{2,1,0:T(8,128)(2,1)S(1)} %get-tuple-element.120.t_ref, f32[256,1]{1,0:T(8,128)S(1)} %get-tuple-element.121.row_cell_ref, ...), custom_call_target="tpu_custom_call" | custom-call | flops 100000000 | bytes 262144 | tf_op jit(solution)/shard_map/lead_cover/pallas_call | solution.py:494
  35.4 1.5 %collective-permute-start.10 = (f32[136,512]{1,0:T(8,128)S(1)}, f32[136,512]{1,0:T(8,128)S(1)}, u32[]{:S(2)}, u32[]{:S(2)}) collective-permute-start(f32[136,512]{1,0:T(8,128)S(1)} %collective-permute-done.refs_1_), channel_id=1, source_target_pairs={{4,0},{8,4},{12,8},{0,12},{20,16},{24,20},{28,24},{16,28},{5,1},{9... | collective-permute-start | bytes 835592 | tf_op jit(solution)/shard_map/ppermute | solution.py:600
  36.9 2.8 %collective-permute-start.8 = (f32[1,32,640]{2,1,0:T(8,128)S(1)}, f32[1,32,640]{2,1,0:T(8,128)S(1)}, u32[]{:S(2)}, u32[]{:S(2)}) collective-permute-start(f32[1,32,640]{2,1,0:T(8,128)S(1)} %subtract_bitcast_fusion), channel_id=1, source_target_pairs={{0,24},{4,28},{8,16},{12,20},{16,8},{20,12},{24,0},{28,4},{1,25},{... | collective-permute-start | bytes 245768 | tf_op jit(solution)/shard_map/ppermute | solution.py:544
  39.7 1.1 collective-permute-start.7
  40.8 4.3 %collective-permute-done.12.refs_7_.refs_3_ = f32[136,512]{1,0:T(8,128)S(1)} collective-permute-done((f32[136,512]{1,0:T(8,128)S(1)}, f32[136,512]{1,0:T(8,128)S(1)}, u32[]{:S(2)}, u32[]{:S(2)}) %collective-permute-start.12) | collective-permute-done | bytes 278560 | tf_op jit(solution)/shard_map/ppermute | solution.py:600
  45.1 1.8 %collective-permute-start.6 = (f32[1,32,640]{2,1,0:T(8,128)S(1)}, f32[1,32,640]{2,1,0:T(8,128)S(1)}, u32[]{:S(2)}, u32[]{:S(2)}) collective-permute-start(f32[1,32,640]{2,1,0:T(8,128)S(1)} %subtract_bitcast_fusion), channel_id=1, source_target_pairs={{0,8},{4,12},{8,0},{12,4},{16,24},{20,28},{24,16},{28,20},{1,9},{5... | collective-permute-start | bytes 245768 | tf_op jit(solution)/shard_map/ppermute | solution.py:544
  46.8 9.3 %cover.2.refs_1_ = f32[224,512]{1,0:T(8,128)S(1)} custom-call(bf16[8,256,512]{2,1,0:T(8,128)(2,1)S(1)} %get-tuple-element.120.t_ref, f32[256,1]{1,0:T(8,128)S(1)} %get-tuple-element.121.row_cell_ref, bf16[256,4096]{1,0:T(8,128)(2,1)S(1)} %get-tuple-element.106.h_ref, f32[1,512]{1,0:T(1,128)S(1)} %get-tuple-element.107.col_cell_ref), custom_call_target="tpu_custom_call" | custom-call | flops 100000000 | bytes 262144 | tf_op jit(solution)/shard_map/cover/pallas_call | solution.py:494
  56.2 0.9 gather_split.1
  57.0 0.7 copy-done
  57.7 1.6 %rest_products.5 = f32[256,1024]{1,0:T(8,128)S(1)} custom-call(s32[2]{0:T(128)S(1)} %pad_add_fusion.place_ref, f32[1024,512]{1,0:T(8,128)S(1)} %copy-done, bf16[1024,512]{1,0:T(8,128)(2,1)S(1)} %get-tuple-element.122.high_ref, bf16[1024,512]{1,0:T(8,128)(2,1)S(1)} %get-tuple-element.123.low_ref), custom_call_target="tpu_custom_call" | custom-call | flops 100000000 | bytes 262144 | tf_op jit(solution)/shard_map/rest_products/pallas_call | solution.py:494
  59.3 1.6 %rest_products.4 = f32[256,1024]{1,0:T(8,128)S(1)} custom-call(s32[2]{0:T(128)S(1)} %pad_add_fusion.place_ref, f32[1024,512]{1,0:T(8,128)S(1)} %copy-done, bf16[1024,512]{1,0:T(8,128)(2,1)S(1)} %get-tuple-element.122.high_ref, bf16[1024,512]{1,0:T(8,128)(2,1)S(1)} %get-tuple-element.123.low_ref), custom_call_target="tpu_custom_call" | custom-call | flops 100000000 | bytes 262144 | tf_op jit(solution)/shard_map/rest_products/pallas_call | solution.py:494
  61.6 0.6 collective-permute-start.15
  62.2 4.6 %collective-permute-start.14 = (f32[4,32,640]{2,1,0:T(8,128)S(1)}, f32[4,32,640]{2,1,0:T(8,128)S(1)}, u32[]{:S(2)}, u32[]{:S(2)}) collective-permute-start(f32[4,32,640]{2,1,0:T(8,128)S(1)} %pad_maximum_fusion.refs_0_), channel_id=1, source_target_pairs={{0,2},{1,3},{2,0},{3,1},{4,6},{5,7},{6,4},{7,5},{8,10},{9,11},{10,... | collective-permute-start | bytes 983048 | tf_op jit(solution)/shard_map/ppermute | solution.py:544
  66.9 1.6 %rest_products.6.refs_3_ = f32[256,1024]{1,0:T(8,128)S(1)} custom-call(s32[2]{0:T(128)S(1)} %pad_add_fusion.place_ref, f32[1024,512]{1,0:T(8,128)S(1)} %copy-done, bf16[1024,512]{1,0:T(8,128)(2,1)S(1)} %get-tuple-element.122.high_ref, bf16[1024,512]{1,0:T(8,128)(2,1)S(1)} %get-tuple-element.123.low_ref), custom_call_target="tpu_custom_call" | custom-call | flops 100000000 | bytes 262144 | tf_op jit(solution)/shard_map/rest_products/pallas_call | solution.py:494
  68.4 11.2 %cover.3.refs_2_ = f32[256,512]{1,0:T(8,128)S(1)} custom-call(bf16[8,256,512]{2,1,0:T(8,128)(2,1)S(1)} %get-tuple-element.120.t_ref, f32[256,1]{1,0:T(8,128)S(1)} %get-tuple-element.121.row_cell_ref, f32[136,512]{1,0:T(8,128)S(1)} %collective-permute-done.9.refs_4_.refs_0_, f32[136,512]{1,0:T(8,128)S(1)} %collective-permute-done.10.refs_5_.refs_1_, ...), custom_call_target="tpu_custom_call" | custom-call | flops 100000000 | bytes 262144 | tf_op jit(solution)/shard_map/cover/pallas_call | solution.py:494
  79.7 1.6 %rest_products.7 = f32[256,1024]{1,0:T(8,128)S(1)} custom-call(s32[2]{0:T(128)S(1)} %pad_add_fusion.place_ref, f32[1024,512]{1,0:T(8,128)S(1)} %copy-done, bf16[1024,512]{1,0:T(8,128)(2,1)S(1)} %get-tuple-element.122.high_ref, bf16[1024,512]{1,0:T(8,128)(2,1)S(1)} %get-tuple-element.123.low_ref, f32[256,1024]{1,0:T(8,128)S(1)} %collective-permute-done.16.refs_0_), custom_call_target="tpu_custom_call" | custom-call | flops 100000000 | bytes 262144 | tf_op jit(solution)/shard_map/rest_products/pallas_call | solution.py:494
  82.4 0.6 collective-permute-start.19
  83.9 32.5 %factor.1 = (bf16[1024,1024]{1,0:T(8,128)(2,1)S(1)}, bf16[1024,1024]{1,0:T(8,128)(2,1)S(1)}, bf16[1024,128]{1,0:T(8,128)(2,1)S(1)}, bf16[1024,128]{1,0:T(8,128)(2,1)S(1)}) custom-call(s32[2]{0:T(128)S(1)} %pad_add_fusion.place_ref, f32[4,32,640]{2,1,0:T(8,128)S(1)} %pad_maximum_fusion.refs_0_, f32[4,32,640]{2,1,0:T(8,128)S(1)} %collective-permute-done.13.refs_1_, ...), custom_call_target="tpu_custom_call" | custom-call | flops 49999998976 | bytes 8388608 | tf_op jit(solution)/shard_map/factor/pallas_call | solution.py:436
  116.5 6.3 %solve.1 = f32[256,1024]{1,0:T(8,128)} custom-call(s32[2]{0:T(128)S(1)} %pad_add_fusion.place_ref, f32[32,512]{1,0:T(8,128)S(1)} %get-tuple-element.98.refs_0_, f32[224,512]{1,0:T(8,128)S(1)} %cover.2.refs_1_, f32[256,512]{1,0:T(8,128)S(1)} %cover.3.refs_2_, f32[256,1024]{1,0:T(8,128)S(1)} %rest_products.6.refs_3_, ...), custom_call_target="tpu_custom_call" | custom-call | flops 100000000 | bytes 262144 | tf_op jit(solution)/shard_map/solve/pallas_call | solution.py:494
  (40 shorter events, 3.5 us)
Async XLA Ops:
  2.8 16.5 %collective-permute-start.2 = (f32[136,512]{1,0:T(8,128)S(1)}, f32[136,512]{1,0:T(8,128)S(1)}, u32[]{:S(2)}, u32[]{:S(2)}) collective-permute-start(f32[136,512]{1,0:T(8,128)S(1)} %pad_maximum_fusion.1.refs_0_), channel_id=1, source_target_pairs={{8,0},{12,4},{0,8},{4,12},{24,16},{28,20},{16,24},{20,28},{9,1},{1... | collective-permute-start | bytes 835592 | tf_op jit(solution)/shard_map/ppermute | solution.py:600
  5.9 13.5 %collective-permute-start.1 = (f32[136,512]{1,0:T(8,128)S(1)}, f32[136,512]{1,0:T(8,128)S(1)}, u32[]{:S(2)}, u32[]{:S(2)}) collective-permute-start(f32[136,512]{1,0:T(8,128)S(1)} %pad_maximum_fusion.1.refs_0_), channel_id=1, source_target_pairs={{4,0},{8,4},{12,8},{0,12},{20,16},{24,20},{28,24},{16,28},{5,1},{9... | collective-permute-start | bytes 835592 | tf_op jit(solution)/shard_map/ppermute | solution.py:600
  7.3 16.5 %collective-permute-start = (f32[136,512]{1,0:T(8,128)S(1)}, f32[136,512]{1,0:T(8,128)S(1)}, u32[]{:S(2)}, u32[]{:S(2)}) collective-permute-start(f32[136,512]{1,0:T(8,128)S(1)} %pad_maximum_fusion.1.refs_0_), channel_id=1, source_target_pairs={{0,16},{4,20},{8,24},{12,28},{16,0},{20,4},{24,8},{28,12},{1,17},{... | collective-permute-start | bytes 835592 | tf_op jit(solution)/shard_map/ppermute | solution.py:544
  25.0 10.3 %collective-permute-start.3 = (f32[32,640]{1,0:T(8,128)S(1)}, f32[32,640]{1,0:T(8,128)S(1)}, u32[]{:S(2)}, u32[]{:S(2)}) collective-permute-start(f32[32,640]{1,0:T(8,128)S(1)} %get-tuple-element.87), channel_id=1, source_target_pairs={{0,1},{1,0},{2,3},{3,2},{4,5},{5,4},{6,7},{7,6},{8,9},{9,8},{10,11... | collective-permute-start | bytes 245768 | tf_op jit(solution)/shard_map/ppermute | solution.py:544
  25.1 10.4 %collective-permute-start.4 = (f32[32,640]{1,0:T(8,128)S(1)}, f32[32,640]{1,0:T(8,128)S(1)}, u32[]{:S(2)}, u32[]{:S(2)}) collective-permute-start(f32[32,640]{1,0:T(8,128)S(1)} %get-tuple-element.88), channel_id=1, source_target_pairs={{0,2},{1,3},{2,0},{3,1},{4,6},{5,7},{6,4},{7,5},{8,10},{9,11},{10,... | collective-permute-start | bytes 245768 | tf_op jit(solution)/shard_map/ppermute | solution.py:544
  26.6 10.2 %collective-permute-start.5 = (f32[32,640]{1,0:T(8,128)S(1)}, f32[32,640]{1,0:T(8,128)S(1)}, u32[]{:S(2)}, u32[]{:S(2)}) collective-permute-start(f32[32,640]{1,0:T(8,128)S(1)} %get-tuple-element.89), channel_id=1, source_target_pairs={{0,3},{1,2},{2,1},{3,0},{4,7},{5,6},{6,5},{7,4},{8,11},{9,10},{10,... | collective-permute-start | bytes 245768 | tf_op jit(solution)/shard_map/ppermute | solution.py:544
  26.9 12.8 %collective-permute-start.9 = (f32[136,512]{1,0:T(8,128)S(1)}, f32[136,512]{1,0:T(8,128)S(1)}, u32[]{:S(2)}, u32[]{:S(2)}) collective-permute-start(f32[136,512]{1,0:T(8,128)S(1)} %pad_maximum_fusion.1.refs_0_), channel_id=1, source_target_pairs={{12,0},{0,4},{4,8},{8,12},{28,16},{16,20},{20,24},{24,28},{13,1},{... | collective-permute-start | bytes 835592 | tf_op jit(solution)/shard_map/ppermute | solution.py:600
  29.1 15.9 %collective-permute-start.12 = (f32[136,512]{1,0:T(8,128)S(1)}, f32[136,512]{1,0:T(8,128)S(1)}, u32[]{:S(2)}, u32[]{:S(2)}) collective-permute-start(f32[136,512]{1,0:T(8,128)S(1)} %collective-permute-done.refs_1_), channel_id=1, source_target_pairs={{12,0},{0,4},{4,8},{8,12},{28,16},{16,20},{20,24},{24,28},{13,1},{... | collective-permute-start | bytes 835592 | tf_op jit(solution)/shard_map/ppermute | solution.py:600
  35.3 20.8 %collective-permute-start.11 = (f32[136,512]{1,0:T(8,128)S(1)}, f32[136,512]{1,0:T(8,128)S(1)}, u32[]{:S(2)}, u32[]{:S(2)}) collective-permute-start(f32[136,512]{1,0:T(8,128)S(1)} %collective-permute-done.refs_1_), channel_id=1, source_target_pairs={{8,0},{12,4},{0,8},{4,12},{24,16},{28,20},{16,24},{20,28},{9,1},{1... | collective-permute-start | bytes 835592 | tf_op jit(solution)/shard_map/ppermute | solution.py:600
  35.4 20.7 %collective-permute-start.10 = (f32[136,512]{1,0:T(8,128)S(1)}, f32[136,512]{1,0:T(8,128)S(1)}, u32[]{:S(2)}, u32[]{:S(2)}) collective-permute-start(f32[136,512]{1,0:T(8,128)S(1)} %collective-permute-done.refs_1_), channel_id=1, source_target_pairs={{4,0},{8,4},{12,8},{0,12},{20,16},{24,20},{28,24},{16,28},{5,1},{9... | collective-permute-start | bytes 835592 | tf_op jit(solution)/shard_map/ppermute | solution.py:600
  36.9 23.9 %collective-permute-start.8 = (f32[1,32,640]{2,1,0:T(8,128)S(1)}, f32[1,32,640]{2,1,0:T(8,128)S(1)}, u32[]{:S(2)}, u32[]{:S(2)}) collective-permute-start(f32[1,32,640]{2,1,0:T(8,128)S(1)} %subtract_bitcast_fusion), channel_id=1, source_target_pairs={{0,24},{4,28},{8,16},{12,20},{16,8},{20,12},{24,0},{28,4},{1,25},{... | collective-permute-start | bytes 245768 | tf_op jit(solution)/shard_map/ppermute | solution.py:544
  39.7 21.2 %collective-permute-start.7 = (f32[1,32,640]{2,1,0:T(8,128)S(1)}, f32[1,32,640]{2,1,0:T(8,128)S(1)}, u32[]{:S(2)}, u32[]{:S(2)}) collective-permute-start(f32[1,32,640]{2,1,0:T(8,128)S(1)} %subtract_bitcast_fusion), channel_id=1, source_target_pairs={{0,16},{4,20},{8,24},{12,28},{16,0},{20,4},{24,8},{28,12},{1,17},{... | collective-permute-start | bytes 245768 | tf_op jit(solution)/shard_map/ppermute | solution.py:544
  45.1 15.8 %collective-permute-start.6 = (f32[1,32,640]{2,1,0:T(8,128)S(1)}, f32[1,32,640]{2,1,0:T(8,128)S(1)}, u32[]{:S(2)}, u32[]{:S(2)}) collective-permute-start(f32[1,32,640]{2,1,0:T(8,128)S(1)} %subtract_bitcast_fusion), channel_id=1, source_target_pairs={{0,8},{4,12},{8,0},{12,4},{16,24},{20,28},{24,16},{28,20},{1,9},{5... | collective-permute-start | bytes 245768 | tf_op jit(solution)/shard_map/ppermute | solution.py:544
  56.1 1.6 %copy-start = (f32[1024,512]{1,0:T(8,128)S(1)}, f32[1024,512]{1,0:T(8,128)}, u32[]{:S(2)}) copy-start(f32[1024,512]{1,0:T(8,128)} %prior_ref.7) | copy-start | bytes 6291460
  60.9 18.8 %collective-permute-start.16 = (f32[256,1024]{1,0:T(8,128)S(1)}, f32[256,1024]{1,0:T(8,128)S(1)}, u32[]{:S(2)}, u32[]{:S(2)}) collective-permute-start(f32[256,1024]{1,0:T(8,128)S(1)} %rest_products.4), channel_id=1, source_target_pairs={{0,1},{1,0},{2,3},{3,2},{4,5},{5,4},{6,7},{7,6},{8,9},{9,8},{10,11... | collective-permute-start | bytes 3145736 | tf_op jit(solution)/shard_map/ppermute | solution.py:544
  61.0 20.3 %collective-permute-start.17 = (f32[4,32,640]{2,1,0:T(8,128)S(1)}, f32[4,32,640]{2,1,0:T(8,128)S(1)}, u32[]{:S(2)}, u32[]{:S(2)}) collective-permute-start(f32[4,32,640]{2,1,0:T(8,128)S(1)} %pad_maximum_fusion.refs_0_), channel_id=1, source_target_pairs={{0,1},{1,0},{2,3},{3,2},{4,5},{5,4},{6,7},{7,6},{8,9},{9,8},{10,11... | collective-permute-start | bytes 983048 | tf_op jit(solution)/shard_map/ppermute | solution.py:544
  61.6 19.7 %collective-permute-start.15 = (f32[4,32,640]{2,1,0:T(8,128)S(1)}, f32[4,32,640]{2,1,0:T(8,128)S(1)}, u32[]{:S(2)}, u32[]{:S(2)}) collective-permute-start(f32[4,32,640]{2,1,0:T(8,128)S(1)} %pad_maximum_fusion.refs_0_), channel_id=1, source_target_pairs={{0,6},{1,7},{2,4},{3,5},{4,2},{5,3},{6,0},{7,1},{8,14},{9,15},{10,... | collective-permute-start | bytes 983048 | tf_op jit(solution)/shard_map/ppermute | solution.py:686
  62.2 19.1 %collective-permute-start.14 = (f32[4,32,640]{2,1,0:T(8,128)S(1)}, f32[4,32,640]{2,1,0:T(8,128)S(1)}, u32[]{:S(2)}, u32[]{:S(2)}) collective-permute-start(f32[4,32,640]{2,1,0:T(8,128)S(1)} %pad_maximum_fusion.refs_0_), channel_id=1, source_target_pairs={{0,2},{1,3},{2,0},{3,1},{4,6},{5,7},{6,4},{7,5},{8,10},{9,11},{10,... | collective-permute-start | bytes 983048 | tf_op jit(solution)/shard_map/ppermute | solution.py:544
  66.8 14.5 %collective-permute-start.13 = (f32[4,32,640]{2,1,0:T(8,128)S(1)}, f32[4,32,640]{2,1,0:T(8,128)S(1)}, u32[]{:S(2)}, u32[]{:S(2)}) collective-permute-start(f32[4,32,640]{2,1,0:T(8,128)S(1)} %pad_maximum_fusion.refs_0_), channel_id=1, source_target_pairs={{0,4},{4,0},{8,12},{12,8},{16,20},{20,16},{24,28},{28,24},{1,5},{5... | collective-permute-start | bytes 983048 | tf_op jit(solution)/shard_map/ppermute | solution.py:544
  81.3 1.7 %collective-permute-start.20 = (f32[4,32,640]{2,1,0:T(8,128)S(1)}, f32[4,32,640]{2,1,0:T(8,128)S(1)}, u32[]{:S(2)}, u32[]{:S(2)}) collective-permute-start(f32[4,32,640]{2,1,0:T(8,128)S(1)} %collective-permute-done.13.refs_1_), channel_id=1, source_target_pairs={{0,1},{1,0},{2,3},{3,2},{4,5},{5,4},{6,7},{7,6},{8,9},{9,8},{10,11... | collective-permute-start | bytes 983048 | tf_op jit(solution)/shard_map/ppermute | solution.py:544
  81.4 2.1 %collective-permute-start.21 = (f32[4,32,640]{2,1,0:T(8,128)S(1)}, f32[4,32,640]{2,1,0:T(8,128)S(1)}, u32[]{:S(2)}, u32[]{:S(2)}) collective-permute-start(f32[4,32,640]{2,1,0:T(8,128)S(1)} %collective-permute-done.14.refs_2_), channel_id=1, source_target_pairs={{0,1},{1,0},{2,3},{3,2},{4,5},{5,4},{6,7},{7,6},{8,9},{9,8},{10,11... | collective-permute-start | bytes 983048 | tf_op jit(solution)/shard_map/ppermute | solution.py:544
  81.9 2.1 %collective-permute-start.22 = (f32[4,32,640]{2,1,0:T(8,128)S(1)}, f32[4,32,640]{2,1,0:T(8,128)S(1)}, u32[]{:S(2)}, u32[]{:S(2)}) collective-permute-start(f32[4,32,640]{2,1,0:T(8,128)S(1)} %collective-permute-done.15.refs_3_), channel_id=1, source_target_pairs={{0,1},{1,0},{2,3},{3,2},{4,5},{5,4},{6,7},{7,6},{8,9},{9,8},{10,11... | collective-permute-start | bytes 983048 | tf_op jit(solution)/shard_map/ppermute | solution.py:544
  82.0 34.5 %collective-permute-start.18 = (f32[256,1024]{1,0:T(8,128)S(1)}, f32[256,1024]{1,0:T(8,128)S(1)}, u32[]{:S(2)}, u32[]{:S(2)}) collective-permute-start(f32[256,1024]{1,0:T(8,128)S(1)} %rest_products.5), channel_id=1, source_target_pairs={{0,1},{1,0},{2,3},{3,2},{4,5},{5,4},{6,7},{7,6},{8,9},{9,8},{10,11... | collective-permute-start | bytes 3145736 | tf_op jit(solution)/shard_map/ppermute | solution.py:544
  82.4 34.1 %collective-permute-start.19 = (f32[256,1024]{1,0:T(8,128)S(1)}, f32[256,1024]{1,0:T(8,128)S(1)}, u32[]{:S(2)}, u32[]{:S(2)}) collective-permute-start(f32[256,1024]{1,0:T(8,128)S(1)} %rest_products.7), channel_id=1, source_target_pairs={{0,2},{1,3},{2,0},{3,1},{4,6},{5,7},{6,4},{7,5},{8,10},{9,11},{10,... | collective-permute-start | bytes 3145736 | tf_op jit(solution)/shard_map/ppermute | solution.py:544

commit v8 on v7

--- a/solution.py
+++ b/solution.py
@@ -248,7 +248,7 @@
     )
     folded_ref[:, : 3 * NB] = mine[:, : 3 * NB]
     folded_ref[:, 3 * NB : 4 * NB] = far[:, 2 * NB : 3 * NB]
-    own_last = (place_ref[0] & 3) < 2
+    own_last = makes_own(place_ref[0])
     folded_ref[:, 4 * NB :] = jnp.where(own_last, mine[:, 3 * NB :], far[:, 3 * NB :])
 
 
@@ -268,7 +268,7 @@
 
 
 def block_cover_kernel(t_ref, row_cell_ref, *refs, points):
-    blocks, (o_ref, h_ref, col_cell_ref, east_ref) = refs[:-4], refs[-4:]
+    blocks, (o_ref, h_ref, col_cell_ref, east_ref) = blocks_in(refs[:-4]), refs[-4:]
     cells = [
         column_counts(ref, h_ref, NB * i, o_ref.shape[1]) for i, ref in enumerate(blocks)
     ]
@@ -380,16 +380,33 @@
     factor_blocks(a_ref, lh_ref, ll_ref, wh_ref, wl_ref)
 
 
+def turned(r, k):
+    at = ((r & 1) << 1 | (r >> 1) & 1) + k
+    return (r & 4) | (at & 1) << 1 | (at >> 1) & 1
+
+
 def block_order(r):
-    here, away, q = r & 4, (r & 4) ^ 4, r & 3
-    turns = [(q + k) & 3 for k in (1, 2, 3)]
-    return [r, r ^ 4, here | turns[0], here | turns[1], here | turns[2]] + [away | t for t in turns]
+    own = [r, r ^ 4, turned(r, 1), turned(r, 2), turned(r, 3)]
+    return own + [turned(r, 3) ^ 4, turned(r, 1) ^ 4, turned(r, 2) ^ 4]
+
+
+def makes_own(r):
+    return (r & 1) == 0
 
 
 def folded_blocks(r):
     order = block_order(r)
-    either = jnp.where((r & 3) < 2, r, r ^ 4)
+    either = jnp.where(makes_own(r), r, r ^ 4)
     return [(r, r), (r, order[1]), (r, order[2]), (order[1], order[2]), (either, order[3])]
+
+
+def blocks_in(refs):
+    return [
+        ref.at[first : first + ref.shape[0] // parts]
+        for ref in refs
+        for parts in [1 + (ref.shape[0] >= 2 * NB)]
+        for first in range(0, ref.shape[0], ref.shape[0] // parts)
+    ]
 
 
 def unfold_kernel(place_ref, *refs):
@@ -451,9 +468,9 @@
     n = o_ref.shape[1]
 
     def put(rows, cols, value):
-        taken = parts_refs[0][rows, cols]
+        taken = parts_refs[0][parts_refs[0].shape[0] - 1, rows, cols]
         for part in parts_refs[1:]:
-            taken = taken + part[rows, cols]
+            taken = taken + part[part.shape[0] - 1, rows, cols]
         o_ref[rows, cols] = value - taken
 
     for (row, block), ref in zip(corners, cover_refs):
@@ -479,7 +496,7 @@
 
 
 def solve(place, covers, corners, parts, factors):
-    rows, n = parts[0].shape
+    rows, n = parts[0].shape[1:]
     return vmem_call(
         functools.partial(solve_kernel, corners=corners),
         jax.ShapeDtypeStruct((rows, n), F32),
@@ -507,7 +524,7 @@
 def fold_products_kernel(place_ref, *refs):
     blocks, shares, total_ref = refs[:4], refs[4:-1], refs[-1]
     own, far, one, two = [split(ref[:NB]) for ref in blocks]
-    own_last = (place_ref[0] & 3) < 2
+    own_last = makes_own(place_ref[0])
     either = split(jnp.where(own_last, blocks[0][:NB], blocks[1][:NB]))
     pairs = [(own, own), (own, far), (own, one), (far, one), (either, two)]
     for k, (left, right) in enumerate(pairs):
@@ -519,7 +536,7 @@
 
 
 def gather_split_kernel(place_ref, *refs):
-    blocks, (high_ref, low_ref) = refs[:-2], refs[-2:]
+    blocks, (high_ref, low_ref) = blocks_in(refs[:-2]), refs[-2:]
     for s, ref in zip(block_order(place_ref[0]), blocks):
         first = pl.multiple_of(s * NB, NB)
         high, low = split(ref[:NB])
@@ -527,17 +544,18 @@
         low_ref[pl.ds(first, NB)] = low
 
 
-def rest_products_kernel(place_ref, prior_ref, high_ref, low_ref, *refs, m):
-    o_ref = refs[-1]
-    rows = o_ref.shape[0]
-    first = pl.multiple_of((place_ref[1] ^ m) * rows, rows)
-    own_high, own_low = split(prior_ref[pl.ds(first, rows)])
-    for c in range(0, o_ref.shape[1], 2 * NB):
-        cols = slice(c, c + 2 * NB)
-        total = dot3(own_high, own_low, high_ref[cols], low_ref[cols])
-        for plus_ref in refs[:-1]:
-            total = total + plus_ref[:, cols]
-        o_ref[:, cols] = total
+def rest_products_kernel(place_ref, prior_ref, high_ref, low_ref, *refs, turns):
+    plus_refs, o_ref = refs[:-1], refs[-1]
+    rows = o_ref.shape[1]
+    for i, m in enumerate(turns):
+        first = pl.multiple_of((place_ref[1] ^ m) * rows, rows)
+        own_high, own_low = split(prior_ref[pl.ds(first, rows)])
+        for c in range(0, o_ref.shape[2], 2 * NB):
+            cols = slice(c, c + 2 * NB)
+            total = dot3(own_high, own_low, high_ref[cols], low_ref[cols])
+            for plus_ref in plus_refs:
+                total = total + plus_ref[i, :, cols]
+            o_ref[i, :, cols] = total
 
 
 def swap(block, axis, bit):
@@ -594,13 +612,13 @@
         mine = covers[0][:per_device] - parts[:per_device]
         diag_rows = lax.all_gather(mine, ("row", "panel"), axis=0, tiled=True)
         corners = [(i * lead, None) for i in range(len(covers))]
-        return solve(place, covers, corners, [parts], factor(factor_kernel, (diag_rows,), B))
+        return solve(place, covers, corners, [parts[None]], factor(factor_kernel, (diag_rows,), B))
 
     def turn(block, k):
-        return lax.ppermute(block, "row", [((d & 4) | ((d + k) & 3), d) for d in range(8)])
+        return lax.ppermute(block, "row", [(turned(d, k), d) for d in range(8)])
 
     own = pack(own_prior, local_points)
-    far, one, two = swap(own, "row", 4), turn(own, 1), turn(own, 2)
+    two, one, far = turn(own, 2), turn(own, 1), swap(own, "row", 4)
     table = row_table(own_points, lines)
     (far, one, two), table = lax.optimization_barrier(((far, one, two), table))
     shares = vmem_call(
@@ -645,13 +663,13 @@
         lambda shares: [swap(share, "panel", m) for m, share in zip((1, 2, 3), shares[1:])],
         lead_cover,
     )
-    rest = [turn(own, 3), turn(far, 1), turn(far, 2), turn(far, 3)]
+    rest = [turn(jnp.concatenate([own, far], 0), 3), turn(far, 1), turn(far, 2)]
     shard = folded - (shares[0] + sums[0] + sums[1] + sums[2])
 
-    def rest_part(panel_prior, m, plus=()):
+    def rest_part(panel_prior, turns, plus=()):
         return vmem_call(
-            functools.partial(rest_products_kernel, m=m),
-            jax.ShapeDtypeStruct((quarter_rows, B), F32),
+            functools.partial(rest_products_kernel, turns=turns),
+            jax.ShapeDtypeStruct((len(turns), quarter_rows, B), F32),
             place,
             [prior_factor, *panel_prior, *plus],
             name="rest_products",
@@ -674,9 +692,9 @@
             [own, far, one, two, *blocks],
             name="gather_split",
         )
-        return cover, panel_prior, rest_part(panel_prior, 3), rest_part(panel_prior, 1)
-
-    along, (cover_first, panel_prior, part_3, part_1) = beside(
+        return cover, panel_prior, rest_part(panel_prior, (3, 1))
+
+    along, (cover_first, panel_prior, for_core) = beside(
         shard[None], lambda x: [swap(x, "row", bit) for bit in (2, 4, 6)], beside_z
     )
     held_rows = jnp.concatenate([shard[None]] + along, 0)
@@ -686,7 +704,7 @@
         return swap(x, "row", 1), swap(x, "panel", 2), lax.ppermute(x, ("row", "panel"), corner)
 
     def beside_xy(x, held):
-        from_3 = swap(part_3, "panel", 1)
+        from_core = swap(for_core, "panel", 1)
         cover = vmem_call(
             functools.partial(block_cover_kernel, points=count),
             jax.ShapeDtypeStruct((quarter_rows, half), F32),
@@ -695,15 +713,14 @@
             [pltpu.VMEM((lines, 8 * half), BF), pltpu.VMEM((1, half), F32), east],
             "cover",
         )
-        part_0, part_2 = rest_part(panel_prior, 0), rest_part(panel_prior, 2, [from_3])
-        return cover, part_0, part_2, swap(x, "panel", 1)
-
-    received, (cover_last, part_0, part_2, held_there) = beside(
+        part_0, part_2 = rest_part(panel_prior, (0,)), rest_part(panel_prior, (2,), [from_core])
+        return cover, part_0, part_2, from_core, swap(x, "panel", 1)
+
+    received, (cover_last, part_0, part_2, from_core, held_there) = beside(
         held_rows, across, beside_xy
     )
     there = [held_there] + [swap(x, "panel", 1) for x in received]
-    part_1, part_2 = lax.optimization_barrier((part_1, part_2))
-    parts = [part_0, swap(part_1, "panel", 1), swap(part_2, "panel", 2)]
+    parts = [part_0, from_core, swap(part_2, "panel", 2)]
     factors = factor(unfold_kernel, (place, held_rows, *received, *there), B)
     corners = [(0, 0), (per_device, 0), (0, 4)]
     return solve(place, [cover_lead, cover_first, cover_last], corners, parts, factors)

time: 123 us -> 115 us (0.935)
  starting transfers between devices: 28.7 us -> 20.8 us
    ppermute x16 -> x15, starting transfers between devices: 17.1 us -> 9.26 us  [swap(): lax.ppermute(block, axis, [(i, i ^ bit) for i in range(lax.axis_size(axis...]
    ppermute x6 -> x5, waiting for transfers between devices: 8.83 us -> 12 us  [turn(): return lax.ppermute(block, 'row', [(turned(d, k), d) for d in range(8)])]
    ppermute x16 -> x15, waiting for transfers between devices: 5.37 us -> 2.78 us  [swap(): lax.ppermute(block, axis, [(i, i ^ bit) for i in range(lax.axis_size(axis...]
    ppermute x6 -> x5, starting transfers between devices: 11 us -> 9.08 us  [turn(): return lax.ppermute(block, 'row', [(turned(d, k), d) for d in range(8)])]
    ppermute x1, starting transfers between devices: 0.63 us -> 2.44 us  [across(): lax.ppermute(x, ('row', 'panel'), corner)]
    pallas_call x10 -> x9, Pallas kernels: 38.6 us -> 37.9 us  [vmem_call(): pl.pallas_call(kernel, out_shape=out_shape, in_specs=[pl.BlockSpec(memory...]
  transfers between devices with their start and end apart: 23 -> 21, of which waited for: 5 -> 4; matrix products, arithmetic and copies ran while one was open for 0% -> 0% of each run, Pallas kernels for 56% -> 59%
where the time goes in v8:
time: 115 us; the launch traced here: 114 us
  Pallas kernels  75 us (65%)
  starting transfers between devices  20.8 us (18%)
  waiting for transfers between devices  14.7 us (13%)
  local copies, waits for them, and re-layouts  1.82 us (2%)
  other arithmetic  1.8 us (2%)
    pallas_call x9, Pallas kernels, vmem_call(): pl.pallas_call(kernel, out_shape=out_shape, in_specs=[pl.BlockSpec(memory...  37.9 us
    pallas_call x1, Pallas kernels, factor(): pl.pallas_call(kernel, out_shape=[jax.ShapeDtypeStruct((n, n), BF)] * 2 +...  32.3 us
    ppermute x5, waiting for transfers between devices, turn(): return lax.ppermute(block, 'row', [(turned(d, k), d) for d in range(8)])  12 us
    ppermute x15, starting transfers between devices, swap(): lax.ppermute(block, axis, [(i, i ^ bit) for i in range(lax.axis_size(axis...  9.26 us
    ppermute x5, starting transfers between devices, turn(): return lax.ppermute(block, 'row', [(turned(d, k), d) for d in range(8)])  9.08 us
    pallas_call x1, Pallas kernels, row_table(): pl.pallas_call(row_table_kernel, out_shape=[jax.ShapeDtypeStruct((8, rows...  4.85 us
    ppermute x15, waiting for transfers between devices, swap(): lax.ppermute(block, axis, [(i, i ^ bit) for i in range(lax.axis_size(axis...  2.78 us
    ppermute x1, starting transfers between devices, across(): lax.ppermute(x, ('row', 'panel'), corner)  2.44 us
  transfers between devices with their start and end apart: 21, of which 4 were waited for; matrix products, arithmetic and copies ran while one was open for 0% of the time, Pallas kernels for 59%

profile of v8, /device:TPU:0, one launch (start us, length us, event | category | flops | bytes accessed | tf_op | source)
XLA Modules:
  0.0 114.4 jit_solution(5530989303610173692)
XLA Ops:
  0.0 0.7 fusion.1
  0.7 0.9 convert_add_fusion.1
  1.8 1.0 slice.16
  2.8 3.0 %collective-permute-start.2 = (f32[136,512]{1,0:T(8,128)S(1)}, f32[136,512]{1,0:T(8,128)S(1)}, u32[]{:S(2)}, u32[]{:S(2)}) collective-permute-start(f32[136,512]{1,0:T(8,128)S(1)} %pad_maximum_fusion.2.refs_0_), channel_id=1, source_target_pairs={{4,0},{0,4},{12,8},{8,12},{20,16},{16,20},{28,24},{24,28},{5,1},{1... | collective-permute-start | bytes 835592 | tf_op jit(solution)/shard_map/ppermute | solution.py:618
  5.8 1.5 %collective-permute-start.1 = (f32[136,512]{1,0:T(8,128)S(1)}, f32[136,512]{1,0:T(8,128)S(1)}, u32[]{:S(2)}, u32[]{:S(2)}) collective-permute-start(f32[136,512]{1,0:T(8,128)S(1)} %pad_maximum_fusion.2.refs_0_), channel_id=1, source_target_pairs={{8,0},{12,4},{4,8},{0,12},{24,16},{28,20},{20,24},{16,28},{9,1},{1... | collective-permute-start | bytes 835592 | tf_op jit(solution)/shard_map/ppermute | solution.py:618
  7.3 2.6 %collective-permute-start = (f32[136,512]{1,0:T(8,128)S(1)}, f32[136,512]{1,0:T(8,128)S(1)}, u32[]{:S(2)}, u32[]{:S(2)}) collective-permute-start(f32[136,512]{1,0:T(8,128)S(1)} %pad_maximum_fusion.2.refs_0_), channel_id=1, source_target_pairs={{0,16},{4,20},{8,24},{12,28},{16,0},{20,4},{24,8},{28,12},{1,17},{... | collective-permute-start | bytes 835592 | tf_op jit(solution)/shard_map/ppermute | solution.py:562
  9.9 4.8 %row_table.1 = (bf16[8,256,512]{2,1,0:T(8,128)(2,1)S(1)}, f32[256,1]{1,0:T(8,128)S(1)}) custom-call(f32[2,16,256]{2,1,0:T(8,128)S(1)} %fusion.row_ref), custom_call_target="tpu_custom_call" | custom-call | flops 100000000 | bytes 262144 | tf_op jit(solution)/shard_map/row_table/pallas_call | solution.py:147
  14.9 4.9 %collective-permute-done.1.refs_2_ = f32[136,512]{1,0:T(8,128)S(1)} collective-permute-done((f32[136,512]{1,0:T(8,128)S(1)}, f32[136,512]{1,0:T(8,128)S(1)}, u32[]{:S(2)}, u32[]{:S(2)}) %collective-permute-start.1) | collective-permute-done | bytes 278560 | tf_op jit(solution)/shard_map/ppermute | solution.py:618
  19.8 2.3 %collective-permute-done.refs_1_ = f32[136,512]{1,0:T(8,128)S(1)} collective-permute-done((f32[136,512]{1,0:T(8,128)S(1)}, f32[136,512]{1,0:T(8,128)S(1)}, u32[]{:S(2)}, u32[]{:S(2)}) %collective-permute-start) | collective-permute-done | bytes 278560 | tf_op jit(solution)/shard_map/ppermute | solution.py:562
  22.1 1.2 %fold_products.1 = (f32[32,640]{1,0:T(8,128)S(1)}, f32[32,640]{1,0:T(8,128)S(1)}, f32[32,640]{1,0:T(8,128)S(1)}, f32[32,640]{1,0:T(8,128)S(1)}) custom-call(s32[2]{0:T(128)S(1)} %pad_add_fusion.place_ref, f32[136,512]{1,0:T(8,128)S(1)} %pad_maximum_fusion.2.refs_0_, f32[136,512]{1,0:T(8,128)S(1)} %collective-permute-done.refs_1_, ...), custom_call_target="tpu_custom_call" | custom-call | flops 100000000 | bytes 262144 | tf_op jit(solution)/shard_map/fold_products/pallas_call | solution.py:511
  23.4 0.5 collective-permute-start.9
  23.9 1.5 %collective-permute-start.4 = (f32[32,640]{1,0:T(8,128)S(1)}, f32[32,640]{1,0:T(8,128)S(1)}, u32[]{:S(2)}, u32[]{:S(2)}) collective-permute-start(f32[32,640]{1,0:T(8,128)S(1)} %get-tuple-element.85), channel_id=1, source_target_pairs={{0,2},{1,3},{2,0},{3,1},{4,6},{5,7},{6,4},{7,5},{8,10},{9,11},{10,... | collective-permute-start | bytes 245768 | tf_op jit(solution)/shard_map/ppermute | solution.py:562
  25.8 1.1 collective-permute-start.11
  26.9 3.4 %lead_cover.1 = (f32[32,640]{1,0:T(8,128)S(1)}, f32[32,512]{1,0:T(8,128)S(1)}, bf16[256,4096]{1,0:T(8,128)(2,1)S(1)}, f32[1,512]{1,0:T(1,128)S(1)}) custom-call(s32[2]{0:T(128)S(1)} %pad_add_fusion.place_ref, bf16[8,256,512]{2,1,0:T(8,128)(2,1)S(1)} %get-tuple-element.116.t_ref, f32[256,1]{1,0:T(8,128)S(1)} %get-tuple-element.117.row_cell_ref, ...), custom_call_target="tpu_custom_call" | custom-call | flops 100000000 | bytes 262144 | tf_op jit(solution)/shard_map/lead_cover/pallas_call | solution.py:511
  30.3 2.9 %collective-permute-start.10 = (f32[136,512]{1,0:T(8,128)S(1)}, f32[136,512]{1,0:T(8,128)S(1)}, u32[]{:S(2)}, u32[]{:S(2)}) collective-permute-start(f32[136,512]{1,0:T(8,128)S(1)} %collective-permute-done.refs_1_), channel_id=1, source_target_pairs={{8,0},{12,4},{4,8},{0,12},{24,16},{28,20},{20,24},{16,28},{9,1},{1... | collective-permute-start | bytes 835592 | tf_op jit(solution)/shard_map/ppermute | solution.py:618
  33.2 0.7 collective-permute-start.8
  34.2 7.0 %collective-permute-done.11.refs_6_.refs_2_ = f32[136,512]{1,0:T(8,128)S(1)} collective-permute-done((f32[136,512]{1,0:T(8,128)S(1)}, f32[136,512]{1,0:T(8,128)S(1)}, u32[]{:S(2)}, u32[]{:S(2)}) %collective-permute-start.11) | collective-permute-done | bytes 278560 | tf_op jit(solution)/shard_map/ppermute | solution.py:618
  41.2 9.3 %cover.2.refs_1_ = f32[224,512]{1,0:T(8,128)S(1)} custom-call(bf16[8,256,512]{2,1,0:T(8,128)(2,1)S(1)} %get-tuple-element.116.t_ref, f32[256,1]{1,0:T(8,128)S(1)} %get-tuple-element.117.row_cell_ref, bf16[256,4096]{1,0:T(8,128)(2,1)S(1)} %get-tuple-element.103.h_ref, f32[1,512]{1,0:T(1,128)S(1)} %get-tuple-element.104.col_cell_ref), custom_call_target="tpu_custom_call" | custom-call | flops 100000000 | bytes 262144 | tf_op jit(solution)/shard_map/cover/pallas_call | solution.py:511
  50.6 0.9 gather_split.1
  51.5 0.7 copy-done
  52.2 2.4 %rest_products.3 = f32[2,256,1024]{2,1,0:T(8,128)S(1)} custom-call(s32[2]{0:T(128)S(1)} %pad_add_fusion.place_ref, f32[1024,512]{1,0:T(8,128)S(1)} %copy-done, bf16[1024,512]{1,0:T(8,128)(2,1)S(1)} %get-tuple-element.118.high_ref, bf16[1024,512]{1,0:T(8,128)(2,1)S(1)} %get-tuple-element.119.low_ref), custom_call_target="tpu_custom_call" | custom-call | flops 100000000 | bytes 262144 | tf_op jit(solution)/shard_map/rest_products/pallas_call | solution.py:511
  54.7 0.5 collective-permute-start.16
  55.3 2.4 %collective-permute-start.14 = (f32[4,32,640]{2,1,0:T(8,128)S(1)}, f32[4,32,640]{2,1,0:T(8,128)S(1)}, u32[]{:S(2)}, u32[]{:S(2)}) collective-permute-start(f32[4,32,640]{2,1,0:T(8,128)S(1)} %pad_maximum_fusion.1.refs_0_), channel_id=1, source_target_pairs={{0,6},{1,7},{2,4},{3,5},{4,2},{5,3},{6,0},{7,1},{8,14},{9,15},{10,... | collective-permute-start | bytes 983048 | tf_op jit(solution)/shard_map/ppermute | solution.py:704
  57.7 0.5 collective-permute-start.13
  58.2 0.5 collective-permute-start.12
  58.7 1.6 %rest_products.4.refs_3_ = f32[1,256,1024]{2,1,0:T(8,128)S(1)} custom-call(s32[2]{0:T(128)S(1)} %pad_add_fusion.place_ref, f32[1024,512]{1,0:T(8,128)S(1)} %copy-done, bf16[1024,512]{1,0:T(8,128)(2,1)S(1)} %get-tuple-element.118.high_ref, bf16[1024,512]{1,0:T(8,128)(2,1)S(1)} %get-tuple-element.119.low_ref), custom_call_target="tpu_custom_call" | custom-call | flops 100000000 | bytes 262144 | tf_op jit(solution)/shard_map/rest_products/pallas_call | solution.py:511
  60.3 11.3 %cover.3.refs_2_ = f32[256,512]{1,0:T(8,128)S(1)} custom-call(bf16[8,256,512]{2,1,0:T(8,128)(2,1)S(1)} %get-tuple-element.116.t_ref, f32[256,1]{1,0:T(8,128)S(1)} %get-tuple-element.117.row_cell_ref, f32[272,512]{1,0:T(8,128)S(1)} %collective-permute-done.9.refs_4_.refs_0_, f32[136,512]{1,0:T(8,128)S(1)} %collective-permute-done.10.refs_5_.refs_1_, ...), custom_call_target="tpu_custom_call" | custom-call | flops 100000000 | bytes 262144 | tf_op jit(solution)/shard_map/cover/pallas_call | solution.py:511
  71.6 1.6 %rest_products.5 = f32[1,256,1024]{2,1,0:T(8,128)S(1)} custom-call(s32[2]{0:T(128)S(1)} %pad_add_fusion.place_ref, f32[1024,512]{1,0:T(8,128)S(1)} %copy-done, bf16[1024,512]{1,0:T(8,128)(2,1)S(1)} %get-tuple-element.118.high_ref, bf16[1024,512]{1,0:T(8,128)(2,1)S(1)} %get-tuple-element.119.low_ref, f32[2,256,1024]{2,1,0:T(8,128)S(1)} %collective-permute-done.15.refs_0_.refs_4_), custom_call_target="tpu_custom_call" | custom-call | flops 100000000 | bytes 262144 | tf_op jit(solution)/shard_map/rest_products/pallas_call | solution.py:511
  73.3 0.5 collective-permute-start.19
  73.9 1.5 %collective-permute-start.17 = (f32[1,256,1024]{2,1,0:T(8,128)S(1)}, f32[1,256,1024]{2,1,0:T(8,128)S(1)}, u32[]{:S(2)}, u32[]{:S(2)}) collective-permute-start(f32[1,256,1024]{2,1,0:T(8,128)S(1)} %rest_products.5), channel_id=1, source_target_pairs={{0,2},{1,3},{2,0},{3,1},{4,6},{5,7},{6,4},{7,5},{8,10},{9,11},{10,... | collective-permute-start | bytes 3145736 | tf_op jit(solution)/shard_map/ppermute | solution.py:562
  75.8 32.3 %factor.1 = (bf16[1024,1024]{1,0:T(8,128)(2,1)S(1)}, bf16[1024,1024]{1,0:T(8,128)(2,1)S(1)}, bf16[1024,128]{1,0:T(8,128)(2,1)S(1)}, bf16[1024,128]{1,0:T(8,128)(2,1)S(1)}) custom-call(s32[2]{0:T(128)S(1)} %pad_add_fusion.place_ref, f32[4,32,640]{2,1,0:T(8,128)S(1)} %pad_maximum_fusion.1.refs_0_, f32[4,32,640]{2,1,0:T(8,128)S(1)} %collective-permute-done.12.refs_1_, ...), custom_call_target="tpu_custom_call" | custom-call | flops 49999998976 | bytes 8388608 | tf_op jit(solution)/shard_map/factor/pallas_call | solution.py:453
  108.1 6.2 %solve.1 = f32[256,1024]{1,0:T(8,128)} custom-call(s32[2]{0:T(128)S(1)} %pad_add_fusion.place_ref, f32[32,512]{1,0:T(8,128)S(1)} %get-tuple-element.95.refs_0_, f32[224,512]{1,0:T(8,128)S(1)} %cover.2.refs_1_, f32[256,512]{1,0:T(8,128)S(1)} %cover.3.refs_2_, f32[1,256,1024]{2,1,0:T(8,128)S(1)} %rest_products.4.refs_3_, ...), custom_call_target="tpu_custom_call" | custom-call | flops 100000000 | bytes 262144 | tf_op jit(solution)/shard_map/solve/pallas_call | solution.py:511
  (36 shorter events, 1.7 us)
Async XLA Ops:
  2.8 12.1 %collective-permute-start.2 = (f32[136,512]{1,0:T(8,128)S(1)}, f32[136,512]{1,0:T(8,128)S(1)}, u32[]{:S(2)}, u32[]{:S(2)}) collective-permute-start(f32[136,512]{1,0:T(8,128)S(1)} %pad_maximum_fusion.2.refs_0_), channel_id=1, source_target_pairs={{4,0},{0,4},{12,8},{8,12},{20,16},{16,20},{28,24},{24,28},{5,1},{1... | collective-permute-start | bytes 835592 | tf_op jit(solution)/shard_map/ppermute | solution.py:618
  5.8 14.0 %collective-permute-start.1 = (f32[136,512]{1,0:T(8,128)S(1)}, f32[136,512]{1,0:T(8,128)S(1)}, u32[]{:S(2)}, u32[]{:S(2)}) collective-permute-start(f32[136,512]{1,0:T(8,128)S(1)} %pad_maximum_fusion.2.refs_0_), channel_id=1, source_target_pairs={{8,0},{12,4},{4,8},{0,12},{24,16},{28,20},{20,24},{16,28},{9,1},{1... | collective-permute-start | bytes 835592 | tf_op jit(solution)/shard_map/ppermute | solution.py:618
  7.3 14.7 %collective-permute-start = (f32[136,512]{1,0:T(8,128)S(1)}, f32[136,512]{1,0:T(8,128)S(1)}, u32[]{:S(2)}, u32[]{:S(2)}) collective-permute-start(f32[136,512]{1,0:T(8,128)S(1)} %pad_maximum_fusion.2.refs_0_), channel_id=1, source_target_pairs={{0,16},{4,20},{8,24},{12,28},{16,0},{20,4},{24,8},{28,12},{1,17},{... | collective-permute-start | bytes 835592 | tf_op jit(solution)/shard_map/ppermute | solution.py:562
  23.4 27.2 %collective-permute-start.9 = (f32[272,512]{1,0:T(8,128)S(1)}, f32[272,512]{1,0:T(8,128)S(1)}, u32[]{:S(2)}, u32[]{:S(2)}) collective-permute-start(f32[272,512]{1,0:T(8,128)S(1)} %pad_maximum_fusion), channel_id=1, source_target_pairs={{12,0},{8,4},{0,8},{4,12},{28,16},{24,20},{16,24},{20,28},{13,1},{... | collective-permute-start | bytes 1671176 | tf_op jit(solution)/shard_map/ppermute | solution.py:618
  23.9 6.4 %collective-permute-start.3 = (f32[32,640]{1,0:T(8,128)S(1)}, f32[32,640]{1,0:T(8,128)S(1)}, u32[]{:S(2)}, u32[]{:S(2)}) collective-permute-start(f32[32,640]{1,0:T(8,128)S(1)} %get-tuple-element.84), channel_id=1, source_target_pairs={{0,1},{1,0},{2,3},{3,2},{4,5},{5,4},{6,7},{7,6},{8,9},{9,8},{10,11... | collective-permute-start | bytes 245768 | tf_op jit(solution)/shard_map/ppermute | solution.py:562
  23.9 9.3 %collective-permute-start.4 = (f32[32,640]{1,0:T(8,128)S(1)}, f32[32,640]{1,0:T(8,128)S(1)}, u32[]{:S(2)}, u32[]{:S(2)}) collective-permute-start(f32[32,640]{1,0:T(8,128)S(1)} %get-tuple-element.85), channel_id=1, source_target_pairs={{0,2},{1,3},{2,0},{3,1},{4,6},{5,7},{6,4},{7,5},{8,10},{9,11},{10,... | collective-permute-start | bytes 245768 | tf_op jit(solution)/shard_map/ppermute | solution.py:562
  25.4 7.8 %collective-permute-start.5 = (f32[32,640]{1,0:T(8,128)S(1)}, f32[32,640]{1,0:T(8,128)S(1)}, u32[]{:S(2)}, u32[]{:S(2)}) collective-permute-start(f32[32,640]{1,0:T(8,128)S(1)} %get-tuple-element.86), channel_id=1, source_target_pairs={{0,3},{1,2},{2,1},{3,0},{4,7},{5,6},{6,5},{7,4},{8,11},{9,10},{10,... | collective-permute-start | bytes 245768 | tf_op jit(solution)/shard_map/ppermute | solution.py:562
  25.8 15.4 %collective-permute-start.11 = (f32[136,512]{1,0:T(8,128)S(1)}, f32[136,512]{1,0:T(8,128)S(1)}, u32[]{:S(2)}, u32[]{:S(2)}) collective-permute-start(f32[136,512]{1,0:T(8,128)S(1)} %collective-permute-done.refs_1_), channel_id=1, source_target_pairs={{4,0},{0,4},{12,8},{8,12},{20,16},{16,20},{28,24},{24,28},{5,1},{1... | collective-permute-start | bytes 835592 | tf_op jit(solution)/shard_map/ppermute | solution.py:618
  30.3 20.3 %collective-permute-start.10 = (f32[136,512]{1,0:T(8,128)S(1)}, f32[136,512]{1,0:T(8,128)S(1)}, u32[]{:S(2)}, u32[]{:S(2)}) collective-permute-start(f32[136,512]{1,0:T(8,128)S(1)} %collective-permute-done.refs_1_), channel_id=1, source_target_pairs={{8,0},{12,4},{4,8},{0,12},{24,16},{28,20},{20,24},{16,28},{9,1},{1... | collective-permute-start | bytes 835592 | tf_op jit(solution)/shard_map/ppermute | solution.py:618
  33.2 21.3 %collective-permute-start.8 = (f32[1,32,640]{2,1,0:T(8,128)S(1)}, f32[1,32,640]{2,1,0:T(8,128)S(1)}, u32[]{:S(2)}, u32[]{:S(2)}) collective-permute-start(f32[1,32,640]{2,1,0:T(8,128)S(1)} %subtract_bitcast_fusion), channel_id=1, source_target_pairs={{0,24},{4,28},{8,16},{12,20},{16,8},{20,12},{24,0},{28,4},{1,25},{... | collective-permute-start | bytes 245768 | tf_op jit(solution)/shard_map/ppermute | solution.py:562
  33.9 20.6 %collective-permute-start.7 = (f32[1,32,640]{2,1,0:T(8,128)S(1)}, f32[1,32,640]{2,1,0:T(8,128)S(1)}, u32[]{:S(2)}, u32[]{:S(2)}) collective-permute-start(f32[1,32,640]{2,1,0:T(8,128)S(1)} %subtract_bitcast_fusion), channel_id=1, source_target_pairs={{0,16},{4,20},{8,24},{12,28},{16,0},{20,4},{24,8},{28,12},{1,17},{... | collective-permute-start | bytes 245768 | tf_op jit(solution)/shard_map/ppermute | solution.py:562
  41.2 13.3 %collective-permute-start.6 = (f32[1,32,640]{2,1,0:T(8,128)S(1)}, f32[1,32,640]{2,1,0:T(8,128)S(1)}, u32[]{:S(2)}, u32[]{:S(2)}) collective-permute-start(f32[1,32,640]{2,1,0:T(8,128)S(1)} %subtract_bitcast_fusion), channel_id=1, source_target_pairs={{0,8},{4,12},{8,0},{12,4},{16,24},{20,28},{24,16},{28,20},{1,9},{5... | collective-permute-start | bytes 245768 | tf_op jit(solution)/shard_map/ppermute | solution.py:562
  50.6 1.6 %copy-start = (f32[1024,512]{1,0:T(8,128)S(1)}, f32[1024,512]{1,0:T(8,128)}, u32[]{:S(2)}) copy-start(f32[1024,512]{1,0:T(8,128)} %prior_ref.5) | copy-start | bytes 6291460
  54.6 17.0 %collective-permute-start.15 = (f32[2,256,1024]{2,1,0:T(8,128)S(1)}, f32[2,256,1024]{2,1,0:T(8,128)S(1)}, u32[]{:S(2)}, u32[]{:S(2)}) collective-permute-start(f32[2,256,1024]{2,1,0:T(8,128)S(1)} %rest_products.3), channel_id=1, source_target_pairs={{0,1},{1,0},{2,3},{3,2},{4,5},{5,4},{6,7},{7,6},{8,9},{9,8},{10,11... | collective-permute-start | bytes 6291464 | tf_op jit(solution)/shard_map/ppermute | solution.py:562
  54.7 18.5 %collective-permute-start.16 = (f32[4,32,640]{2,1,0:T(8,128)S(1)}, f32[4,32,640]{2,1,0:T(8,128)S(1)}, u32[]{:S(2)}, u32[]{:S(2)}) collective-permute-start(f32[4,32,640]{2,1,0:T(8,128)S(1)} %pad_maximum_fusion.1.refs_0_), channel_id=1, source_target_pairs={{0,1},{1,0},{2,3},{3,2},{4,5},{5,4},{6,7},{7,6},{8,9},{9,8},{10,11... | collective-permute-start | bytes 983048 | tf_op jit(solution)/shard_map/ppermute | solution.py:562
  55.3 17.9 %collective-permute-start.14 = (f32[4,32,640]{2,1,0:T(8,128)S(1)}, f32[4,32,640]{2,1,0:T(8,128)S(1)}, u32[]{:S(2)}, u32[]{:S(2)}) collective-permute-start(f32[4,32,640]{2,1,0:T(8,128)S(1)} %pad_maximum_fusion.1.refs_0_), channel_id=1, source_target_pairs={{0,6},{1,7},{2,4},{3,5},{4,2},{5,3},{6,0},{7,1},{8,14},{9,15},{10,... | collective-permute-start | bytes 983048 | tf_op jit(solution)/shard_map/ppermute | solution.py:704
  57.7 15.5 %collective-permute-start.13 = (f32[4,32,640]{2,1,0:T(8,128)S(1)}, f32[4,32,640]{2,1,0:T(8,128)S(1)}, u32[]{:S(2)}, u32[]{:S(2)}) collective-permute-start(f32[4,32,640]{2,1,0:T(8,128)S(1)} %pad_maximum_fusion.1.refs_0_), channel_id=1, source_target_pairs={{0,2},{1,3},{2,0},{3,1},{4,6},{5,7},{6,4},{7,5},{8,10},{9,11},{10,... | collective-permute-start | bytes 983048 | tf_op jit(solution)/shard_map/ppermute | solution.py:562
  58.2 15.0 %collective-permute-start.12 = (f32[4,32,640]{2,1,0:T(8,128)S(1)}, f32[4,32,640]{2,1,0:T(8,128)S(1)}, u32[]{:S(2)}, u32[]{:S(2)}) collective-permute-start(f32[4,32,640]{2,1,0:T(8,128)S(1)} %pad_maximum_fusion.1.refs_0_), channel_id=1, source_target_pairs={{0,4},{4,0},{8,12},{12,8},{16,20},{20,16},{24,28},{28,24},{1,5},{5... | collective-permute-start | bytes 983048 | tf_op jit(solution)/shard_map/ppermute | solution.py:562
  73.2 2.2 %collective-permute-start.18 = (f32[4,32,640]{2,1,0:T(8,128)S(1)}, f32[4,32,640]{2,1,0:T(8,128)S(1)}, u32[]{:S(2)}, u32[]{:S(2)}) collective-permute-start(f32[4,32,640]{2,1,0:T(8,128)S(1)} %collective-permute-done.12.refs_1_), channel_id=1, source_target_pairs={{0,1},{1,0},{2,3},{3,2},{4,5},{5,4},{6,7},{7,6},{8,9},{9,8},{10,11... | collective-permute-start | bytes 983048 | tf_op jit(solution)/shard_map/ppermute | solution.py:562
  73.3 2.1 %collective-permute-start.19 = (f32[4,32,640]{2,1,0:T(8,128)S(1)}, f32[4,32,640]{2,1,0:T(8,128)S(1)}, u32[]{:S(2)}, u32[]{:S(2)}) collective-permute-start(f32[4,32,640]{2,1,0:T(8,128)S(1)} %collective-permute-done.13.refs_2_), channel_id=1, source_target_pairs={{0,1},{1,0},{2,3},{3,2},{4,5},{5,4},{6,7},{7,6},{8,9},{9,8},{10,11... | collective-permute-start | bytes 983048 | tf_op jit(solution)/shard_map/ppermute | solution.py:562
  73.8 2.1 %collective-permute-start.20 = (f32[4,32,640]{2,1,0:T(8,128)S(1)}, f32[4,32,640]{2,1,0:T(8,128)S(1)}, u32[]{:S(2)}, u32[]{:S(2)}) collective-permute-start(f32[4,32,640]{2,1,0:T(8,128)S(1)} %collective-permute-done.14.refs_3_), channel_id=1, source_target_pairs={{0,1},{1,0},{2,3},{3,2},{4,5},{5,4},{6,7},{7,6},{8,9},{9,8},{10,11... | collective-permute-start | bytes 983048 | tf_op jit(solution)/shard_map/ppermute | solution.py:562
  73.9 34.3 %collective-permute-start.17 = (f32[1,256,1024]{2,1,0:T(8,128)S(1)}, f32[1,256,1024]{2,1,0:T(8,128)S(1)}, u32[]{:S(2)}, u32[]{:S(2)}) collective-permute-start(f32[1,256,1024]{2,1,0:T(8,128)S(1)} %rest_products.5), channel_id=1, source_target_pairs={{0,2},{1,3},{2,0},{3,1},{4,6},{5,7},{6,4},{7,5},{8,10},{9,11},{10,... | collective-permute-start | bytes 3145736 | tf_op jit(solution)/shard_map/ppermute | solution.py:562

commit v9 on v8

--- a/solution.py
+++ b/solution.py
@@ -202,17 +202,23 @@
 
 def cover_chunk(table, row_cell, col_cell, h_ref, east_ref, points):
     chunk, cols = east_ref.shape[1:]
+    stride = h_ref.shape[1] // 8
+    together = 1 + (cols % (2 * NB) > 0)
     cell = jnp.broadcast_to(row_cell, (chunk, cols)) - col_cell
     for t in range(15):
         apart = cell + float(t - 7)
         east_ref[t] = jnp.exp2(apart * apart * SCALE)
     table = table.reshape(8 * chunk, table.shape[2])
     total = jnp.zeros((chunk, cols), F32)
-    for q in range(8):
-        counts = h_ref[:, q * cols : (q + 1) * cols]
+    for first in range(0, 8, together):
+        offsets = range(first, first + together)
+        counts = [h_ref[:, (q + 1) * stride - cols : (q + 1) * stride] for q in offsets]
+        counts = jnp.concatenate(counts, 1)
         part = jnp.dot(table, jnp.concatenate([counts, counts], 0), preferred_element_type=F32)
         for p in range(8):
-            total = total + part[p * chunk : (p + 1) * chunk] * east_ref[p - q + 7]
+            for i, q in enumerate(offsets):
+                piece = part[p * chunk : (p + 1) * chunk, i * cols : (i + 1) * cols]
+                total = total + piece * east_ref[p - q + 7]
     return total * (1.0 / (points * points))
 
 
@@ -252,28 +258,30 @@
     folded_ref[:, 4 * NB :] = jnp.where(own_last, mine[:, 3 * NB :], far[:, 3 * NB :])
 
 
-def later_cover_kernel(t_ref, row_cell_ref, h_ref, col_cell_ref, o_ref, east_ref, *, points):
-    chunk = east_ref.shape[1]
-    skipped = t_ref.shape[1] - o_ref.shape[0]
+def later_cover_kernel(t_ref, row_cell_ref, h_ref, col_cell_ref, o_ref, east_ref, *, points, start):
+    chunk, cols = east_ref.shape[1:]
+    col_cell = col_cell_ref[:, col_cell_ref.shape[1] - cols :]
 
     def row_chunk(index, _):
         first = pl.multiple_of(index * chunk, chunk)
-        here = pl.ds(pl.multiple_of(first + skipped, chunk), chunk)
+        here = pl.ds(pl.multiple_of(first + start, chunk), chunk)
         o_ref[pl.ds(first, chunk)] = cover_chunk(
-            t_ref[:, here], row_cell_ref[here], col_cell_ref[...], h_ref, east_ref, points
+            t_ref[:, here], row_cell_ref[here], col_cell, h_ref, east_ref, points
         )
         return 0
 
     lax.fori_loop(0, o_ref.shape[0] // chunk, row_chunk, 0)
 
 
-def block_cover_kernel(t_ref, row_cell_ref, *refs, points):
+def block_cover_kernel(t_ref, row_cell_ref, *refs, points, start):
     blocks, (o_ref, h_ref, col_cell_ref, east_ref) = blocks_in(refs[:-4]), refs[-4:]
     cells = [
         column_counts(ref, h_ref, NB * i, o_ref.shape[1]) for i, ref in enumerate(blocks)
     ]
     col_cell_ref[...] = jnp.concatenate(cells, 1)
-    later_cover_kernel(t_ref, row_cell_ref, h_ref, col_cell_ref, o_ref, east_ref, points=points)
+    later_cover_kernel(
+        t_ref, row_cell_ref, h_ref, col_cell_ref, o_ref, east_ref, points=points, start=start
+    )
 
 
 def inverse_factor(tiles):
@@ -620,7 +628,23 @@
     own = pack(own_prior, local_points)
     two, one, far = turn(own, 2), turn(own, 1), swap(own, "row", 4)
     table = row_table(own_points, lines)
-    (far, one, two), table = lax.optimization_barrier(((far, one, two), table))
+
+    def block_cover(held, blocks, start, cols):
+        return vmem_call(
+            functools.partial(block_cover_kernel, points=count, start=start),
+            jax.ShapeDtypeStruct((quarter_rows - start, cols), F32),
+            None,
+            [*held, *blocks],
+            [
+                pltpu.VMEM((lines, 8 * cols), BF),
+                pltpu.VMEM((1, cols), F32),
+                pltpu.VMEM((15, per_device, cols), F32),
+            ],
+            "cover",
+        )
+
+    cover_own = block_cover(table, [own], per_device, NB)
+    (far, one, two), table, cover_own = lax.optimization_barrier(((far, one, two), table, cover_own))
     shares = vmem_call(
         fold_products_kernel,
         [jax.ShapeDtypeStruct((per_device, 5 * NB), F32)] * 4,
@@ -675,15 +699,20 @@
             name="rest_products",
         )
 
-    def beside_z(_, held):
-        cover = vmem_call(
-            functools.partial(later_cover_kernel, points=count),
-            jax.ShapeDtypeStruct((quarter_rows - per_device, half), F32),
+    def later_cover(held, start, rows):
+        return vmem_call(
+            functools.partial(later_cover_kernel, points=count, start=start),
+            jax.ShapeDtypeStruct((rows, half - NB), F32),
             None,
             [*held, *counts],
-            [east],
+            [pltpu.VMEM((15, per_device, half - NB), F32)],
             "cover",
         )
+
+    middle = quarter_rows // 2
+
+    def beside_far_z(_, held):
+        cover = later_cover(held, middle, quarter_rows - middle)
         cover, blocks = lax.optimization_barrier((cover, rest))
         panel_prior = vmem_call(
             gather_split_kernel,
@@ -694,10 +723,17 @@
         )
         return cover, panel_prior, rest_part(panel_prior, (3, 1))
 
-    along, (cover_first, panel_prior, for_core) = beside(
-        shard[None], lambda x: [swap(x, "row", bit) for bit in (2, 4, 6)], beside_z
-    )
-    held_rows = jnp.concatenate([shard[None]] + along, 0)
+    shard = shard[None]
+    near_rows, cover_first = beside(
+        shard,
+        lambda x: swap(x, "row", 2),
+        lambda _, held: later_cover(held, per_device, middle - per_device),
+    )
+    near_rows = jnp.concatenate([shard, near_rows], 0)
+    far_rows, (cover_second, panel_prior, for_core) = beside(
+        near_rows, lambda x: swap(x, "row", 4), beside_far_z
+    )
+    held_rows = jnp.concatenate([near_rows, far_rows], 0)
 
     def across(x):
         corner = [(i, i ^ 6) for i in range(32)]
@@ -705,14 +741,7 @@
 
     def beside_xy(x, held):
         from_core = swap(for_core, "panel", 1)
-        cover = vmem_call(
-            functools.partial(block_cover_kernel, points=count),
-            jax.ShapeDtypeStruct((quarter_rows, half), F32),
-            None,
-            [*held, *rest],
-            [pltpu.VMEM((lines, 8 * half), BF), pltpu.VMEM((1, half), F32), east],
-            "cover",
-        )
+        cover = block_cover(held, rest, 0, half)
         part_0, part_2 = rest_part(panel_prior, (0,)), rest_part(panel_prior, (2,), [from_core])
         return cover, part_0, part_2, from_core, swap(x, "panel", 1)
 
@@ -722,8 +751,9 @@
     there = [held_there] + [swap(x, "panel", 1) for x in received]
     parts = [part_0, from_core, swap(part_2, "panel", 2)]
     factors = factor(unfold_kernel, (place, held_rows, *received, *there), B)
-    corners = [(0, 0), (per_device, 0), (0, 4)]
-    return solve(place, [cover_lead, cover_first, cover_last], corners, parts, factors)
+    covers = [cover_lead, cover_own, cover_first, cover_second, cover_last]
+    corners = [(0, 0), (per_device, 0), (per_device, 1), (middle, 1), (0, 4)]
+    return solve(place, covers, corners, parts, factors)
 
 
 def solution(mesh):

time: 115 us -> 115 us (level)
  Pallas kernels: 75 us -> 76.3 us
    ppermute x15 -> x14, waiting for transfers between devices: 2.78 us -> 10.2 us  [swap(): lax.ppermute(block, axis, [(i, i ^ bit) for i in range(lax.axis_size(axis...]
    ppermute x5, waiting for transfers between devices: 12 us -> 4.88 us  [turn(): return lax.ppermute(block, 'row', [(turned(d, k), d) for d in range(8)])]
    ppermute x15 -> x14, starting transfers between devices: 9.26 us -> 11.8 us  [swap(): lax.ppermute(block, axis, [(i, i ^ bit) for i in range(lax.axis_size(axis...]
    ppermute x5, starting transfers between devices: 9.08 us -> 6.63 us  [turn(): return lax.ppermute(block, 'row', [(turned(d, k), d) for d in range(8)])]
    pallas_call x9 -> x11, Pallas kernels: 37.9 us -> 39.2 us  [vmem_call(): pl.pallas_call(kernel, out_shape=out_shape, in_specs=[pl.BlockSpec(memory...]
  transfers between devices with their start and end apart: 21 -> 20, of which waited for: 4 -> 6; matrix products, arithmetic and copies ran while one was open for 0% -> 0% of each run, Pallas kernels for 59% -> 60%
where the time goes in v9:
time: 115 us
  Pallas kernels  76.3 us (66%)
  starting transfers between devices  20 us (17%)
  waiting for transfers between devices  15.1 us (13%)
  other arithmetic  1.82 us (2%)
    pallas_call x11, Pallas kernels, vmem_call(): pl.pallas_call(kernel, out_shape=out_shape, in_specs=[pl.BlockSpec(memory...  39.2 us
    pallas_call x1, Pallas kernels, factor(): pl.pallas_call(kernel, out_shape=[jax.ShapeDtypeStruct((n, n), BF)] * 2 +...  32.3 us
    ppermute x14, starting transfers between devices, swap(): lax.ppermute(block, axis, [(i, i ^ bit) for i in range(lax.axis_size(axis...  11.8 us
    ppermute x14, waiting for transfers between devices, swap(): lax.ppermute(block, axis, [(i, i ^ bit) for i in range(lax.axis_size(axis...  10.2 us
    ppermute x5, starting transfers between devices, turn(): return lax.ppermute(block, 'row', [(turned(d, k), d) for d in range(8)])  6.63 us
    ppermute x5, waiting for transfers between devices, turn(): return lax.ppermute(block, 'row', [(turned(d, k), d) for d in range(8)])  4.88 us
    pallas_call x1, Pallas kernels, row_table(): pl.pallas_call(row_table_kernel, out_shape=[jax.ShapeDtypeStruct((8, rows...  4.85 us
  transfers between devices with their start and end apart: 20, of which 6 were waited for; matrix products, arithmetic and copies ran while one was open for 0% of the time, Pallas kernels for 60%

profile of v9, /device:TPU:0, one launch (start us, length us, event | category | flops | bytes accessed | tf_op | source)
XLA Modules:
  0.0 114.7 jit_solution(11559729647954461081)
XLA Ops:
  0.0 0.7 fusion.1
  0.7 0.9 convert_add_fusion.1
  1.8 1.0 slice.16
  2.8 3.0 %collective-permute-start.2 = (f32[136,512]{1,0:T(8,128)S(1)}, f32[136,512]{1,0:T(8,128)S(1)}, u32[]{:S(2)}, u32[]{:S(2)}) collective-permute-start(f32[136,512]{1,0:T(8,128)S(1)} %pad_maximum_fusion.2.refs_0_), channel_id=1, source_target_pairs={{4,0},{0,4},{12,8},{8,12},{20,16},{16,20},{28,24},{24,28},{5,1},{1... | collective-permute-start | bytes 835592 | tf_op jit(solution)/shard_map/ppermute | solution.py:626
  5.8 1.5 %collective-permute-start.1 = (f32[136,512]{1,0:T(8,128)S(1)}, f32[136,512]{1,0:T(8,128)S(1)}, u32[]{:S(2)}, u32[]{:S(2)}) collective-permute-start(f32[136,512]{1,0:T(8,128)S(1)} %pad_maximum_fusion.2.refs_0_), channel_id=1, source_target_pairs={{8,0},{12,4},{4,8},{0,12},{24,16},{28,20},{20,24},{16,28},{9,1},{1... | collective-permute-start | bytes 835592 | tf_op jit(solution)/shard_map/ppermute | solution.py:626
  7.3 2.6 %collective-permute-start = (f32[136,512]{1,0:T(8,128)S(1)}, f32[136,512]{1,0:T(8,128)S(1)}, u32[]{:S(2)}, u32[]{:S(2)}) collective-permute-start(f32[136,512]{1,0:T(8,128)S(1)} %pad_maximum_fusion.2.refs_0_), channel_id=1, source_target_pairs={{0,16},{4,20},{8,24},{12,28},{16,0},{20,4},{24,8},{28,12},{1,17},{... | collective-permute-start | bytes 835592 | tf_op jit(solution)/shard_map/ppermute | solution.py:570
  9.9 4.8 %row_table.1 = (bf16[8,256,512]{2,1,0:T(8,128)(2,1)S(1)}, f32[256,1]{1,0:T(8,128)S(1)}) custom-call(f32[2,16,256]{2,1,0:T(8,128)S(1)} %fusion.row_ref), custom_call_target="tpu_custom_call" | custom-call | flops 100000000 | bytes 262144 | tf_op jit(solution)/shard_map/row_table/pallas_call | solution.py:147
  14.8 3.4 %cover.4.refs_1_ = f32[224,128]{1,0:T(8,128)S(1)} custom-call(bf16[8,256,512]{2,1,0:T(8,128)(2,1)S(1)} %get-tuple-element.124.t_ref, f32[256,1]{1,0:T(8,128)S(1)} %get-tuple-element.125.row_cell_ref, f32[136,512]{1,0:T(8,128)S(1)} %pad_maximum_fusion.2.refs_0_), custom_call_target="tpu_custom_call" | custom-call | flops 100000000 | bytes 262144 | tf_op jit(solution)/shard_map/cover/pallas_call | solution.py:519
  18.3 1.5 %collective-permute-done.1.refs_2_ = f32[136,512]{1,0:T(8,128)S(1)} collective-permute-done((f32[136,512]{1,0:T(8,128)S(1)}, f32[136,512]{1,0:T(8,128)S(1)}, u32[]{:S(2)}, u32[]{:S(2)}) %collective-permute-start.1) | collective-permute-done | bytes 278560 | tf_op jit(solution)/shard_map/ppermute | solution.py:626
  19.8 2.3 %collective-permute-done.refs_1_ = f32[136,512]{1,0:T(8,128)S(1)} collective-permute-done((f32[136,512]{1,0:T(8,128)S(1)}, f32[136,512]{1,0:T(8,128)S(1)}, u32[]{:S(2)}, u32[]{:S(2)}) %collective-permute-start) | collective-permute-done | bytes 278560 | tf_op jit(solution)/shard_map/ppermute | solution.py:570
  22.1 1.2 %fold_products.1 = (f32[32,640]{1,0:T(8,128)S(1)}, f32[32,640]{1,0:T(8,128)S(1)}, f32[32,640]{1,0:T(8,128)S(1)}, f32[32,640]{1,0:T(8,128)S(1)}) custom-call(s32[2]{0:T(128)S(1)} %pad_add_fusion.place_ref, f32[136,512]{1,0:T(8,128)S(1)} %pad_maximum_fusion.2.refs_0_, f32[136,512]{1,0:T(8,128)S(1)} %collective-permute-done.refs_1_, ...), custom_call_target="tpu_custom_call" | custom-call | flops 100000000 | bytes 262144 | tf_op jit(solution)/shard_map/fold_products/pallas_call | solution.py:519
  23.4 1.6 %collective-permute-start.4 = (f32[32,640]{1,0:T(8,128)S(1)}, f32[32,640]{1,0:T(8,128)S(1)}, u32[]{:S(2)}, u32[]{:S(2)}) collective-permute-start(f32[32,640]{1,0:T(8,128)S(1)} %get-tuple-element.89), channel_id=1, source_target_pairs={{0,2},{1,3},{2,0},{3,1},{4,6},{5,7},{6,4},{7,5},{8,10},{9,11},{10,... | collective-permute-start | bytes 245768 | tf_op jit(solution)/shard_map/ppermute | solution.py:570
  25.3 0.5 collective-permute-start.8
  25.9 3.4 %lead_cover.1 = (f32[32,640]{1,0:T(8,128)S(1)}, f32[32,512]{1,0:T(8,128)S(1)}, bf16[256,4096]{1,0:T(8,128)(2,1)S(1)}, f32[1,512]{1,0:T(1,128)S(1)}) custom-call(s32[2]{0:T(128)S(1)} %pad_add_fusion.place_ref, bf16[8,256,512]{2,1,0:T(8,128)(2,1)S(1)} %get-tuple-element.124.t_ref, f32[256,1]{1,0:T(8,128)S(1)} %get-tuple-element.125.row_cell_ref, ...), custom_call_target="tpu_custom_call" | custom-call | flops 100000000 | bytes 262144 | tf_op jit(solution)/shard_map/lead_cover/pallas_call | solution.py:519
  29.8 2.1 %collective-permute-start.6 = (f32[1,32,640]{2,1,0:T(8,128)S(1)}, f32[1,32,640]{2,1,0:T(8,128)S(1)}, u32[]{:S(2)}, u32[]{:S(2)}) collective-permute-start(f32[1,32,640]{2,1,0:T(8,128)S(1)} %subtract_bitcast_fusion), channel_id=1, source_target_pairs={{0,8},{4,12},{8,0},{12,4},{16,24},{20,28},{24,16},{28,20},{1,9},{5... | collective-permute-start | bytes 245768 | tf_op jit(solution)/shard_map/ppermute | solution.py:570
  31.9 0.5 collective-permute-start.10
  32.4 1.0 collective-permute-start.9
  33.4 3.1 %cover.5.refs_2_ = f32[96,384]{1,0:T(8,128)S(1)} custom-call(bf16[8,256,512]{2,1,0:T(8,128)(2,1)S(1)} %get-tuple-element.124.t_ref, f32[256,1]{1,0:T(8,128)S(1)} %get-tuple-element.125.row_cell_ref, bf16[256,4096]{1,0:T(8,128)(2,1)S(1)} %get-tuple-element.108.h_ref, f32[1,512]{1,0:T(1,128)S(1)} %get-tuple-element.109.col_cell_ref), custom_call_target="tpu_custom_call" | custom-call | flops 100000000 | bytes 262144 | tf_op jit(solution)/shard_map/cover/pallas_call | solution.py:519
  36.5 7.0 %collective-permute-done.6 = f32[1,32,640]{2,1,0:T(8,128)S(1)} collective-permute-done((f32[1,32,640]{2,1,0:T(8,128)S(1)}, f32[1,32,640]{2,1,0:T(8,128)S(1)}, u32[]{:S(2)}, u32[]{:S(2)}) %collective-permute-start.6) | collective-permute-done | bytes 81952 | tf_op jit(solution)/shard_map/ppermute | solution.py:570
  44.0 4.1 %cover.6.refs_3_ = f32[128,384]{1,0:T(8,128)S(1)} custom-call(bf16[8,256,512]{2,1,0:T(8,128)(2,1)S(1)} %get-tuple-element.124.t_ref, f32[256,1]{1,0:T(8,128)S(1)} %get-tuple-element.125.row_cell_ref, bf16[256,4096]{1,0:T(8,128)(2,1)S(1)} %get-tuple-element.108.h_ref, f32[1,512]{1,0:T(1,128)S(1)} %get-tuple-element.109.col_cell_ref), custom_call_target="tpu_custom_call" | custom-call | flops 100000000 | bytes 262144 | tf_op jit(solution)/shard_map/cover/pallas_call | solution.py:519
  48.1 3.4 %collective-permute-done.9.refs_5_.refs_1_ = f32[136,512]{1,0:T(8,128)S(1)} collective-permute-done((f32[136,512]{1,0:T(8,128)S(1)}, f32[136,512]{1,0:T(8,128)S(1)}, u32[]{:S(2)}, u32[]{:S(2)}) %collective-permute-start.9) | collective-permute-done | bytes 278560 | tf_op jit(solution)/shard_map/ppermute | solution.py:626
  51.5 0.9 gather_split.1
  52.4 2.4 %rest_products.3 = f32[2,256,1024]{2,1,0:T(8,128)S(1)} custom-call(s32[2]{0:T(128)S(1)} %pad_add_fusion.place_ref, f32[1024,512]{1,0:T(8,128)S(1)} %copy-done, bf16[1024,512]{1,0:T(8,128)(2,1)S(1)} %get-tuple-element.126.high_ref, bf16[1024,512]{1,0:T(8,128)(2,1)S(1)} %get-tuple-element.127.low_ref), custom_call_target="tpu_custom_call" | custom-call | flops 100000000 | bytes 262144 | tf_op jit(solution)/shard_map/rest_products/pallas_call | solution.py:519
  54.9 0.6 collective-permute-start.15
  55.5 1.5 %collective-permute-start.13 = (f32[4,32,640]{2,1,0:T(8,128)S(1)}, f32[4,32,640]{2,1,0:T(8,128)S(1)}, u32[]{:S(2)}, u32[]{:S(2)}) collective-permute-start(f32[4,32,640]{2,1,0:T(8,128)S(1)} %pad_maximum_fusion.1.refs_0_), channel_id=1, source_target_pairs={{0,6},{1,7},{2,4},{3,5},{4,2},{5,3},{6,0},{7,1},{8,14},{9,15},{10,... | collective-permute-start | bytes 983048 | tf_op jit(solution)/shard_map/ppermute | solution.py:740
  57.5 1.5 %collective-permute-start.11 = (f32[4,32,640]{2,1,0:T(8,128)S(1)}, f32[4,32,640]{2,1,0:T(8,128)S(1)}, u32[]{:S(2)}, u32[]{:S(2)}) collective-permute-start(f32[4,32,640]{2,1,0:T(8,128)S(1)} %pad_maximum_fusion.1.refs_0_), channel_id=1, source_target_pairs={{0,4},{4,0},{8,12},{12,8},{16,20},{20,16},{24,28},{28,24},{1,5},{5... | collective-permute-start | bytes 983048 | tf_op jit(solution)/shard_map/ppermute | solution.py:570
  59.0 1.6 %rest_products.4.refs_5_ = f32[1,256,1024]{2,1,0:T(8,128)S(1)} custom-call(s32[2]{0:T(128)S(1)} %pad_add_fusion.place_ref, f32[1024,512]{1,0:T(8,128)S(1)} %copy-done, bf16[1024,512]{1,0:T(8,128)(2,1)S(1)} %get-tuple-element.126.high_ref, bf16[1024,512]{1,0:T(8,128)(2,1)S(1)} %get-tuple-element.127.low_ref), custom_call_target="tpu_custom_call" | custom-call | flops 100000000 | bytes 262144 | tf_op jit(solution)/shard_map/rest_products/pallas_call | solution.py:519
  60.5 11.3 %cover.7.refs_4_ = f32[256,512]{1,0:T(8,128)S(1)} custom-call(bf16[8,256,512]{2,1,0:T(8,128)(2,1)S(1)} %get-tuple-element.124.t_ref, f32[256,1]{1,0:T(8,128)S(1)} %get-tuple-element.125.row_cell_ref, f32[272,512]{1,0:T(8,128)S(1)} %collective-permute-done.8.refs_4_.refs_0_, f32[136,512]{1,0:T(8,128)S(1)} %collective-permute-done.9.refs_5_.refs_1_, ...), custom_call_target="tpu_custom_call" | custom-call | flops 100000000 | bytes 262144 | tf_op jit(solution)/shard_map/cover/pallas_call | solution.py:519
  71.8 1.6 %rest_products.5 = f32[1,256,1024]{2,1,0:T(8,128)S(1)} custom-call(s32[2]{0:T(128)S(1)} %pad_add_fusion.place_ref, f32[1024,512]{1,0:T(8,128)S(1)} %copy-done, bf16[1024,512]{1,0:T(8,128)(2,1)S(1)} %get-tuple-element.126.high_ref, bf16[1024,512]{1,0:T(8,128)(2,1)S(1)} %get-tuple-element.127.low_ref, f32[2,256,1024]{2,1,0:T(8,128)S(1)} %collective-permute-done.14.refs_0_.refs_6_), custom_call_target="tpu_custom_call" | custom-call | flops 100000000 | bytes 262144 | tf_op jit(solution)/shard_map/rest_products/pallas_call | solution.py:519
  74.1 1.5 %collective-permute-start.16 = (f32[1,256,1024]{2,1,0:T(8,128)S(1)}, f32[1,256,1024]{2,1,0:T(8,128)S(1)}, u32[]{:S(2)}, u32[]{:S(2)}) collective-permute-start(f32[1,256,1024]{2,1,0:T(8,128)S(1)} %rest_products.5), channel_id=1, source_target_pairs={{0,2},{1,3},{2,0},{3,1},{4,6},{5,7},{6,4},{7,5},{8,10},{9,11},{10,... | collective-permute-start | bytes 3145736 | tf_op jit(solution)/shard_map/ppermute | solution.py:570
  76.1 32.3 %factor.1 = (bf16[1024,1024]{1,0:T(8,128)(2,1)S(1)}, bf16[1024,1024]{1,0:T(8,128)(2,1)S(1)}, bf16[1024,128]{1,0:T(8,128)(2,1)S(1)}, bf16[1024,128]{1,0:T(8,128)(2,1)S(1)}) custom-call(s32[2]{0:T(128)S(1)} %pad_add_fusion.place_ref, f32[4,32,640]{2,1,0:T(8,128)S(1)} %pad_maximum_fusion.1.refs_0_, f32[4,32,640]{2,1,0:T(8,128)S(1)} %collective-permute-done.11.refs_1_, ...), custom_call_target="tpu_custom_call" | custom-call | flops 49999998976 | bytes 8388608 | tf_op jit(solution)/shard_map/factor/pallas_call | solution.py:461
  108.4 6.2 %solve.1 = f32[256,1024]{1,0:T(8,128)} custom-call(s32[2]{0:T(128)S(1)} %pad_add_fusion.place_ref, f32[32,512]{1,0:T(8,128)S(1)} %get-tuple-element.99.refs_0_, f32[224,128]{1,0:T(8,128)S(1)} %cover.4.refs_1_, f32[96,384]{1,0:T(8,128)S(1)} %cover.5.refs_2_, f32[128,384]{1,0:T(8,128)S(1)} %cover.6.refs_3_, f32[256,512]{1,0:T(8,128)S(1)} %cover.7.refs_4_, ...), custom_call_target="tpu_custom_call" | custom-call | flops 100000000 | bytes 262144 | tf_op jit(solution)/shard_map/solve/pallas_call | solution.py:519
  (37 shorter events, 3.3 us)
Async XLA Ops:
  2.8 15.5 %collective-permute-start.2 = (f32[136,512]{1,0:T(8,128)S(1)}, f32[136,512]{1,0:T(8,128)S(1)}, u32[]{:S(2)}, u32[]{:S(2)}) collective-permute-start(f32[136,512]{1,0:T(8,128)S(1)} %pad_maximum_fusion.2.refs_0_), channel_id=1, source_target_pairs={{4,0},{0,4},{12,8},{8,12},{20,16},{16,20},{28,24},{24,28},{5,1},{1... | collective-permute-start | bytes 835592 | tf_op jit(solution)/shard_map/ppermute | solution.py:626
  5.8 14.0 %collective-permute-start.1 = (f32[136,512]{1,0:T(8,128)S(1)}, f32[136,512]{1,0:T(8,128)S(1)}, u32[]{:S(2)}, u32[]{:S(2)}) collective-permute-start(f32[136,512]{1,0:T(8,128)S(1)} %pad_maximum_fusion.2.refs_0_), channel_id=1, source_target_pairs={{8,0},{12,4},{4,8},{0,12},{24,16},{28,20},{20,24},{16,28},{9,1},{1... | collective-permute-start | bytes 835592 | tf_op jit(solution)/shard_map/ppermute | solution.py:626
  7.3 14.7 %collective-permute-start = (f32[136,512]{1,0:T(8,128)S(1)}, f32[136,512]{1,0:T(8,128)S(1)}, u32[]{:S(2)}, u32[]{:S(2)}) collective-permute-start(f32[136,512]{1,0:T(8,128)S(1)} %pad_maximum_fusion.2.refs_0_), channel_id=1, source_target_pairs={{0,16},{4,20},{8,24},{12,28},{16,0},{20,4},{24,8},{28,12},{1,17},{... | collective-permute-start | bytes 835592 | tf_op jit(solution)/shard_map/ppermute | solution.py:570
  23.3 6.0 %collective-permute-start.3 = (f32[32,640]{1,0:T(8,128)S(1)}, f32[32,640]{1,0:T(8,128)S(1)}, u32[]{:S(2)}, u32[]{:S(2)}) collective-permute-start(f32[32,640]{1,0:T(8,128)S(1)} %get-tuple-element.88), channel_id=1, source_target_pairs={{0,1},{1,0},{2,3},{3,2},{4,5},{5,4},{6,7},{7,6},{8,9},{9,8},{10,11... | collective-permute-start | bytes 245768 | tf_op jit(solution)/shard_map/ppermute | solution.py:570
  23.4 5.9 %collective-permute-start.4 = (f32[32,640]{1,0:T(8,128)S(1)}, f32[32,640]{1,0:T(8,128)S(1)}, u32[]{:S(2)}, u32[]{:S(2)}) collective-permute-start(f32[32,640]{1,0:T(8,128)S(1)} %get-tuple-element.89), channel_id=1, source_target_pairs={{0,2},{1,3},{2,0},{3,1},{4,6},{5,7},{6,4},{7,5},{8,10},{9,11},{10,... | collective-permute-start | bytes 245768 | tf_op jit(solution)/shard_map/ppermute | solution.py:570
  25.0 4.7 %collective-permute-start.5 = (f32[32,640]{1,0:T(8,128)S(1)}, f32[32,640]{1,0:T(8,128)S(1)}, u32[]{:S(2)}, u32[]{:S(2)}) collective-permute-start(f32[32,640]{1,0:T(8,128)S(1)} %get-tuple-element.90), channel_id=1, source_target_pairs={{0,3},{1,2},{2,1},{3,0},{4,7},{5,6},{6,5},{7,4},{8,11},{9,10},{10,... | collective-permute-start | bytes 245768 | tf_op jit(solution)/shard_map/ppermute | solution.py:570
  25.3 26.2 %collective-permute-start.8 = (f32[272,512]{1,0:T(8,128)S(1)}, f32[272,512]{1,0:T(8,128)S(1)}, u32[]{:S(2)}, u32[]{:S(2)}) collective-permute-start(f32[272,512]{1,0:T(8,128)S(1)} %pad_maximum_fusion), channel_id=1, source_target_pairs={{12,0},{8,4},{0,8},{4,12},{28,16},{24,20},{16,24},{20,28},{13,1},{... | collective-permute-start | bytes 1671176 | tf_op jit(solution)/shard_map/ppermute | solution.py:626
  29.8 13.8 %collective-permute-start.6 = (f32[1,32,640]{2,1,0:T(8,128)S(1)}, f32[1,32,640]{2,1,0:T(8,128)S(1)}, u32[]{:S(2)}, u32[]{:S(2)}) collective-permute-start(f32[1,32,640]{2,1,0:T(8,128)S(1)} %subtract_bitcast_fusion), channel_id=1, source_target_pairs={{0,8},{4,12},{8,0},{12,4},{16,24},{20,28},{24,16},{28,20},{1,9},{5... | collective-permute-start | bytes 245768 | tf_op jit(solution)/shard_map/ppermute | solution.py:570
  31.9 16.3 %collective-permute-start.10 = (f32[136,512]{1,0:T(8,128)S(1)}, f32[136,512]{1,0:T(8,128)S(1)}, u32[]{:S(2)}, u32[]{:S(2)}) collective-permute-start(f32[136,512]{1,0:T(8,128)S(1)} %collective-permute-done.refs_1_), channel_id=1, source_target_pairs={{4,0},{0,4},{12,8},{8,12},{20,16},{16,20},{28,24},{24,28},{5,1},{1... | collective-permute-start | bytes 835592 | tf_op jit(solution)/shard_map/ppermute | solution.py:626
  32.4 19.1 %collective-permute-start.9 = (f32[136,512]{1,0:T(8,128)S(1)}, f32[136,512]{1,0:T(8,128)S(1)}, u32[]{:S(2)}, u32[]{:S(2)}) collective-permute-start(f32[136,512]{1,0:T(8,128)S(1)} %collective-permute-done.refs_1_), channel_id=1, source_target_pairs={{8,0},{12,4},{4,8},{0,12},{24,16},{28,20},{20,24},{16,28},{9,1},{1... | collective-permute-start | bytes 835592 | tf_op jit(solution)/shard_map/ppermute | solution.py:626
  43.6 11.2 %collective-permute-start.7 = (f32[2,32,640]{2,1,0:T(8,128)S(1)}, f32[2,32,640]{2,1,0:T(8,128)S(1)}, u32[]{:S(2)}, u32[]{:S(2)}) collective-permute-start(f32[2,32,640]{2,1,0:T(8,128)S(1)} %pad_maximum_fusion.3), channel_id=1, source_target_pairs={{0,16},{4,20},{8,24},{12,28},{16,0},{20,4},{24,8},{28,12},{1,17},{... | collective-permute-start | bytes 491528 | tf_op jit(solution)/shard_map/ppermute | solution.py:570
  48.1 4.3 %copy-start = (f32[1024,512]{1,0:T(8,128)S(1)}, f32[1024,512]{1,0:T(8,128)}, u32[]{:S(2)}) copy-start(f32[1024,512]{1,0:T(8,128)} %prior_ref.5) | copy-start | bytes 6291460
  54.8 17.0 %collective-permute-start.14 = (f32[2,256,1024]{2,1,0:T(8,128)S(1)}, f32[2,256,1024]{2,1,0:T(8,128)S(1)}, u32[]{:S(2)}, u32[]{:S(2)}) collective-permute-start(f32[2,256,1024]{2,1,0:T(8,128)S(1)} %rest_products.3), channel_id=1, source_target_pairs={{0,1},{1,0},{2,3},{3,2},{4,5},{5,4},{6,7},{7,6},{8,9},{9,8},{10,11... | collective-permute-start | bytes 6291464 | tf_op jit(solution)/shard_map/ppermute | solution.py:570
  54.9 18.5 %collective-permute-start.15 = (f32[4,32,640]{2,1,0:T(8,128)S(1)}, f32[4,32,640]{2,1,0:T(8,128)S(1)}, u32[]{:S(2)}, u32[]{:S(2)}) collective-permute-start(f32[4,32,640]{2,1,0:T(8,128)S(1)} %pad_maximum_fusion.1.refs_0_), channel_id=1, source_target_pairs={{0,1},{1,0},{2,3},{3,2},{4,5},{5,4},{6,7},{7,6},{8,9},{9,8},{10,11... | collective-permute-start | bytes 983048 | tf_op jit(solution)/shard_map/ppermute | solution.py:570
  55.5 18.0 %collective-permute-start.13 = (f32[4,32,640]{2,1,0:T(8,128)S(1)}, f32[4,32,640]{2,1,0:T(8,128)S(1)}, u32[]{:S(2)}, u32[]{:S(2)}) collective-permute-start(f32[4,32,640]{2,1,0:T(8,128)S(1)} %pad_maximum_fusion.1.refs_0_), channel_id=1, source_target_pairs={{0,6},{1,7},{2,4},{3,5},{4,2},{5,3},{6,0},{7,1},{8,14},{9,15},{10,... | collective-permute-start | bytes 983048 | tf_op jit(solution)/shard_map/ppermute | solution.py:740
  57.0 16.5 %collective-permute-start.12 = (f32[4,32,640]{2,1,0:T(8,128)S(1)}, f32[4,32,640]{2,1,0:T(8,128)S(1)}, u32[]{:S(2)}, u32[]{:S(2)}) collective-permute-start(f32[4,32,640]{2,1,0:T(8,128)S(1)} %pad_maximum_fusion.1.refs_0_), channel_id=1, source_target_pairs={{0,2},{1,3},{2,0},{3,1},{4,6},{5,7},{6,4},{7,5},{8,10},{9,11},{10,... | collective-permute-start | bytes 983048 | tf_op jit(solution)/shard_map/ppermute | solution.py:570
  57.5 16.0 %collective-permute-start.11 = (f32[4,32,640]{2,1,0:T(8,128)S(1)}, f32[4,32,640]{2,1,0:T(8,128)S(1)}, u32[]{:S(2)}, u32[]{:S(2)}) collective-permute-start(f32[4,32,640]{2,1,0:T(8,128)S(1)} %pad_maximum_fusion.1.refs_0_), channel_id=1, source_target_pairs={{0,4},{4,0},{8,12},{12,8},{16,20},{20,16},{24,28},{28,24},{1,5},{5... | collective-permute-start | bytes 983048 | tf_op jit(solution)/shard_map/ppermute | solution.py:570
  73.4 2.2 %collective-permute-start.17 = (f32[4,32,640]{2,1,0:T(8,128)S(1)}, f32[4,32,640]{2,1,0:T(8,128)S(1)}, u32[]{:S(2)}, u32[]{:S(2)}) collective-permute-start(f32[4,32,640]{2,1,0:T(8,128)S(1)} %collective-permute-done.11.refs_1_), channel_id=1, source_target_pairs={{0,1},{1,0},{2,3},{3,2},{4,5},{5,4},{6,7},{7,6},{8,9},{9,8},{10,11... | collective-permute-start | bytes 983048 | tf_op jit(solution)/shard_map/ppermute | solution.py:570
  73.5 2.1 %collective-permute-start.18 = (f32[4,32,640]{2,1,0:T(8,128)S(1)}, f32[4,32,640]{2,1,0:T(8,128)S(1)}, u32[]{:S(2)}, u32[]{:S(2)}) collective-permute-start(f32[4,32,640]{2,1,0:T(8,128)S(1)} %collective-permute-done.12.refs_2_), channel_id=1, source_target_pairs={{0,1},{1,0},{2,3},{3,2},{4,5},{5,4},{6,7},{7,6},{8,9},{9,8},{10,11... | collective-permute-start | bytes 983048 | tf_op jit(solution)/shard_map/ppermute | solution.py:570
  74.0 2.1 %collective-permute-start.19 = (f32[4,32,640]{2,1,0:T(8,128)S(1)}, f32[4,32,640]{2,1,0:T(8,128)S(1)}, u32[]{:S(2)}, u32[]{:S(2)}) collective-permute-start(f32[4,32,640]{2,1,0:T(8,128)S(1)} %collective-permute-done.13.refs_3_), channel_id=1, source_target_pairs={{0,1},{1,0},{2,3},{3,2},{4,5},{5,4},{6,7},{7,6},{8,9},{9,8},{10,11... | collective-permute-start | bytes 983048 | tf_op jit(solution)/shard_map/ppermute | solution.py:570
  74.1 34.3 %collective-permute-start.16 = (f32[1,256,1024]{2,1,0:T(8,128)S(1)}, f32[1,256,1024]{2,1,0:T(8,128)S(1)}, u32[]{:S(2)}, u32[]{:S(2)}) collective-permute-start(f32[1,256,1024]{2,1,0:T(8,128)S(1)} %rest_products.5), channel_id=1, source_target_pairs={{0,2},{1,3},{2,0},{3,1},{4,6},{5,7},{6,4},{7,5},{8,10},{9,11},{10,... | collective-permute-start | bytes 3145736 | tf_op jit(solution)/shard_map/ppermute | solution.py:570

commit v10 on v9

--- a/solution.py
+++ b/solution.py
@@ -394,8 +394,7 @@
 
 
 def block_order(r):
-    own = [r, r ^ 4, turned(r, 1), turned(r, 2), turned(r, 3)]
-    return own + [turned(r, 3) ^ 4, turned(r, 1) ^ 4, turned(r, 2) ^ 4]
+    return [r, r ^ 4, turned(r, 1), turned(r, 2), turned(r, 3), r ^ 5, r ^ 6, r ^ 7]
 
 
 def makes_own(r):
@@ -653,7 +652,7 @@
         [pltpu.VMEM((NB, 5 * NB), F32)],
         "fold_products",
     )
-    shares, own, far = lax.optimization_barrier((shares, own, far))
+    shares, own, far, one = lax.optimization_barrier((shares, own, far, one))
 
     def beside(operands, transfer, work):
         operands, held = lax.optimization_barrier((operands, table))
@@ -687,7 +686,8 @@
         lambda shares: [swap(share, "panel", m) for m, share in zip((1, 2, 3), shares[1:])],
         lead_cover,
     )
-    rest = [turn(jnp.concatenate([own, far], 0), 3), turn(far, 1), turn(far, 2)]
+    from_x = swap(jnp.concatenate([one, far], 0), "row", 1)
+    from_z = swap(far, "row", 2)
     shard = folded - (shares[0] + sums[0] + sums[1] + sums[2])
 
     def rest_part(panel_prior, turns, plus=()):
@@ -711,7 +711,9 @@
 
     middle = quarter_rows // 2
 
-    def beside_far_z(_, held):
+    def beside_far_z(x, held):
+        x, blocks = lax.optimization_barrier((x, [from_x, from_z]))
+        rest = blocks + [swap(blocks[0][blocks[0].shape[0] // 2 :], "row", 2)]
         cover = later_cover(held, middle, quarter_rows - middle)
         cover, blocks = lax.optimization_barrier((cover, rest))
         panel_prior = vmem_call(
@@ -721,7 +723,7 @@
             [own, far, one, two, *blocks],
             name="gather_split",
         )
-        return cover, panel_prior, rest_part(panel_prior, (3, 1))
+        return cover, panel_prior, rest_part(panel_prior, (3, 1)), rest
 
     shard = shard[None]
     near_rows, cover_first = beside(
@@ -730,7 +732,7 @@
         lambda _, held: later_cover(held, per_device, middle - per_device),
     )
     near_rows = jnp.concatenate([shard, near_rows], 0)
-    far_rows, (cover_second, panel_prior, for_core) = beside(
+    far_rows, (cover_second, panel_prior, for_core, rest) = beside(
         near_rows, lambda x: swap(x, "row", 4), beside_far_z
     )
     held_rows = jnp.concatenate([near_rows, far_rows], 0)

time: 115 us -> 112 us (0.974)
  waiting for transfers between devices: 15.1 us -> 11.6 us
    ppermute x5 -> x2, waiting for transfers between devices: 4.88 us -> 1.51 us  [turn(): return lax.ppermute(block, 'row', [(turned(d, k), d) for d in range(8)])]
    ppermute x14 -> x17, starting transfers between devices: 11.8 us -> 15 us  [swap(): lax.ppermute(block, axis, [(i, i ^ bit) for i in range(lax.axis_size(axis...]
    ppermute x5 -> x2, starting transfers between devices: 6.63 us -> 4.55 us  [turn(): return lax.ppermute(block, 'row', [(turned(d, k), d) for d in range(8)])]
    ppermute x14 -> x17, waiting for transfers between devices: 10.2 us -> 10.1 us  [swap(): lax.ppermute(block, axis, [(i, i ^ bit) for i in range(lax.axis_size(axis...]
  transfers between devices with their start and end apart: 20 -> 20, of which waited for: 6 -> 6; matrix products, arithmetic and copies ran while one was open for 0% -> 0% of each run, Pallas kernels for 60% -> 61%
where the time goes in v10:
time: 112 us
  Pallas kernels  76.3 us (68%)
  starting transfers between devices  21.1 us (19%)
  waiting for transfers between devices  11.6 us (10%)
  other arithmetic  1.81 us (2%)
  local copies, waits for them, and re-layouts  1.16 us (1%)
    pallas_call x11, Pallas kernels, vmem_call(): pl.pallas_call(kernel, out_shape=out_shape, in_specs=[pl.BlockSpec(memory...  39.2 us
    pallas_call x1, Pallas kernels, factor(): pl.pallas_call(kernel, out_shape=[jax.ShapeDtypeStruct((n, n), BF)] * 2 +...  32.3 us
    ppermute x17, starting transfers between devices, swap(): lax.ppermute(block, axis, [(i, i ^ bit) for i in range(lax.axis_size(axis...  15 us
    ppermute x17, waiting for transfers between devices, swap(): lax.ppermute(block, axis, [(i, i ^ bit) for i in range(lax.axis_size(axis...  10.1 us
    pallas_call x1, Pallas kernels, row_table(): pl.pallas_call(row_table_kernel, out_shape=[jax.ShapeDtypeStruct((8, rows...  4.85 us
    ppermute x2, starting transfers between devices, turn(): return lax.ppermute(block, 'row', [(turned(d, k), d) for d in range(8)])  4.55 us
  transfers between devices with their start and end apart: 20, of which 6 were waited for; matrix products, arithmetic and copies ran while one was open for 0% of the time, Pallas kernels for 61%

profile of v10, /device:TPU:0, one launch (start us, length us, event | category | flops | bytes accessed | tf_op | source)
XLA Modules:
  0.0 112.2 jit_solution(2836066381821972825)
XLA Ops:
  0.0 0.7 fusion.1
  0.7 0.9 convert_add_fusion.1
  1.8 1.0 slice.20
  2.8 3.0 %collective-permute-start.2 = (f32[136,512]{1,0:T(8,128)S(1)}, f32[136,512]{1,0:T(8,128)S(1)}, u32[]{:S(2)}, u32[]{:S(2)}) collective-permute-start(f32[136,512]{1,0:T(8,128)S(1)} %pad_maximum_fusion.2.refs_0_), channel_id=1, source_target_pairs={{4,0},{0,4},{12,8},{8,12},{20,16},{16,20},{28,24},{24,28},{5,1},{1... | collective-permute-start | bytes 835592 | tf_op jit(solution)/shard_map/ppermute | solution.py:625
  5.8 1.5 %collective-permute-start.1 = (f32[136,512]{1,0:T(8,128)S(1)}, f32[136,512]{1,0:T(8,128)S(1)}, u32[]{:S(2)}, u32[]{:S(2)}) collective-permute-start(f32[136,512]{1,0:T(8,128)S(1)} %pad_maximum_fusion.2.refs_0_), channel_id=1, source_target_pairs={{8,0},{12,4},{4,8},{0,12},{24,16},{28,20},{20,24},{16,28},{9,1},{1... | collective-permute-start | bytes 835592 | tf_op jit(solution)/shard_map/ppermute | solution.py:625
  7.3 2.6 %collective-permute-start = (f32[136,512]{1,0:T(8,128)S(1)}, f32[136,512]{1,0:T(8,128)S(1)}, u32[]{:S(2)}, u32[]{:S(2)}) collective-permute-start(f32[136,512]{1,0:T(8,128)S(1)} %pad_maximum_fusion.2.refs_0_), channel_id=1, source_target_pairs={{0,16},{4,20},{8,24},{12,28},{16,0},{20,4},{24,8},{28,12},{1,17},{... | collective-permute-start | bytes 835592 | tf_op jit(solution)/shard_map/ppermute | solution.py:569
  9.9 4.8 %row_table.1 = (bf16[8,256,512]{2,1,0:T(8,128)(2,1)S(1)}, f32[256,1]{1,0:T(8,128)S(1)}) custom-call(f32[2,16,256]{2,1,0:T(8,128)S(1)} %fusion.row_ref), custom_call_target="tpu_custom_call" | custom-call | flops 100000000 | bytes 262144 | tf_op jit(solution)/shard_map/row_table/pallas_call | solution.py:147
  14.8 3.4 %cover.4.refs_1_ = f32[224,128]{1,0:T(8,128)S(1)} custom-call(bf16[8,256,512]{2,1,0:T(8,128)(2,1)S(1)} %get-tuple-element.133.t_ref, f32[256,1]{1,0:T(8,128)S(1)} %get-tuple-element.134.row_cell_ref, f32[136,512]{1,0:T(8,128)S(1)} %pad_maximum_fusion.2.refs_0_), custom_call_target="tpu_custom_call" | custom-call | flops 100000000 | bytes 262144 | tf_op jit(solution)/shard_map/cover/pallas_call | solution.py:518
  18.3 1.5 %collective-permute-done.1.refs_2_ = f32[136,512]{1,0:T(8,128)S(1)} collective-permute-done((f32[136,512]{1,0:T(8,128)S(1)}, f32[136,512]{1,0:T(8,128)S(1)}, u32[]{:S(2)}, u32[]{:S(2)}) %collective-permute-start.1) | collective-permute-done | bytes 278560 | tf_op jit(solution)/shard_map/ppermute | solution.py:625
  19.8 2.3 %collective-permute-done.refs_1_ = f32[136,512]{1,0:T(8,128)S(1)} collective-permute-done((f32[136,512]{1,0:T(8,128)S(1)}, f32[136,512]{1,0:T(8,128)S(1)}, u32[]{:S(2)}, u32[]{:S(2)}) %collective-permute-start) | collective-permute-done | bytes 278560 | tf_op jit(solution)/shard_map/ppermute | solution.py:569
  22.1 1.2 %fold_products.1 = (f32[32,640]{1,0:T(8,128)S(1)}, f32[32,640]{1,0:T(8,128)S(1)}, f32[32,640]{1,0:T(8,128)S(1)}, f32[32,640]{1,0:T(8,128)S(1)}) custom-call(s32[2]{0:T(128)S(1)} %pad_add_fusion.place_ref, f32[136,512]{1,0:T(8,128)S(1)} %pad_maximum_fusion.2.refs_0_, f32[136,512]{1,0:T(8,128)S(1)} %collective-permute-done.refs_1_, ...), custom_call_target="tpu_custom_call" | custom-call | flops 100000000 | bytes 262144 | tf_op jit(solution)/shard_map/fold_products/pallas_call | solution.py:518
  23.4 1.6 %collective-permute-start.8 = (f32[272,512]{1,0:T(8,128)S(1)}, f32[272,512]{1,0:T(8,128)S(1)}, u32[]{:S(2)}, u32[]{:S(2)}) collective-permute-start(f32[272,512]{1,0:T(8,128)S(1)} %pad_maximum_fusion), channel_id=1, source_target_pairs={{0,4},{4,0},{8,12},{12,8},{16,20},{20,16},{24,28},{28,24},{1,5},{5... | collective-permute-start | bytes 1671176 | tf_op jit(solution)/shard_map/ppermute | solution.py:569
  25.0 1.5 %collective-permute-start.4 = (f32[32,640]{1,0:T(8,128)S(1)}, f32[32,640]{1,0:T(8,128)S(1)}, u32[]{:S(2)}, u32[]{:S(2)}) collective-permute-start(f32[32,640]{1,0:T(8,128)S(1)} %get-tuple-element.95), channel_id=1, source_target_pairs={{0,2},{1,3},{2,0},{3,1},{4,6},{5,7},{6,4},{7,5},{8,10},{9,11},{10,... | collective-permute-start | bytes 245768 | tf_op jit(solution)/shard_map/ppermute | solution.py:569
  26.8 3.4 %lead_cover.1 = (f32[32,640]{1,0:T(8,128)S(1)}, f32[32,512]{1,0:T(8,128)S(1)}, bf16[256,4096]{1,0:T(8,128)(2,1)S(1)}, f32[1,512]{1,0:T(1,128)S(1)}) custom-call(s32[2]{0:T(128)S(1)} %pad_add_fusion.place_ref, bf16[8,256,512]{2,1,0:T(8,128)(2,1)S(1)} %get-tuple-element.133.t_ref, f32[256,1]{1,0:T(8,128)S(1)} %get-tuple-element.134.row_cell_ref, ...), custom_call_target="tpu_custom_call" | custom-call | flops 100000000 | bytes 262144 | tf_op jit(solution)/shard_map/lead_cover/pallas_call | solution.py:518
  30.3 0.9 collective-permute-done.5
  31.2 1.2 %collective-permute-start.6 = (f32[1,32,640]{2,1,0:T(8,128)S(1)}, f32[1,32,640]{2,1,0:T(8,128)S(1)}, u32[]{:S(2)}, u32[]{:S(2)}) collective-permute-start(f32[1,32,640]{2,1,0:T(8,128)S(1)} %subtract_bitcast_fusion), channel_id=1, source_target_pairs={{0,8},{4,12},{8,0},{12,4},{16,24},{20,28},{24,16},{28,20},{1,9},{5... | collective-permute-start | bytes 245768 | tf_op jit(solution)/shard_map/ppermute | solution.py:569
  32.4 3.1 %cover.5.refs_2_ = f32[96,384]{1,0:T(8,128)S(1)} custom-call(bf16[8,256,512]{2,1,0:T(8,128)(2,1)S(1)} %get-tuple-element.133.t_ref, f32[256,1]{1,0:T(8,128)S(1)} %get-tuple-element.134.row_cell_ref, bf16[256,4096]{1,0:T(8,128)(2,1)S(1)} %get-tuple-element.115.h_ref, f32[1,512]{1,0:T(1,128)S(1)} %get-tuple-element.116.col_cell_ref), custom_call_target="tpu_custom_call" | custom-call | flops 100000000 | bytes 262144 | tf_op jit(solution)/shard_map/cover/pallas_call | solution.py:518
  35.5 1.9 %collective-permute-done.6 = f32[1,32,640]{2,1,0:T(8,128)S(1)} collective-permute-done((f32[1,32,640]{2,1,0:T(8,128)S(1)}, f32[1,32,640]{2,1,0:T(8,128)S(1)}, u32[]{:S(2)}, u32[]{:S(2)}) %collective-permute-start.6) | collective-permute-done | bytes 81952 | tf_op jit(solution)/shard_map/ppermute | solution.py:569
  37.8 2.7 %collective-permute-start.7 = (f32[2,32,640]{2,1,0:T(8,128)S(1)}, f32[2,32,640]{2,1,0:T(8,128)S(1)}, u32[]{:S(2)}, u32[]{:S(2)}) collective-permute-start(f32[2,32,640]{2,1,0:T(8,128)S(1)} %pad_maximum_fusion.3), channel_id=1, source_target_pairs={{0,16},{4,20},{8,24},{12,28},{16,0},{20,4},{24,8},{28,12},{1,17},{... | collective-permute-start | bytes 491528 | tf_op jit(solution)/shard_map/ppermute | solution.py:569
  40.5 4.1 %cover.6.refs_3_ = f32[128,384]{1,0:T(8,128)S(1)} custom-call(bf16[8,256,512]{2,1,0:T(8,128)(2,1)S(1)} %get-tuple-element.133.t_ref, f32[256,1]{1,0:T(8,128)S(1)} %get-tuple-element.134.row_cell_ref, bf16[256,4096]{1,0:T(8,128)(2,1)S(1)} %get-tuple-element.115.h_ref, f32[1,512]{1,0:T(1,128)S(1)} %get-tuple-element.116.col_cell_ref), custom_call_target="tpu_custom_call" | custom-call | flops 100000000 | bytes 262144 | tf_op jit(solution)/shard_map/cover/pallas_call | solution.py:518
  44.7 4.4 %collective-permute-done.10.refs_6_.refs_2_ = f32[136,512]{1,0:T(8,128)S(1)} collective-permute-done((f32[136,512]{1,0:T(8,128)S(1)}, f32[136,512]{1,0:T(8,128)S(1)}, u32[]{:S(2)}, u32[]{:S(2)}) %collective-permute-start.10) | collective-permute-done | bytes 278560 | tf_op jit(solution)/shard_map/ppermute | solution.py:569
  49.1 0.9 gather_split.1
  50.0 2.4 %rest_products.3 = f32[2,256,1024]{2,1,0:T(8,128)S(1)} custom-call(s32[2]{0:T(128)S(1)} %pad_add_fusion.place_ref, f32[1024,512]{1,0:T(8,128)S(1)} %copy-done, bf16[1024,512]{1,0:T(8,128)(2,1)S(1)} %get-tuple-element.138.high_ref, bf16[1024,512]{1,0:T(8,128)(2,1)S(1)} %get-tuple-element.139.low_ref), custom_call_target="tpu_custom_call" | custom-call | flops 100000000 | bytes 262144 | tf_op jit(solution)/shard_map/rest_products/pallas_call | solution.py:518
  52.5 0.6 collective-permute-start.15
  53.0 1.5 %collective-permute-start.13 = (f32[4,32,640]{2,1,0:T(8,128)S(1)}, f32[4,32,640]{2,1,0:T(8,128)S(1)}, u32[]{:S(2)}, u32[]{:S(2)}) collective-permute-start(f32[4,32,640]{2,1,0:T(8,128)S(1)} %pad_maximum_fusion.1.refs_0_), channel_id=1, source_target_pairs={{0,6},{1,7},{2,4},{3,5},{4,2},{5,3},{6,0},{7,1},{8,14},{9,15},{10,... | collective-permute-start | bytes 983048 | tf_op jit(solution)/shard_map/ppermute | solution.py:742
  55.0 1.5 %collective-permute-start.11 = (f32[4,32,640]{2,1,0:T(8,128)S(1)}, f32[4,32,640]{2,1,0:T(8,128)S(1)}, u32[]{:S(2)}, u32[]{:S(2)}) collective-permute-start(f32[4,32,640]{2,1,0:T(8,128)S(1)} %pad_maximum_fusion.1.refs_0_), channel_id=1, source_target_pairs={{0,4},{4,0},{8,12},{12,8},{16,20},{20,16},{24,28},{28,24},{1,5},{5... | collective-permute-start | bytes 983048 | tf_op jit(solution)/shard_map/ppermute | solution.py:569
  56.5 1.6 %rest_products.4.refs_5_ = f32[1,256,1024]{2,1,0:T(8,128)S(1)} custom-call(s32[2]{0:T(128)S(1)} %pad_add_fusion.place_ref, f32[1024,512]{1,0:T(8,128)S(1)} %copy-done, bf16[1024,512]{1,0:T(8,128)(2,1)S(1)} %get-tuple-element.138.high_ref, bf16[1024,512]{1,0:T(8,128)(2,1)S(1)} %get-tuple-element.139.low_ref), custom_call_target="tpu_custom_call" | custom-call | flops 100000000 | bytes 262144 | tf_op jit(solution)/shard_map/rest_products/pallas_call | solution.py:518
  58.1 11.3 %cover.7.refs_4_ = f32[256,512]{1,0:T(8,128)S(1)} custom-call(bf16[8,256,512]{2,1,0:T(8,128)(2,1)S(1)} %get-tuple-element.133.t_ref, f32[256,1]{1,0:T(8,128)S(1)} %get-tuple-element.134.row_cell_ref, f32[272,512]{1,0:T(8,128)S(1)} %collective-permute-done.8.refs_4_.refs_0_, f32[136,512]{1,0:T(8,128)S(1)} %collective-permute-done.9.refs_5_.refs_1_, ...), custom_call_target="tpu_custom_call" | custom-call | flops 100000000 | bytes 262144 | tf_op jit(solution)/shard_map/cover/pallas_call | solution.py:518
  69.4 1.6 %rest_products.5 = f32[1,256,1024]{2,1,0:T(8,128)S(1)} custom-call(s32[2]{0:T(128)S(1)} %pad_add_fusion.place_ref, f32[1024,512]{1,0:T(8,128)S(1)} %copy-done, bf16[1024,512]{1,0:T(8,128)(2,1)S(1)} %get-tuple-element.138.high_ref, bf16[1024,512]{1,0:T(8,128)(2,1)S(1)} %get-tuple-element.139.low_ref, f32[2,256,1024]{2,1,0:T(8,128)S(1)} %collective-permute-done.14.refs_0_.refs_6_), custom_call_target="tpu_custom_call" | custom-call | flops 100000000 | bytes 262144 | tf_op jit(solution)/shard_map/rest_products/pallas_call | solution.py:518
  71.7 1.5 %collective-permute-start.16 = (f32[1,256,1024]{2,1,0:T(8,128)S(1)}, f32[1,256,1024]{2,1,0:T(8,128)S(1)}, u32[]{:S(2)}, u32[]{:S(2)}) collective-permute-start(f32[1,256,1024]{2,1,0:T(8,128)S(1)} %rest_products.5), channel_id=1, source_target_pairs={{0,2},{1,3},{2,0},{3,1},{4,6},{5,7},{6,4},{7,5},{8,10},{9,11},{10,... | collective-permute-start | bytes 3145736 | tf_op jit(solution)/shard_map/ppermute | solution.py:569
  73.6 32.3 %factor.1 = (bf16[1024,1024]{1,0:T(8,128)(2,1)S(1)}, bf16[1024,1024]{1,0:T(8,128)(2,1)S(1)}, bf16[1024,128]{1,0:T(8,128)(2,1)S(1)}, bf16[1024,128]{1,0:T(8,128)(2,1)S(1)}) custom-call(s32[2]{0:T(128)S(1)} %pad_add_fusion.place_ref, f32[4,32,640]{2,1,0:T(8,128)S(1)} %pad_maximum_fusion.1.refs_0_, f32[4,32,640]{2,1,0:T(8,128)S(1)} %collective-permute-done.11.refs_1_, ...), custom_call_target="tpu_custom_call" | custom-call | flops 49999998976 | bytes 8388608 | tf_op jit(solution)/shard_map/factor/pallas_call | solution.py:460
  106.0 6.3 %solve.1 = f32[256,1024]{1,0:T(8,128)} custom-call(s32[2]{0:T(128)S(1)} %pad_add_fusion.place_ref, f32[32,512]{1,0:T(8,128)S(1)} %get-tuple-element.106.refs_0_, f32[224,128]{1,0:T(8,128)S(1)} %cover.4.refs_1_, f32[96,384]{1,0:T(8,128)S(1)} %cover.5.refs_2_, f32[128,384]{1,0:T(8,128)S(1)} %cover.6.refs_3_, f32[256,512]{1,0:T(8,128)S(1)} %cover.7.refs_4_, ...), custom_call_target="tpu_custom_call" | custom-call | flops 100000000 | bytes 262144 | tf_op jit(solution)/shard_map/solve/pallas_call | solution.py:518
  (38 shorter events, 2.8 us)
Async XLA Ops:
  2.8 15.5 %collective-permute-start.2 = (f32[136,512]{1,0:T(8,128)S(1)}, f32[136,512]{1,0:T(8,128)S(1)}, u32[]{:S(2)}, u32[]{:S(2)}) collective-permute-start(f32[136,512]{1,0:T(8,128)S(1)} %pad_maximum_fusion.2.refs_0_), channel_id=1, source_target_pairs={{4,0},{0,4},{12,8},{8,12},{20,16},{16,20},{28,24},{24,28},{5,1},{1... | collective-permute-start | bytes 835592 | tf_op jit(solution)/shard_map/ppermute | solution.py:625
  5.8 14.0 %collective-permute-start.1 = (f32[136,512]{1,0:T(8,128)S(1)}, f32[136,512]{1,0:T(8,128)S(1)}, u32[]{:S(2)}, u32[]{:S(2)}) collective-permute-start(f32[136,512]{1,0:T(8,128)S(1)} %pad_maximum_fusion.2.refs_0_), channel_id=1, source_target_pairs={{8,0},{12,4},{4,8},{0,12},{24,16},{28,20},{20,24},{16,28},{9,1},{1... | collective-permute-start | bytes 835592 | tf_op jit(solution)/shard_map/ppermute | solution.py:625
  7.3 14.7 %collective-permute-start = (f32[136,512]{1,0:T(8,128)S(1)}, f32[136,512]{1,0:T(8,128)S(1)}, u32[]{:S(2)}, u32[]{:S(2)}) collective-permute-start(f32[136,512]{1,0:T(8,128)S(1)} %pad_maximum_fusion.2.refs_0_), channel_id=1, source_target_pairs={{0,16},{4,20},{8,24},{12,28},{16,0},{20,4},{24,8},{28,12},{1,17},{... | collective-permute-start | bytes 835592 | tf_op jit(solution)/shard_map/ppermute | solution.py:569
  23.4 14.1 %collective-permute-start.8 = (f32[272,512]{1,0:T(8,128)S(1)}, f32[272,512]{1,0:T(8,128)S(1)}, u32[]{:S(2)}, u32[]{:S(2)}) collective-permute-start(f32[272,512]{1,0:T(8,128)S(1)} %pad_maximum_fusion), channel_id=1, source_target_pairs={{0,4},{4,0},{8,12},{12,8},{16,20},{20,16},{24,28},{28,24},{1,5},{5... | collective-permute-start | bytes 1671176 | tf_op jit(solution)/shard_map/ppermute | solution.py:569
  24.9 5.3 %collective-permute-start.3 = (f32[32,640]{1,0:T(8,128)S(1)}, f32[32,640]{1,0:T(8,128)S(1)}, u32[]{:S(2)}, u32[]{:S(2)}) collective-permute-start(f32[32,640]{1,0:T(8,128)S(1)} %get-tuple-element.94), channel_id=1, source_target_pairs={{0,1},{1,0},{2,3},{3,2},{4,5},{5,4},{6,7},{7,6},{8,9},{9,8},{10,11... | collective-permute-start | bytes 245768 | tf_op jit(solution)/shard_map/ppermute | solution.py:569
  25.0 5.3 %collective-permute-start.4 = (f32[32,640]{1,0:T(8,128)S(1)}, f32[32,640]{1,0:T(8,128)S(1)}, u32[]{:S(2)}, u32[]{:S(2)}) collective-permute-start(f32[32,640]{1,0:T(8,128)S(1)} %get-tuple-element.95), channel_id=1, source_target_pairs={{0,2},{1,3},{2,0},{3,1},{4,6},{5,7},{6,4},{7,5},{8,10},{9,11},{10,... | collective-permute-start | bytes 245768 | tf_op jit(solution)/shard_map/ppermute | solution.py:569
  26.5 4.7 %collective-permute-start.5 = (f32[32,640]{1,0:T(8,128)S(1)}, f32[32,640]{1,0:T(8,128)S(1)}, u32[]{:S(2)}, u32[]{:S(2)}) collective-permute-start(f32[32,640]{1,0:T(8,128)S(1)} %get-tuple-element.96), channel_id=1, source_target_pairs={{0,3},{1,2},{2,1},{3,0},{4,7},{5,6},{6,5},{7,4},{8,11},{9,10},{10,... | collective-permute-start | bytes 245768 | tf_op jit(solution)/shard_map/ppermute | solution.py:569
  26.8 10.6 %collective-permute-start.9 = (f32[136,512]{1,0:T(8,128)S(1)}, f32[136,512]{1,0:T(8,128)S(1)}, u32[]{:S(2)}, u32[]{:S(2)}) collective-permute-start(f32[136,512]{1,0:T(8,128)S(1)} %collective-permute-done.refs_1_), channel_id=1, source_target_pairs={{0,8},{4,12},{8,0},{12,4},{16,24},{20,28},{24,16},{28,20},{1,9},{5... | collective-permute-start | bytes 835592 | tf_op jit(solution)/shard_map/ppermute | solution.py:569
  31.2 6.2 %collective-permute-start.6 = (f32[1,32,640]{2,1,0:T(8,128)S(1)}, f32[1,32,640]{2,1,0:T(8,128)S(1)}, u32[]{:S(2)}, u32[]{:S(2)}) collective-permute-start(f32[1,32,640]{2,1,0:T(8,128)S(1)} %subtract_bitcast_fusion), channel_id=1, source_target_pairs={{0,8},{4,12},{8,0},{12,4},{16,24},{20,28},{24,16},{28,20},{1,9},{5... | collective-permute-start | bytes 245768 | tf_op jit(solution)/shard_map/ppermute | solution.py:569
  37.5 11.6 %collective-permute-start.10 = (f32[136,512]{1,0:T(8,128)S(1)}, f32[136,512]{1,0:T(8,128)S(1)}, u32[]{:S(2)}, u32[]{:S(2)}) collective-permute-start(f32[136,512]{1,0:T(8,128)S(1)} %slice.19), channel_id=1, source_target_pairs={{0,8},{4,12},{8,0},{12,4},{16,24},{20,28},{24,16},{28,20},{1,9},{5... | collective-permute-start | bytes 835592 | tf_op jit(solution)/shard_map/ppermute | solution.py:569
  37.8 14.5 %collective-permute-start.7 = (f32[2,32,640]{2,1,0:T(8,128)S(1)}, f32[2,32,640]{2,1,0:T(8,128)S(1)}, u32[]{:S(2)}, u32[]{:S(2)}) collective-permute-start(f32[2,32,640]{2,1,0:T(8,128)S(1)} %pad_maximum_fusion.3), channel_id=1, source_target_pairs={{0,16},{4,20},{8,24},{12,28},{16,0},{20,4},{24,8},{28,12},{1,17},{... | collective-permute-start | bytes 491528 | tf_op jit(solution)/shard_map/ppermute | solution.py:569
  44.7 5.3 %copy-start = (f32[1024,512]{1,0:T(8,128)S(1)}, f32[1024,512]{1,0:T(8,128)}, u32[]{:S(2)}) copy-start(f32[1024,512]{1,0:T(8,128)} %prior_ref.5) | copy-start | bytes 6291460
  52.4 17.0 %collective-permute-start.14 = (f32[2,256,1024]{2,1,0:T(8,128)S(1)}, f32[2,256,1024]{2,1,0:T(8,128)S(1)}, u32[]{:S(2)}, u32[]{:S(2)}) collective-permute-start(f32[2,256,1024]{2,1,0:T(8,128)S(1)} %rest_products.3), channel_id=1, source_target_pairs={{0,1},{1,0},{2,3},{3,2},{4,5},{5,4},{6,7},{7,6},{8,9},{9,8},{10,11... | collective-permute-start | bytes 6291464 | tf_op jit(solution)/shard_map/ppermute | solution.py:569
  52.5 18.5 %collective-permute-start.15 = (f32[4,32,640]{2,1,0:T(8,128)S(1)}, f32[4,32,640]{2,1,0:T(8,128)S(1)}, u32[]{:S(2)}, u32[]{:S(2)}) collective-permute-start(f32[4,32,640]{2,1,0:T(8,128)S(1)} %pad_maximum_fusion.1.refs_0_), channel_id=1, source_target_pairs={{0,1},{1,0},{2,3},{3,2},{4,5},{5,4},{6,7},{7,6},{8,9},{9,8},{10,11... | collective-permute-start | bytes 983048 | tf_op jit(solution)/shard_map/ppermute | solution.py:569
  53.0 17.9 %collective-permute-start.13 = (f32[4,32,640]{2,1,0:T(8,128)S(1)}, f32[4,32,640]{2,1,0:T(8,128)S(1)}, u32[]{:S(2)}, u32[]{:S(2)}) collective-permute-start(f32[4,32,640]{2,1,0:T(8,128)S(1)} %pad_maximum_fusion.1.refs_0_), channel_id=1, source_target_pairs={{0,6},{1,7},{2,4},{3,5},{4,2},{5,3},{6,0},{7,1},{8,14},{9,15},{10,... | collective-permute-start | bytes 983048 | tf_op jit(solution)/shard_map/ppermute | solution.py:742
  54.5 16.5 %collective-permute-start.12 = (f32[4,32,640]{2,1,0:T(8,128)S(1)}, f32[4,32,640]{2,1,0:T(8,128)S(1)}, u32[]{:S(2)}, u32[]{:S(2)}) collective-permute-start(f32[4,32,640]{2,1,0:T(8,128)S(1)} %pad_maximum_fusion.1.refs_0_), channel_id=1, source_target_pairs={{0,2},{1,3},{2,0},{3,1},{4,6},{5,7},{6,4},{7,5},{8,10},{9,11},{10,... | collective-permute-start | bytes 983048 | tf_op jit(solution)/shard_map/ppermute | solution.py:569
  55.0 16.0 %collective-permute-start.11 = (f32[4,32,640]{2,1,0:T(8,128)S(1)}, f32[4,32,640]{2,1,0:T(8,128)S(1)}, u32[]{:S(2)}, u32[]{:S(2)}) collective-permute-start(f32[4,32,640]{2,1,0:T(8,128)S(1)} %pad_maximum_fusion.1.refs_0_), channel_id=1, source_target_pairs={{0,4},{4,0},{8,12},{12,8},{16,20},{20,16},{24,28},{28,24},{1,5},{5... | collective-permute-start | bytes 983048 | tf_op jit(solution)/shard_map/ppermute | solution.py:569
  71.0 2.2 %collective-permute-start.17 = (f32[4,32,640]{2,1,0:T(8,128)S(1)}, f32[4,32,640]{2,1,0:T(8,128)S(1)}, u32[]{:S(2)}, u32[]{:S(2)}) collective-permute-start(f32[4,32,640]{2,1,0:T(8,128)S(1)} %collective-permute-done.11.refs_1_), channel_id=1, source_target_pairs={{0,1},{1,0},{2,3},{3,2},{4,5},{5,4},{6,7},{7,6},{8,9},{9,8},{10,11... | collective-permute-start | bytes 983048 | tf_op jit(solution)/shard_map/ppermute | solution.py:569
  71.1 2.1 %collective-permute-start.18 = (f32[4,32,640]{2,1,0:T(8,128)S(1)}, f32[4,32,640]{2,1,0:T(8,128)S(1)}, u32[]{:S(2)}, u32[]{:S(2)}) collective-permute-start(f32[4,32,640]{2,1,0:T(8,128)S(1)} %collective-permute-done.12.refs_2_), channel_id=1, source_target_pairs={{0,1},{1,0},{2,3},{3,2},{4,5},{5,4},{6,7},{7,6},{8,9},{9,8},{10,11... | collective-permute-start | bytes 983048 | tf_op jit(solution)/shard_map/ppermute | solution.py:569
  71.6 2.1 %collective-permute-start.19 = (f32[4,32,640]{2,1,0:T(8,128)S(1)}, f32[4,32,640]{2,1,0:T(8,128)S(1)}, u32[]{:S(2)}, u32[]{:S(2)}) collective-permute-start(f32[4,32,640]{2,1,0:T(8,128)S(1)} %collective-permute-done.13.refs_3_), channel_id=1, source_target_pairs={{0,1},{1,0},{2,3},{3,2},{4,5},{5,4},{6,7},{7,6},{8,9},{9,8},{10,11... | collective-permute-start | bytes 983048 | tf_op jit(solution)/shard_map/ppermute | solution.py:569
  71.7 34.3 %collective-permute-start.16 = (f32[1,256,1024]{2,1,0:T(8,128)S(1)}, f32[1,256,1024]{2,1,0:T(8,128)S(1)}, u32[]{:S(2)}, u32[]{:S(2)}) collective-permute-start(f32[1,256,1024]{2,1,0:T(8,128)S(1)} %rest_products.5), channel_id=1, source_target_pairs={{0,2},{1,3},{2,0},{3,1},{4,6},{5,7},{6,4},{7,5},{8,10},{9,11},{10,... | collective-permute-start | bytes 3145736 | tf_op jit(solution)/shard_map/ppermute | solution.py:569

commit v11 on v10

--- a/solution.py
+++ b/solution.py
@@ -13,6 +13,7 @@
 F32 = jnp.float32
 BF = jnp.bfloat16
 NT = (((1,), (1,)), ((), ()))
+NN = (((1,), (0,)), ((), ()))
 SCALE = -1.4426950408889634 / 64.0
 CENTRE = 1024.0
 
@@ -348,8 +349,8 @@
     return high, (x - high.astype(F32)).astype(BF)
 
 
-def dot3(ah, al, bh, bl):
-    dot = functools.partial(lax.dot_general, dimension_numbers=NT, preferred_element_type=F32)
+def dot3(ah, al, bh, bl, numbers=NT):
+    dot = functools.partial(lax.dot_general, dimension_numbers=numbers, preferred_element_type=F32)
     return dot(ah, bh) + (dot(ah, bl) + dot(al, bh))
 
 
@@ -488,18 +489,36 @@
         for c, s in enumerate(block_order(place_ref[0])[block : block + ref.shape[1] // NB]):
             cols = pl.ds(pl.multiple_of(s * NB, NB), NB)
             put(rows, cols, ref[:, NB * c : NB * c + NB])
-    for c in range(0, n, NB):
-        here = o_ref[:, c : c + NB]
+    wide = 2 * NB
+    inverses = []
+    for c in range(0, n, wide):
+        upper, lower = slice(c, c + NB), slice(c + NB, c + wide)
+        corner = dot3(lh_ref[lower, upper], ll_ref[lower, upper], wh_ref[upper], wl_ref[upper], NN)
+        corner = split(-dot3(wh_ref[lower], wl_ref[lower], *split(corner), NN))
+        zero = jnp.zeros((NB, NB), BF)
+        inverses.append(
+            [
+                jnp.concatenate(
+                    [
+                        jnp.concatenate([ref[upper], zero], 1),
+                        jnp.concatenate([part, ref[lower]], 1),
+                    ],
+                    0,
+                )
+                for ref, part in zip((wh_ref, wl_ref), corner)
+            ]
+        )
+    for c, inverse in zip(range(0, n, wide), inverses):
+        here = o_ref[:, c : c + wide]
         if c:
             here = here - dot3(
-                xh_ref[:, :c], xl_ref[:, :c], lh_ref[c : c + NB, :c], ll_ref[c : c + NB, :c]
+                xh_ref[:, :c], xl_ref[:, :c], lh_ref[c : c + wide, :c], ll_ref[c : c + wide, :c]
             )
-        bh, bl = split(here)
-        x = dot3(bh, bl, wh_ref[c : c + NB], wl_ref[c : c + NB])
-        o_ref[:, c : c + NB] = x
+        x = dot3(*split(here), *inverse)
+        o_ref[:, c : c + wide] = x
         xh, xl = split(x)
-        xh_ref[:, c : c + NB] = xh
-        xl_ref[:, c : c + NB] = xl
+        xh_ref[:, c : c + wide] = xh
+        xl_ref[:, c : c + wide] = xl
 
 
 def solve(place, covers, corners, parts, factors):
@@ -643,6 +662,8 @@
         )
 
     cover_own = block_cover(table, [own], per_device, NB)
+    one, cover_own = lax.optimization_barrier((one, cover_own))
+    from_x = swap(one, "row", 1)
     (far, one, two), table, cover_own = lax.optimization_barrier(((far, one, two), table, cover_own))
     shares = vmem_call(
         fold_products_kernel,
@@ -652,7 +673,7 @@
         [pltpu.VMEM((NB, 5 * NB), F32)],
         "fold_products",
     )
-    shares, own, far, one = lax.optimization_barrier((shares, own, far, one))
+    shares, own, far = lax.optimization_barrier((shares, own, far))
 
     def beside(operands, transfer, work):
         operands, held = lax.optimization_barrier((operands, table))
@@ -686,8 +707,9 @@
         lambda shares: [swap(share, "panel", m) for m, share in zip((1, 2, 3), shares[1:])],
         lead_cover,
     )
-    from_x = swap(jnp.concatenate([one, far], 0), "row", 1)
-    from_z = swap(far, "row", 2)
+    sums, from_x = lax.optimization_barrier((sums, from_x))
+    far_x = swap(far, "row", 1)
+    far_z = swap(far, "row", 2)
     shard = folded - (shares[0] + sums[0] + sums[1] + sums[2])
 
     def rest_part(panel_prior, turns, plus=()):
@@ -711,9 +733,8 @@
 
     middle = quarter_rows // 2
 
-    def beside_far_z(x, held):
-        x, blocks = lax.optimization_barrier((x, [from_x, from_z]))
-        rest = blocks + [swap(blocks[0][blocks[0].shape[0] // 2 :], "row", 2)]
+    def beside_far_z(_, held):
+        rest = [from_x, far_x, far_z, last]
         cover = later_cover(held, middle, quarter_rows - middle)
         cover, blocks = lax.optimization_barrier((cover, rest))
         panel_prior = vmem_call(
@@ -732,6 +753,8 @@
         lambda _, held: later_cover(held, per_device, middle - per_device),
     )
     near_rows = jnp.concatenate([shard, near_rows], 0)
+    cover_first, from_x, far_x, far_z = lax.optimization_barrier((cover_first, from_x, far_x, far_z))
+    last = swap(far_x, "row", 2)
     far_rows, (cover_second, panel_prior, for_core, rest) = beside(
         near_rows, lambda x: swap(x, "row", 4), beside_far_z
     )

time: 112 us -> 112 us (level)
  starting transfers between devices: 21.1 us -> 23.7 us
  waiting for transfers between devices: 11.6 us -> 9.51 us
    ppermute x17 -> x18, starting transfers between devices: 15 us -> 16.7 us  [swap(): lax.ppermute(block, axis, [(i, i ^ bit) for i in range(lax.axis_size(axis...]
    ppermute x2, waiting for transfers between devices: 1.51 us -> 0.01 us  [turn(): return lax.ppermute(block, 'row', [(turned(d, k), d) for d in range(8)])]
    ppermute x17 -> x18, waiting for transfers between devices: 10.1 us -> 9.5 us  [swap(): lax.ppermute(block, axis, [(i, i ^ bit) for i in range(lax.axis_size(axis...]
  transfers between devices with their start and end apart: 20 -> 21, of which waited for: 6 -> 5; matrix products, arithmetic and copies ran while one was open for 0% -> 0% of each run, Pallas kernels for 61% -> 63%
where the time goes in v11:
time: 112 us
  Pallas kernels  75.4 us (67%)
  starting transfers between devices  23.7 us (21%)
  waiting for transfers between devices  9.51 us (8%)
  other arithmetic  1.77 us (2%)
  local copies, waits for them, and re-layouts  1.14 us (1%)
    pallas_call x11, Pallas kernels, vmem_call(): pl.pallas_call(kernel, out_shape=out_shape, in_specs=[pl.BlockSpec(memory...  38.5 us
    pallas_call x1, Pallas kernels, factor(): pl.pallas_call(kernel, out_shape=[jax.ShapeDtypeStruct((n, n), BF)] * 2 +...  32.1 us
    ppermute x18, starting transfers between devices, swap(): lax.ppermute(block, axis, [(i, i ^ bit) for i in range(lax.axis_size(axis...  16.7 us
    ppermute x18, waiting for transfers between devices, swap(): lax.ppermute(block, axis, [(i, i ^ bit) for i in range(lax.axis_size(axis...  9.5 us
    pallas_call x1, Pallas kernels, row_table(): pl.pallas_call(row_table_kernel, out_shape=[jax.ShapeDtypeStruct((8, rows...  4.85 us
    ppermute x2, starting transfers between devices, turn(): return lax.ppermute(block, 'row', [(turned(d, k), d) for d in range(8)])  4.54 us
    ppermute x1, starting transfers between devices, across(): lax.ppermute(x, ('row', 'panel'), corner)  2.42 us
  transfers between devices with their start and end apart: 21, of which 5 were waited for; matrix products, arithmetic and copies ran while one was open for 0% of the time, Pallas kernels for 63%

profile of v11, /device:TPU:0, one launch (start us, length us, event | category | flops | bytes accessed | tf_op | source)
XLA Modules:
  0.0 111.8 jit_solution(7994182142708222288)
XLA Ops:
  0.0 0.7 fusion.1
  0.7 0.9 convert_add_fusion.1
  1.8 1.0 slice.16
  2.8 4.0 %collective-permute-start.1 = (f32[136,512]{1,0:T(8,128)S(1)}, f32[136,512]{1,0:T(8,128)S(1)}, u32[]{:S(2)}, u32[]{:S(2)}) collective-permute-start(f32[136,512]{1,0:T(8,128)S(1)} %pad_maximum_fusion.1.refs_0_), channel_id=1, source_target_pairs={{8,0},{12,4},{4,8},{0,12},{24,16},{28,20},{20,24},{16,28},{9,1},{1... | collective-permute-start | bytes 835592 | tf_op jit(solution)/shard_map/ppermute | solution.py:644
  7.3 2.6 %collective-permute-start = (f32[136,512]{1,0:T(8,128)S(1)}, f32[136,512]{1,0:T(8,128)S(1)}, u32[]{:S(2)}, u32[]{:S(2)}) collective-permute-start(f32[136,512]{1,0:T(8,128)S(1)} %pad_maximum_fusion.1.refs_0_), channel_id=1, source_target_pairs={{0,16},{4,20},{8,24},{12,28},{16,0},{20,4},{24,8},{28,12},{1,17},{... | collective-permute-start | bytes 835592 | tf_op jit(solution)/shard_map/ppermute | solution.py:588
  9.9 4.8 %row_table.1 = (bf16[8,256,512]{2,1,0:T(8,128)(2,1)S(1)}, f32[256,1]{1,0:T(8,128)S(1)}) custom-call(f32[2,16,256]{2,1,0:T(8,128)S(1)} %fusion.row_ref), custom_call_target="tpu_custom_call" | custom-call | flops 100000000 | bytes 262144 | tf_op jit(solution)/shard_map/row_table/pallas_call | solution.py:148
  14.8 3.4 %cover.4.refs_1_ = f32[224,128]{1,0:T(8,128)S(1)} custom-call(bf16[8,256,512]{2,1,0:T(8,128)(2,1)S(1)} %get-tuple-element.150.t_ref, f32[256,1]{1,0:T(8,128)S(1)} %get-tuple-element.151.row_cell_ref, f32[136,512]{1,0:T(8,128)S(1)} %pad_maximum_fusion.1.refs_0_), custom_call_target="tpu_custom_call" | custom-call | flops 100000000 | bytes 262144 | tf_op jit(solution)/shard_map/cover/pallas_call | solution.py:537
  18.2 1.6 %collective-permute-start.6 = (f32[136,512]{1,0:T(8,128)S(1)}, f32[136,512]{1,0:T(8,128)}, u32[]{:S(2)}, u32[]{:S(2)}) collective-permute-start(f32[136,512]{1,0:T(8,128)S(1)} %collective-permute-done.1.refs_2_), channel_id=1, source_target_pairs={{0,4},{4,0},{8,12},{12,8},{16,20},{20,16},{24,28},{28,24},{1,5},{5... | collective-permute-start | bytes 835592 | tf_op jit(solution)/shard_map/ppermute | solution.py:588
  19.8 2.3 %collective-permute-done.refs_1_ = f32[136,512]{1,0:T(8,128)S(1)} collective-permute-done((f32[136,512]{1,0:T(8,128)S(1)}, f32[136,512]{1,0:T(8,128)S(1)}, u32[]{:S(2)}, u32[]{:S(2)}) %collective-permute-start) | collective-permute-done | bytes 278560 | tf_op jit(solution)/shard_map/ppermute | solution.py:588
  22.1 1.2 %fold_products.1 = (f32[32,640]{1,0:T(8,128)S(1)}, f32[32,640]{1,0:T(8,128)S(1)}, f32[32,640]{1,0:T(8,128)S(1)}, f32[32,640]{1,0:T(8,128)S(1)}) custom-call(s32[2]{0:T(128)S(1)} %pad_add_fusion.place_ref, f32[136,512]{1,0:T(8,128)S(1)} %pad_maximum_fusion.1.refs_0_, f32[136,512]{1,0:T(8,128)S(1)} %collective-permute-done.refs_1_, ...), custom_call_target="tpu_custom_call" | custom-call | flops 100000000 | bytes 262144 | tf_op jit(solution)/shard_map/fold_products/pallas_call | solution.py:537
  23.4 1.6 %collective-permute-start.4 = (f32[32,640]{1,0:T(8,128)S(1)}, f32[32,640]{1,0:T(8,128)S(1)}, u32[]{:S(2)}, u32[]{:S(2)}) collective-permute-start(f32[32,640]{1,0:T(8,128)S(1)} %get-tuple-element.106), channel_id=1, source_target_pairs={{0,2},{1,3},{2,0},{3,1},{4,6},{5,7},{6,4},{7,5},{8,10},{9,11},{10,... | collective-permute-start | bytes 245768 | tf_op jit(solution)/shard_map/ppermute | solution.py:588
  25.3 3.4 %lead_cover.1 = (f32[32,640]{1,0:T(8,128)S(1)}, f32[32,512]{1,0:T(8,128)S(1)}, bf16[256,4096]{1,0:T(8,128)(2,1)S(1)}, f32[1,512]{1,0:T(1,128)S(1)}) custom-call(s32[2]{0:T(128)S(1)} %pad_add_fusion.place_ref, bf16[8,256,512]{2,1,0:T(8,128)(2,1)S(1)} %get-tuple-element.150.t_ref, f32[256,1]{1,0:T(8,128)S(1)} %get-tuple-element.151.row_cell_ref, ...), custom_call_target="tpu_custom_call" | custom-call | flops 100000000 | bytes 262144 | tf_op jit(solution)/shard_map/lead_cover/pallas_call | solution.py:537
  28.7 1.6 %collective-permute-start.8 = (f32[136,512]{1,0:T(8,128)S(1)}, f32[136,512]{1,0:T(8,128)S(1)}, u32[]{:S(2)}, u32[]{:S(2)}) collective-permute-start(f32[136,512]{1,0:T(8,128)S(1)} %collective-permute-done.refs_1_), channel_id=1, source_target_pairs={{0,4},{4,0},{8,12},{12,8},{16,20},{20,16},{24,28},{28,24},{1,5},{5... | collective-permute-start | bytes 835592 | tf_op jit(solution)/shard_map/ppermute | solution.py:588
  30.3 2.1 %collective-permute-start.7 = (f32[1,32,640]{2,1,0:T(8,128)S(1)}, f32[1,32,640]{2,1,0:T(8,128)S(1)}, u32[]{:S(2)}, u32[]{:S(2)}) collective-permute-start(f32[1,32,640]{2,1,0:T(8,128)S(1)} %subtract_bitcast_fusion), channel_id=1, source_target_pairs={{0,8},{4,12},{8,0},{12,4},{16,24},{20,28},{24,16},{28,20},{1,9},{5... | collective-permute-start | bytes 245768 | tf_op jit(solution)/shard_map/ppermute | solution.py:588
  32.3 3.0 %cover.5.refs_2_ = f32[96,384]{1,0:T(8,128)S(1)} custom-call(bf16[8,256,512]{2,1,0:T(8,128)(2,1)S(1)} %get-tuple-element.150.t_ref, f32[256,1]{1,0:T(8,128)S(1)} %get-tuple-element.151.row_cell_ref, bf16[256,4096]{1,0:T(8,128)(2,1)S(1)} %get-tuple-element.128.h_ref, f32[1,512]{1,0:T(1,128)S(1)} %get-tuple-element.129.col_cell_ref), custom_call_target="tpu_custom_call" | custom-call | flops 100000000 | bytes 262144 | tf_op jit(solution)/shard_map/cover/pallas_call | solution.py:537
  35.4 0.6 collective-permute-done.7
  35.9 1.7 %collective-permute-done.8.refs_5_.refs_1_ = f32[136,512]{1,0:T(8,128)S(1)} collective-permute-done((f32[136,512]{1,0:T(8,128)S(1)}, f32[136,512]{1,0:T(8,128)S(1)}, u32[]{:S(2)}, u32[]{:S(2)}) %collective-permute-start.8) | collective-permute-done | bytes 278560 | tf_op jit(solution)/shard_map/ppermute | solution.py:588
  37.6 1.7 %collective-permute-start.11 = (f32[136,512]{1,0:T(8,128)S(1)}, f32[136,512]{1,0:T(8,128)S(1)}, u32[]{:S(2)}, u32[]{:S(2)}) collective-permute-start(f32[136,512]{1,0:T(8,128)S(1)} %collective-permute-done.8.refs_5_.refs_1_), channel_id=1, source_target_pairs={{0,8},{4,12},{8,0},{12,4},{16,24},{20,28},{24,16},{28,20},{1,9},{5... | collective-permute-start | bytes 835592 | tf_op jit(solution)/shard_map/ppermute | solution.py:588
  39.4 1.4 %collective-permute-start.10 = (f32[2,32,640]{2,1,0:T(8,128)S(1)}, f32[2,32,640]{2,1,0:T(8,128)S(1)}, u32[]{:S(2)}, u32[]{:S(2)}) collective-permute-start(f32[2,32,640]{2,1,0:T(8,128)S(1)} %pad_maximum_fusion.2), channel_id=1, source_target_pairs={{0,16},{4,20},{8,24},{12,28},{16,0},{20,4},{24,8},{28,12},{1,17},{... | collective-permute-start | bytes 491528 | tf_op jit(solution)/shard_map/ppermute | solution.py:588
  40.8 4.0 %cover.6.refs_3_ = f32[128,384]{1,0:T(8,128)S(1)} custom-call(bf16[8,256,512]{2,1,0:T(8,128)(2,1)S(1)} %get-tuple-element.150.t_ref, f32[256,1]{1,0:T(8,128)S(1)} %get-tuple-element.151.row_cell_ref, bf16[256,4096]{1,0:T(8,128)(2,1)S(1)} %get-tuple-element.128.h_ref, f32[1,512]{1,0:T(1,128)S(1)} %get-tuple-element.129.col_cell_ref), custom_call_target="tpu_custom_call" | custom-call | flops 100000000 | bytes 262144 | tf_op jit(solution)/shard_map/cover/pallas_call | solution.py:537
  44.8 4.5 %collective-permute-done.11.refs_7_.refs_3_ = f32[136,512]{1,0:T(8,128)S(1)} collective-permute-done((f32[136,512]{1,0:T(8,128)S(1)}, f32[136,512]{1,0:T(8,128)S(1)}, u32[]{:S(2)}, u32[]{:S(2)}) %collective-permute-start.11) | collective-permute-done | bytes 278560 | tf_op jit(solution)/shard_map/ppermute | solution.py:588
  49.3 1.3 %gather_split.1 = (bf16[1024,512]{1,0:T(8,128)(2,1)S(1)}, bf16[1024,512]{1,0:T(8,128)(2,1)S(1)}) custom-call(s32[2]{0:T(128)S(1)} %pad_add_fusion.place_ref, f32[136,512]{1,0:T(8,128)S(1)} %pad_maximum_fusion.1.refs_0_, f32[136,512]{1,0:T(8,128)S(1)} %collective-permute-done.refs_1_, f32[136,512]{1,0:T(8,128)S(1)} %collective-permute-done.1.refs_2_, ...), custom_call_target="tpu_custom_call" | custom-call | flops 100000000 | bytes 262144 | tf_op jit(solution)/shard_map/gather_split/pallas_call | solution.py:537
  50.6 2.4 %rest_products.3 = f32[2,256,1024]{2,1,0:T(8,128)S(1)} custom-call(s32[2]{0:T(128)S(1)} %pad_add_fusion.place_ref, f32[1024,512]{1,0:T(8,128)S(1)} %copy-done, bf16[1024,512]{1,0:T(8,128)(2,1)S(1)} %get-tuple-element.156.high_ref, bf16[1024,512]{1,0:T(8,128)(2,1)S(1)} %get-tuple-element.157.low_ref), custom_call_target="tpu_custom_call" | custom-call | flops 100000000 | bytes 262144 | tf_op jit(solution)/shard_map/rest_products/pallas_call | solution.py:537
  53.1 0.6 collective-permute-start.16
  53.6 2.4 %collective-permute-start.14 = (f32[4,32,640]{2,1,0:T(8,128)S(1)}, f32[4,32,640]{2,1,0:T(8,128)S(1)}, u32[]{:S(2)}, u32[]{:S(2)}) collective-permute-start(f32[4,32,640]{2,1,0:T(8,128)S(1)} %pad_maximum_fusion.refs_0_), channel_id=1, source_target_pairs={{0,6},{1,7},{2,4},{3,5},{4,2},{5,3},{6,0},{7,1},{8,14},{9,15},{10,... | collective-permute-start | bytes 983048 | tf_op jit(solution)/shard_map/ppermute | solution.py:765
  56.6 0.6 collective-permute-start.12
  57.1 1.6 %rest_products.4.refs_5_ = f32[1,256,1024]{2,1,0:T(8,128)S(1)} custom-call(s32[2]{0:T(128)S(1)} %pad_add_fusion.place_ref, f32[1024,512]{1,0:T(8,128)S(1)} %copy-done, bf16[1024,512]{1,0:T(8,128)(2,1)S(1)} %get-tuple-element.156.high_ref, bf16[1024,512]{1,0:T(8,128)(2,1)S(1)} %get-tuple-element.157.low_ref), custom_call_target="tpu_custom_call" | custom-call | flops 100000000 | bytes 262144 | tf_op jit(solution)/shard_map/rest_products/pallas_call | solution.py:537
  58.7 11.9 %cover.7.refs_4_ = f32[256,512]{1,0:T(8,128)S(1)} custom-call(bf16[8,256,512]{2,1,0:T(8,128)(2,1)S(1)} %get-tuple-element.150.t_ref, f32[256,1]{1,0:T(8,128)S(1)} %get-tuple-element.151.row_cell_ref, f32[136,512]{1,0:T(8,128)} %collective-permute-done.6.refs_4_.refs_0_, f32[136,512]{1,0:T(8,128)S(1)} %collective-permute-done.8.refs_5_.refs_1_, ...), custom_call_target="tpu_custom_call" | custom-call | flops 100000000 | bytes 262144 | tf_op jit(solution)/shard_map/cover/pallas_call | solution.py:537
  70.6 1.6 %rest_products.5 = f32[1,256,1024]{2,1,0:T(8,128)S(1)} custom-call(s32[2]{0:T(128)S(1)} %pad_add_fusion.place_ref, f32[1024,512]{1,0:T(8,128)S(1)} %copy-done, bf16[1024,512]{1,0:T(8,128)(2,1)S(1)} %get-tuple-element.156.high_ref, bf16[1024,512]{1,0:T(8,128)(2,1)S(1)} %get-tuple-element.157.low_ref, f32[2,256,1024]{2,1,0:T(8,128)S(1)} %collective-permute-done.15.refs_0_.refs_6_), custom_call_target="tpu_custom_call" | custom-call | flops 100000000 | bytes 262144 | tf_op jit(solution)/shard_map/rest_products/pallas_call | solution.py:537
  72.9 1.5 %collective-permute-start.17 = (f32[1,256,1024]{2,1,0:T(8,128)S(1)}, f32[1,256,1024]{2,1,0:T(8,128)S(1)}, u32[]{:S(2)}, u32[]{:S(2)}) collective-permute-start(f32[1,256,1024]{2,1,0:T(8,128)S(1)} %rest_products.5), channel_id=1, source_target_pairs={{0,2},{1,3},{2,0},{3,1},{4,6},{5,7},{6,4},{7,5},{8,10},{9,11},{10,... | collective-permute-start | bytes 3145736 | tf_op jit(solution)/shard_map/ppermute | solution.py:588
  74.9 32.1 %factor.1 = (bf16[1024,1024]{1,0:T(8,128)(2,1)S(1)}, bf16[1024,1024]{1,0:T(8,128)(2,1)S(1)}, bf16[1024,128]{1,0:T(8,128)(2,1)S(1)}, bf16[1024,128]{1,0:T(8,128)(2,1)S(1)}) custom-call(s32[2]{0:T(128)S(1)} %pad_add_fusion.place_ref, f32[4,32,640]{2,1,0:T(8,128)S(1)} %pad_maximum_fusion.refs_0_, f32[4,32,640]{2,1,0:T(8,128)S(1)} %collective-permute-done.12.refs_1_, ...), custom_call_target="tpu_custom_call" | custom-call | flops 49999998976 | bytes 8388608 | tf_op jit(solution)/shard_map/factor/pallas_call | solution.py:461
  107.0 4.8 %solve.1 = f32[256,1024]{1,0:T(8,128)} custom-call(s32[2]{0:T(128)S(1)} %pad_add_fusion.place_ref, f32[32,512]{1,0:T(8,128)S(1)} %get-tuple-element.116.refs_0_, f32[224,128]{1,0:T(8,128)S(1)} %cover.4.refs_1_, f32[96,384]{1,0:T(8,128)S(1)} %cover.5.refs_2_, f32[128,384]{1,0:T(8,128)S(1)} %cover.6.refs_3_, f32[256,512]{1,0:T(8,128)S(1)} %cover.7.refs_4_, ...), custom_call_target="tpu_custom_call" | custom-call | flops 100000000 | bytes 262144 | tf_op jit(solution)/shard_map/solve/pallas_call | solution.py:537
  (38 shorter events, 3.0 us)
Async XLA Ops:
  2.8 15.4 %collective-permute-start.1 = (f32[136,512]{1,0:T(8,128)S(1)}, f32[136,512]{1,0:T(8,128)S(1)}, u32[]{:S(2)}, u32[]{:S(2)}) collective-permute-start(f32[136,512]{1,0:T(8,128)S(1)} %pad_maximum_fusion.1.refs_0_), channel_id=1, source_target_pairs={{8,0},{12,4},{4,8},{0,12},{24,16},{28,20},{20,24},{16,28},{9,1},{1... | collective-permute-start | bytes 835592 | tf_op jit(solution)/shard_map/ppermute | solution.py:644
  6.8 13.0 %collective-permute-start.2 = (f32[136,512]{1,0:T(8,128)S(1)}, f32[136,512]{1,0:T(8,128)S(1)}, u32[]{:S(2)}, u32[]{:S(2)}) collective-permute-start(f32[136,512]{1,0:T(8,128)S(1)} %pad_maximum_fusion.1.refs_0_), channel_id=1, source_target_pairs={{4,0},{0,4},{12,8},{8,12},{20,16},{16,20},{28,24},{24,28},{5,1},{1... | collective-permute-start | bytes 835592 | tf_op jit(solution)/shard_map/ppermute | solution.py:644
  7.3 14.7 %collective-permute-start = (f32[136,512]{1,0:T(8,128)S(1)}, f32[136,512]{1,0:T(8,128)S(1)}, u32[]{:S(2)}, u32[]{:S(2)}) collective-permute-start(f32[136,512]{1,0:T(8,128)S(1)} %pad_maximum_fusion.1.refs_0_), channel_id=1, source_target_pairs={{0,16},{4,20},{8,24},{12,28},{16,0},{20,4},{24,8},{28,12},{1,17},{... | collective-permute-start | bytes 835592 | tf_op jit(solution)/shard_map/ppermute | solution.py:588
  18.2 12.0 %collective-permute-start.6 = (f32[136,512]{1,0:T(8,128)S(1)}, f32[136,512]{1,0:T(8,128)}, u32[]{:S(2)}, u32[]{:S(2)}) collective-permute-start(f32[136,512]{1,0:T(8,128)S(1)} %collective-permute-done.1.refs_2_), channel_id=1, source_target_pairs={{0,4},{4,0},{8,12},{12,8},{16,20},{20,16},{24,28},{28,24},{1,5},{5... | collective-permute-start | bytes 835592 | tf_op jit(solution)/shard_map/ppermute | solution.py:588
  23.3 5.3 %collective-permute-start.3 = (f32[32,640]{1,0:T(8,128)S(1)}, f32[32,640]{1,0:T(8,128)S(1)}, u32[]{:S(2)}, u32[]{:S(2)}) collective-permute-start(f32[32,640]{1,0:T(8,128)S(1)} %get-tuple-element.105), channel_id=1, source_target_pairs={{0,1},{1,0},{2,3},{3,2},{4,5},{5,4},{6,7},{7,6},{8,9},{9,8},{10,11... | collective-permute-start | bytes 245768 | tf_op jit(solution)/shard_map/ppermute | solution.py:588
  23.4 6.8 %collective-permute-start.4 = (f32[32,640]{1,0:T(8,128)S(1)}, f32[32,640]{1,0:T(8,128)S(1)}, u32[]{:S(2)}, u32[]{:S(2)}) collective-permute-start(f32[32,640]{1,0:T(8,128)S(1)} %get-tuple-element.106), channel_id=1, source_target_pairs={{0,2},{1,3},{2,0},{3,1},{4,6},{5,7},{6,4},{7,5},{8,10},{9,11},{10,... | collective-permute-start | bytes 245768 | tf_op jit(solution)/shard_map/ppermute | solution.py:588
  25.0 5.2 %collective-permute-start.5 = (f32[32,640]{1,0:T(8,128)S(1)}, f32[32,640]{1,0:T(8,128)S(1)}, u32[]{:S(2)}, u32[]{:S(2)}) collective-permute-start(f32[32,640]{1,0:T(8,128)S(1)} %get-tuple-element.107), channel_id=1, source_target_pairs={{0,3},{1,2},{2,1},{3,0},{4,7},{5,6},{6,5},{7,4},{8,11},{9,10},{10,... | collective-permute-start | bytes 245768 | tf_op jit(solution)/shard_map/ppermute | solution.py:588
  25.3 10.7 %collective-permute-start.9 = (f32[136,512]{1,0:T(8,128)S(1)}, f32[136,512]{1,0:T(8,128)S(1)}, u32[]{:S(2)}, u32[]{:S(2)}) collective-permute-start(f32[136,512]{1,0:T(8,128)S(1)} %collective-permute-done.refs_1_), channel_id=1, source_target_pairs={{0,8},{4,12},{8,0},{12,4},{16,24},{20,28},{24,16},{28,20},{1,9},{5... | collective-permute-start | bytes 835592 | tf_op jit(solution)/shard_map/ppermute | solution.py:588
  28.7 9.0 %collective-permute-start.8 = (f32[136,512]{1,0:T(8,128)S(1)}, f32[136,512]{1,0:T(8,128)S(1)}, u32[]{:S(2)}, u32[]{:S(2)}) collective-permute-start(f32[136,512]{1,0:T(8,128)S(1)} %collective-permute-done.refs_1_), channel_id=1, source_target_pairs={{0,4},{4,0},{8,12},{12,8},{16,20},{20,16},{24,28},{28,24},{1,5},{5... | collective-permute-start | bytes 835592 | tf_op jit(solution)/shard_map/ppermute | solution.py:588
  30.3 5.7 %collective-permute-start.7 = (f32[1,32,640]{2,1,0:T(8,128)S(1)}, f32[1,32,640]{2,1,0:T(8,128)S(1)}, u32[]{:S(2)}, u32[]{:S(2)}) collective-permute-start(f32[1,32,640]{2,1,0:T(8,128)S(1)} %subtract_bitcast_fusion), channel_id=1, source_target_pairs={{0,8},{4,12},{8,0},{12,4},{16,24},{20,28},{24,16},{28,20},{1,9},{5... | collective-permute-start | bytes 245768 | tf_op jit(solution)/shard_map/ppermute | solution.py:588
  37.6 11.6 %collective-permute-start.11 = (f32[136,512]{1,0:T(8,128)S(1)}, f32[136,512]{1,0:T(8,128)S(1)}, u32[]{:S(2)}, u32[]{:S(2)}) collective-permute-start(f32[136,512]{1,0:T(8,128)S(1)} %collective-permute-done.8.refs_5_.refs_1_), channel_id=1, source_target_pairs={{0,8},{4,12},{8,0},{12,4},{16,24},{20,28},{24,16},{28,20},{1,9},{5... | collective-permute-start | bytes 835592 | tf_op jit(solution)/shard_map/ppermute | solution.py:588
  39.4 13.6 %collective-permute-start.10 = (f32[2,32,640]{2,1,0:T(8,128)S(1)}, f32[2,32,640]{2,1,0:T(8,128)S(1)}, u32[]{:S(2)}, u32[]{:S(2)}) collective-permute-start(f32[2,32,640]{2,1,0:T(8,128)S(1)} %pad_maximum_fusion.2), channel_id=1, source_target_pairs={{0,16},{4,20},{8,24},{12,28},{16,0},{20,4},{24,8},{28,12},{1,17},{... | collective-permute-start | bytes 491528 | tf_op jit(solution)/shard_map/ppermute | solution.py:588
  44.8 5.8 %copy-start = (f32[1024,512]{1,0:T(8,128)S(1)}, f32[1024,512]{1,0:T(8,128)}, u32[]{:S(2)}) copy-start(f32[1024,512]{1,0:T(8,128)} %prior_ref.5) | copy-start | bytes 6291460
  53.0 17.6 %collective-permute-start.15 = (f32[2,256,1024]{2,1,0:T(8,128)S(1)}, f32[2,256,1024]{2,1,0:T(8,128)S(1)}, u32[]{:S(2)}, u32[]{:S(2)}) collective-permute-start(f32[2,256,1024]{2,1,0:T(8,128)S(1)} %rest_products.3), channel_id=1, source_target_pairs={{0,1},{1,0},{2,3},{3,2},{4,5},{5,4},{6,7},{7,6},{8,9},{9,8},{10,11... | collective-permute-start | bytes 6291464 | tf_op jit(solution)/shard_map/ppermute | solution.py:588
  53.1 19.1 %collective-permute-start.16 = (f32[4,32,640]{2,1,0:T(8,128)S(1)}, f32[4,32,640]{2,1,0:T(8,128)S(1)}, u32[]{:S(2)}, u32[]{:S(2)}) collective-permute-start(f32[4,32,640]{2,1,0:T(8,128)S(1)} %pad_maximum_fusion.refs_0_), channel_id=1, source_target_pairs={{0,1},{1,0},{2,3},{3,2},{4,5},{5,4},{6,7},{7,6},{8,9},{9,8},{10,11... | collective-permute-start | bytes 983048 | tf_op jit(solution)/shard_map/ppermute | solution.py:588
  53.6 18.6 %collective-permute-start.14 = (f32[4,32,640]{2,1,0:T(8,128)S(1)}, f32[4,32,640]{2,1,0:T(8,128)S(1)}, u32[]{:S(2)}, u32[]{:S(2)}) collective-permute-start(f32[4,32,640]{2,1,0:T(8,128)S(1)} %pad_maximum_fusion.refs_0_), channel_id=1, source_target_pairs={{0,6},{1,7},{2,4},{3,5},{4,2},{5,3},{6,0},{7,1},{8,14},{9,15},{10,... | collective-permute-start | bytes 983048 | tf_op jit(solution)/shard_map/ppermute | solution.py:765
  56.0 16.2 %collective-permute-start.13 = (f32[4,32,640]{2,1,0:T(8,128)S(1)}, f32[4,32,640]{2,1,0:T(8,128)S(1)}, u32[]{:S(2)}, u32[]{:S(2)}) collective-permute-start(f32[4,32,640]{2,1,0:T(8,128)S(1)} %pad_maximum_fusion.refs_0_), channel_id=1, source_target_pairs={{0,2},{1,3},{2,0},{3,1},{4,6},{5,7},{6,4},{7,5},{8,10},{9,11},{10,... | collective-permute-start | bytes 983048 | tf_op jit(solution)/shard_map/ppermute | solution.py:588
  56.6 15.7 %collective-permute-start.12 = (f32[4,32,640]{2,1,0:T(8,128)S(1)}, f32[4,32,640]{2,1,0:T(8,128)S(1)}, u32[]{:S(2)}, u32[]{:S(2)}) collective-permute-start(f32[4,32,640]{2,1,0:T(8,128)S(1)} %pad_maximum_fusion.refs_0_), channel_id=1, source_target_pairs={{0,4},{4,0},{8,12},{12,8},{16,20},{20,16},{24,28},{28,24},{1,5},{5... | collective-permute-start | bytes 983048 | tf_op jit(solution)/shard_map/ppermute | solution.py:588
  72.2 2.2 %collective-permute-start.18 = (f32[4,32,640]{2,1,0:T(8,128)S(1)}, f32[4,32,640]{2,1,0:T(8,128)S(1)}, u32[]{:S(2)}, u32[]{:S(2)}) collective-permute-start(f32[4,32,640]{2,1,0:T(8,128)S(1)} %collective-permute-done.12.refs_1_), channel_id=1, source_target_pairs={{0,1},{1,0},{2,3},{3,2},{4,5},{5,4},{6,7},{7,6},{8,9},{9,8},{10,11... | collective-permute-start | bytes 983048 | tf_op jit(solution)/shard_map/ppermute | solution.py:588
  72.3 2.1 %collective-permute-start.19 = (f32[4,32,640]{2,1,0:T(8,128)S(1)}, f32[4,32,640]{2,1,0:T(8,128)S(1)}, u32[]{:S(2)}, u32[]{:S(2)}) collective-permute-start(f32[4,32,640]{2,1,0:T(8,128)S(1)} %collective-permute-done.13.refs_2_), channel_id=1, source_target_pairs={{0,1},{1,0},{2,3},{3,2},{4,5},{5,4},{6,7},{7,6},{8,9},{9,8},{10,11... | collective-permute-start | bytes 983048 | tf_op jit(solution)/shard_map/ppermute | solution.py:588
  72.8 2.1 %collective-permute-start.20 = (f32[4,32,640]{2,1,0:T(8,128)S(1)}, f32[4,32,640]{2,1,0:T(8,128)S(1)}, u32[]{:S(2)}, u32[]{:S(2)}) collective-permute-start(f32[4,32,640]{2,1,0:T(8,128)S(1)} %collective-permute-done.14.refs_3_), channel_id=1, source_target_pairs={{0,1},{1,0},{2,3},{3,2},{4,5},{5,4},{6,7},{7,6},{8,9},{9,8},{10,11... | collective-permute-start | bytes 983048 | tf_op jit(solution)/shard_map/ppermute | solution.py:588
  72.9 34.1 %collective-permute-start.17 = (f32[1,256,1024]{2,1,0:T(8,128)S(1)}, f32[1,256,1024]{2,1,0:T(8,128)S(1)}, u32[]{:S(2)}, u32[]{:S(2)}) collective-permute-start(f32[1,256,1024]{2,1,0:T(8,128)S(1)} %rest_products.5), channel_id=1, source_target_pairs={{0,2},{1,3},{2,0},{3,1},{4,6},{5,7},{6,4},{7,5},{8,10},{9,11},{10,... | collective-permute-start | bytes 3145736 | tf_op jit(solution)/shard_map/ppermute | solution.py:588

commit v12 on v11

--- a/solution.py
+++ b/solution.py
@@ -754,7 +754,7 @@
     )
     near_rows = jnp.concatenate([shard, near_rows], 0)
     cover_first, from_x, far_x, far_z = lax.optimization_barrier((cover_first, from_x, far_x, far_z))
-    last = swap(far_x, "row", 2)
+    last = swap(far_z, "row", 1)
     far_rows, (cover_second, panel_prior, for_core, rest) = beside(
         near_rows, lambda x: swap(x, "row", 4), beside_far_z
     )

time: 112 us -> 109 us (0.973)
  waiting for transfers between devices: 9.51 us -> 5.73 us
    ppermute x18, waiting for transfers between devices: 9.5 us -> 5.72 us  [swap(): lax.ppermute(block, axis, [(i, i ^ bit) for i in range(lax.axis_size(axis...]
  transfers between devices with their start and end apart: 21 -> 21, of which waited for: 5 -> 5; matrix products, arithmetic and copies ran while one was open for 0% -> 0% of each run, Pallas kernels for 63% -> 65%
where the time goes in v12:
time: 109 us; the launch traced here: 108 us
  Pallas kernels  75.4 us (69%)
  starting transfers between devices  23.9 us (22%)
  waiting for transfers between devices  5.73 us (5%)
  other arithmetic  1.77 us (2%)
  local copies, waits for them, and re-layouts  1.14 us (1%)
    pallas_call x11, Pallas kernels, vmem_call(): pl.pallas_call(kernel, out_shape=out_shape, in_specs=[pl.BlockSpec(memory...  38.5 us
    pallas_call x1, Pallas kernels, factor(): pl.pallas_call(kernel, out_shape=[jax.ShapeDtypeStruct((n, n), BF)] * 2 +...  32.1 us
    ppermute x18, starting transfers between devices, swap(): lax.ppermute(block, axis, [(i, i ^ bit) for i in range(lax.axis_size(axis...  17 us
    ppermute x18, waiting for transfers between devices, swap(): lax.ppermute(block, axis, [(i, i ^ bit) for i in range(lax.axis_size(axis...  5.72 us
    pallas_call x1, Pallas kernels, row_table(): pl.pallas_call(row_table_kernel, out_shape=[jax.ShapeDtypeStruct((8, rows...  4.85 us
    ppermute x2, starting transfers between devices, turn(): return lax.ppermute(block, 'row', [(turned(d, k), d) for d in range(8)])  4.54 us
    ppermute x1, starting transfers between devices, across(): lax.ppermute(x, ('row', 'panel'), corner)  2.42 us
  transfers between devices with their start and end apart: 21, of which 5 were waited for; matrix products, arithmetic and copies ran while one was open for 0% of the time, Pallas kernels for 65%

profile of v12, /device:TPU:0, one launch (start us, length us, event | category | flops | bytes accessed | tf_op | source)
XLA Modules:
  0.0 108.3 jit_solution(10062615052407617891)
XLA Ops:
  0.0 0.7 fusion.1
  0.7 0.9 convert_add_fusion.1
  1.8 1.0 slice.16
  2.8 4.0 %collective-permute-start.1 = (f32[136,512]{1,0:T(8,128)S(1)}, f32[136,512]{1,0:T(8,128)S(1)}, u32[]{:S(2)}, u32[]{:S(2)}) collective-permute-start(f32[136,512]{1,0:T(8,128)S(1)} %pad_maximum_fusion.1.refs_0_), channel_id=1, source_target_pairs={{8,0},{12,4},{4,8},{0,12},{24,16},{28,20},{20,24},{16,28},{9,1},{1... | collective-permute-start | bytes 835592 | tf_op jit(solution)/shard_map/ppermute | solution.py:644
  7.3 2.6 %collective-permute-start = (f32[136,512]{1,0:T(8,128)S(1)}, f32[136,512]{1,0:T(8,128)S(1)}, u32[]{:S(2)}, u32[]{:S(2)}) collective-permute-start(f32[136,512]{1,0:T(8,128)S(1)} %pad_maximum_fusion.1.refs_0_), channel_id=1, source_target_pairs={{0,16},{4,20},{8,24},{12,28},{16,0},{20,4},{24,8},{28,12},{1,17},{... | collective-permute-start | bytes 835592 | tf_op jit(solution)/shard_map/ppermute | solution.py:588
  9.9 4.8 %row_table.1 = (bf16[8,256,512]{2,1,0:T(8,128)(2,1)S(1)}, f32[256,1]{1,0:T(8,128)S(1)}) custom-call(f32[2,16,256]{2,1,0:T(8,128)S(1)} %fusion.row_ref), custom_call_target="tpu_custom_call" | custom-call | flops 100000000 | bytes 262144 | tf_op jit(solution)/shard_map/row_table/pallas_call | solution.py:148
  14.8 3.4 %cover.4.refs_1_ = f32[224,128]{1,0:T(8,128)S(1)} custom-call(bf16[8,256,512]{2,1,0:T(8,128)(2,1)S(1)} %get-tuple-element.150.t_ref, f32[256,1]{1,0:T(8,128)S(1)} %get-tuple-element.151.row_cell_ref, f32[136,512]{1,0:T(8,128)S(1)} %pad_maximum_fusion.1.refs_0_), custom_call_target="tpu_custom_call" | custom-call | flops 100000000 | bytes 262144 | tf_op jit(solution)/shard_map/cover/pallas_call | solution.py:537
  18.2 1.6 %collective-permute-start.6 = (f32[136,512]{1,0:T(8,128)S(1)}, f32[136,512]{1,0:T(8,128)}, u32[]{:S(2)}, u32[]{:S(2)}) collective-permute-start(f32[136,512]{1,0:T(8,128)S(1)} %collective-permute-done.1.refs_2_), channel_id=1, source_target_pairs={{0,4},{4,0},{8,12},{12,8},{16,20},{20,16},{24,28},{28,24},{1,5},{5... | collective-permute-start | bytes 835592 | tf_op jit(solution)/shard_map/ppermute | solution.py:588
  19.8 2.3 %collective-permute-done.refs_1_ = f32[136,512]{1,0:T(8,128)S(1)} collective-permute-done((f32[136,512]{1,0:T(8,128)S(1)}, f32[136,512]{1,0:T(8,128)S(1)}, u32[]{:S(2)}, u32[]{:S(2)}) %collective-permute-start) | collective-permute-done | bytes 278560 | tf_op jit(solution)/shard_map/ppermute | solution.py:588
  22.1 1.2 %fold_products.1 = (f32[32,640]{1,0:T(8,128)S(1)}, f32[32,640]{1,0:T(8,128)S(1)}, f32[32,640]{1,0:T(8,128)S(1)}, f32[32,640]{1,0:T(8,128)S(1)}) custom-call(s32[2]{0:T(128)S(1)} %pad_add_fusion.place_ref, f32[136,512]{1,0:T(8,128)S(1)} %pad_maximum_fusion.1.refs_0_, f32[136,512]{1,0:T(8,128)S(1)} %collective-permute-done.refs_1_, ...), custom_call_target="tpu_custom_call" | custom-call | flops 100000000 | bytes 262144 | tf_op jit(solution)/shard_map/fold_products/pallas_call | solution.py:537
  23.4 1.6 %collective-permute-start.4 = (f32[32,640]{1,0:T(8,128)S(1)}, f32[32,640]{1,0:T(8,128)S(1)}, u32[]{:S(2)}, u32[]{:S(2)}) collective-permute-start(f32[32,640]{1,0:T(8,128)S(1)} %get-tuple-element.106), channel_id=1, source_target_pairs={{0,2},{1,3},{2,0},{3,1},{4,6},{5,7},{6,4},{7,5},{8,10},{9,11},{10,... | collective-permute-start | bytes 245768 | tf_op jit(solution)/shard_map/ppermute | solution.py:588
  25.3 3.4 %lead_cover.1 = (f32[32,640]{1,0:T(8,128)S(1)}, f32[32,512]{1,0:T(8,128)S(1)}, bf16[256,4096]{1,0:T(8,128)(2,1)S(1)}, f32[1,512]{1,0:T(1,128)S(1)}) custom-call(s32[2]{0:T(128)S(1)} %pad_add_fusion.place_ref, bf16[8,256,512]{2,1,0:T(8,128)(2,1)S(1)} %get-tuple-element.150.t_ref, f32[256,1]{1,0:T(8,128)S(1)} %get-tuple-element.151.row_cell_ref, ...), custom_call_target="tpu_custom_call" | custom-call | flops 100000000 | bytes 262144 | tf_op jit(solution)/shard_map/lead_cover/pallas_call | solution.py:537
  28.7 1.6 %collective-permute-start.8 = (f32[136,512]{1,0:T(8,128)S(1)}, f32[136,512]{1,0:T(8,128)S(1)}, u32[]{:S(2)}, u32[]{:S(2)}) collective-permute-start(f32[136,512]{1,0:T(8,128)S(1)} %collective-permute-done.refs_1_), channel_id=1, source_target_pairs={{0,4},{4,0},{8,12},{12,8},{16,20},{20,16},{24,28},{28,24},{1,5},{5... | collective-permute-start | bytes 835592 | tf_op jit(solution)/shard_map/ppermute | solution.py:588
  30.3 2.1 %collective-permute-start.7 = (f32[1,32,640]{2,1,0:T(8,128)S(1)}, f32[1,32,640]{2,1,0:T(8,128)S(1)}, u32[]{:S(2)}, u32[]{:S(2)}) collective-permute-start(f32[1,32,640]{2,1,0:T(8,128)S(1)} %subtract_bitcast_fusion), channel_id=1, source_target_pairs={{0,8},{4,12},{8,0},{12,4},{16,24},{20,28},{24,16},{28,20},{1,9},{5... | collective-permute-start | bytes 245768 | tf_op jit(solution)/shard_map/ppermute | solution.py:588
  32.3 3.0 %cover.5.refs_2_ = f32[96,384]{1,0:T(8,128)S(1)} custom-call(bf16[8,256,512]{2,1,0:T(8,128)(2,1)S(1)} %get-tuple-element.150.t_ref, f32[256,1]{1,0:T(8,128)S(1)} %get-tuple-element.151.row_cell_ref, bf16[256,4096]{1,0:T(8,128)(2,1)S(1)} %get-tuple-element.128.h_ref, f32[1,512]{1,0:T(1,128)S(1)} %get-tuple-element.129.col_cell_ref), custom_call_target="tpu_custom_call" | custom-call | flops 100000000 | bytes 262144 | tf_op jit(solution)/shard_map/cover/pallas_call | solution.py:537
  35.4 0.6 collective-permute-done.7
  35.9 1.7 %collective-permute-done.8.refs_5_.refs_1_ = f32[136,512]{1,0:T(8,128)S(1)} collective-permute-done((f32[136,512]{1,0:T(8,128)S(1)}, f32[136,512]{1,0:T(8,128)S(1)}, u32[]{:S(2)}, u32[]{:S(2)}) %collective-permute-start.8) | collective-permute-done | bytes 278560 | tf_op jit(solution)/shard_map/ppermute | solution.py:588
  37.6 1.5 %collective-permute-start.11 = (f32[136,512]{1,0:T(8,128)S(1)}, f32[136,512]{1,0:T(8,128)S(1)}, u32[]{:S(2)}, u32[]{:S(2)}) collective-permute-start(f32[136,512]{1,0:T(8,128)S(1)} %collective-permute-done.9.refs_6_.refs_2_), channel_id=1, source_target_pairs={{0,4},{4,0},{8,12},{12,8},{16,20},{20,16},{24,28},{28,24},{1,5},{5... | collective-permute-start | bytes 835592 | tf_op jit(solution)/shard_map/ppermute | solution.py:588
  39.1 1.9 %collective-permute-start.10 = (f32[2,32,640]{2,1,0:T(8,128)S(1)}, f32[2,32,640]{2,1,0:T(8,128)S(1)}, u32[]{:S(2)}, u32[]{:S(2)}) collective-permute-start(f32[2,32,640]{2,1,0:T(8,128)S(1)} %pad_maximum_fusion.2), channel_id=1, source_target_pairs={{0,16},{4,20},{8,24},{12,28},{16,0},{20,4},{24,8},{28,12},{1,17},{... | collective-permute-start | bytes 491528 | tf_op jit(solution)/shard_map/ppermute | solution.py:588
  41.0 4.0 %cover.6.refs_3_ = f32[128,384]{1,0:T(8,128)S(1)} custom-call(bf16[8,256,512]{2,1,0:T(8,128)(2,1)S(1)} %get-tuple-element.150.t_ref, f32[256,1]{1,0:T(8,128)S(1)} %get-tuple-element.151.row_cell_ref, bf16[256,4096]{1,0:T(8,128)(2,1)S(1)} %get-tuple-element.128.h_ref, f32[1,512]{1,0:T(1,128)S(1)} %get-tuple-element.129.col_cell_ref), custom_call_target="tpu_custom_call" | custom-call | flops 100000000 | bytes 262144 | tf_op jit(solution)/shard_map/cover/pallas_call | solution.py:537
  45.1 0.7 collective-permute-done.11.refs_7_.refs_3_
  45.7 1.3 %gather_split.1 = (bf16[1024,512]{1,0:T(8,128)(2,1)S(1)}, bf16[1024,512]{1,0:T(8,128)(2,1)S(1)}) custom-call(s32[2]{0:T(128)S(1)} %pad_add_fusion.place_ref, f32[136,512]{1,0:T(8,128)S(1)} %pad_maximum_fusion.1.refs_0_, f32[136,512]{1,0:T(8,128)S(1)} %collective-permute-done.refs_1_, f32[136,512]{1,0:T(8,128)S(1)} %collective-permute-done.1.refs_2_, ...), custom_call_target="tpu_custom_call" | custom-call | flops 100000000 | bytes 262144 | tf_op jit(solution)/shard_map/gather_split/pallas_call | solution.py:537
  47.0 2.4 %rest_products.3 = f32[2,256,1024]{2,1,0:T(8,128)S(1)} custom-call(s32[2]{0:T(128)S(1)} %pad_add_fusion.place_ref, f32[1024,512]{1,0:T(8,128)S(1)} %copy-done, bf16[1024,512]{1,0:T(8,128)(2,1)S(1)} %get-tuple-element.156.high_ref, bf16[1024,512]{1,0:T(8,128)(2,1)S(1)} %get-tuple-element.157.low_ref), custom_call_target="tpu_custom_call" | custom-call | flops 100000000 | bytes 262144 | tf_op jit(solution)/shard_map/rest_products/pallas_call | solution.py:537
  49.6 0.6 collective-permute-start.16
  50.1 2.4 %collective-permute-start.14 = (f32[4,32,640]{2,1,0:T(8,128)S(1)}, f32[4,32,640]{2,1,0:T(8,128)S(1)}, u32[]{:S(2)}, u32[]{:S(2)}) collective-permute-start(f32[4,32,640]{2,1,0:T(8,128)S(1)} %pad_maximum_fusion.refs_0_), channel_id=1, source_target_pairs={{0,6},{1,7},{2,4},{3,5},{4,2},{5,3},{6,0},{7,1},{8,14},{9,15},{10,... | collective-permute-start | bytes 983048 | tf_op jit(solution)/shard_map/ppermute | solution.py:765
  53.0 0.6 collective-permute-start.12
  53.6 1.6 %rest_products.4.refs_5_ = f32[1,256,1024]{2,1,0:T(8,128)S(1)} custom-call(s32[2]{0:T(128)S(1)} %pad_add_fusion.place_ref, f32[1024,512]{1,0:T(8,128)S(1)} %copy-done, bf16[1024,512]{1,0:T(8,128)(2,1)S(1)} %get-tuple-element.156.high_ref, bf16[1024,512]{1,0:T(8,128)(2,1)S(1)} %get-tuple-element.157.low_ref), custom_call_target="tpu_custom_call" | custom-call | flops 100000000 | bytes 262144 | tf_op jit(solution)/shard_map/rest_products/pallas_call | solution.py:537
  55.2 11.9 %cover.7.refs_4_ = f32[256,512]{1,0:T(8,128)S(1)} custom-call(bf16[8,256,512]{2,1,0:T(8,128)(2,1)S(1)} %get-tuple-element.150.t_ref, f32[256,1]{1,0:T(8,128)S(1)} %get-tuple-element.151.row_cell_ref, f32[136,512]{1,0:T(8,128)} %collective-permute-done.6.refs_4_.refs_0_, f32[136,512]{1,0:T(8,128)S(1)} %collective-permute-done.8.refs_5_.refs_1_, ...), custom_call_target="tpu_custom_call" | custom-call | flops 100000000 | bytes 262144 | tf_op jit(solution)/shard_map/cover/pallas_call | solution.py:537
  67.1 1.6 %rest_products.5 = f32[1,256,1024]{2,1,0:T(8,128)S(1)} custom-call(s32[2]{0:T(128)S(1)} %pad_add_fusion.place_ref, f32[1024,512]{1,0:T(8,128)S(1)} %copy-done, bf16[1024,512]{1,0:T(8,128)(2,1)S(1)} %get-tuple-element.156.high_ref, bf16[1024,512]{1,0:T(8,128)(2,1)S(1)} %get-tuple-element.157.low_ref, f32[2,256,1024]{2,1,0:T(8,128)S(1)} %collective-permute-done.15.refs_0_.refs_6_), custom_call_target="tpu_custom_call" | custom-call | flops 100000000 | bytes 262144 | tf_op jit(solution)/shard_map/rest_products/pallas_call | solution.py:537
  69.4 1.5 %collective-permute-start.17 = (f32[1,256,1024]{2,1,0:T(8,128)S(1)}, f32[1,256,1024]{2,1,0:T(8,128)S(1)}, u32[]{:S(2)}, u32[]{:S(2)}) collective-permute-start(f32[1,256,1024]{2,1,0:T(8,128)S(1)} %rest_products.5), channel_id=1, source_target_pairs={{0,2},{1,3},{2,0},{3,1},{4,6},{5,7},{6,4},{7,5},{8,10},{9,11},{10,... | collective-permute-start | bytes 3145736 | tf_op jit(solution)/shard_map/ppermute | solution.py:588
  71.3 32.1 %factor.1 = (bf16[1024,1024]{1,0:T(8,128)(2,1)S(1)}, bf16[1024,1024]{1,0:T(8,128)(2,1)S(1)}, bf16[1024,128]{1,0:T(8,128)(2,1)S(1)}, bf16[1024,128]{1,0:T(8,128)(2,1)S(1)}) custom-call(s32[2]{0:T(128)S(1)} %pad_add_fusion.place_ref, f32[4,32,640]{2,1,0:T(8,128)S(1)} %pad_maximum_fusion.refs_0_, f32[4,32,640]{2,1,0:T(8,128)S(1)} %collective-permute-done.12.refs_1_, ...), custom_call_target="tpu_custom_call" | custom-call | flops 49999998976 | bytes 8388608 | tf_op jit(solution)/shard_map/factor/pallas_call | solution.py:461
  103.5 4.8 %solve.1 = f32[256,1024]{1,0:T(8,128)} custom-call(s32[2]{0:T(128)S(1)} %pad_add_fusion.place_ref, f32[32,512]{1,0:T(8,128)S(1)} %get-tuple-element.116.refs_0_, f32[224,128]{1,0:T(8,128)S(1)} %cover.4.refs_1_, f32[96,384]{1,0:T(8,128)S(1)} %cover.5.refs_2_, f32[128,384]{1,0:T(8,128)S(1)} %cover.6.refs_3_, f32[256,512]{1,0:T(8,128)S(1)} %cover.7.refs_4_, ...), custom_call_target="tpu_custom_call" | custom-call | flops 100000000 | bytes 262144 | tf_op jit(solution)/shard_map/solve/pallas_call | solution.py:537
  (38 shorter events, 3.0 us)
Async XLA Ops:
  2.8 15.4 %collective-permute-start.1 = (f32[136,512]{1,0:T(8,128)S(1)}, f32[136,512]{1,0:T(8,128)S(1)}, u32[]{:S(2)}, u32[]{:S(2)}) collective-permute-start(f32[136,512]{1,0:T(8,128)S(1)} %pad_maximum_fusion.1.refs_0_), channel_id=1, source_target_pairs={{8,0},{12,4},{4,8},{0,12},{24,16},{28,20},{20,24},{16,28},{9,1},{1... | collective-permute-start | bytes 835592 | tf_op jit(solution)/shard_map/ppermute | solution.py:644
  6.8 13.0 %collective-permute-start.2 = (f32[136,512]{1,0:T(8,128)S(1)}, f32[136,512]{1,0:T(8,128)S(1)}, u32[]{:S(2)}, u32[]{:S(2)}) collective-permute-start(f32[136,512]{1,0:T(8,128)S(1)} %pad_maximum_fusion.1.refs_0_), channel_id=1, source_target_pairs={{4,0},{0,4},{12,8},{8,12},{20,16},{16,20},{28,24},{24,28},{5,1},{1... | collective-permute-start | bytes 835592 | tf_op jit(solution)/shard_map/ppermute | solution.py:644
  7.3 14.7 %collective-permute-start = (f32[136,512]{1,0:T(8,128)S(1)}, f32[136,512]{1,0:T(8,128)S(1)}, u32[]{:S(2)}, u32[]{:S(2)}) collective-permute-start(f32[136,512]{1,0:T(8,128)S(1)} %pad_maximum_fusion.1.refs_0_), channel_id=1, source_target_pairs={{0,16},{4,20},{8,24},{12,28},{16,0},{20,4},{24,8},{28,12},{1,17},{... | collective-permute-start | bytes 835592 | tf_op jit(solution)/shard_map/ppermute | solution.py:588
  18.2 12.0 %collective-permute-start.6 = (f32[136,512]{1,0:T(8,128)S(1)}, f32[136,512]{1,0:T(8,128)}, u32[]{:S(2)}, u32[]{:S(2)}) collective-permute-start(f32[136,512]{1,0:T(8,128)S(1)} %collective-permute-done.1.refs_2_), channel_id=1, source_target_pairs={{0,4},{4,0},{8,12},{12,8},{16,20},{20,16},{24,28},{28,24},{1,5},{5... | collective-permute-start | bytes 835592 | tf_op jit(solution)/shard_map/ppermute | solution.py:588
  23.3 5.3 %collective-permute-start.3 = (f32[32,640]{1,0:T(8,128)S(1)}, f32[32,640]{1,0:T(8,128)S(1)}, u32[]{:S(2)}, u32[]{:S(2)}) collective-permute-start(f32[32,640]{1,0:T(8,128)S(1)} %get-tuple-element.105), channel_id=1, source_target_pairs={{0,1},{1,0},{2,3},{3,2},{4,5},{5,4},{6,7},{7,6},{8,9},{9,8},{10,11... | collective-permute-start | bytes 245768 | tf_op jit(solution)/shard_map/ppermute | solution.py:588
  23.4 6.8 %collective-permute-start.4 = (f32[32,640]{1,0:T(8,128)S(1)}, f32[32,640]{1,0:T(8,128)S(1)}, u32[]{:S(2)}, u32[]{:S(2)}) collective-permute-start(f32[32,640]{1,0:T(8,128)S(1)} %get-tuple-element.106), channel_id=1, source_target_pairs={{0,2},{1,3},{2,0},{3,1},{4,6},{5,7},{6,4},{7,5},{8,10},{9,11},{10,... | collective-permute-start | bytes 245768 | tf_op jit(solution)/shard_map/ppermute | solution.py:588
  25.0 5.2 %collective-permute-start.5 = (f32[32,640]{1,0:T(8,128)S(1)}, f32[32,640]{1,0:T(8,128)S(1)}, u32[]{:S(2)}, u32[]{:S(2)}) collective-permute-start(f32[32,640]{1,0:T(8,128)S(1)} %get-tuple-element.107), channel_id=1, source_target_pairs={{0,3},{1,2},{2,1},{3,0},{4,7},{5,6},{6,5},{7,4},{8,11},{9,10},{10,... | collective-permute-start | bytes 245768 | tf_op jit(solution)/shard_map/ppermute | solution.py:588
  25.3 10.7 %collective-permute-start.9 = (f32[136,512]{1,0:T(8,128)S(1)}, f32[136,512]{1,0:T(8,128)S(1)}, u32[]{:S(2)}, u32[]{:S(2)}) collective-permute-start(f32[136,512]{1,0:T(8,128)S(1)} %collective-permute-done.refs_1_), channel_id=1, source_target_pairs={{0,8},{4,12},{8,0},{12,4},{16,24},{20,28},{24,16},{28,20},{1,9},{5... | collective-permute-start | bytes 835592 | tf_op jit(solution)/shard_map/ppermute | solution.py:588
  28.7 9.0 %collective-permute-start.8 = (f32[136,512]{1,0:T(8,128)S(1)}, f32[136,512]{1,0:T(8,128)S(1)}, u32[]{:S(2)}, u32[]{:S(2)}) collective-permute-start(f32[136,512]{1,0:T(8,128)S(1)} %collective-permute-done.refs_1_), channel_id=1, source_target_pairs={{0,4},{4,0},{8,12},{12,8},{16,20},{20,16},{24,28},{28,24},{1,5},{5... | collective-permute-start | bytes 835592 | tf_op jit(solution)/shard_map/ppermute | solution.py:588
  30.3 5.7 %collective-permute-start.7 = (f32[1,32,640]{2,1,0:T(8,128)S(1)}, f32[1,32,640]{2,1,0:T(8,128)S(1)}, u32[]{:S(2)}, u32[]{:S(2)}) collective-permute-start(f32[1,32,640]{2,1,0:T(8,128)S(1)} %subtract_bitcast_fusion), channel_id=1, source_target_pairs={{0,8},{4,12},{8,0},{12,4},{16,24},{20,28},{24,16},{28,20},{1,9},{5... | collective-permute-start | bytes 245768 | tf_op jit(solution)/shard_map/ppermute | solution.py:588
  37.6 8.1 %collective-permute-start.11 = (f32[136,512]{1,0:T(8,128)S(1)}, f32[136,512]{1,0:T(8,128)S(1)}, u32[]{:S(2)}, u32[]{:S(2)}) collective-permute-start(f32[136,512]{1,0:T(8,128)S(1)} %collective-permute-done.9.refs_6_.refs_2_), channel_id=1, source_target_pairs={{0,4},{4,0},{8,12},{12,8},{16,20},{20,16},{24,28},{28,24},{1,5},{5... | collective-permute-start | bytes 835592 | tf_op jit(solution)/shard_map/ppermute | solution.py:588
  39.1 10.3 %collective-permute-start.10 = (f32[2,32,640]{2,1,0:T(8,128)S(1)}, f32[2,32,640]{2,1,0:T(8,128)S(1)}, u32[]{:S(2)}, u32[]{:S(2)}) collective-permute-start(f32[2,32,640]{2,1,0:T(8,128)S(1)} %pad_maximum_fusion.2), channel_id=1, source_target_pairs={{0,16},{4,20},{8,24},{12,28},{16,0},{20,4},{24,8},{28,12},{1,17},{... | collective-permute-start | bytes 491528 | tf_op jit(solution)/shard_map/ppermute | solution.py:588
  45.0 2.0 %copy-start = (f32[1024,512]{1,0:T(8,128)S(1)}, f32[1024,512]{1,0:T(8,128)}, u32[]{:S(2)}) copy-start(f32[1024,512]{1,0:T(8,128)} %prior_ref.5) | copy-start | bytes 6291460
  49.4 17.6 %collective-permute-start.15 = (f32[2,256,1024]{2,1,0:T(8,128)S(1)}, f32[2,256,1024]{2,1,0:T(8,128)S(1)}, u32[]{:S(2)}, u32[]{:S(2)}) collective-permute-start(f32[2,256,1024]{2,1,0:T(8,128)S(1)} %rest_products.3), channel_id=1, source_target_pairs={{0,1},{1,0},{2,3},{3,2},{4,5},{5,4},{6,7},{7,6},{8,9},{9,8},{10,11... | collective-permute-start | bytes 6291464 | tf_op jit(solution)/shard_map/ppermute | solution.py:588
  49.6 19.1 %collective-permute-start.16 = (f32[4,32,640]{2,1,0:T(8,128)S(1)}, f32[4,32,640]{2,1,0:T(8,128)S(1)}, u32[]{:S(2)}, u32[]{:S(2)}) collective-permute-start(f32[4,32,640]{2,1,0:T(8,128)S(1)} %pad_maximum_fusion.refs_0_), channel_id=1, source_target_pairs={{0,1},{1,0},{2,3},{3,2},{4,5},{5,4},{6,7},{7,6},{8,9},{9,8},{10,11... | collective-permute-start | bytes 983048 | tf_op jit(solution)/shard_map/ppermute | solution.py:588
  50.1 18.6 %collective-permute-start.14 = (f32[4,32,640]{2,1,0:T(8,128)S(1)}, f32[4,32,640]{2,1,0:T(8,128)S(1)}, u32[]{:S(2)}, u32[]{:S(2)}) collective-permute-start(f32[4,32,640]{2,1,0:T(8,128)S(1)} %pad_maximum_fusion.refs_0_), channel_id=1, source_target_pairs={{0,6},{1,7},{2,4},{3,5},{4,2},{5,3},{6,0},{7,1},{8,14},{9,15},{10,... | collective-permute-start | bytes 983048 | tf_op jit(solution)/shard_map/ppermute | solution.py:765
  52.5 16.2 %collective-permute-start.13 = (f32[4,32,640]{2,1,0:T(8,128)S(1)}, f32[4,32,640]{2,1,0:T(8,128)S(1)}, u32[]{:S(2)}, u32[]{:S(2)}) collective-permute-start(f32[4,32,640]{2,1,0:T(8,128)S(1)} %pad_maximum_fusion.refs_0_), channel_id=1, source_target_pairs={{0,2},{1,3},{2,0},{3,1},{4,6},{5,7},{6,4},{7,5},{8,10},{9,11},{10,... | collective-permute-start | bytes 983048 | tf_op jit(solution)/shard_map/ppermute | solution.py:588
  53.0 15.7 %collective-permute-start.12 = (f32[4,32,640]{2,1,0:T(8,128)S(1)}, f32[4,32,640]{2,1,0:T(8,128)S(1)}, u32[]{:S(2)}, u32[]{:S(2)}) collective-permute-start(f32[4,32,640]{2,1,0:T(8,128)S(1)} %pad_maximum_fusion.refs_0_), channel_id=1, source_target_pairs={{0,4},{4,0},{8,12},{12,8},{16,20},{20,16},{24,28},{28,24},{1,5},{5... | collective-permute-start | bytes 983048 | tf_op jit(solution)/shard_map/ppermute | solution.py:588
  68.7 2.2 %collective-permute-start.18 = (f32[4,32,640]{2,1,0:T(8,128)S(1)}, f32[4,32,640]{2,1,0:T(8,128)S(1)}, u32[]{:S(2)}, u32[]{:S(2)}) collective-permute-start(f32[4,32,640]{2,1,0:T(8,128)S(1)} %collective-permute-done.12.refs_1_), channel_id=1, source_target_pairs={{0,1},{1,0},{2,3},{3,2},{4,5},{5,4},{6,7},{7,6},{8,9},{9,8},{10,11... | collective-permute-start | bytes 983048 | tf_op jit(solution)/shard_map/ppermute | solution.py:588
  68.8 2.1 %collective-permute-start.19 = (f32[4,32,640]{2,1,0:T(8,128)S(1)}, f32[4,32,640]{2,1,0:T(8,128)S(1)}, u32[]{:S(2)}, u32[]{:S(2)}) collective-permute-start(f32[4,32,640]{2,1,0:T(8,128)S(1)} %collective-permute-done.13.refs_2_), channel_id=1, source_target_pairs={{0,1},{1,0},{2,3},{3,2},{4,5},{5,4},{6,7},{7,6},{8,9},{9,8},{10,11... | collective-permute-start | bytes 983048 | tf_op jit(solution)/shard_map/ppermute | solution.py:588
  69.3 2.1 %collective-permute-start.20 = (f32[4,32,640]{2,1,0:T(8,128)S(1)}, f32[4,32,640]{2,1,0:T(8,128)S(1)}, u32[]{:S(2)}, u32[]{:S(2)}) collective-permute-start(f32[4,32,640]{2,1,0:T(8,128)S(1)} %collective-permute-done.14.refs_3_), channel_id=1, source_target_pairs={{0,1},{1,0},{2,3},{3,2},{4,5},{5,4},{6,7},{7,6},{8,9},{9,8},{10,11... | collective-permute-start | bytes 983048 | tf_op jit(solution)/shard_map/ppermute | solution.py:588
  69.4 34.1 %collective-permute-start.17 = (f32[1,256,1024]{2,1,0:T(8,128)S(1)}, f32[1,256,1024]{2,1,0:T(8,128)S(1)}, u32[]{:S(2)}, u32[]{:S(2)}) collective-permute-start(f32[1,256,1024]{2,1,0:T(8,128)S(1)} %rest_products.5), channel_id=1, source_target_pairs={{0,2},{1,3},{2,0},{3,1},{4,6},{5,7},{6,4},{7,5},{8,10},{9,11},{10,... | collective-permute-start | bytes 3145736 | tf_op jit(solution)/shard_map/ppermute | solution.py:588

commit v13 on v12

--- a/solution.py
+++ b/solution.py
@@ -227,7 +227,8 @@
     place_ref, t_ref, row_cell_ref, *refs, points
 ):
     blocks, refs = refs[:4], refs[4:]
-    folded_ref, own_ref, h_ref, col_cell_ref, east_ref, far_ref, far_cell_ref, far_table_ref = refs
+    folded_ref, own_ref, h_ref, col_cell_ref, east_ref, far_east_ref = refs[:6]
+    far_ref, far_cell_ref, far_table_ref = refs[6:]
     rows, cols = own_ref.shape
     lines = h_ref.shape[0]
     cells = [column_counts(ref, h_ref, NB * i, cols) for i, ref in enumerate(blocks)]
@@ -251,12 +252,17 @@
     mine = mine + jnp.where(col == first + row, 1.0, 0.0)
     own_ref[...] = mine
     far = cover_chunk(
-        far_table_ref[...], far_cell_ref[pl.ds(first, rows)], col_cell, h_ref, east_ref, points
+        far_table_ref[...],
+        far_cell_ref[pl.ds(first, rows)],
+        col_cell[:, 2 * NB :],
+        h_ref,
+        far_east_ref,
+        points,
     )
     folded_ref[:, : 3 * NB] = mine[:, : 3 * NB]
-    folded_ref[:, 3 * NB : 4 * NB] = far[:, 2 * NB : 3 * NB]
+    folded_ref[:, 3 * NB : 4 * NB] = far[:, :NB]
     own_last = makes_own(place_ref[0])
-    folded_ref[:, 4 * NB :] = jnp.where(own_last, mine[:, 3 * NB :], far[:, 3 * NB :])
+    folded_ref[:, 4 * NB :] = jnp.where(own_last, mine[:, 3 * NB :], far[:, NB:])
 
 
 def later_cover_kernel(t_ref, row_cell_ref, h_ref, col_cell_ref, o_ref, east_ref, *, points, start):
@@ -570,18 +576,19 @@
         low_ref[pl.ds(first, NB)] = low
 
 
-def rest_products_kernel(place_ref, prior_ref, high_ref, low_ref, *refs, turns):
-    plus_refs, o_ref = refs[:-1], refs[-1]
-    rows = o_ref.shape[1]
-    for i, m in enumerate(turns):
+def rest_products_kernel(place_ref, prior_ref, high_ref, low_ref, *refs, turns, outs):
+    plus_refs, members = refs[:-outs], [ref.at[i] for ref in refs[-outs:] for i in range(ref.shape[0])]
+    for m, o_ref in zip(turns, members):
+        rows = o_ref.shape[0]
         first = pl.multiple_of((place_ref[1] ^ m) * rows, rows)
         own_high, own_low = split(prior_ref[pl.ds(first, rows)])
-        for c in range(0, o_ref.shape[2], 2 * NB):
+        for c in range(0, o_ref.shape[1], 2 * NB):
             cols = slice(c, c + 2 * NB)
             total = dot3(own_high, own_low, high_ref[cols], low_ref[cols])
-            for plus_ref in plus_refs:
-                total = total + plus_ref[i, :, cols]
-            o_ref[i, :, cols] = total
+            if m == turns[-1]:
+                for plus_ref in plus_refs:
+                    total = total + plus_ref[0, :, cols]
+            o_ref[:, cols] = total
 
 
 def swap(block, axis, bit):
@@ -680,7 +687,6 @@
         return lax.optimization_barrier((transfer(operands), work(operands, held)))
 
     half = 4 * NB
-    east = pltpu.VMEM((15, per_device, half), F32)
 
     def lead_cover(_, held):
         return vmem_call(
@@ -694,7 +700,8 @@
             place,
             [*held, own, far, one, two],
             [
-                east,
+                pltpu.VMEM((15, per_device, half), F32),
+                pltpu.VMEM((15, per_device, 2 * NB), F32),
                 pltpu.VMEM((2, NB, count), F32),
                 pltpu.VMEM((NB, 1), F32),
                 pltpu.VMEM((8, per_device, 2 * lines), BF),
@@ -712,10 +719,10 @@
     far_z = swap(far, "row", 2)
     shard = folded - (shares[0] + sums[0] + sums[1] + sums[2])
 
-    def rest_part(panel_prior, turns, plus=()):
+    def rest_part(panel_prior, turns, members, plus=()):
         return vmem_call(
-            functools.partial(rest_products_kernel, turns=turns),
-            jax.ShapeDtypeStruct((len(turns), quarter_rows, B), F32),
+            functools.partial(rest_products_kernel, turns=turns, outs=len(members)),
+            [jax.ShapeDtypeStruct((n, quarter_rows, B), F32) for n in members],
             place,
             [prior_factor, *panel_prior, *plus],
             name="rest_products",
@@ -734,7 +741,8 @@
     middle = quarter_rows // 2
 
     def beside_far_z(_, held):
-        rest = [from_x, far_x, far_z, last]
+        held, arrived = lax.optimization_barrier((held, far_x))
+        rest = [from_x, arrived, far_z, last]
         cover = later_cover(held, middle, quarter_rows - middle)
         cover, blocks = lax.optimization_barrier((cover, rest))
         panel_prior = vmem_call(
@@ -744,7 +752,7 @@
             [own, far, one, two, *blocks],
             name="gather_split",
         )
-        return cover, panel_prior, rest_part(panel_prior, (3, 1)), rest
+        return cover, panel_prior, rest_part(panel_prior, (3, 1), (2,))[0], rest
 
     shard = shard[None]
     near_rows, cover_first = beside(
@@ -753,7 +761,7 @@
         lambda _, held: later_cover(held, per_device, middle - per_device),
     )
     near_rows = jnp.concatenate([shard, near_rows], 0)
-    cover_first, from_x, far_x, far_z = lax.optimization_barrier((cover_first, from_x, far_x, far_z))
+    cover_first, from_x, far_z = lax.optimization_barrier((cover_first, from_x, far_z))
     last = swap(far_z, "row", 1)
     far_rows, (cover_second, panel_prior, for_core, rest) = beside(
         near_rows, lambda x: swap(x, "row", 4), beside_far_z
@@ -767,7 +775,7 @@
     def beside_xy(x, held):
         from_core = swap(for_core, "panel", 1)
         cover = block_cover(held, rest, 0, half)
-        part_0, part_2 = rest_part(panel_prior, (0,)), rest_part(panel_prior, (2,), [from_core])
+        part_0, part_2 = rest_part(panel_prior, (0, 2), (1, 1), [from_core])
         return cover, part_0, part_2, from_core, swap(x, "panel", 1)
 
     received, (cover_last, part_0, part_2, from_core, held_there) = beside(

time: 109 us -> 107 us (0.982)
  starting transfers between devices: 23.9 us -> 21.5 us
  waiting for transfers between devices: 5.73 us -> 7.5 us
    ppermute x18, starting transfers between devices: 17 us -> 14.5 us  [swap(): lax.ppermute(block, axis, [(i, i ^ bit) for i in range(lax.axis_size(axis...]
    ppermute x18, waiting for transfers between devices: 5.72 us -> 7.49 us  [swap(): lax.ppermute(block, axis, [(i, i ^ bit) for i in range(lax.axis_size(axis...]
    pallas_call x11 -> x10, Pallas kernels: 38.5 us -> 37.6 us  [vmem_call(): pl.pallas_call(kernel, out_shape=out_shape, in_specs=[pl.BlockSpec(memory...]
  transfers between devices with their start and end apart: 21 -> 21, of which waited for: 5 -> 6; matrix products, arithmetic and copies ran while one was open for 0% -> 0% of each run, Pallas kernels for 65% -> 65%
where the time goes in v13:
time: 107 us
  Pallas kernels  74.7 us (70%)
  starting transfers between devices  21.5 us (20%)
  waiting for transfers between devices  7.5 us (7%)
  other arithmetic  1.76 us (2%)
  local copies, waits for them, and re-layouts  1.14 us (1%)
    pallas_call x10, Pallas kernels, vmem_call(): pl.pallas_call(kernel, out_shape=out_shape, in_specs=[pl.BlockSpec(memory...  37.6 us
    pallas_call x1, Pallas kernels, factor(): pl.pallas_call(kernel, out_shape=[jax.ShapeDtypeStruct((n, n), BF)] * 2 +...  32.3 us
    ppermute x18, starting transfers between devices, swap(): lax.ppermute(block, axis, [(i, i ^ bit) for i in range(lax.axis_size(axis...  14.5 us
    ppermute x18, waiting for transfers between devices, swap(): lax.ppermute(block, axis, [(i, i ^ bit) for i in range(lax.axis_size(axis...  7.49 us
    pallas_call x1, Pallas kernels, row_table(): pl.pallas_call(row_table_kernel, out_shape=[jax.ShapeDtypeStruct((8, rows...  4.85 us
    ppermute x2, starting transfers between devices, turn(): return lax.ppermute(block, 'row', [(turned(d, k), d) for d in range(8)])  4.54 us
    ppermute x1, starting transfers between devices, across(): lax.ppermute(x, ('row', 'panel'), corner)  2.45 us
  transfers between devices with their start and end apart: 21, of which 6 were waited for; matrix products, arithmetic and copies ran while one was open for 0% of the time, Pallas kernels for 65%

profile of v13, /device:TPU:0, one launch (start us, length us, event | category | flops | bytes accessed | tf_op | source)
XLA Modules:
  0.0 106.9 jit_solution(5888350521508289480)
XLA Ops:
  0.0 0.7 fusion.1
  0.7 0.9 convert_add_fusion.1
  1.8 1.0 slice.16
  2.8 4.0 %collective-permute-start.1 = (f32[136,512]{1,0:T(8,128)S(1)}, f32[136,512]{1,0:T(8,128)S(1)}, u32[]{:S(2)}, u32[]{:S(2)}) collective-permute-start(f32[136,512]{1,0:T(8,128)S(1)} %pad_maximum_fusion.1.refs_0_), channel_id=1, source_target_pairs={{8,0},{12,4},{4,8},{0,12},{24,16},{28,20},{20,24},{16,28},{9,1},{1... | collective-permute-start | bytes 835592 | tf_op jit(solution)/shard_map/ppermute | solution.py:651
  6.8 0.5 collective-permute-start.2
  7.3 2.6 %collective-permute-start = (f32[136,512]{1,0:T(8,128)S(1)}, f32[136,512]{1,0:T(8,128)S(1)}, u32[]{:S(2)}, u32[]{:S(2)}) collective-permute-start(f32[136,512]{1,0:T(8,128)S(1)} %pad_maximum_fusion.1.refs_0_), channel_id=1, source_target_pairs={{0,16},{4,20},{8,24},{12,28},{16,0},{20,4},{24,8},{28,12},{1,17},{... | collective-permute-start | bytes 835592 | tf_op jit(solution)/shard_map/ppermute | solution.py:595
  9.9 4.8 %row_table.1 = (bf16[8,256,512]{2,1,0:T(8,128)(2,1)S(1)}, f32[256,1]{1,0:T(8,128)S(1)}) custom-call(f32[2,16,256]{2,1,0:T(8,128)S(1)} %fusion.row_ref), custom_call_target="tpu_custom_call" | custom-call | flops 100000000 | bytes 262144 | tf_op jit(solution)/shard_map/row_table/pallas_call | solution.py:148
  14.8 3.4 %cover.4.refs_1_ = f32[224,128]{1,0:T(8,128)S(1)} custom-call(bf16[8,256,512]{2,1,0:T(8,128)(2,1)S(1)} %get-tuple-element.156.t_ref, f32[256,1]{1,0:T(8,128)S(1)} %get-tuple-element.157.row_cell_ref, f32[136,512]{1,0:T(8,128)S(1)} %pad_maximum_fusion.1.refs_0_), custom_call_target="tpu_custom_call" | custom-call | flops 100000000 | bytes 262144 | tf_op jit(solution)/shard_map/cover/pallas_call | solution.py:543
  18.2 1.6 %collective-permute-start.6 = (f32[136,512]{1,0:T(8,128)S(1)}, f32[136,512]{1,0:T(8,128)}, u32[]{:S(2)}, u32[]{:S(2)}) collective-permute-start(f32[136,512]{1,0:T(8,128)S(1)} %collective-permute-done.1.refs_2_), channel_id=1, source_target_pairs={{0,4},{4,0},{8,12},{12,8},{16,20},{20,16},{24,28},{28,24},{1,5},{5... | collective-permute-start | bytes 835592 | tf_op jit(solution)/shard_map/ppermute | solution.py:595
  19.8 2.3 %collective-permute-done.refs_1_ = f32[136,512]{1,0:T(8,128)S(1)} collective-permute-done((f32[136,512]{1,0:T(8,128)S(1)}, f32[136,512]{1,0:T(8,128)S(1)}, u32[]{:S(2)}, u32[]{:S(2)}) %collective-permute-start) | collective-permute-done | bytes 278560 | tf_op jit(solution)/shard_map/ppermute | solution.py:595
  22.1 1.2 %fold_products.1 = (f32[32,640]{1,0:T(8,128)S(1)}, f32[32,640]{1,0:T(8,128)S(1)}, f32[32,640]{1,0:T(8,128)S(1)}, f32[32,640]{1,0:T(8,128)S(1)}) custom-call(s32[2]{0:T(128)S(1)} %pad_add_fusion.place_ref, f32[136,512]{1,0:T(8,128)S(1)} %pad_maximum_fusion.1.refs_0_, f32[136,512]{1,0:T(8,128)S(1)} %collective-permute-done.refs_1_, ...), custom_call_target="tpu_custom_call" | custom-call | flops 100000000 | bytes 262144 | tf_op jit(solution)/shard_map/fold_products/pallas_call | solution.py:543
  23.4 1.6 %collective-permute-start.4 = (f32[32,640]{1,0:T(8,128)S(1)}, f32[32,640]{1,0:T(8,128)S(1)}, u32[]{:S(2)}, u32[]{:S(2)}) collective-permute-start(f32[32,640]{1,0:T(8,128)S(1)} %get-tuple-element.110), channel_id=1, source_target_pairs={{0,2},{1,3},{2,0},{3,1},{4,6},{5,7},{6,4},{7,5},{8,10},{9,11},{10,... | collective-permute-start | bytes 245768 | tf_op jit(solution)/shard_map/ppermute | solution.py:595
  25.3 3.4 %lead_cover.1 = (f32[32,640]{1,0:T(8,128)S(1)}, f32[32,512]{1,0:T(8,128)S(1)}, bf16[256,4096]{1,0:T(8,128)(2,1)S(1)}, f32[1,512]{1,0:T(1,128)S(1)}) custom-call(s32[2]{0:T(128)S(1)} %pad_add_fusion.place_ref, bf16[8,256,512]{2,1,0:T(8,128)(2,1)S(1)} %get-tuple-element.156.t_ref, f32[256,1]{1,0:T(8,128)S(1)} %get-tuple-element.157.row_cell_ref, ...), custom_call_target="tpu_custom_call" | custom-call | flops 100000000 | bytes 262144 | tf_op jit(solution)/shard_map/lead_cover/pallas_call | solution.py:543
  28.7 1.1 collective-permute-done.5
  29.8 1.1 collective-permute-start.7
  30.8 1.5 %collective-permute-start.10 = (f32[136,512]{1,0:T(8,128)S(1)}, f32[136,512]{1,0:T(8,128)S(1)}, u32[]{:S(2)}, u32[]{:S(2)}) collective-permute-start(f32[136,512]{1,0:T(8,128)S(1)} %collective-permute-done.refs_1_), channel_id=1, source_target_pairs={{0,4},{4,0},{8,12},{12,8},{16,20},{20,16},{24,28},{28,24},{1,5},{5... | collective-permute-start | bytes 835592 | tf_op jit(solution)/shard_map/ppermute | solution.py:595
  32.3 3.0 %cover.5.refs_2_ = f32[96,384]{1,0:T(8,128)S(1)} custom-call(bf16[8,256,512]{2,1,0:T(8,128)(2,1)S(1)} %get-tuple-element.156.t_ref, f32[256,1]{1,0:T(8,128)S(1)} %get-tuple-element.157.row_cell_ref, bf16[256,4096]{1,0:T(8,128)(2,1)S(1)} %get-tuple-element.132.h_ref, f32[1,512]{1,0:T(1,128)S(1)} %get-tuple-element.133.col_cell_ref), custom_call_target="tpu_custom_call" | custom-call | flops 100000000 | bytes 262144 | tf_op jit(solution)/shard_map/cover/pallas_call | solution.py:543
  35.3 0.6 collective-permute-done.7
  35.9 1.5 %collective-permute-start.11 = (f32[136,512]{1,0:T(8,128)S(1)}, f32[136,512]{1,0:T(8,128)S(1)}, u32[]{:S(2)}, u32[]{:S(2)}) collective-permute-start(f32[136,512]{1,0:T(8,128)S(1)} %collective-permute-done.8.refs_6_.refs_2_), channel_id=1, source_target_pairs={{0,4},{4,0},{8,12},{12,8},{16,20},{20,16},{24,28},{28,24},{1,5},{5... | collective-permute-start | bytes 835592 | tf_op jit(solution)/shard_map/ppermute | solution.py:595
  37.4 0.7 collective-permute-start.9
  38.1 2.1 %collective-permute-done.10.refs_5_.refs_1_ = f32[136,512]{1,0:T(8,128)S(1)} collective-permute-done((f32[136,512]{1,0:T(8,128)S(1)}, f32[136,512]{1,0:T(8,128)S(1)}, u32[]{:S(2)}, u32[]{:S(2)}) %collective-permute-start.10) | collective-permute-done | bytes 278560 | tf_op jit(solution)/shard_map/ppermute | solution.py:595
  40.2 4.0 %cover.6.refs_3_ = f32[128,384]{1,0:T(8,128)S(1)} custom-call(bf16[8,256,512]{2,1,0:T(8,128)(2,1)S(1)} %get-tuple-element.156.t_ref, f32[256,1]{1,0:T(8,128)S(1)} %get-tuple-element.157.row_cell_ref, bf16[256,4096]{1,0:T(8,128)(2,1)S(1)} %get-tuple-element.132.h_ref, f32[1,512]{1,0:T(1,128)S(1)} %get-tuple-element.133.col_cell_ref), custom_call_target="tpu_custom_call" | custom-call | flops 100000000 | bytes 262144 | tf_op jit(solution)/shard_map/cover/pallas_call | solution.py:543
  44.2 0.9 collective-permute-done.11.refs_7_.refs_3_
  45.1 1.3 %gather_split.1 = (bf16[1024,512]{1,0:T(8,128)(2,1)S(1)}, bf16[1024,512]{1,0:T(8,128)(2,1)S(1)}) custom-call(s32[2]{0:T(128)S(1)} %pad_add_fusion.place_ref, f32[136,512]{1,0:T(8,128)S(1)} %pad_maximum_fusion.1.refs_0_, f32[136,512]{1,0:T(8,128)S(1)} %collective-permute-done.refs_1_, f32[136,512]{1,0:T(8,128)S(1)} %collective-permute-done.1.refs_2_, ...), custom_call_target="tpu_custom_call" | custom-call | flops 100000000 | bytes 262144 | tf_op jit(solution)/shard_map/gather_split/pallas_call | solution.py:543
  46.4 2.4 %rest_products.2 = f32[2,256,1024]{2,1,0:T(8,128)S(1)} custom-call(s32[2]{0:T(128)S(1)} %pad_add_fusion.place_ref, f32[1024,512]{1,0:T(8,128)S(1)} %copy-done, bf16[1024,512]{1,0:T(8,128)(2,1)S(1)} %get-tuple-element.162.high_ref, bf16[1024,512]{1,0:T(8,128)(2,1)S(1)} %get-tuple-element.163.low_ref), custom_call_target="tpu_custom_call" | custom-call | flops 100000000 | bytes 262144 | tf_op jit(solution)/shard_map/rest_products/pallas_call | solution.py:543
  48.9 0.6 collective-permute-start.16
  49.5 2.5 %collective-permute-start.14 = (f32[4,32,640]{2,1,0:T(8,128)S(1)}, f32[4,32,640]{2,1,0:T(8,128)S(1)}, u32[]{:S(2)}, u32[]{:S(2)}) collective-permute-start(f32[4,32,640]{2,1,0:T(8,128)S(1)} %pad_maximum_fusion.refs_0_), channel_id=1, source_target_pairs={{0,6},{1,7},{2,4},{3,5},{4,2},{5,3},{6,0},{7,1},{8,14},{9,15},{10,... | collective-permute-start | bytes 983048 | tf_op jit(solution)/shard_map/ppermute | solution.py:773
  53.0 11.7 %cover.7.refs_4_ = f32[256,512]{1,0:T(8,128)S(1)} custom-call(bf16[8,256,512]{2,1,0:T(8,128)(2,1)S(1)} %get-tuple-element.156.t_ref, f32[256,1]{1,0:T(8,128)S(1)} %get-tuple-element.157.row_cell_ref, f32[136,512]{1,0:T(8,128)} %collective-permute-done.6.refs_4_.refs_0_, f32[136,512]{1,0:T(8,128)S(1)} %collective-permute-done.10.refs_5_.refs_1_, ...), custom_call_target="tpu_custom_call" | custom-call | flops 100000000 | bytes 262144 | tf_op jit(solution)/shard_map/cover/pallas_call | solution.py:543
  64.7 2.4 %rest_products.3 = (f32[1,256,1024]{2,1,0:T(8,128)S(1)}, f32[1,256,1024]{2,1,0:T(8,128)S(1)}) custom-call(s32[2]{0:T(128)S(1)} %pad_add_fusion.place_ref, f32[1024,512]{1,0:T(8,128)S(1)} %copy-done, bf16[1024,512]{1,0:T(8,128)(2,1)S(1)} %get-tuple-element.162.high_ref, bf16[1024,512]{1,0:T(8,128)(2,1)S(1)} %get-tuple-element.163.low_ref, ...), custom_call_target="tpu_custom_call" | custom-call | flops 100000000 | bytes 262144 | tf_op jit(solution)/shard_map/rest_products/pallas_call | solution.py:543
  67.8 1.5 %collective-permute-start.17 = (f32[1,256,1024]{2,1,0:T(8,128)S(1)}, f32[1,256,1024]{2,1,0:T(8,128)S(1)}, u32[]{:S(2)}, u32[]{:S(2)}) collective-permute-start(f32[1,256,1024]{2,1,0:T(8,128)S(1)} %get-tuple-element.170), channel_id=1, source_target_pairs={{0,2},{1,3},{2,0},{3,1},{4,6},{5,7},{6,4},{7,5},{8,10},{9,11},{10,... | collective-permute-start | bytes 3145736 | tf_op jit(solution)/shard_map/ppermute | solution.py:595
  69.8 32.3 %factor.1 = (bf16[1024,1024]{1,0:T(8,128)(2,1)S(1)}, bf16[1024,1024]{1,0:T(8,128)(2,1)S(1)}, bf16[1024,128]{1,0:T(8,128)(2,1)S(1)}, bf16[1024,128]{1,0:T(8,128)(2,1)S(1)}) custom-call(s32[2]{0:T(128)S(1)} %pad_add_fusion.place_ref, f32[4,32,640]{2,1,0:T(8,128)S(1)} %pad_maximum_fusion.refs_0_, f32[4,32,640]{2,1,0:T(8,128)S(1)} %collective-permute-done.12.refs_1_, ...), custom_call_target="tpu_custom_call" | custom-call | flops 49999998976 | bytes 8388608 | tf_op jit(solution)/shard_map/factor/pallas_call | solution.py:467
  102.1 4.8 %solve.1 = f32[256,1024]{1,0:T(8,128)} custom-call(s32[2]{0:T(128)S(1)} %pad_add_fusion.place_ref, f32[32,512]{1,0:T(8,128)S(1)} %get-tuple-element.120.refs_0_, f32[224,128]{1,0:T(8,128)S(1)} %cover.4.refs_1_, f32[96,384]{1,0:T(8,128)S(1)} %cover.5.refs_2_, f32[128,384]{1,0:T(8,128)S(1)} %cover.6.refs_3_, f32[256,512]{1,0:T(8,128)S(1)} %cover.7.refs_4_, ...), custom_call_target="tpu_custom_call" | custom-call | flops 100000000 | bytes 262144 | tf_op jit(solution)/shard_map/solve/pallas_call | solution.py:543
  (37 shorter events, 3.0 us)
Async XLA Ops:
  2.8 15.4 %collective-permute-start.1 = (f32[136,512]{1,0:T(8,128)S(1)}, f32[136,512]{1,0:T(8,128)S(1)}, u32[]{:S(2)}, u32[]{:S(2)}) collective-permute-start(f32[136,512]{1,0:T(8,128)S(1)} %pad_maximum_fusion.1.refs_0_), channel_id=1, source_target_pairs={{8,0},{12,4},{4,8},{0,12},{24,16},{28,20},{20,24},{16,28},{9,1},{1... | collective-permute-start | bytes 835592 | tf_op jit(solution)/shard_map/ppermute | solution.py:651
  6.8 13.0 %collective-permute-start.2 = (f32[136,512]{1,0:T(8,128)S(1)}, f32[136,512]{1,0:T(8,128)S(1)}, u32[]{:S(2)}, u32[]{:S(2)}) collective-permute-start(f32[136,512]{1,0:T(8,128)S(1)} %pad_maximum_fusion.1.refs_0_), channel_id=1, source_target_pairs={{4,0},{0,4},{12,8},{8,12},{20,16},{16,20},{28,24},{24,28},{5,1},{1... | collective-permute-start | bytes 835592 | tf_op jit(solution)/shard_map/ppermute | solution.py:651
  7.3 14.7 %collective-permute-start = (f32[136,512]{1,0:T(8,128)S(1)}, f32[136,512]{1,0:T(8,128)S(1)}, u32[]{:S(2)}, u32[]{:S(2)}) collective-permute-start(f32[136,512]{1,0:T(8,128)S(1)} %pad_maximum_fusion.1.refs_0_), channel_id=1, source_target_pairs={{0,16},{4,20},{8,24},{12,28},{16,0},{20,4},{24,8},{28,12},{1,17},{... | collective-permute-start | bytes 835592 | tf_op jit(solution)/shard_map/ppermute | solution.py:595
  18.2 11.6 %collective-permute-start.6 = (f32[136,512]{1,0:T(8,128)S(1)}, f32[136,512]{1,0:T(8,128)}, u32[]{:S(2)}, u32[]{:S(2)}) collective-permute-start(f32[136,512]{1,0:T(8,128)S(1)} %collective-permute-done.1.refs_2_), channel_id=1, source_target_pairs={{0,4},{4,0},{8,12},{12,8},{16,20},{20,16},{24,28},{28,24},{1,5},{5... | collective-permute-start | bytes 835592 | tf_op jit(solution)/shard_map/ppermute | solution.py:595
  23.3 5.3 %collective-permute-start.3 = (f32[32,640]{1,0:T(8,128)S(1)}, f32[32,640]{1,0:T(8,128)S(1)}, u32[]{:S(2)}, u32[]{:S(2)}) collective-permute-start(f32[32,640]{1,0:T(8,128)S(1)} %get-tuple-element.109), channel_id=1, source_target_pairs={{0,1},{1,0},{2,3},{3,2},{4,5},{5,4},{6,7},{7,6},{8,9},{9,8},{10,11... | collective-permute-start | bytes 245768 | tf_op jit(solution)/shard_map/ppermute | solution.py:595
  23.4 5.2 %collective-permute-start.4 = (f32[32,640]{1,0:T(8,128)S(1)}, f32[32,640]{1,0:T(8,128)S(1)}, u32[]{:S(2)}, u32[]{:S(2)}) collective-permute-start(f32[32,640]{1,0:T(8,128)S(1)} %get-tuple-element.110), channel_id=1, source_target_pairs={{0,2},{1,3},{2,0},{3,1},{4,6},{5,7},{6,4},{7,5},{8,10},{9,11},{10,... | collective-permute-start | bytes 245768 | tf_op jit(solution)/shard_map/ppermute | solution.py:595
  25.0 4.7 %collective-permute-start.5 = (f32[32,640]{1,0:T(8,128)S(1)}, f32[32,640]{1,0:T(8,128)S(1)}, u32[]{:S(2)}, u32[]{:S(2)}) collective-permute-start(f32[32,640]{1,0:T(8,128)S(1)} %get-tuple-element.111), channel_id=1, source_target_pairs={{0,3},{1,2},{2,1},{3,0},{4,7},{5,6},{6,5},{7,4},{8,11},{9,10},{10,... | collective-permute-start | bytes 245768 | tf_op jit(solution)/shard_map/ppermute | solution.py:595
  25.3 10.7 %collective-permute-start.8 = (f32[136,512]{1,0:T(8,128)S(1)}, f32[136,512]{1,0:T(8,128)S(1)}, u32[]{:S(2)}, u32[]{:S(2)}) collective-permute-start(f32[136,512]{1,0:T(8,128)S(1)} %collective-permute-done.refs_1_), channel_id=1, source_target_pairs={{0,8},{4,12},{8,0},{12,4},{16,24},{20,28},{24,16},{28,20},{1,9},{5... | collective-permute-start | bytes 835592 | tf_op jit(solution)/shard_map/ppermute | solution.py:595
  29.8 6.2 %collective-permute-start.7 = (f32[1,32,640]{2,1,0:T(8,128)S(1)}, f32[1,32,640]{2,1,0:T(8,128)S(1)}, u32[]{:S(2)}, u32[]{:S(2)}) collective-permute-start(f32[1,32,640]{2,1,0:T(8,128)S(1)} %subtract_bitcast_fusion), channel_id=1, source_target_pairs={{0,8},{4,12},{8,0},{12,4},{16,24},{20,28},{24,16},{28,20},{1,9},{5... | collective-permute-start | bytes 245768 | tf_op jit(solution)/shard_map/ppermute | solution.py:595
  30.8 9.3 %collective-permute-start.10 = (f32[136,512]{1,0:T(8,128)S(1)}, f32[136,512]{1,0:T(8,128)S(1)}, u32[]{:S(2)}, u32[]{:S(2)}) collective-permute-start(f32[136,512]{1,0:T(8,128)S(1)} %collective-permute-done.refs_1_), channel_id=1, source_target_pairs={{0,4},{4,0},{8,12},{12,8},{16,20},{20,16},{24,28},{28,24},{1,5},{5... | collective-permute-start | bytes 835592 | tf_op jit(solution)/shard_map/ppermute | solution.py:595
  35.9 9.2 %collective-permute-start.11 = (f32[136,512]{1,0:T(8,128)S(1)}, f32[136,512]{1,0:T(8,128)S(1)}, u32[]{:S(2)}, u32[]{:S(2)}) collective-permute-start(f32[136,512]{1,0:T(8,128)S(1)} %collective-permute-done.8.refs_6_.refs_2_), channel_id=1, source_target_pairs={{0,4},{4,0},{8,12},{12,8},{16,20},{20,16},{24,28},{28,24},{1,5},{5... | collective-permute-start | bytes 835592 | tf_op jit(solution)/shard_map/ppermute | solution.py:595
  37.4 11.4 %collective-permute-start.9 = (f32[2,32,640]{2,1,0:T(8,128)S(1)}, f32[2,32,640]{2,1,0:T(8,128)S(1)}, u32[]{:S(2)}, u32[]{:S(2)}) collective-permute-start(f32[2,32,640]{2,1,0:T(8,128)S(1)} %pad_maximum_fusion.2), channel_id=1, source_target_pairs={{0,16},{4,20},{8,24},{12,28},{16,0},{20,4},{24,8},{28,12},{1,17},{... | collective-permute-start | bytes 491528 | tf_op jit(solution)/shard_map/ppermute | solution.py:595
  44.2 2.2 %copy-start = (f32[1024,512]{1,0:T(8,128)S(1)}, f32[1024,512]{1,0:T(8,128)}, u32[]{:S(2)}) copy-start(f32[1024,512]{1,0:T(8,128)} %prior_ref.3) | copy-start | bytes 6291460
  48.8 15.9 %collective-permute-start.15 = (f32[2,256,1024]{2,1,0:T(8,128)S(1)}, f32[2,256,1024]{2,1,0:T(8,128)S(1)}, u32[]{:S(2)}, u32[]{:S(2)}) collective-permute-start(f32[2,256,1024]{2,1,0:T(8,128)S(1)} %rest_products.2), channel_id=1, source_target_pairs={{0,1},{1,0},{2,3},{3,2},{4,5},{5,4},{6,7},{7,6},{8,9},{9,8},{10,11... | collective-permute-start | bytes 6291464 | tf_op jit(solution)/shard_map/ppermute | solution.py:595
  48.9 18.2 %collective-permute-start.16 = (f32[4,32,640]{2,1,0:T(8,128)S(1)}, f32[4,32,640]{2,1,0:T(8,128)S(1)}, u32[]{:S(2)}, u32[]{:S(2)}) collective-permute-start(f32[4,32,640]{2,1,0:T(8,128)S(1)} %pad_maximum_fusion.refs_0_), channel_id=1, source_target_pairs={{0,1},{1,0},{2,3},{3,2},{4,5},{5,4},{6,7},{7,6},{8,9},{9,8},{10,11... | collective-permute-start | bytes 983048 | tf_op jit(solution)/shard_map/ppermute | solution.py:595
  49.5 17.6 %collective-permute-start.14 = (f32[4,32,640]{2,1,0:T(8,128)S(1)}, f32[4,32,640]{2,1,0:T(8,128)S(1)}, u32[]{:S(2)}, u32[]{:S(2)}) collective-permute-start(f32[4,32,640]{2,1,0:T(8,128)S(1)} %pad_maximum_fusion.refs_0_), channel_id=1, source_target_pairs={{0,6},{1,7},{2,4},{3,5},{4,2},{5,3},{6,0},{7,1},{8,14},{9,15},{10,... | collective-permute-start | bytes 983048 | tf_op jit(solution)/shard_map/ppermute | solution.py:773
  51.9 15.2 %collective-permute-start.13 = (f32[4,32,640]{2,1,0:T(8,128)S(1)}, f32[4,32,640]{2,1,0:T(8,128)S(1)}, u32[]{:S(2)}, u32[]{:S(2)}) collective-permute-start(f32[4,32,640]{2,1,0:T(8,128)S(1)} %pad_maximum_fusion.refs_0_), channel_id=1, source_target_pairs={{0,2},{1,3},{2,0},{3,1},{4,6},{5,7},{6,4},{7,5},{8,10},{9,11},{10,... | collective-permute-start | bytes 983048 | tf_op jit(solution)/shard_map/ppermute | solution.py:595
  52.5 14.8 %collective-permute-start.12 = (f32[4,32,640]{2,1,0:T(8,128)S(1)}, f32[4,32,640]{2,1,0:T(8,128)S(1)}, u32[]{:S(2)}, u32[]{:S(2)}) collective-permute-start(f32[4,32,640]{2,1,0:T(8,128)S(1)} %pad_maximum_fusion.refs_0_), channel_id=1, source_target_pairs={{0,4},{4,0},{8,12},{12,8},{16,20},{20,16},{24,28},{28,24},{1,5},{5... | collective-permute-start | bytes 983048 | tf_op jit(solution)/shard_map/ppermute | solution.py:595
  67.2 2.1 %collective-permute-start.18 = (f32[4,32,640]{2,1,0:T(8,128)S(1)}, f32[4,32,640]{2,1,0:T(8,128)S(1)}, u32[]{:S(2)}, u32[]{:S(2)}) collective-permute-start(f32[4,32,640]{2,1,0:T(8,128)S(1)} %collective-permute-done.12.refs_1_), channel_id=1, source_target_pairs={{0,1},{1,0},{2,3},{3,2},{4,5},{5,4},{6,7},{7,6},{8,9},{9,8},{10,11... | collective-permute-start | bytes 983048 | tf_op jit(solution)/shard_map/ppermute | solution.py:595
  67.3 2.1 %collective-permute-start.19 = (f32[4,32,640]{2,1,0:T(8,128)S(1)}, f32[4,32,640]{2,1,0:T(8,128)S(1)}, u32[]{:S(2)}, u32[]{:S(2)}) collective-permute-start(f32[4,32,640]{2,1,0:T(8,128)S(1)} %collective-permute-done.13.refs_2_), channel_id=1, source_target_pairs={{0,1},{1,0},{2,3},{3,2},{4,5},{5,4},{6,7},{7,6},{8,9},{9,8},{10,11... | collective-permute-start | bytes 983048 | tf_op jit(solution)/shard_map/ppermute | solution.py:595
  67.8 2.1 %collective-permute-start.20 = (f32[4,32,640]{2,1,0:T(8,128)S(1)}, f32[4,32,640]{2,1,0:T(8,128)S(1)}, u32[]{:S(2)}, u32[]{:S(2)}) collective-permute-start(f32[4,32,640]{2,1,0:T(8,128)S(1)} %collective-permute-done.14.refs_3_), channel_id=1, source_target_pairs={{0,1},{1,0},{2,3},{3,2},{4,5},{5,4},{6,7},{7,6},{8,9},{9,8},{10,11... | collective-permute-start | bytes 983048 | tf_op jit(solution)/shard_map/ppermute | solution.py:595
  67.8 34.3 %collective-permute-start.17 = (f32[1,256,1024]{2,1,0:T(8,128)S(1)}, f32[1,256,1024]{2,1,0:T(8,128)S(1)}, u32[]{:S(2)}, u32[]{:S(2)}) collective-permute-start(f32[1,256,1024]{2,1,0:T(8,128)S(1)} %get-tuple-element.170), channel_id=1, source_target_pairs={{0,2},{1,3},{2,0},{3,1},{4,6},{5,7},{6,4},{7,5},{8,10},{9,11},{10,... | collective-permute-start | bytes 3145736 | tf_op jit(solution)/shard_map/ppermute | solution.py:595

commit v14 on v13

--- a/solution.py
+++ b/solution.py
@@ -741,8 +741,7 @@
     middle = quarter_rows // 2
 
     def beside_far_z(_, held):
-        held, arrived = lax.optimization_barrier((held, far_x))
-        rest = [from_x, arrived, far_z, last]
+        rest = [from_x, far_x, far_z, last]
         cover = later_cover(held, middle, quarter_rows - middle)
         cover, blocks = lax.optimization_barrier((cover, rest))
         panel_prior = vmem_call(

time: 107 us -> 107 us (level)
  transfers between devices with their start and end apart: 21 -> 21, of which waited for: 6 -> 5; matrix products, arithmetic and copies ran while one was open for 0% -> 0% of each run, Pallas kernels for 65% -> 65%
where the time goes in v14:
time: 107 us
  Pallas kernels  74.7 us (70%)
  starting transfers between devices  21.5 us (20%)
  waiting for transfers between devices  7.49 us (7%)
  other arithmetic  1.76 us (2%)
  local copies, waits for them, and re-layouts  1.14 us (1%)
    pallas_call x10, Pallas kernels, vmem_call(): pl.pallas_call(kernel, out_shape=out_shape, in_specs=[pl.BlockSpec(memory...  37.6 us
    pallas_call x1, Pallas kernels, factor(): pl.pallas_call(kernel, out_shape=[jax.ShapeDtypeStruct((n, n), BF)] * 2 +...  32.3 us
    ppermute x18, starting transfers between devices, swap(): lax.ppermute(block, axis, [(i, i ^ bit) for i in range(lax.axis_size(axis...  14.5 us
    ppermute x18, waiting for transfers between devices, swap(): lax.ppermute(block, axis, [(i, i ^ bit) for i in range(lax.axis_size(axis...  7.48 us
    pallas_call x1, Pallas kernels, row_table(): pl.pallas_call(row_table_kernel, out_shape=[jax.ShapeDtypeStruct((8, rows...  4.85 us
    ppermute x2, starting transfers between devices, turn(): return lax.ppermute(block, 'row', [(turned(d, k), d) for d in range(8)])  4.54 us
    ppermute x1, starting transfers between devices, across(): lax.ppermute(x, ('row', 'panel'), corner)  2.45 us
  transfers between devices with their start and end apart: 21, of which 5 were waited for; matrix products, arithmetic and copies ran while one was open for 0% of the time, Pallas kernels for 65%

profile of v14, /device:TPU:0, one launch (start us, length us, event | category | flops | bytes accessed | tf_op | source)
XLA Modules:
  0.0 106.9 jit_solution(14368206666702441178)
XLA Ops:
  0.0 0.7 fusion.1
  0.7 0.9 convert_add_fusion.1
  1.8 1.0 slice.16
  2.8 4.0 %collective-permute-start.1 = (f32[136,512]{1,0:T(8,128)S(1)}, f32[136,512]{1,0:T(8,128)S(1)}, u32[]{:S(2)}, u32[]{:S(2)}) collective-permute-start(f32[136,512]{1,0:T(8,128)S(1)} %pad_maximum_fusion.1.refs_0_), channel_id=1, source_target_pairs={{8,0},{12,4},{4,8},{0,12},{24,16},{28,20},{20,24},{16,28},{9,1},{1... | collective-permute-start | bytes 835592 | tf_op jit(solution)/shard_map/ppermute | solution.py:651
  6.8 0.5 collective-permute-start.2
  7.3 2.6 %collective-permute-start = (f32[136,512]{1,0:T(8,128)S(1)}, f32[136,512]{1,0:T(8,128)S(1)}, u32[]{:S(2)}, u32[]{:S(2)}) collective-permute-start(f32[136,512]{1,0:T(8,128)S(1)} %pad_maximum_fusion.1.refs_0_), channel_id=1, source_target_pairs={{0,16},{4,20},{8,24},{12,28},{16,0},{20,4},{24,8},{28,12},{1,17},{... | collective-permute-start | bytes 835592 | tf_op jit(solution)/shard_map/ppermute | solution.py:595
  9.9 4.8 %row_table.1 = (bf16[8,256,512]{2,1,0:T(8,128)(2,1)S(1)}, f32[256,1]{1,0:T(8,128)S(1)}) custom-call(f32[2,16,256]{2,1,0:T(8,128)S(1)} %fusion.row_ref), custom_call_target="tpu_custom_call" | custom-call | flops 100000000 | bytes 262144 | tf_op jit(solution)/shard_map/row_table/pallas_call | solution.py:148
  14.8 3.4 %cover.4.refs_1_ = f32[224,128]{1,0:T(8,128)S(1)} custom-call(bf16[8,256,512]{2,1,0:T(8,128)(2,1)S(1)} %get-tuple-element.150.t_ref, f32[256,1]{1,0:T(8,128)S(1)} %get-tuple-element.151.row_cell_ref, f32[136,512]{1,0:T(8,128)S(1)} %pad_maximum_fusion.1.refs_0_), custom_call_target="tpu_custom_call" | custom-call | flops 100000000 | bytes 262144 | tf_op jit(solution)/shard_map/cover/pallas_call | solution.py:543
  18.2 1.6 %collective-permute-start.6 = (f32[136,512]{1,0:T(8,128)S(1)}, f32[136,512]{1,0:T(8,128)}, u32[]{:S(2)}, u32[]{:S(2)}) collective-permute-start(f32[136,512]{1,0:T(8,128)S(1)} %collective-permute-done.1.refs_2_), channel_id=1, source_target_pairs={{0,4},{4,0},{8,12},{12,8},{16,20},{20,16},{24,28},{28,24},{1,5},{5... | collective-permute-start | bytes 835592 | tf_op jit(solution)/shard_map/ppermute | solution.py:595
  19.8 2.3 %collective-permute-done.refs_1_ = f32[136,512]{1,0:T(8,128)S(1)} collective-permute-done((f32[136,512]{1,0:T(8,128)S(1)}, f32[136,512]{1,0:T(8,128)S(1)}, u32[]{:S(2)}, u32[]{:S(2)}) %collective-permute-start) | collective-permute-done | bytes 278560 | tf_op jit(solution)/shard_map/ppermute | solution.py:595
  22.1 1.2 %fold_products.1 = (f32[32,640]{1,0:T(8,128)S(1)}, f32[32,640]{1,0:T(8,128)S(1)}, f32[32,640]{1,0:T(8,128)S(1)}, f32[32,640]{1,0:T(8,128)S(1)}) custom-call(s32[2]{0:T(128)S(1)} %pad_add_fusion.place_ref, f32[136,512]{1,0:T(8,128)S(1)} %pad_maximum_fusion.1.refs_0_, f32[136,512]{1,0:T(8,128)S(1)} %collective-permute-done.refs_1_, ...), custom_call_target="tpu_custom_call" | custom-call | flops 100000000 | bytes 262144 | tf_op jit(solution)/shard_map/fold_products/pallas_call | solution.py:543
  23.4 1.6 %collective-permute-start.4 = (f32[32,640]{1,0:T(8,128)S(1)}, f32[32,640]{1,0:T(8,128)S(1)}, u32[]{:S(2)}, u32[]{:S(2)}) collective-permute-start(f32[32,640]{1,0:T(8,128)S(1)} %get-tuple-element.107), channel_id=1, source_target_pairs={{0,2},{1,3},{2,0},{3,1},{4,6},{5,7},{6,4},{7,5},{8,10},{9,11},{10,... | collective-permute-start | bytes 245768 | tf_op jit(solution)/shard_map/ppermute | solution.py:595
  25.3 3.4 %lead_cover.1 = (f32[32,640]{1,0:T(8,128)S(1)}, f32[32,512]{1,0:T(8,128)S(1)}, bf16[256,4096]{1,0:T(8,128)(2,1)S(1)}, f32[1,512]{1,0:T(1,128)S(1)}) custom-call(s32[2]{0:T(128)S(1)} %pad_add_fusion.place_ref, bf16[8,256,512]{2,1,0:T(8,128)(2,1)S(1)} %get-tuple-element.150.t_ref, f32[256,1]{1,0:T(8,128)S(1)} %get-tuple-element.151.row_cell_ref, ...), custom_call_target="tpu_custom_call" | custom-call | flops 100000000 | bytes 262144 | tf_op jit(solution)/shard_map/lead_cover/pallas_call | solution.py:543
  28.7 1.1 collective-permute-done.5
  29.8 1.1 collective-permute-start.7
  30.8 1.5 %collective-permute-start.10 = (f32[136,512]{1,0:T(8,128)S(1)}, f32[136,512]{1,0:T(8,128)S(1)}, u32[]{:S(2)}, u32[]{:S(2)}) collective-permute-start(f32[136,512]{1,0:T(8,128)S(1)} %collective-permute-done.refs_1_), channel_id=1, source_target_pairs={{0,4},{4,0},{8,12},{12,8},{16,20},{20,16},{24,28},{28,24},{1,5},{5... | collective-permute-start | bytes 835592 | tf_op jit(solution)/shard_map/ppermute | solution.py:595
  32.3 3.0 %cover.5.refs_2_ = f32[96,384]{1,0:T(8,128)S(1)} custom-call(bf16[8,256,512]{2,1,0:T(8,128)(2,1)S(1)} %get-tuple-element.150.t_ref, f32[256,1]{1,0:T(8,128)S(1)} %get-tuple-element.151.row_cell_ref, bf16[256,4096]{1,0:T(8,128)(2,1)S(1)} %get-tuple-element.129.h_ref, f32[1,512]{1,0:T(1,128)S(1)} %get-tuple-element.130.col_cell_ref), custom_call_target="tpu_custom_call" | custom-call | flops 100000000 | bytes 262144 | tf_op jit(solution)/shard_map/cover/pallas_call | solution.py:543
  35.3 0.6 collective-permute-done.7
  35.9 1.5 %collective-permute-start.11 = (f32[136,512]{1,0:T(8,128)S(1)}, f32[136,512]{1,0:T(8,128)S(1)}, u32[]{:S(2)}, u32[]{:S(2)}) collective-permute-start(f32[136,512]{1,0:T(8,128)S(1)} %collective-permute-done.8.refs_6_.refs_2_), channel_id=1, source_target_pairs={{0,4},{4,0},{8,12},{12,8},{16,20},{20,16},{24,28},{28,24},{1,5},{5... | collective-permute-start | bytes 835592 | tf_op jit(solution)/shard_map/ppermute | solution.py:595
  37.4 0.7 collective-permute-start.9
  38.1 4.0 %cover.6.refs_3_ = f32[128,384]{1,0:T(8,128)S(1)} custom-call(bf16[8,256,512]{2,1,0:T(8,128)(2,1)S(1)} %get-tuple-element.150.t_ref, f32[256,1]{1,0:T(8,128)S(1)} %get-tuple-element.151.row_cell_ref, bf16[256,4096]{1,0:T(8,128)(2,1)S(1)} %get-tuple-element.129.h_ref, f32[1,512]{1,0:T(1,128)S(1)} %get-tuple-element.130.col_cell_ref), custom_call_target="tpu_custom_call" | custom-call | flops 100000000 | bytes 262144 | tf_op jit(solution)/shard_map/cover/pallas_call | solution.py:543
  42.1 3.0 %collective-permute-done.11.refs_7_.refs_3_ = f32[136,512]{1,0:T(8,128)S(1)} collective-permute-done((f32[136,512]{1,0:T(8,128)S(1)}, f32[136,512]{1,0:T(8,128)S(1)}, u32[]{:S(2)}, u32[]{:S(2)}) %collective-permute-start.11) | collective-permute-done | bytes 278560 | tf_op jit(solution)/shard_map/ppermute | solution.py:595
  45.1 1.3 %gather_split.1 = (bf16[1024,512]{1,0:T(8,128)(2,1)S(1)}, bf16[1024,512]{1,0:T(8,128)(2,1)S(1)}) custom-call(s32[2]{0:T(128)S(1)} %pad_add_fusion.place_ref, f32[136,512]{1,0:T(8,128)S(1)} %pad_maximum_fusion.1.refs_0_, f32[136,512]{1,0:T(8,128)S(1)} %collective-permute-done.refs_1_, f32[136,512]{1,0:T(8,128)S(1)} %collective-permute-done.1.refs_2_, ...), custom_call_target="tpu_custom_call" | custom-call | flops 100000000 | bytes 262144 | tf_op jit(solution)/shard_map/gather_split/pallas_call | solution.py:543
  46.4 2.4 %rest_products.2 = f32[2,256,1024]{2,1,0:T(8,128)S(1)} custom-call(s32[2]{0:T(128)S(1)} %pad_add_fusion.place_ref, f32[1024,512]{1,0:T(8,128)S(1)} %copy-done, bf16[1024,512]{1,0:T(8,128)(2,1)S(1)} %get-tuple-element.156.high_ref, bf16[1024,512]{1,0:T(8,128)(2,1)S(1)} %get-tuple-element.157.low_ref), custom_call_target="tpu_custom_call" | custom-call | flops 100000000 | bytes 262144 | tf_op jit(solution)/shard_map/rest_products/pallas_call | solution.py:543
  48.9 0.6 collective-permute-start.16
  49.5 2.5 %collective-permute-start.14 = (f32[4,32,640]{2,1,0:T(8,128)S(1)}, f32[4,32,640]{2,1,0:T(8,128)S(1)}, u32[]{:S(2)}, u32[]{:S(2)}) collective-permute-start(f32[4,32,640]{2,1,0:T(8,128)S(1)} %pad_maximum_fusion.refs_0_), channel_id=1, source_target_pairs={{0,6},{1,7},{2,4},{3,5},{4,2},{5,3},{6,0},{7,1},{8,14},{9,15},{10,... | collective-permute-start | bytes 983048 | tf_op jit(solution)/shard_map/ppermute | solution.py:772
  52.5 0.5 collective-permute-start.12
  53.0 11.7 %cover.7.refs_4_ = f32[256,512]{1,0:T(8,128)S(1)} custom-call(bf16[8,256,512]{2,1,0:T(8,128)(2,1)S(1)} %get-tuple-element.150.t_ref, f32[256,1]{1,0:T(8,128)S(1)} %get-tuple-element.151.row_cell_ref, f32[136,512]{1,0:T(8,128)} %collective-permute-done.6.refs_4_.refs_0_, f32[136,512]{1,0:T(8,128)S(1)} %collective-permute-done.10.refs_5_.refs_1_, ...), custom_call_target="tpu_custom_call" | custom-call | flops 100000000 | bytes 262144 | tf_op jit(solution)/shard_map/cover/pallas_call | solution.py:543
  64.7 2.4 %rest_products.3 = (f32[1,256,1024]{2,1,0:T(8,128)S(1)}, f32[1,256,1024]{2,1,0:T(8,128)S(1)}) custom-call(s32[2]{0:T(128)S(1)} %pad_add_fusion.place_ref, f32[1024,512]{1,0:T(8,128)S(1)} %copy-done, bf16[1024,512]{1,0:T(8,128)(2,1)S(1)} %get-tuple-element.156.high_ref, bf16[1024,512]{1,0:T(8,128)(2,1)S(1)} %get-tuple-element.157.low_ref, ...), custom_call_target="tpu_custom_call" | custom-call | flops 100000000 | bytes 262144 | tf_op jit(solution)/shard_map/rest_products/pallas_call | solution.py:543
  67.8 1.5 %collective-permute-start.17 = (f32[1,256,1024]{2,1,0:T(8,128)S(1)}, f32[1,256,1024]{2,1,0:T(8,128)S(1)}, u32[]{:S(2)}, u32[]{:S(2)}) collective-permute-start(f32[1,256,1024]{2,1,0:T(8,128)S(1)} %get-tuple-element.164), channel_id=1, source_target_pairs={{0,2},{1,3},{2,0},{3,1},{4,6},{5,7},{6,4},{7,5},{8,10},{9,11},{10,... | collective-permute-start | bytes 3145736 | tf_op jit(solution)/shard_map/ppermute | solution.py:595
  69.8 32.3 %factor.1 = (bf16[1024,1024]{1,0:T(8,128)(2,1)S(1)}, bf16[1024,1024]{1,0:T(8,128)(2,1)S(1)}, bf16[1024,128]{1,0:T(8,128)(2,1)S(1)}, bf16[1024,128]{1,0:T(8,128)(2,1)S(1)}) custom-call(s32[2]{0:T(128)S(1)} %pad_add_fusion.place_ref, f32[4,32,640]{2,1,0:T(8,128)S(1)} %pad_maximum_fusion.refs_0_, f32[4,32,640]{2,1,0:T(8,128)S(1)} %collective-permute-done.12.refs_1_, ...), custom_call_target="tpu_custom_call" | custom-call | flops 49999998976 | bytes 8388608 | tf_op jit(solution)/shard_map/factor/pallas_call | solution.py:467
  102.1 4.8 %solve.1 = f32[256,1024]{1,0:T(8,128)} custom-call(s32[2]{0:T(128)S(1)} %pad_add_fusion.place_ref, f32[32,512]{1,0:T(8,128)S(1)} %get-tuple-element.117.refs_0_, f32[224,128]{1,0:T(8,128)S(1)} %cover.4.refs_1_, f32[96,384]{1,0:T(8,128)S(1)} %cover.5.refs_2_, f32[128,384]{1,0:T(8,128)S(1)} %cover.6.refs_3_, f32[256,512]{1,0:T(8,128)S(1)} %cover.7.refs_4_, ...), custom_call_target="tpu_custom_call" | custom-call | flops 100000000 | bytes 262144 | tf_op jit(solution)/shard_map/solve/pallas_call | solution.py:543
  (37 shorter events, 2.4 us)
Async XLA Ops:
  2.8 15.4 %collective-permute-start.1 = (f32[136,512]{1,0:T(8,128)S(1)}, f32[136,512]{1,0:T(8,128)S(1)}, u32[]{:S(2)}, u32[]{:S(2)}) collective-permute-start(f32[136,512]{1,0:T(8,128)S(1)} %pad_maximum_fusion.1.refs_0_), channel_id=1, source_target_pairs={{8,0},{12,4},{4,8},{0,12},{24,16},{28,20},{20,24},{16,28},{9,1},{1... | collective-permute-start | bytes 835592 | tf_op jit(solution)/shard_map/ppermute | solution.py:651
  6.8 13.0 %collective-permute-start.2 = (f32[136,512]{1,0:T(8,128)S(1)}, f32[136,512]{1,0:T(8,128)S(1)}, u32[]{:S(2)}, u32[]{:S(2)}) collective-permute-start(f32[136,512]{1,0:T(8,128)S(1)} %pad_maximum_fusion.1.refs_0_), channel_id=1, source_target_pairs={{4,0},{0,4},{12,8},{8,12},{20,16},{16,20},{28,24},{24,28},{5,1},{1... | collective-permute-start | bytes 835592 | tf_op jit(solution)/shard_map/ppermute | solution.py:651
  7.3 14.7 %collective-permute-start = (f32[136,512]{1,0:T(8,128)S(1)}, f32[136,512]{1,0:T(8,128)S(1)}, u32[]{:S(2)}, u32[]{:S(2)}) collective-permute-start(f32[136,512]{1,0:T(8,128)S(1)} %pad_maximum_fusion.1.refs_0_), channel_id=1, source_target_pairs={{0,16},{4,20},{8,24},{12,28},{16,0},{20,4},{24,8},{28,12},{1,17},{... | collective-permute-start | bytes 835592 | tf_op jit(solution)/shard_map/ppermute | solution.py:595
  18.2 11.6 %collective-permute-start.6 = (f32[136,512]{1,0:T(8,128)S(1)}, f32[136,512]{1,0:T(8,128)}, u32[]{:S(2)}, u32[]{:S(2)}) collective-permute-start(f32[136,512]{1,0:T(8,128)S(1)} %collective-permute-done.1.refs_2_), channel_id=1, source_target_pairs={{0,4},{4,0},{8,12},{12,8},{16,20},{20,16},{24,28},{28,24},{1,5},{5... | collective-permute-start | bytes 835592 | tf_op jit(solution)/shard_map/ppermute | solution.py:595
  23.3 5.3 %collective-permute-start.3 = (f32[32,640]{1,0:T(8,128)S(1)}, f32[32,640]{1,0:T(8,128)S(1)}, u32[]{:S(2)}, u32[]{:S(2)}) collective-permute-start(f32[32,640]{1,0:T(8,128)S(1)} %get-tuple-element.106), channel_id=1, source_target_pairs={{0,1},{1,0},{2,3},{3,2},{4,5},{5,4},{6,7},{7,6},{8,9},{9,8},{10,11... | collective-permute-start | bytes 245768 | tf_op jit(solution)/shard_map/ppermute | solution.py:595
  23.4 5.2 %collective-permute-start.4 = (f32[32,640]{1,0:T(8,128)S(1)}, f32[32,640]{1,0:T(8,128)S(1)}, u32[]{:S(2)}, u32[]{:S(2)}) collective-permute-start(f32[32,640]{1,0:T(8,128)S(1)} %get-tuple-element.107), channel_id=1, source_target_pairs={{0,2},{1,3},{2,0},{3,1},{4,6},{5,7},{6,4},{7,5},{8,10},{9,11},{10,... | collective-permute-start | bytes 245768 | tf_op jit(solution)/shard_map/ppermute | solution.py:595
  25.0 4.7 %collective-permute-start.5 = (f32[32,640]{1,0:T(8,128)S(1)}, f32[32,640]{1,0:T(8,128)S(1)}, u32[]{:S(2)}, u32[]{:S(2)}) collective-permute-start(f32[32,640]{1,0:T(8,128)S(1)} %get-tuple-element.108), channel_id=1, source_target_pairs={{0,3},{1,2},{2,1},{3,0},{4,7},{5,6},{6,5},{7,4},{8,11},{9,10},{10,... | collective-permute-start | bytes 245768 | tf_op jit(solution)/shard_map/ppermute | solution.py:595
  25.3 10.7 %collective-permute-start.8 = (f32[136,512]{1,0:T(8,128)S(1)}, f32[136,512]{1,0:T(8,128)S(1)}, u32[]{:S(2)}, u32[]{:S(2)}) collective-permute-start(f32[136,512]{1,0:T(8,128)S(1)} %collective-permute-done.refs_1_), channel_id=1, source_target_pairs={{0,8},{4,12},{8,0},{12,4},{16,24},{20,28},{24,16},{28,20},{1,9},{5... | collective-permute-start | bytes 835592 | tf_op jit(solution)/shard_map/ppermute | solution.py:595
  29.8 6.2 %collective-permute-start.7 = (f32[1,32,640]{2,1,0:T(8,128)S(1)}, f32[1,32,640]{2,1,0:T(8,128)S(1)}, u32[]{:S(2)}, u32[]{:S(2)}) collective-permute-start(f32[1,32,640]{2,1,0:T(8,128)S(1)} %subtract_bitcast_fusion), channel_id=1, source_target_pairs={{0,8},{4,12},{8,0},{12,4},{16,24},{20,28},{24,16},{28,20},{1,9},{5... | collective-permute-start | bytes 245768 | tf_op jit(solution)/shard_map/ppermute | solution.py:595
  30.8 11.3 %collective-permute-start.10 = (f32[136,512]{1,0:T(8,128)S(1)}, f32[136,512]{1,0:T(8,128)S(1)}, u32[]{:S(2)}, u32[]{:S(2)}) collective-permute-start(f32[136,512]{1,0:T(8,128)S(1)} %collective-permute-done.refs_1_), channel_id=1, source_target_pairs={{0,4},{4,0},{8,12},{12,8},{16,20},{20,16},{24,28},{28,24},{1,5},{5... | collective-permute-start | bytes 835592 | tf_op jit(solution)/shard_map/ppermute | solution.py:595
  35.9 9.2 %collective-permute-start.11 = (f32[136,512]{1,0:T(8,128)S(1)}, f32[136,512]{1,0:T(8,128)S(1)}, u32[]{:S(2)}, u32[]{:S(2)}) collective-permute-start(f32[136,512]{1,0:T(8,128)S(1)} %collective-permute-done.8.refs_6_.refs_2_), channel_id=1, source_target_pairs={{0,4},{4,0},{8,12},{12,8},{16,20},{20,16},{24,28},{28,24},{1,5},{5... | collective-permute-start | bytes 835592 | tf_op jit(solution)/shard_map/ppermute | solution.py:595
  37.4 11.4 %collective-permute-start.9 = (f32[2,32,640]{2,1,0:T(8,128)S(1)}, f32[2,32,640]{2,1,0:T(8,128)S(1)}, u32[]{:S(2)}, u32[]{:S(2)}) collective-permute-start(f32[2,32,640]{2,1,0:T(8,128)S(1)} %pad_maximum_fusion.2), channel_id=1, source_target_pairs={{0,16},{4,20},{8,24},{12,28},{16,0},{20,4},{24,8},{28,12},{1,17},{... | collective-permute-start | bytes 491528 | tf_op jit(solution)/shard_map/ppermute | solution.py:595
  42.1 4.3 %copy-start = (f32[1024,512]{1,0:T(8,128)S(1)}, f32[1024,512]{1,0:T(8,128)}, u32[]{:S(2)}) copy-start(f32[1024,512]{1,0:T(8,128)} %prior_ref.3) | copy-start | bytes 6291460
  48.8 15.9 %collective-permute-start.15 = (f32[2,256,1024]{2,1,0:T(8,128)S(1)}, f32[2,256,1024]{2,1,0:T(8,128)S(1)}, u32[]{:S(2)}, u32[]{:S(2)}) collective-permute-start(f32[2,256,1024]{2,1,0:T(8,128)S(1)} %rest_products.2), channel_id=1, source_target_pairs={{0,1},{1,0},{2,3},{3,2},{4,5},{5,4},{6,7},{7,6},{8,9},{9,8},{10,11... | collective-permute-start | bytes 6291464 | tf_op jit(solution)/shard_map/ppermute | solution.py:595
  48.9 18.2 %collective-permute-start.16 = (f32[4,32,640]{2,1,0:T(8,128)S(1)}, f32[4,32,640]{2,1,0:T(8,128)S(1)}, u32[]{:S(2)}, u32[]{:S(2)}) collective-permute-start(f32[4,32,640]{2,1,0:T(8,128)S(1)} %pad_maximum_fusion.refs_0_), channel_id=1, source_target_pairs={{0,1},{1,0},{2,3},{3,2},{4,5},{5,4},{6,7},{7,6},{8,9},{9,8},{10,11... | collective-permute-start | bytes 983048 | tf_op jit(solution)/shard_map/ppermute | solution.py:595
  49.5 17.6 %collective-permute-start.14 = (f32[4,32,640]{2,1,0:T(8,128)S(1)}, f32[4,32,640]{2,1,0:T(8,128)S(1)}, u32[]{:S(2)}, u32[]{:S(2)}) collective-permute-start(f32[4,32,640]{2,1,0:T(8,128)S(1)} %pad_maximum_fusion.refs_0_), channel_id=1, source_target_pairs={{0,6},{1,7},{2,4},{3,5},{4,2},{5,3},{6,0},{7,1},{8,14},{9,15},{10,... | collective-permute-start | bytes 983048 | tf_op jit(solution)/shard_map/ppermute | solution.py:772
  51.9 15.2 %collective-permute-start.13 = (f32[4,32,640]{2,1,0:T(8,128)S(1)}, f32[4,32,640]{2,1,0:T(8,128)S(1)}, u32[]{:S(2)}, u32[]{:S(2)}) collective-permute-start(f32[4,32,640]{2,1,0:T(8,128)S(1)} %pad_maximum_fusion.refs_0_), channel_id=1, source_target_pairs={{0,2},{1,3},{2,0},{3,1},{4,6},{5,7},{6,4},{7,5},{8,10},{9,11},{10,... | collective-permute-start | bytes 983048 | tf_op jit(solution)/shard_map/ppermute | solution.py:595
  52.5 14.8 %collective-permute-start.12 = (f32[4,32,640]{2,1,0:T(8,128)S(1)}, f32[4,32,640]{2,1,0:T(8,128)S(1)}, u32[]{:S(2)}, u32[]{:S(2)}) collective-permute-start(f32[4,32,640]{2,1,0:T(8,128)S(1)} %pad_maximum_fusion.refs_0_), channel_id=1, source_target_pairs={{0,4},{4,0},{8,12},{12,8},{16,20},{20,16},{24,28},{28,24},{1,5},{5... | collective-permute-start | bytes 983048 | tf_op jit(solution)/shard_map/ppermute | solution.py:595
  67.2 2.1 %collective-permute-start.18 = (f32[4,32,640]{2,1,0:T(8,128)S(1)}, f32[4,32,640]{2,1,0:T(8,128)S(1)}, u32[]{:S(2)}, u32[]{:S(2)}) collective-permute-start(f32[4,32,640]{2,1,0:T(8,128)S(1)} %collective-permute-done.12.refs_1_), channel_id=1, source_target_pairs={{0,1},{1,0},{2,3},{3,2},{4,5},{5,4},{6,7},{7,6},{8,9},{9,8},{10,11... | collective-permute-start | bytes 983048 | tf_op jit(solution)/shard_map/ppermute | solution.py:595
  67.3 2.1 %collective-permute-start.19 = (f32[4,32,640]{2,1,0:T(8,128)S(1)}, f32[4,32,640]{2,1,0:T(8,128)S(1)}, u32[]{:S(2)}, u32[]{:S(2)}) collective-permute-start(f32[4,32,640]{2,1,0:T(8,128)S(1)} %collective-permute-done.13.refs_2_), channel_id=1, source_target_pairs={{0,1},{1,0},{2,3},{3,2},{4,5},{5,4},{6,7},{7,6},{8,9},{9,8},{10,11... | collective-permute-start | bytes 983048 | tf_op jit(solution)/shard_map/ppermute | solution.py:595
  67.8 2.1 %collective-permute-start.20 = (f32[4,32,640]{2,1,0:T(8,128)S(1)}, f32[4,32,640]{2,1,0:T(8,128)S(1)}, u32[]{:S(2)}, u32[]{:S(2)}) collective-permute-start(f32[4,32,640]{2,1,0:T(8,128)S(1)} %collective-permute-done.14.refs_3_), channel_id=1, source_target_pairs={{0,1},{1,0},{2,3},{3,2},{4,5},{5,4},{6,7},{7,6},{8,9},{9,8},{10,11... | collective-permute-start | bytes 983048 | tf_op jit(solution)/shard_map/ppermute | solution.py:595
  67.8 34.3 %collective-permute-start.17 = (f32[1,256,1024]{2,1,0:T(8,128)S(1)}, f32[1,256,1024]{2,1,0:T(8,128)S(1)}, u32[]{:S(2)}, u32[]{:S(2)}) collective-permute-start(f32[1,256,1024]{2,1,0:T(8,128)S(1)} %get-tuple-element.164), channel_id=1, source_target_pairs={{0,2},{1,3},{2,0},{3,1},{4,6},{5,7},{6,4},{7,5},{8,10},{9,11},{10,... | collective-permute-start | bytes 3145736 | tf_op jit(solution)/shard_map/ppermute | solution.py:595

commit v15 on v14

--- a/solution.py
+++ b/solution.py
@@ -578,17 +578,18 @@
 
 def rest_products_kernel(place_ref, prior_ref, high_ref, low_ref, *refs, turns, outs):
     plus_refs, members = refs[:-outs], [ref.at[i] for ref in refs[-outs:] for i in range(ref.shape[0])]
-    for m, o_ref in zip(turns, members):
-        rows = o_ref.shape[0]
-        first = pl.multiple_of((place_ref[1] ^ m) * rows, rows)
-        own_high, own_low = split(prior_ref[pl.ds(first, rows)])
-        for c in range(0, o_ref.shape[1], 2 * NB):
-            cols = slice(c, c + 2 * NB)
-            total = dot3(own_high, own_low, high_ref[cols], low_ref[cols])
-            if m == turns[-1]:
+    rows, width = members[0].shape
+    own = [prior_ref[pl.ds(pl.multiple_of((place_ref[1] ^ m) * rows, rows), rows)] for m in turns]
+    own_high, own_low = split(jnp.concatenate(own, 0))
+    for c in range(0, width, 2 * NB):
+        cols = slice(c, c + 2 * NB)
+        total = dot3(own_high, own_low, high_ref[cols], low_ref[cols])
+        for i, o_ref in enumerate(members):
+            part = total[i * rows : (i + 1) * rows]
+            if i == len(members) - 1:
                 for plus_ref in plus_refs:
-                    total = total + plus_ref[0, :, cols]
-            o_ref[:, cols] = total
+                    part = part + plus_ref[0, :, cols]
+            o_ref[:, cols] = part
 
 
 def swap(block, axis, bit):

time: 107 us -> 107 us (level)
  transfers between devices with their start and end apart: 21 -> 21, of which waited for: 5 -> 6; matrix products, arithmetic and copies ran while one was open for 0% -> 0% of each run, Pallas kernels for 65% -> 65%
where the time goes in v15:
time: 107 us
  Pallas kernels  74.7 us (70%)
  starting transfers between devices  21.5 us (20%)
  waiting for transfers between devices  7.51 us (7%)
  other arithmetic  1.76 us (2%)
  local copies, waits for them, and re-layouts  1.14 us (1%)
    pallas_call x10, Pallas kernels, vmem_call(): pl.pallas_call(kernel, out_shape=out_shape, in_specs=[pl.BlockSpec(memory...  37.5 us
    pallas_call x1, Pallas kernels, factor(): pl.pallas_call(kernel, out_shape=[jax.ShapeDtypeStruct((n, n), BF)] * 2 +...  32.3 us
    ppermute x18, starting transfers between devices, swap(): lax.ppermute(block, axis, [(i, i ^ bit) for i in range(lax.axis_size(axis...  14.5 us
    ppermute x18, waiting for transfers between devices, swap(): lax.ppermute(block, axis, [(i, i ^ bit) for i in range(lax.axis_size(axis...  7.5 us
    pallas_call x1, Pallas kernels, row_table(): pl.pallas_call(row_table_kernel, out_shape=[jax.ShapeDtypeStruct((8, rows...  4.85 us
    ppermute x2, starting transfers between devices, turn(): return lax.ppermute(block, 'row', [(turned(d, k), d) for d in range(8)])  4.54 us
    ppermute x1, starting transfers between devices, across(): lax.ppermute(x, ('row', 'panel'), corner)  2.45 us
  transfers between devices with their start and end apart: 21, of which 6 were waited for; matrix products, arithmetic and copies ran while one was open for 0% of the time, Pallas kernels for 65%

profile of v15, /device:TPU:0, one launch (start us, length us, event | category | flops | bytes accessed | tf_op | source)
XLA Modules:
  0.0 106.9 jit_solution(8095706818516099121)
XLA Ops:
  0.0 0.7 fusion.1
  0.7 0.9 convert_add_fusion.1
  1.8 1.0 slice.16
  2.8 4.0 %collective-permute-start.1 = (f32[136,512]{1,0:T(8,128)S(1)}, f32[136,512]{1,0:T(8,128)S(1)}, u32[]{:S(2)}, u32[]{:S(2)}) collective-permute-start(f32[136,512]{1,0:T(8,128)S(1)} %pad_maximum_fusion.1.refs_0_), channel_id=1, source_target_pairs={{8,0},{12,4},{4,8},{0,12},{24,16},{28,20},{20,24},{16,28},{9,1},{1... | collective-permute-start | bytes 835592 | tf_op jit(solution)/shard_map/ppermute | solution.py:652
  6.8 0.5 collective-permute-start.2
  7.3 2.6 %collective-permute-start = (f32[136,512]{1,0:T(8,128)S(1)}, f32[136,512]{1,0:T(8,128)S(1)}, u32[]{:S(2)}, u32[]{:S(2)}) collective-permute-start(f32[136,512]{1,0:T(8,128)S(1)} %pad_maximum_fusion.1.refs_0_), channel_id=1, source_target_pairs={{0,16},{4,20},{8,24},{12,28},{16,0},{20,4},{24,8},{28,12},{1,17},{... | collective-permute-start | bytes 835592 | tf_op jit(solution)/shard_map/ppermute | solution.py:596
  9.9 4.8 %row_table.1 = (bf16[8,256,512]{2,1,0:T(8,128)(2,1)S(1)}, f32[256,1]{1,0:T(8,128)S(1)}) custom-call(f32[2,16,256]{2,1,0:T(8,128)S(1)} %fusion.row_ref), custom_call_target="tpu_custom_call" | custom-call | flops 100000000 | bytes 262144 | tf_op jit(solution)/shard_map/row_table/pallas_call | solution.py:148
  14.8 3.4 %cover.4.refs_1_ = f32[224,128]{1,0:T(8,128)S(1)} custom-call(bf16[8,256,512]{2,1,0:T(8,128)(2,1)S(1)} %get-tuple-element.150.t_ref, f32[256,1]{1,0:T(8,128)S(1)} %get-tuple-element.151.row_cell_ref, f32[136,512]{1,0:T(8,128)S(1)} %pad_maximum_fusion.1.refs_0_), custom_call_target="tpu_custom_call" | custom-call | flops 100000000 | bytes 262144 | tf_op jit(solution)/shard_map/cover/pallas_call | solution.py:543
  18.2 1.6 %collective-permute-start.6 = (f32[136,512]{1,0:T(8,128)S(1)}, f32[136,512]{1,0:T(8,128)}, u32[]{:S(2)}, u32[]{:S(2)}) collective-permute-start(f32[136,512]{1,0:T(8,128)S(1)} %collective-permute-done.1.refs_2_), channel_id=1, source_target_pairs={{0,4},{4,0},{8,12},{12,8},{16,20},{20,16},{24,28},{28,24},{1,5},{5... | collective-permute-start | bytes 835592 | tf_op jit(solution)/shard_map/ppermute | solution.py:596
  19.8 2.3 %collective-permute-done.refs_1_ = f32[136,512]{1,0:T(8,128)S(1)} collective-permute-done((f32[136,512]{1,0:T(8,128)S(1)}, f32[136,512]{1,0:T(8,128)S(1)}, u32[]{:S(2)}, u32[]{:S(2)}) %collective-permute-start) | collective-permute-done | bytes 278560 | tf_op jit(solution)/shard_map/ppermute | solution.py:596
  22.1 1.2 %fold_products.1 = (f32[32,640]{1,0:T(8,128)S(1)}, f32[32,640]{1,0:T(8,128)S(1)}, f32[32,640]{1,0:T(8,128)S(1)}, f32[32,640]{1,0:T(8,128)S(1)}) custom-call(s32[2]{0:T(128)S(1)} %pad_add_fusion.place_ref, f32[136,512]{1,0:T(8,128)S(1)} %pad_maximum_fusion.1.refs_0_, f32[136,512]{1,0:T(8,128)S(1)} %collective-permute-done.refs_1_, ...), custom_call_target="tpu_custom_call" | custom-call | flops 100000000 | bytes 262144 | tf_op jit(solution)/shard_map/fold_products/pallas_call | solution.py:543
  23.4 1.6 %collective-permute-start.4 = (f32[32,640]{1,0:T(8,128)S(1)}, f32[32,640]{1,0:T(8,128)S(1)}, u32[]{:S(2)}, u32[]{:S(2)}) collective-permute-start(f32[32,640]{1,0:T(8,128)S(1)} %get-tuple-element.107), channel_id=1, source_target_pairs={{0,2},{1,3},{2,0},{3,1},{4,6},{5,7},{6,4},{7,5},{8,10},{9,11},{10,... | collective-permute-start | bytes 245768 | tf_op jit(solution)/shard_map/ppermute | solution.py:596
  25.3 3.4 %lead_cover.1 = (f32[32,640]{1,0:T(8,128)S(1)}, f32[32,512]{1,0:T(8,128)S(1)}, bf16[256,4096]{1,0:T(8,128)(2,1)S(1)}, f32[1,512]{1,0:T(1,128)S(1)}) custom-call(s32[2]{0:T(128)S(1)} %pad_add_fusion.place_ref, bf16[8,256,512]{2,1,0:T(8,128)(2,1)S(1)} %get-tuple-element.150.t_ref, f32[256,1]{1,0:T(8,128)S(1)} %get-tuple-element.151.row_cell_ref, ...), custom_call_target="tpu_custom_call" | custom-call | flops 100000000 | bytes 262144 | tf_op jit(solution)/shard_map/lead_cover/pallas_call | solution.py:543
  28.7 1.1 collective-permute-done.5
  29.8 1.1 collective-permute-start.7
  30.8 1.5 %collective-permute-start.10 = (f32[136,512]{1,0:T(8,128)S(1)}, f32[136,512]{1,0:T(8,128)S(1)}, u32[]{:S(2)}, u32[]{:S(2)}) collective-permute-start(f32[136,512]{1,0:T(8,128)S(1)} %collective-permute-done.refs_1_), channel_id=1, source_target_pairs={{0,4},{4,0},{8,12},{12,8},{16,20},{20,16},{24,28},{28,24},{1,5},{5... | collective-permute-start | bytes 835592 | tf_op jit(solution)/shard_map/ppermute | solution.py:596
  32.3 3.0 %cover.5.refs_2_ = f32[96,384]{1,0:T(8,128)S(1)} custom-call(bf16[8,256,512]{2,1,0:T(8,128)(2,1)S(1)} %get-tuple-element.150.t_ref, f32[256,1]{1,0:T(8,128)S(1)} %get-tuple-element.151.row_cell_ref, bf16[256,4096]{1,0:T(8,128)(2,1)S(1)} %get-tuple-element.129.h_ref, f32[1,512]{1,0:T(1,128)S(1)} %get-tuple-element.130.col_cell_ref), custom_call_target="tpu_custom_call" | custom-call | flops 100000000 | bytes 262144 | tf_op jit(solution)/shard_map/cover/pallas_call | solution.py:543
  35.3 0.6 collective-permute-done.7
  35.9 1.5 %collective-permute-start.11 = (f32[136,512]{1,0:T(8,128)S(1)}, f32[136,512]{1,0:T(8,128)S(1)}, u32[]{:S(2)}, u32[]{:S(2)}) collective-permute-start(f32[136,512]{1,0:T(8,128)S(1)} %collective-permute-done.8.refs_6_.refs_2_), channel_id=1, source_target_pairs={{0,4},{4,0},{8,12},{12,8},{16,20},{20,16},{24,28},{28,24},{1,5},{5... | collective-permute-start | bytes 835592 | tf_op jit(solution)/shard_map/ppermute | solution.py:596
  37.4 0.7 collective-permute-start.9
  38.1 4.0 %cover.6.refs_3_ = f32[128,384]{1,0:T(8,128)S(1)} custom-call(bf16[8,256,512]{2,1,0:T(8,128)(2,1)S(1)} %get-tuple-element.150.t_ref, f32[256,1]{1,0:T(8,128)S(1)} %get-tuple-element.151.row_cell_ref, bf16[256,4096]{1,0:T(8,128)(2,1)S(1)} %get-tuple-element.129.h_ref, f32[1,512]{1,0:T(1,128)S(1)} %get-tuple-element.130.col_cell_ref), custom_call_target="tpu_custom_call" | custom-call | flops 100000000 | bytes 262144 | tf_op jit(solution)/shard_map/cover/pallas_call | solution.py:543
  42.1 3.0 %collective-permute-done.11.refs_7_.refs_3_ = f32[136,512]{1,0:T(8,128)S(1)} collective-permute-done((f32[136,512]{1,0:T(8,128)S(1)}, f32[136,512]{1,0:T(8,128)S(1)}, u32[]{:S(2)}, u32[]{:S(2)}) %collective-permute-start.11) | collective-permute-done | bytes 278560 | tf_op jit(solution)/shard_map/ppermute | solution.py:596
  45.1 1.3 %gather_split.1 = (bf16[1024,512]{1,0:T(8,128)(2,1)S(1)}, bf16[1024,512]{1,0:T(8,128)(2,1)S(1)}) custom-call(s32[2]{0:T(128)S(1)} %pad_add_fusion.place_ref, f32[136,512]{1,0:T(8,128)S(1)} %pad_maximum_fusion.1.refs_0_, f32[136,512]{1,0:T(8,128)S(1)} %collective-permute-done.refs_1_, f32[136,512]{1,0:T(8,128)S(1)} %collective-permute-done.1.refs_2_, ...), custom_call_target="tpu_custom_call" | custom-call | flops 100000000 | bytes 262144 | tf_op jit(solution)/shard_map/gather_split/pallas_call | solution.py:543
  46.4 2.4 %rest_products.2 = f32[2,256,1024]{2,1,0:T(8,128)S(1)} custom-call(s32[2]{0:T(128)S(1)} %pad_add_fusion.place_ref, f32[1024,512]{1,0:T(8,128)S(1)} %copy-done, bf16[1024,512]{1,0:T(8,128)(2,1)S(1)} %get-tuple-element.156.high_ref, bf16[1024,512]{1,0:T(8,128)(2,1)S(1)} %get-tuple-element.157.low_ref), custom_call_target="tpu_custom_call" | custom-call | flops 100000000 | bytes 262144 | tf_op jit(solution)/shard_map/rest_products/pallas_call | solution.py:543
  48.9 0.6 collective-permute-start.16
  49.5 2.5 %collective-permute-start.14 = (f32[4,32,640]{2,1,0:T(8,128)S(1)}, f32[4,32,640]{2,1,0:T(8,128)S(1)}, u32[]{:S(2)}, u32[]{:S(2)}) collective-permute-start(f32[4,32,640]{2,1,0:T(8,128)S(1)} %pad_maximum_fusion.refs_0_), channel_id=1, source_target_pairs={{0,6},{1,7},{2,4},{3,5},{4,2},{5,3},{6,0},{7,1},{8,14},{9,15},{10,... | collective-permute-start | bytes 983048 | tf_op jit(solution)/shard_map/ppermute | solution.py:773
  52.4 0.5 collective-permute-start.12
  53.0 11.7 %cover.7.refs_4_ = f32[256,512]{1,0:T(8,128)S(1)} custom-call(bf16[8,256,512]{2,1,0:T(8,128)(2,1)S(1)} %get-tuple-element.150.t_ref, f32[256,1]{1,0:T(8,128)S(1)} %get-tuple-element.151.row_cell_ref, f32[136,512]{1,0:T(8,128)} %collective-permute-done.6.refs_4_.refs_0_, f32[136,512]{1,0:T(8,128)S(1)} %collective-permute-done.10.refs_5_.refs_1_, ...), custom_call_target="tpu_custom_call" | custom-call | flops 100000000 | bytes 262144 | tf_op jit(solution)/shard_map/cover/pallas_call | solution.py:543
  64.7 2.4 %rest_products.3 = (f32[1,256,1024]{2,1,0:T(8,128)S(1)}, f32[1,256,1024]{2,1,0:T(8,128)S(1)}) custom-call(s32[2]{0:T(128)S(1)} %pad_add_fusion.place_ref, f32[1024,512]{1,0:T(8,128)S(1)} %copy-done, bf16[1024,512]{1,0:T(8,128)(2,1)S(1)} %get-tuple-element.156.high_ref, bf16[1024,512]{1,0:T(8,128)(2,1)S(1)} %get-tuple-element.157.low_ref, ...), custom_call_target="tpu_custom_call" | custom-call | flops 100000000 | bytes 262144 | tf_op jit(solution)/shard_map/rest_products/pallas_call | solution.py:543
  67.8 1.5 %collective-permute-start.17 = (f32[1,256,1024]{2,1,0:T(8,128)S(1)}, f32[1,256,1024]{2,1,0:T(8,128)S(1)}, u32[]{:S(2)}, u32[]{:S(2)}) collective-permute-start(f32[1,256,1024]{2,1,0:T(8,128)S(1)} %get-tuple-element.164), channel_id=1, source_target_pairs={{0,2},{1,3},{2,0},{3,1},{4,6},{5,7},{6,4},{7,5},{8,10},{9,11},{10,... | collective-permute-start | bytes 3145736 | tf_op jit(solution)/shard_map/ppermute | solution.py:596
  69.8 32.3 %factor.1 = (bf16[1024,1024]{1,0:T(8,128)(2,1)S(1)}, bf16[1024,1024]{1,0:T(8,128)(2,1)S(1)}, bf16[1024,128]{1,0:T(8,128)(2,1)S(1)}, bf16[1024,128]{1,0:T(8,128)(2,1)S(1)}) custom-call(s32[2]{0:T(128)S(1)} %pad_add_fusion.place_ref, f32[4,32,640]{2,1,0:T(8,128)S(1)} %pad_maximum_fusion.refs_0_, f32[4,32,640]{2,1,0:T(8,128)S(1)} %collective-permute-done.12.refs_1_, ...), custom_call_target="tpu_custom_call" | custom-call | flops 49999998976 | bytes 8388608 | tf_op jit(solution)/shard_map/factor/pallas_call | solution.py:467
  102.1 4.8 %solve.1 = f32[256,1024]{1,0:T(8,128)} custom-call(s32[2]{0:T(128)S(1)} %pad_add_fusion.place_ref, f32[32,512]{1,0:T(8,128)S(1)} %get-tuple-element.117.refs_0_, f32[224,128]{1,0:T(8,128)S(1)} %cover.4.refs_1_, f32[96,384]{1,0:T(8,128)S(1)} %cover.5.refs_2_, f32[128,384]{1,0:T(8,128)S(1)} %cover.6.refs_3_, f32[256,512]{1,0:T(8,128)S(1)} %cover.7.refs_4_, ...), custom_call_target="tpu_custom_call" | custom-call | flops 100000000 | bytes 262144 | tf_op jit(solution)/shard_map/solve/pallas_call | solution.py:543
  (37 shorter events, 2.4 us)
Async XLA Ops:
  2.8 15.4 %collective-permute-start.1 = (f32[136,512]{1,0:T(8,128)S(1)}, f32[136,512]{1,0:T(8,128)S(1)}, u32[]{:S(2)}, u32[]{:S(2)}) collective-permute-start(f32[136,512]{1,0:T(8,128)S(1)} %pad_maximum_fusion.1.refs_0_), channel_id=1, source_target_pairs={{8,0},{12,4},{4,8},{0,12},{24,16},{28,20},{20,24},{16,28},{9,1},{1... | collective-permute-start | bytes 835592 | tf_op jit(solution)/shard_map/ppermute | solution.py:652
  6.8 13.0 %collective-permute-start.2 = (f32[136,512]{1,0:T(8,128)S(1)}, f32[136,512]{1,0:T(8,128)S(1)}, u32[]{:S(2)}, u32[]{:S(2)}) collective-permute-start(f32[136,512]{1,0:T(8,128)S(1)} %pad_maximum_fusion.1.refs_0_), channel_id=1, source_target_pairs={{4,0},{0,4},{12,8},{8,12},{20,16},{16,20},{28,24},{24,28},{5,1},{1... | collective-permute-start | bytes 835592 | tf_op jit(solution)/shard_map/ppermute | solution.py:652
  7.3 14.7 %collective-permute-start = (f32[136,512]{1,0:T(8,128)S(1)}, f32[136,512]{1,0:T(8,128)S(1)}, u32[]{:S(2)}, u32[]{:S(2)}) collective-permute-start(f32[136,512]{1,0:T(8,128)S(1)} %pad_maximum_fusion.1.refs_0_), channel_id=1, source_target_pairs={{0,16},{4,20},{8,24},{12,28},{16,0},{20,4},{24,8},{28,12},{1,17},{... | collective-permute-start | bytes 835592 | tf_op jit(solution)/shard_map/ppermute | solution.py:596
  18.2 11.6 %collective-permute-start.6 = (f32[136,512]{1,0:T(8,128)S(1)}, f32[136,512]{1,0:T(8,128)}, u32[]{:S(2)}, u32[]{:S(2)}) collective-permute-start(f32[136,512]{1,0:T(8,128)S(1)} %collective-permute-done.1.refs_2_), channel_id=1, source_target_pairs={{0,4},{4,0},{8,12},{12,8},{16,20},{20,16},{24,28},{28,24},{1,5},{5... | collective-permute-start | bytes 835592 | tf_op jit(solution)/shard_map/ppermute | solution.py:596
  23.3 5.3 %collective-permute-start.3 = (f32[32,640]{1,0:T(8,128)S(1)}, f32[32,640]{1,0:T(8,128)S(1)}, u32[]{:S(2)}, u32[]{:S(2)}) collective-permute-start(f32[32,640]{1,0:T(8,128)S(1)} %get-tuple-element.106), channel_id=1, source_target_pairs={{0,1},{1,0},{2,3},{3,2},{4,5},{5,4},{6,7},{7,6},{8,9},{9,8},{10,11... | collective-permute-start | bytes 245768 | tf_op jit(solution)/shard_map/ppermute | solution.py:596
  23.4 5.2 %collective-permute-start.4 = (f32[32,640]{1,0:T(8,128)S(1)}, f32[32,640]{1,0:T(8,128)S(1)}, u32[]{:S(2)}, u32[]{:S(2)}) collective-permute-start(f32[32,640]{1,0:T(8,128)S(1)} %get-tuple-element.107), channel_id=1, source_target_pairs={{0,2},{1,3},{2,0},{3,1},{4,6},{5,7},{6,4},{7,5},{8,10},{9,11},{10,... | collective-permute-start | bytes 245768 | tf_op jit(solution)/shard_map/ppermute | solution.py:596
  25.0 4.7 %collective-permute-start.5 = (f32[32,640]{1,0:T(8,128)S(1)}, f32[32,640]{1,0:T(8,128)S(1)}, u32[]{:S(2)}, u32[]{:S(2)}) collective-permute-start(f32[32,640]{1,0:T(8,128)S(1)} %get-tuple-element.108), channel_id=1, source_target_pairs={{0,3},{1,2},{2,1},{3,0},{4,7},{5,6},{6,5},{7,4},{8,11},{9,10},{10,... | collective-permute-start | bytes 245768 | tf_op jit(solution)/shard_map/ppermute | solution.py:596
  25.3 10.7 %collective-permute-start.8 = (f32[136,512]{1,0:T(8,128)S(1)}, f32[136,512]{1,0:T(8,128)S(1)}, u32[]{:S(2)}, u32[]{:S(2)}) collective-permute-start(f32[136,512]{1,0:T(8,128)S(1)} %collective-permute-done.refs_1_), channel_id=1, source_target_pairs={{0,8},{4,12},{8,0},{12,4},{16,24},{20,28},{24,16},{28,20},{1,9},{5... | collective-permute-start | bytes 835592 | tf_op jit(solution)/shard_map/ppermute | solution.py:596
  29.8 6.2 %collective-permute-start.7 = (f32[1,32,640]{2,1,0:T(8,128)S(1)}, f32[1,32,640]{2,1,0:T(8,128)S(1)}, u32[]{:S(2)}, u32[]{:S(2)}) collective-permute-start(f32[1,32,640]{2,1,0:T(8,128)S(1)} %subtract_bitcast_fusion), channel_id=1, source_target_pairs={{0,8},{4,12},{8,0},{12,4},{16,24},{20,28},{24,16},{28,20},{1,9},{5... | collective-permute-start | bytes 245768 | tf_op jit(solution)/shard_map/ppermute | solution.py:596
  30.8 11.3 %collective-permute-start.10 = (f32[136,512]{1,0:T(8,128)S(1)}, f32[136,512]{1,0:T(8,128)S(1)}, u32[]{:S(2)}, u32[]{:S(2)}) collective-permute-start(f32[136,512]{1,0:T(8,128)S(1)} %collective-permute-done.refs_1_), channel_id=1, source_target_pairs={{0,4},{4,0},{8,12},{12,8},{16,20},{20,16},{24,28},{28,24},{1,5},{5... | collective-permute-start | bytes 835592 | tf_op jit(solution)/shard_map/ppermute | solution.py:596
  35.9 9.2 %collective-permute-start.11 = (f32[136,512]{1,0:T(8,128)S(1)}, f32[136,512]{1,0:T(8,128)S(1)}, u32[]{:S(2)}, u32[]{:S(2)}) collective-permute-start(f32[136,512]{1,0:T(8,128)S(1)} %collective-permute-done.8.refs_6_.refs_2_), channel_id=1, source_target_pairs={{0,4},{4,0},{8,12},{12,8},{16,20},{20,16},{24,28},{28,24},{1,5},{5... | collective-permute-start | bytes 835592 | tf_op jit(solution)/shard_map/ppermute | solution.py:596
  37.4 11.4 %collective-permute-start.9 = (f32[2,32,640]{2,1,0:T(8,128)S(1)}, f32[2,32,640]{2,1,0:T(8,128)S(1)}, u32[]{:S(2)}, u32[]{:S(2)}) collective-permute-start(f32[2,32,640]{2,1,0:T(8,128)S(1)} %pad_maximum_fusion.2), channel_id=1, source_target_pairs={{0,16},{4,20},{8,24},{12,28},{16,0},{20,4},{24,8},{28,12},{1,17},{... | collective-permute-start | bytes 491528 | tf_op jit(solution)/shard_map/ppermute | solution.py:596
  42.1 4.3 %copy-start = (f32[1024,512]{1,0:T(8,128)S(1)}, f32[1024,512]{1,0:T(8,128)}, u32[]{:S(2)}) copy-start(f32[1024,512]{1,0:T(8,128)} %prior_ref.3) | copy-start | bytes 6291460
  48.8 15.9 %collective-permute-start.15 = (f32[2,256,1024]{2,1,0:T(8,128)S(1)}, f32[2,256,1024]{2,1,0:T(8,128)S(1)}, u32[]{:S(2)}, u32[]{:S(2)}) collective-permute-start(f32[2,256,1024]{2,1,0:T(8,128)S(1)} %rest_products.2), channel_id=1, source_target_pairs={{0,1},{1,0},{2,3},{3,2},{4,5},{5,4},{6,7},{7,6},{8,9},{9,8},{10,11... | collective-permute-start | bytes 6291464 | tf_op jit(solution)/shard_map/ppermute | solution.py:596
  48.9 18.2 %collective-permute-start.16 = (f32[4,32,640]{2,1,0:T(8,128)S(1)}, f32[4,32,640]{2,1,0:T(8,128)S(1)}, u32[]{:S(2)}, u32[]{:S(2)}) collective-permute-start(f32[4,32,640]{2,1,0:T(8,128)S(1)} %pad_maximum_fusion.refs_0_), channel_id=1, source_target_pairs={{0,1},{1,0},{2,3},{3,2},{4,5},{5,4},{6,7},{7,6},{8,9},{9,8},{10,11... | collective-permute-start | bytes 983048 | tf_op jit(solution)/shard_map/ppermute | solution.py:596
  49.5 17.6 %collective-permute-start.14 = (f32[4,32,640]{2,1,0:T(8,128)S(1)}, f32[4,32,640]{2,1,0:T(8,128)S(1)}, u32[]{:S(2)}, u32[]{:S(2)}) collective-permute-start(f32[4,32,640]{2,1,0:T(8,128)S(1)} %pad_maximum_fusion.refs_0_), channel_id=1, source_target_pairs={{0,6},{1,7},{2,4},{3,5},{4,2},{5,3},{6,0},{7,1},{8,14},{9,15},{10,... | collective-permute-start | bytes 983048 | tf_op jit(solution)/shard_map/ppermute | solution.py:773
  51.9 15.2 %collective-permute-start.13 = (f32[4,32,640]{2,1,0:T(8,128)S(1)}, f32[4,32,640]{2,1,0:T(8,128)S(1)}, u32[]{:S(2)}, u32[]{:S(2)}) collective-permute-start(f32[4,32,640]{2,1,0:T(8,128)S(1)} %pad_maximum_fusion.refs_0_), channel_id=1, source_target_pairs={{0,2},{1,3},{2,0},{3,1},{4,6},{5,7},{6,4},{7,5},{8,10},{9,11},{10,... | collective-permute-start | bytes 983048 | tf_op jit(solution)/shard_map/ppermute | solution.py:596
  52.4 14.8 %collective-permute-start.12 = (f32[4,32,640]{2,1,0:T(8,128)S(1)}, f32[4,32,640]{2,1,0:T(8,128)S(1)}, u32[]{:S(2)}, u32[]{:S(2)}) collective-permute-start(f32[4,32,640]{2,1,0:T(8,128)S(1)} %pad_maximum_fusion.refs_0_), channel_id=1, source_target_pairs={{0,4},{4,0},{8,12},{12,8},{16,20},{20,16},{24,28},{28,24},{1,5},{5... | collective-permute-start | bytes 983048 | tf_op jit(solution)/shard_map/ppermute | solution.py:596
  67.2 2.1 %collective-permute-start.18 = (f32[4,32,640]{2,1,0:T(8,128)S(1)}, f32[4,32,640]{2,1,0:T(8,128)S(1)}, u32[]{:S(2)}, u32[]{:S(2)}) collective-permute-start(f32[4,32,640]{2,1,0:T(8,128)S(1)} %collective-permute-done.12.refs_1_), channel_id=1, source_target_pairs={{0,1},{1,0},{2,3},{3,2},{4,5},{5,4},{6,7},{7,6},{8,9},{9,8},{10,11... | collective-permute-start | bytes 983048 | tf_op jit(solution)/shard_map/ppermute | solution.py:596
  67.2 2.1 %collective-permute-start.19 = (f32[4,32,640]{2,1,0:T(8,128)S(1)}, f32[4,32,640]{2,1,0:T(8,128)S(1)}, u32[]{:S(2)}, u32[]{:S(2)}) collective-permute-start(f32[4,32,640]{2,1,0:T(8,128)S(1)} %collective-permute-done.13.refs_2_), channel_id=1, source_target_pairs={{0,1},{1,0},{2,3},{3,2},{4,5},{5,4},{6,7},{7,6},{8,9},{9,8},{10,11... | collective-permute-start | bytes 983048 | tf_op jit(solution)/shard_map/ppermute | solution.py:596
  67.7 2.1 %collective-permute-start.20 = (f32[4,32,640]{2,1,0:T(8,128)S(1)}, f32[4,32,640]{2,1,0:T(8,128)S(1)}, u32[]{:S(2)}, u32[]{:S(2)}) collective-permute-start(f32[4,32,640]{2,1,0:T(8,128)S(1)} %collective-permute-done.14.refs_3_), channel_id=1, source_target_pairs={{0,1},{1,0},{2,3},{3,2},{4,5},{5,4},{6,7},{7,6},{8,9},{9,8},{10,11... | collective-permute-start | bytes 983048 | tf_op jit(solution)/shard_map/ppermute | solution.py:596
  67.8 34.3 %collective-permute-start.17 = (f32[1,256,1024]{2,1,0:T(8,128)S(1)}, f32[1,256,1024]{2,1,0:T(8,128)S(1)}, u32[]{:S(2)}, u32[]{:S(2)}) collective-permute-start(f32[1,256,1024]{2,1,0:T(8,128)S(1)} %get-tuple-element.164), channel_id=1, source_target_pairs={{0,2},{1,3},{2,0},{3,1},{4,6},{5,7},{6,4},{7,5},{8,10},{9,11},{10,... | collective-permute-start | bytes 3145736 | tf_op jit(solution)/shard_map/ppermute | solution.py:596
